TPU v7x, 32 devices: a whole 2x2x4 slice. The times are simulated.
32 devices in a mesh: dp: 8 (over y, x, core), band: 4 (over z).
Axes of the slice: x: 2, y: 2, z: 4, core: 2. Of those that a mesh axis runs over, the one named last changes fastest.
Arguments:
- tokens: bfloat16 [24, 580, 768], P('dp', 'band'), may hold values from -6 to 6
- cotangent: bfloat16 [24, 580, 768], P('dp', 'band'), may hold values from -6 to 6
- lengths: int32 [24], P('dp'), may hold values from 257 to 577, as said below
- slot_of_block: int32 [864], replicated, may hold values from 0 to 863, as said below
- master: float32 [864, 128, 128], P('dp')
- statistics: float32 [864, 2, 128, 128], P('dp')
- inverse_roots: float32 [864, 2, 128, 128], P('dp')
- gain_values: float32 [4, 768], replicated, may hold values from 0.5 to 1.5
- gain_moments: float32 [4, 768], replicated, may hold values from 7.0627216e-08 to 1.1300355e-06
Outputs:
- layer_output: bfloat16 [24, 580, 768], P('dp', 'band')
- input_grad: bfloat16 [24, 580, 768], P('dp', 'band')
- weight_grads: float32 [864, 128, 128], P('dp')
- grad_norm: float32 [], replicated
- new_statistics: float32 [864, 2, 128, 128], P('dp')
- new_master: float32 [864, 128, 128], P('dp')
- master_copy: bfloat16 [864, 128, 128], P('dp')
- gain_grads: float32 [4, 768], replicated
- new_moments: float32 [4, 768], replicated
- new_gains: float32 [4, 768], replicated
Inputs may be any that keep to these rules, and one draw needn't show every extreme that they name: `lengths`: each image holds 257 or 577 tokens; each aligned run of 3 images holds one of 577 or more. `slot_of_block`: distinct slots; slots 0 and 863 are always used.
All inputs are finite; a program needn't handle non-finite values.
Results may differ from a plain program's by a relative error of at most 0.02.
Values may be sent and summed in bfloat16 or wider, within the bound.
No kernel may reach another device: no remote copies, remote signals or barrier semaphores. Data moves between devices by JAX's collectives and lax.ppermute only.
A program may use at most 384 MiB of HBM per device.

v0:
```python
import jax
import jax.numpy as jnp
from jax import lax
from jax.sharding import PartitionSpec as P

D = 768
HEADS = 12
HEAD_DIM = 64
FF = 2048
LAYERS = 2
BLOCK = 128


epsilon = 1e-05
rope_base = 10000.0
decay_rate = 0.5
step_rate = 0.4
gain_rate = 0.2
clip_limit = 1.0
masked_score = -1e30
highest = lax.Precision.HIGHEST


def matrix_shapes():
    return [(D, 3 * D), (D, D), (D, 2 * FF), (FF, D)]


def assemble(blocks):
    layers_out = []
    offset = 0
    for layer_index in range(LAYERS):
        matrices = []
        for rows_all, cols_all in matrix_shapes():
            block_count = rows_all // BLOCK * (cols_all // BLOCK)
            block_view = blocks[offset : offset + block_count].reshape(
                rows_all // BLOCK, cols_all // BLOCK, BLOCK, BLOCK
            )
            matrices.append(block_view.transpose(0, 2, 1, 3).reshape(rows_all, cols_all))
            offset = offset + block_count
        layers_out.append(matrices)
    return layers_out


def disassemble(layers_in):
    tiled_parts = []
    for matrices in layers_in:
        for matrix in matrices:
            rows_all, cols_all = matrix.shape
            tiled = matrix.reshape(rows_all // BLOCK, BLOCK, cols_all // BLOCK, BLOCK).transpose(
                0, 2, 1, 3
            )
            tiled_parts.append(tiled.reshape(-1, BLOCK, BLOCK))
    return jnp.concatenate(tiled_parts, 0)


def rope_tables(positions):
    half_dim = HEAD_DIM // 2
    frequency = rope_base ** (-(jnp.arange(half_dim, dtype=jnp.float32) * 2.0 / HEAD_DIM))
    angles = positions.astype(jnp.float32)[:, None] * frequency[None, :]
    return (jnp.cos(angles), jnp.sin(angles))


def rotate(values, cosine_table, sine_table):
    half_dim = HEAD_DIM // 2
    first_half = values[..., :half_dim]
    second_half = values[..., half_dim:]
    cosine = cosine_table[:, None, :]
    sine_part = sine_table[:, None, :]
    return jnp.concatenate(
        [
            first_half * cosine - second_half * sine_part,
            second_half * cosine + first_half * sine_part,
        ],
        -1,
    )


def rotate_back(values, cosine_table, sine_table):
    half_dim = HEAD_DIM // 2
    first_half = values[..., :half_dim]
    second_half = values[..., half_dim:]
    cosine = cosine_table[:, None, :]
    sine_part = sine_table[:, None, :]
    return jnp.concatenate(
        [
            first_half * cosine + second_half * sine_part,
            second_half * cosine - first_half * sine_part,
        ],
        -1,
    )


def rms_scale(hidden, gain):
    return hidden * lax.rsqrt(jnp.mean(hidden * hidden, -1, keepdims=True) + epsilon) * gain


def gated(gate_up):
    return jax.nn.silu(gate_up[..., :FF]) * gate_up[..., FF:]


def shampoo_stats(statistics, grad_tiles):
    left_new = jnp.einsum("sij,skj->sik", grad_tiles, grad_tiles, precision=highest)
    right_new = jnp.einsum("sji,sjk->sik", grad_tiles, grad_tiles, precision=highest)
    return decay_rate * statistics + (1.0 - decay_rate) * jnp.stack([left_new, right_new], 1)


def precondition(root_pair, grad_tiles):
    left_applied = jnp.einsum("sij,sjk->sik", root_pair[:, 0], grad_tiles, precision=highest)
    return jnp.einsum("sij,sjk->sik", left_applied, root_pair[:, 1], precision=highest)


def masked_scores(queries, key_heads, allowed):
    scores = jnp.einsum(
        "gqhe,gkhe->ghqk", queries, key_heads, preferred_element_type=jnp.float32
    ) * HEAD_DIM ** (-0.5)
    return jnp.where(allowed, scores, masked_score)


def shards(
    tokens,
    cotangent,
    lengths,
    slot_of_block,
    master,
    statistics,
    inverse_roots,
    gain_values,
    gain_moments,
):
    images, band_rows, model_width = tokens.shape
    band_index = lax.axis_index("band")
    whole_rows = band_rows * lax.axis_size("band")
    gathered = lax.all_gather(master.astype(jnp.bfloat16), "dp", axis=0, tiled=True)
    weights = assemble(gathered[slot_of_block])
    query_pos = band_index * band_rows + jnp.arange(band_rows, dtype=jnp.int32)
    key_pos = jnp.arange(whole_rows, dtype=jnp.int32)
    cosine_table, sine_table = rope_tables(query_pos)
    allowed = (key_pos[None, None, None, :] <= query_pos[None, None, :, None]) & (
        key_pos[None, None, None, :] < lengths[:, None, None, None]
    )
    valid = (query_pos[None, :] < lengths[:, None]).astype(jnp.float32)
    hidden = tokens.astype(jnp.float32)
    saved = []
    for layer_index in range(LAYERS):
        w_qkv, w_out, w_gate_up, w_down = weights[layer_index]
        gain_pair = gain_values[2 * layer_index : 2 * layer_index + 2]
        normed = rms_scale(hidden, gain_pair[0]).astype(jnp.bfloat16)
        projected = jnp.einsum("gsd,de->gse", normed, w_qkv, preferred_element_type=jnp.float32)
        shaped = projected.reshape(images, band_rows, 3, HEADS, HEAD_DIM)
        queries = rotate(shaped[:, :, 0], cosine_table, sine_table).astype(jnp.bfloat16)
        key_rows = (
            rotate(shaped[:, :, 1], cosine_table, sine_table)
            .astype(jnp.bfloat16)
            .reshape(images, band_rows, model_width)
        )
        value_rows = shaped[:, :, 2].astype(jnp.bfloat16).reshape(images, band_rows, model_width)
        key_whole, value_whole = (
            lax.all_gather(key_rows, "band", axis=1, tiled=True),
            lax.all_gather(value_rows, "band", axis=1, tiled=True),
        )
        key_heads = key_whole.reshape(images, whole_rows, HEADS, HEAD_DIM)
        value_heads = value_whole.reshape(images, whole_rows, HEADS, HEAD_DIM)
        scores = masked_scores(queries, key_heads, allowed)
        row_top = jnp.max(scores, -1, keepdims=True)
        exp_scores = jnp.where(allowed, jnp.exp(scores - row_top), 0.0)
        row_total = jnp.sum(exp_scores, -1, keepdims=True)
        probabilities = (exp_scores / row_total).astype(jnp.bfloat16)
        mixed_heads = jnp.einsum(
            "ghqk,gkhe->gqhe", probabilities, value_heads, preferred_element_type=jnp.float32
        )
        mixed_heads = mixed_heads.astype(jnp.bfloat16).reshape(images, band_rows, model_width)
        middle = hidden + jnp.einsum(
            "gsd,de->gse", mixed_heads, w_out, preferred_element_type=jnp.float32
        )
        normed_two = rms_scale(middle, gain_pair[1]).astype(jnp.bfloat16)
        gate_up = jnp.einsum(
            "gsd,de->gse", normed_two, w_gate_up, preferred_element_type=jnp.float32
        )
        activated = gated(gate_up).astype(jnp.bfloat16)
        stored_keys = (key_rows, value_rows)
        saved.append(
            (
                hidden,
                normed,
                queries,
                stored_keys,
                row_top,
                row_total,
                mixed_heads,
                middle,
                normed_two,
                gate_up,
                activated,
            )
        )
        hidden = middle + jnp.einsum(
            "gsf,fd->gsd", activated, w_down, preferred_element_type=jnp.float32
        )
    layer_output = hidden.astype(jnp.bfloat16)
    back = cotangent.astype(jnp.float32) * valid[:, :, None]
    weight_parts = [None] * LAYERS
    gain_parts = [None] * (2 * LAYERS)
    scale_factor = HEAD_DIM ** (-0.5)
    for layer_index in range(LAYERS - 1, -1, -1):
        (
            hidden_in,
            normed,
            queries,
            stored_keys,
            row_top,
            row_total,
            mixed_heads,
            middle,
            normed_two,
            gate_up,
            activated,
        ) = saved[layer_index]
        w_qkv, w_out, w_gate_up, w_down = weights[layer_index]
        gain_pair = gain_values[2 * layer_index : 2 * layer_index + 2]
        back_ffn = back.astype(jnp.bfloat16)
        grad_down = jnp.einsum(
            "gsf,gsd->fd", activated, back_ffn, preferred_element_type=jnp.float32
        )
        back_act = jnp.einsum("gsd,fd->gsf", back_ffn, w_down, preferred_element_type=jnp.float32)
        gate_value, gate_pull = jax.vjp(gated, gate_up)
        back_gate_up = gate_pull(back_act)[0].astype(jnp.bfloat16)
        grad_gate_up = jnp.einsum(
            "gsd,gse->de", normed_two, back_gate_up, preferred_element_type=jnp.float32
        )
        back_normed_two = jnp.einsum(
            "gse,de->gsd", back_gate_up, w_gate_up, preferred_element_type=jnp.float32
        )
        norm_value, norm_pull = jax.vjp(rms_scale, middle, gain_pair[1])
        back_from_norm, gain_second = norm_pull(back_normed_two)
        back_middle = back + back_from_norm
        back_attn = back_middle.astype(jnp.bfloat16)
        grad_out = jnp.einsum(
            "gsd,gse->de", mixed_heads, back_attn, preferred_element_type=jnp.float32
        )
        back_mixed = jnp.einsum("gse,de->gsd", back_attn, w_out, preferred_element_type=jnp.float32)
        back_mixed = back_mixed.astype(jnp.bfloat16).reshape(images, band_rows, HEADS, HEAD_DIM)
        key_whole, value_whole = (
            lax.all_gather(stored_keys[0], "band", axis=1, tiled=True),
            lax.all_gather(stored_keys[1], "band", axis=1, tiled=True),
        )
        key_heads = key_whole.reshape(images, whole_rows, HEADS, HEAD_DIM)
        value_heads = value_whole.reshape(images, whole_rows, HEADS, HEAD_DIM)
        scores = masked_scores(queries, key_heads, allowed)
        soft = jnp.where(allowed, jnp.exp(scores - row_top), 0.0) / row_total
        probabilities = soft.astype(jnp.bfloat16)
        back_probs = jnp.einsum(
            "gqhe,gkhe->ghqk", back_mixed, value_heads, preferred_element_type=jnp.float32
        )
        row_dot = jnp.sum(soft * back_probs, -1, keepdims=True)
        back_scores = (soft * (back_probs - row_dot)).astype(jnp.bfloat16)
        back_queries = (
            jnp.einsum(
                "ghqk,gkhe->gqhe", back_scores, key_heads, preferred_element_type=jnp.float32
            )
            * scale_factor
        )
        grad_value = jnp.einsum(
            "ghqk,gqhe->gkhe", probabilities, back_mixed, preferred_element_type=jnp.float32
        )
        grad_key = (
            jnp.einsum("ghqk,gqhe->gkhe", back_scores, queries, preferred_element_type=jnp.float32)
            * scale_factor
        )
        back_keys, back_values = (
            lax.psum_scatter(
                grad_key.reshape(images, whole_rows, model_width).astype(jnp.bfloat16),
                "band",
                scatter_dimension=1,
                tiled=True,
            ).astype(jnp.float32),
            lax.psum_scatter(
                grad_value.reshape(images, whole_rows, model_width).astype(jnp.bfloat16),
                "band",
                scatter_dimension=1,
                tiled=True,
            ).astype(jnp.float32),
        )
        back_projected = jnp.stack(
            [
                rotate_back(back_queries, cosine_table, sine_table),
                rotate_back(
                    back_keys.reshape(images, band_rows, HEADS, HEAD_DIM), cosine_table, sine_table
                ),
                back_values.reshape(images, band_rows, HEADS, HEAD_DIM),
            ],
            2,
        )
        back_projected = back_projected.reshape(images, band_rows, 3 * model_width).astype(
            jnp.bfloat16
        )
        grad_qkv = jnp.einsum(
            "gsd,gse->de", normed, back_projected, preferred_element_type=jnp.float32
        )
        back_normed = jnp.einsum(
            "gse,de->gsd", back_projected, w_qkv, preferred_element_type=jnp.float32
        )
        norm_value, norm_pull = jax.vjp(rms_scale, hidden_in, gain_pair[0])
        back_from_input, gain_first = norm_pull(back_normed)
        back = back_middle + back_from_input
        weight_parts[layer_index] = [grad_qkv, grad_out, grad_gate_up, grad_down]
        gain_parts[2 * layer_index] = gain_first
        gain_parts[2 * layer_index + 1] = gain_second
    input_grad = back.astype(jnp.bfloat16)
    local_tiles = disassemble(weight_parts)
    slot_layout = (
        jnp.zeros((gathered.shape[0], BLOCK, BLOCK), jnp.float32).at[slot_of_block].set(local_tiles)
    )
    owned = lax.psum_scatter(slot_layout, "dp", scatter_dimension=0, tiled=True)
    owned = lax.psum(owned.astype(jnp.bfloat16), "band").astype(jnp.float32)
    gain_total = lax.psum(jnp.stack(gain_parts, 0), ("dp", "band"))
    owned_squares = lax.psum(jnp.sum(owned * owned), "dp")
    grad_norm = jnp.sqrt(owned_squares + jnp.sum(gain_total * gain_total))
    factor = jnp.minimum(1.0, clip_limit / grad_norm)
    weight_grads = owned * factor
    new_statistics = shampoo_stats(statistics, weight_grads)
    new_master = master - step_rate * precondition(inverse_roots, weight_grads)
    gain_grads = gain_total * factor
    new_moments = decay_rate * gain_moments + (1.0 - decay_rate) * gain_grads * gain_grads
    new_gains = gain_values - gain_rate * gain_grads / (jnp.sqrt(new_moments) + epsilon)
    return (
        layer_output,
        input_grad,
        weight_grads,
        grad_norm,
        new_statistics,
        new_master,
        new_master.astype(jnp.bfloat16),
        gain_grads,
        new_moments,
        new_gains,
    )


def solution(mesh):
    return jax.shard_map(
        shards,
        mesh=mesh,
        in_specs=(
            P("dp", "band", None),
            P("dp", "band", None),
            P("dp"),
            P(),
            P("dp", None, None),
            P("dp", None, None, None),
            P("dp", None, None, None),
            P(),
            P(),
        ),
        out_specs=(
            P("dp", "band", None),
            P("dp", "band", None),
            P("dp", None, None),
            P(),
            P("dp", None, None, None),
            P("dp", None, None),
            P("dp", None, None),
            P(),
            P(),
            P(),
        ),
        check_vma=False,
    )
```

profile of v0, /device:TPU:16, one launch (start us, length us, event | category | flops | bytes accessed | tf_op | source)
XLA Modules:
  0.0 2022.5 jit_solution(8086009466033957382)
XLA Ops:
  15.8 136.9 %all-gather.6.cloned.1.call-done = bf16[864,128,128]{2,1,0:T(8,128)(2,1)} async-done(((bf16[108,128,128]{2,1,0:T(8,128)(2,1)}), bf16[864,128,128]{2,1,0:T(8,128)(2,1)}) %all-gather.6.cloned.1.call-update) | async-done | bytes 28311568 | tf_op jit(solution)/shard_map/all_gather | solution.py:133
  152.7 30.7 %gather_fusion = bf16[864,128,128]{2,1,0:T(8,128)(2,1)} fusion(bf16[864,128,128]{2,1,0:T(8,128)(2,1)} %all-gather.6.cloned.1.call-done, s32[1024]{0:T(1024)S(1)} %pad_clamp_fusion), kind=kCustom, calls=%fused_computation | custom fusion | bytes 56626560 | tf_op jit(solution)/shard_map/gather | solution.py:134
  258.0 10.3 reshape.506
  289.3 23.0 %fusion.137 = (f32[3,12,145]{2,1,0:T(8,128)}, f32[3,12,145,580]{3,2,1,0:T(8,128)}) fusion(pred[3,145,580]{2,1,0:T(8,128)(4,1)} %broadcast_and_fusion, bf16[3,580,12,64]{1,3,2,0:T(8,128)(2,1)S(1)} %bitcast.378, bf16[3,145,12,32]{1,3,2,0:T(8,128)(2,1)} %get-tuple-element.117, bf16[3,145,12,32]{1,3,2,0:T(8,128)(2,1)S(1)} %copy-done.48), kind=kOutput, calls=%fused_computation.264 | convolution fusion | flops 404007648 | bytes 15724380 | tf_op jit(solution)/shard_map/sub | solution.py:165
  312.3 41.1 %all-gather.8.cloned.1.call-done = bf16[3,580,768]{2,0,1:T(4,128)(2,1)} async-done(((bf16[3,145,768]{2,0,1:T(4,128)(2,1)}), bf16[3,580,768]{2,0,1:T(4,128)(2,1)}) %all-gather.8.cloned.1.call-update) | async-done | bytes 2672656 | tf_op jit(solution)/shard_map/all_gather | solution.py:159
  415.9 10.3 reshape.511
  426.2 34.5 %all-gather.14.cloned.1.call-done = bf16[3,580,768]{2,0,1:T(4,128)(2,1)} async-done(((bf16[3,145,768]{2,0,1:T(4,128)(2,1)}), bf16[3,580,768]{2,0,1:T(4,128)(2,1)}) %all-gather.14.cloned.1.call-update) | async-done | bytes 2672656 | tf_op jit(solution)/shard_map/all_gather | solution.py:158
  467.2 12.4 fusion.138
  479.6 51.5 %all-gather.12.cloned.1.call-done = bf16[3,580,768]{2,0,1:T(4,128)(2,1)} async-done(((bf16[3,145,768]{2,0,1:T(4,128)(2,1)}), bf16[3,580,768]{2,0,1:T(4,128)(2,1)}) %all-gather.12.cloned.1.call-update) | async-done | bytes 2672656 | tf_op jit(solution)/shard_map/all_gather | solution.py:159
  648.6 12.4 copy.359
  666.9 196.7 %all-reduce.18.cloned.1.call-done = (bf16[3,580,768]{2,0,1:T(4,128)(2,1)}, bf16[3,580,768]{2,0,1:T(4,128)(2,1)}) async-done(((bf16[3,580,768]{2,0,1:T(4,128)(2,1)}, bf16[3,580,768]{2,0,1:T(4,128)(2,1)}), (bf16[3,580,768]{2,0,1:T(4,128)(2,1)}, bf16[3,580,768]{2,0,1:T(4,128)(2,1)})) %all-reduce.18.cloned.1.call-update) | async-done | bytes 5345296
  913.9 10.3 multiply_reduce_fusion
  932.0 10.3 multiply_convert_fusion
  954.3 12.4 bitcast_bitcast_fusion
  966.6 16.4 copy.297
  1032.6 12.1 copy.357
  1044.7 12.4 bitcast_bitcast_fusion.1
  1057.0 17.0 copy.288
  1084.3 119.3 %all-reduce.16.cloned.1.call-done = (bf16[3,580,768]{2,0,1:T(4,128)(2,1)}, bf16[3,580,768]{2,0,1:T(4,128)(2,1)}) async-done(((bf16[3,580,768]{2,0,1:T(4,128)(2,1)}, bf16[3,580,768]{2,0,1:T(4,128)(2,1)}), (bf16[3,580,768]{2,0,1:T(4,128)(2,1)}, bf16[3,580,768]{2,0,1:T(4,128)(2,1)})) %all-reduce.16.cloned.1.call-update) | async-done | bytes 5345296
  1240.7 11.8 constant_dynamic-update-slice_fusion.5
  1264.2 11.8 constant_dynamic-update-slice_fusion.1
  1279.1 18.1 broadcast_in_dim.92
  1297.2 155.8 %scatter_fusion = f32[864,128,128]{2,1,0:T(8,128)} fusion(f32[864,128,128]{2,1,0:T(8,128)} %broadcast_in_dim.92, s32[864]{0:T(1024)S(1)} %copy-done.76, f32[864,128,128]{2,1,0:T(8,128)} %constant_dynamic-update-slice_fusion), kind=kCustom, calls=%fused_computation.1 | custom fusion | bytes 169872768 | tf_op jit(solution)/shard_map/scatter | solution.py:311
  1453.1 318.5 %reduce-scatter.2.cloned.1.call-done = f32[108,128,128]{2,1,0:T(8,128)} async-done(((f32[864,128,128]{2,1,0:T(8,128)}), f32[108,128,128]{2,1,0:T(8,128)}) %reduce-scatter.2.cloned.1.call-update) | async-done | bytes 7077904 | tf_op jit(solution)/shard_map/reduce_scatter | solution.py:313
  1783.7 44.5 %psum.23 = f32[4,768]{1,0:T(4,128)S(1)} all-reduce(f32[4,768]{1,0:T(4,128)S(1)} %pad_maximum_fusion.18), channel_id=1, replica_groups=mesh['dp'=8,'band'=4] {'dp','band'}, use_global_device_ids=true, to_apply=%region_27.28 | all-reduce | flops 3072 | bytes 24576 | tf_op jit(solution)/shard_map/psum | solution.py:315
  1828.2 82.9 %all-reduce.14.cloned.1.call-done = bf16[108,128,128]{2,1,0:T(8,128)(2,1)} async-done(((bf16[108,128,128]{2,1,0:T(8,128)(2,1)}), bf16[108,128,128]{2,1,0:T(8,128)(2,1)}) %all-reduce.14.cloned.1.call-update) | async-done | bytes 3538960 | tf_op jit(solution)/shard_map/psum | solution.py:314
  1916.3 14.5 psum.22
  1933.1 14.1 convolution_bitcast_fusion.2
  1947.3 16.8 convolution_bitcast_fusion.3
  1975.0 12.0 fusion.139
  1987.0 14.6 fusion.2
  2001.5 12.9 copy.306
  (420 shorter events, 505.4 us)
Async XLA Ops:
  7.2 145.5 %all-gather.6.cloned.1.call-start = ((), (), s32[]{:S(2)}) async-start(), calls=%async_computation.1 | async-start | bytes 31850496 | tf_op jit(solution)/shard_map/all_gather | solution.py:133
  12.9 270.0 %all-gather.10.cloned.1.call-start = ((), (), s32[]{:S(2)}) async-start(), calls=%async_computation.3 | async-start | bytes 4454400 | tf_op jit(solution)/shard_map/all_gather | solution.py:158
  14.7 184.8 %copy-start.79 = (f32[768]{0:T(1024)}, f32[768]{0:T(1024)S(1)}, u32[]{:S(2)}) copy-start(f32[768]{0:T(1024)S(1)} %get-tuple-element.71) | copy-start | bytes 9220
  14.7 356.3 %copy-start.63 = (f32[768]{0:T(1024)}, f32[768]{0:T(1024)S(1)}, u32[]{:S(2)}) copy-start(f32[768]{0:T(1024)S(1)} %get-tuple-element.70) | copy-start | bytes 9220
  14.7 365.7 %copy-start.81 = (f32[768]{0:T(1024)}, f32[768]{0:T(1024)S(1)}, u32[]{:S(2)}) copy-start(f32[768]{0:T(1024)S(1)} %get-tuple-element.69) | copy-start | bytes 9220
  15.0 137.7 %copy-start.77 = (f32[3,145]{1,0:T(4,128)}, f32[3,145]{1,0:T(4,128)S(1)}, u32[]{:S(2)}) copy-start(f32[3,145]{1,0:T(4,128)S(1)} %fusion.67) | copy-start | bytes 5224
  15.0 184.6 %copy-start.83 = (f32[3,145]{1,0:T(4,128)}, f32[3,145]{1,0:T(4,128)S(1)}, u32[]{:S(2)}) copy-start(f32[3,145]{1,0:T(4,128)S(1)} %fusion.107) | copy-start | bytes 5224
  213.7 139.8 %all-gather.8.cloned.1.call-start = ((), (), s32[]{:S(2)}) async-start(), calls=%async_computation.2 | async-start | bytes 4454400 | tf_op jit(solution)/shard_map/all_gather | solution.py:159
  219.1 241.6 %all-gather.14.cloned.1.call-start = ((), (), s32[]{:S(2)}) async-start(), calls=%async_computation.5 | async-start | bytes 4454400 | tf_op jit(solution)/shard_map/all_gather | solution.py:158
  289.3 23.0 %copy-start.8 = (bf16[3,580,768]{1,2,0:T(8,128)(2,1)}, bf16[3,580,768]{1,2,0:T(8,128)(2,1)S(1)}, u32[]{:S(2)}) copy-start(bf16[3,580,768]{1,2,0:T(8,128)(2,1)S(1)} %copy.243) | copy-start | bytes 8017924
  312.3 48.7 %copy-start.72 = (f32[3,12,145]{2,1,0:T(8,128)S(1)}, f32[3,12,145]{2,1,0:T(8,128)}, u32[]{:S(2)}) copy-start(f32[3,12,145]{2,1,0:T(8,128)} %get-tuple-element.134) | copy-start | bytes 62644
  353.4 17.7 slice-start.6
  391.6 139.6 %all-gather.12.cloned.1.call-start = ((), (), s32[]{:S(2)}) async-start(), calls=%async_computation.4 | async-start | bytes 4454400 | tf_op jit(solution)/shard_map/all_gather | solution.py:159
  395.1 468.5 %all-reduce.18.cloned.1.call-start = ((), (), s32[]{:S(2)}) async-start(), calls=%async_computation.9 | async-start | bytes 14254080
  426.2 41.0 %copy-start.51 = (bf16[3,145,12,32]{1,3,2,0:T(8,128)(2,1)S(1)}, bf16[3,145,12,32]{1,3,2,0:T(8,128)(2,1)}, u32[]{:S(2)}) copy-start(bf16[3,145,12,32]{1,3,2,0:T(8,128)(2,1)} %get-tuple-element.112) | copy-start | bytes 1002244
  479.6 59.3 %copy-start.74 = (f32[3,12,145]{2,1,0:T(8,128)S(1)}, f32[3,12,145]{2,1,0:T(8,128)}, u32[]{:S(2)}) copy-start(f32[3,12,145]{2,1,0:T(8,128)} %get-tuple-element.140) | copy-start | bytes 62644
  531.2 20.4 %slice-start.14 = ((s8[6291456]{0:T(1024)(128)(4,1)}), s8[2097152]{0:T(1024)(128)(4,1)S(1)}, s32[]{:S(2)}) async-start(s8[6291456]{0:T(1024)(128)(4,1)} %bitcast.370), calls=%async_computation.24 | async-start | bytes 4194304
  551.5 87.3 %copy-start.6 = (f32[3,145,768]{2,1,0:T(8,128)}, f32[3,145,768]{2,1,0:T(8,128)S(1)}, u32[]{:S(2)}) copy-start(f32[3,145,768]{2,1,0:T(8,128)S(1)} %get-tuple-element.143) | copy-start | bytes 4008964
  614.0 589.6 %all-reduce.16.cloned.1.call-start = ((), (), s32[]{:S(2)}) async-start(), calls=%async_computation.8 | async-start | bytes 14254080
  953.8 817.8 %reduce-scatter.2.cloned.1.call-start = ((), (), s32[]{:S(2)}) async-start(), calls=%async_computation.6 | async-start | bytes 63700992 | tf_op jit(solution)/shard_map/reduce_scatter | solution.py:313
  966.6 16.4 copy-start.69
  966.6 16.4 copy-start.92
  966.6 16.4 copy-start.101
  1057.0 17.1 copy-start.43
  1057.0 17.1 copy-start.44
  1279.1 18.1 copy-start.76
  1453.0 458.1 %all-reduce.14.cloned.1.call-start = ((), (), s32[]{:S(2)}) async-start(), calls=%async_computation.7 | async-start | bytes 7077888 | tf_op jit(solution)/shard_map/psum | solution.py:314
  1911.1 21.0 %copy-start.12 = (bf16[108,128,128]{2,1,0:T(8,128)(2,1)S(1)}, bf16[108,128,128]{2,1,0:T(8,128)(2,1)}, u32[]{:S(2)}) copy-start(bf16[108,128,128]{2,1,0:T(8,128)(2,1)} %all-reduce.14.cloned.1.call-done) | copy-start | bytes 10616836
  1933.1 31.6 %copy-start = (f32[108,128,128]{2,1,0:T(8,128)}, f32[108,128,128]{2,1,0:T(8,128)S(1)}, u32[]{:S(2)}) copy-start(f32[108,128,128]{2,1,0:T(8,128)S(1)} %convert_multiply_fusion) | copy-start | bytes 21233668
  1947.2 16.8 copy-start.71
  1947.2 16.8 copy-start.93
  1947.3 27.7 %slice-start.4 = ((s8[7077888]{0:T(1024)(128)(4,1)}), s8[4194304]{0:T(1024)(128)(4,1)S(1)}, s32[]{:S(2)}) async-start(s8[7077888]{0:T(1024)(128)(4,1)} %bitcast.358), calls=%async_computation.14 | async-start | bytes 8388608
  (96 other events, 505.4 us)
Sparse Core Ops, SparseCore 0:
  13.0 139.6 all-gather.5
  213.8 68.9 all-gather.9
  284.4 68.9 all-gather.7
  391.7 68.9 all-gather.13
  462.1 68.9 all-gather.11
  614.1 249.4 all-reduce.17
  953.9 249.6 all-reduce.15
  1453.1 318.4 reduce-scatter.1
  1777.4 133.7 all-reduce.13
where the time goes:
time: 2040 us; the launch traced here: 2020 us
  waiting for transfers between devices  988 us (48%)
  local copies, waits for them, and re-layouts  618 us (30%)
  matrix products  258 us (13%)
  other arithmetic  80.5 us (4%)
  blocking collectives  59 us (3%)
    reduce_scatter x1, waiting for transfers between devices, shards(): owned = lax.psum_scatter(slot_layout, 'dp', scatter_dimension=0, tiled=True)  319 us
    unnamed x11, waiting for transfers between devices  316 us
    scatter x1, local copies, waits for them, and re-layouts, shards(): jnp.zeros((gathered.shape[0], BLOCK, BLOCK), jnp.float32).at[slot_of_block]  156 us
    all_gather x1, waiting for transfers between devices, shards(): lax.all_gather(master.astype(jnp.bfloat16), 'dp', axis=0, tiled=True)  137 us
    unnamed x257, local copies, waits for them, and re-layouts  117 us
    all_gather x2, waiting for transfers between devices, shards(): lax.all_gather(value_rows, 'band', axis=1, tiled=True)  92.7 us
    psum x1, waiting for transfers between devices, shards(): owned = lax.psum(owned.astype(jnp.bfloat16), 'band').astype(jnp.float32)  82.9 us
    transpose x6, local copies, waits for them, and re-layouts, disassemble(): matrix.reshape(rows_all // BLOCK, BLOCK, cols_all // BLOCK, BLOCK)  71.5 us
  transfers between devices with their start and end apart: 9, of which 9 were waited for; matrix products, arithmetic and copies ran while one was open for 16% of the time, Pallas kernels for 0%

commit v1 on v0

v1 whole, which is shorter than its diff:
```python
import functools

import jax
import jax.numpy as jnp
from jax import lax
from jax.experimental import pallas as pl
from jax.experimental.pallas import tpu as pltpu
from jax.sharding import PartitionSpec as P

D = 768
HEADS = 12
HEAD_DIM = 64
FF = 2048
LAYERS = 2
BLOCK = 128
PAIR = 2 * HEAD_DIM

epsilon = 1e-05
rope_base = 10000.0
decay_rate = 0.5
step_rate = 0.4
gain_rate = 0.2
clip_limit = 1.0
masked_score = -1e30
VMEM_BYTES = 62 * 2**20

f32 = jnp.float32
bf16 = jnp.bfloat16

GRIDS = [
    (D // BLOCK, 3 * D // BLOCK),
    (D // BLOCK, D // BLOCK),
    (D // BLOCK, 2 * FF // BLOCK),
    (FF // BLOCK, D // BLOCK),
]
COUNTS = [r * c for r, c in GRIDS]
OFFSETS = [sum(COUNTS[:i]) for i in range(4)]
PER_LAYER = sum(COUNTS)
FF_STEP = 512


def round_up(n, m):
    return -(-n // m) * m


def nn(a, b):
    return lax.dot_general(a, b, (((1,), (0,)), ((), ())), preferred_element_type=f32)


def nt(a, b):
    return lax.dot_general(a, b, (((1,), (1,)), ((), ())), preferred_element_type=f32)


def tn(a, b):
    return lax.dot_general(a, b, (((0,), (0,)), ((), ())), preferred_element_type=f32)


def query_blocks(rows, step=256):
    return [(s, min(s + step, rows)) for s in range(0, rows, step)]


def swap_halves(t):
    lane = lax.broadcasted_iota(jnp.int32, t.shape, 1)
    half = HEAD_DIM // 2
    return jnp.where(lane % HEAD_DIM < half, pltpu.roll(t, PAIR - half, 1), pltpu.roll(t, half, 1))


def rms(m):
    return lax.rsqrt(jnp.mean(m * m, -1, keepdims=True) + epsilon)


def rms_back(u, m, g):
    r = rms(m)
    t = u * g
    dot = jnp.mean(t * m, -1, keepdims=True)
    return r * t - m * (r * r * r * dot), jnp.sum(u * m * r, 0, keepdims=True)


def forward_kernel(
    slots, length, x_ref, g_ref, cos_ref, sin_ref, w_hbm,
    xn_ref, normed_ref, q_ref, k_ref, v_ref, st_ref, mixed_ref, mid_ref, n2_ref, gu_ref,
    wqkv_o, wout_o, wgu_o, wd_o,
    wqkv, wout, wgu, wd, bias, sem_in, sem_out,
):
    rows = x_ref.shape[0]
    key_rows = q_ref.shape[0]
    held = (wqkv, wout, wgu, wd)
    for m in range(4):
        tile_rows, tile_cols = GRIDS[m]

        @pl.loop(0, tile_rows)
        def _(i, m=m, tile_cols=tile_cols):
            for j in range(tile_cols):
                slot = slots[OFFSETS[m] + i * tile_cols + j]
                pltpu.make_async_copy(
                    w_hbm.at[slot],
                    held[m].at[pl.ds(pl.multiple_of(i * BLOCK, BLOCK), BLOCK), pl.ds(j * BLOCK, BLOCK)],
                    sem_in.at[m],
                ).start()

    def arrive(m):
        pltpu.make_async_copy(held[m], held[m], sem_in.at[m]).wait()

    outs = (wqkv_o, wout_o, wgu_o, wd_o)

    def leave(m):
        return pltpu.make_async_copy(held[m], outs[m], sem_out.at[m])

    query = lax.broadcasted_iota(jnp.int32, bias.shape, 0)
    key = lax.broadcasted_iota(jnp.int32, bias.shape, 1)
    bias[...] = jnp.where((key <= query) & (key < length[0]), 0.0, masked_score)
    x = x_ref[...]
    normed_ref[...] = (x * rms(x) * g_ref[0:1, :]).astype(bf16)
    tail = key_rows - rows
    for ref in (q_ref, k_ref, v_ref):
        ref[rows:, :] = jnp.zeros((tail, D), bf16)
    arrive(0)
    leave(0).start()

    @pl.loop(0, 2)
    def _(part):
        acc = nn(normed_ref[...], wqkv[:, pl.ds(pl.multiple_of(part * D, D), D)])
        scale = jnp.where(part == 0, HEAD_DIM ** (-0.5), 1.0)
        for p in range(HEADS // 2):
            t = acc[:, p * PAIR : (p + 1) * PAIR]
            rot = ((t * cos_ref[...] + swap_halves(t) * sin_ref[...]) * scale).astype(bf16)

            @pl.when(part == 0)
            def _(p=p, rot=rot):
                q_ref[0:rows, p * PAIR : (p + 1) * PAIR] = rot

            @pl.when(part == 1)
            def _(p=p, rot=rot):
                k_ref[0:rows, p * PAIR : (p + 1) * PAIR] = rot

    v_ref[0:rows, :] = nn(normed_ref[...], wqkv[:, 2 * D :]).astype(bf16)
    st_ref[...] = jnp.zeros(st_ref.shape, f32)

    @pl.loop(0, HEADS // 2)
    def _(p):
        cols = pl.ds(pl.multiple_of(p * PAIR, PAIR), PAIR)
        kp = k_ref[:, cols]
        vp = v_ref[:, cols]
        low = lax.broadcasted_iota(jnp.int32, kp.shape, 1) < HEAD_DIM
        keys = (jnp.where(low, kp, 0), jnp.where(low, 0, kp))
        values = (jnp.where(low, vp, 1), jnp.where(low, 1, vp))
        for q0, q1 in query_blocks(rows):
            kend = min(round_up(q1, BLOCK), key_rows)
            qp = q_ref[q0:q1, cols]
            mask = bias[q0:q1, :kend]
            parts = []
            tops = []
            for h in range(2):
                s = nt(qp, keys[h][:kend]) + mask
                top = jnp.max(s, -1, keepdims=True)
                e = jnp.exp(s - top).astype(bf16)
                parts.append(nn(e, values[h][:kend]))
                tops.append(top)
            lane = lax.broadcasted_iota(jnp.int32, parts[0].shape, 1)
            low_q = lane < HEAD_DIM
            total = pltpu.roll(jnp.where(low_q, parts[1], parts[0]), HEAD_DIM, 1)
            mixed_ref[q0:q1, cols] = (jnp.where(low_q, parts[0], parts[1]) / total).astype(bf16)
            log_total = jnp.log(total)
            other = pltpu.roll(log_total, HEAD_DIM, 1)
            first = tops[0] + jnp.where(low_q, log_total, other)
            second = tops[1] + jnp.where(low_q, other, log_total)
            old = st_ref[q0:q1, :]
            st_ref[q0:q1, :] = jnp.where(
                lane == 2 * p, first, jnp.where(lane == 2 * p + 1, second, old)
            )

    arrive(1)
    leave(1).start()
    middle = x_ref[...] + nn(mixed_ref[...], wout[...])
    mid_ref[...] = middle
    n2_ref[...] = (middle * rms(middle) * g_ref[1:2, :]).astype(bf16)
    arrive(2)
    leave(2).start()
    arrive(3)
    leave(3).start()
    xn_ref[...] = mid_ref[...]

    @pl.loop(0, FF // FF_STEP)
    def _(t):
        at = pl.multiple_of(t * FF_STEP, FF_STEP)
        gate = nn(n2_ref[...], wgu[:, pl.ds(at, FF_STEP)])
        up = nn(n2_ref[...], wgu[:, pl.ds(FF + at, FF_STEP)])
        act = (gate / (1.0 + jnp.exp(-gate)) * up).astype(bf16)
        gu_ref[:, pl.ds(at, FF_STEP)] = gate.astype(bf16)
        gu_ref[:, pl.ds(FF + at, FF_STEP)] = up.astype(bf16)
        xn_ref[...] += nn(act, wd[pl.ds(at, FF_STEP), :])

    for m in range(4):
        leave(m).wait()


def backward_kernel(
    slots, spare, length, back_ref, g_ref, cos_ref, sin_ref,
    x_ref, normed_ref, q_ref, k_ref, v_ref, st_ref, mixed_ref, mid_ref, n2_ref, gu_ref,
    wqkv_i, wout_i, wgu_i, wd_i, *rest,
):
    (
        dx_ref, gain_ref, tiles_out,
        wqkv, wout, wgu, wd, gqkv, gout, ggu, gd, zero, bias, turned, sums, big, mixed_back, dproj,
        sem_in, sem_out, sem_zero,
    ) = rest[-21:]
    rows = x_ref.shape[0]
    key_rows = q_ref.shape[0]
    held = (wqkv, wout, wgu, wd)
    given = (wqkv_i, wout_i, wgu_i, wd_i)

    def arrive(m):
        return pltpu.make_async_copy(given[m], held[m], sem_in.at[m])

    for m in (3, 2, 1, 0):
        arrive(m).start()
    grads = (gqkv, gout, ggu, gd)

    def send(m, i0, i1, j0, count_j):
        @pl.loop(i0, i1)
        def _(i):
            for jj in range(count_j):
                j = j0 + jj
                slot = slots[OFFSETS[m] + i * GRIDS[m][1] + j]
                pltpu.make_async_copy(
                    grads[m].at[
                        pl.ds(pl.multiple_of(i * BLOCK, BLOCK), BLOCK),
                        pl.ds(pl.multiple_of(j * BLOCK, BLOCK), BLOCK),
                    ],
                    tiles_out.at[slot],
                    sem_out.at[m],
                ).start()

    spares = spare.shape[0] - 1
    if spares > 0:
        zero[...] = jnp.zeros(zero.shape, bf16)

        @pl.loop(0, spares)
        def _(i):
            pltpu.make_async_copy(zero, tiles_out.at[spare[i]], sem_zero).start()

    key = lax.broadcasted_iota(jnp.int32, bias.shape, 0)
    query = lax.broadcasted_iota(jnp.int32, bias.shape, 1)
    bias[...] = jnp.where((key <= query) & (key < length[0]), 0.0, masked_score)
    levels = st_ref[...].T
    for h in range(HEADS):
        turned[h] = levels[h : h + 1, :]
    big[...] = jnp.zeros(big.shape, f32)
    back_b = back_ref[...].astype(bf16)
    arrive(3).wait()
    arrive(2).wait()

    @pl.loop(0, FF // FF_STEP)
    def _(t):
        at = pl.multiple_of(t * FF_STEP, FF_STEP)
        here = pl.ds(at, FF_STEP)
        there = pl.ds(FF + at, FF_STEP)
        back_ffn = back_ref[...].astype(bf16)
        d_act = nt(back_ffn, wd[here, :])
        gate = gu_ref[:, here].astype(f32)
        up = gu_ref[:, there].astype(f32)
        sig = 1.0 / (1.0 + jnp.exp(-gate))
        silu = gate * sig
        act = (silu * up).astype(bf16)
        d_gate = (d_act * up * (sig * (1.0 + gate * (1.0 - sig)))).astype(bf16)
        d_up = (d_act * silu).astype(bf16)
        gd[here, :] = tn(act, back_ffn).astype(bf16)
        ggu[:, here] = tn(n2_ref[...], d_gate).astype(bf16)
        ggu[:, there] = tn(n2_ref[...], d_up).astype(bf16)
        per = FF_STEP // BLOCK
        send(3, t * per, (t + 1) * per, 0, D // BLOCK)
        send(2, 0, D // BLOCK, t * per, per)
        send(2, 0, D // BLOCK, FF // BLOCK + t * per, per)
        big[...] += nt(d_gate, wgu[:, here]) + nt(d_up, wgu[:, there])

    step, gain_two = rms_back(big[...], mid_ref[...], g_ref[1:2, :])
    gain_ref[1:2, :] = gain_two
    dx_ref[...] = back_ref[...] + step
    arrive(1).wait()
    back_attn = dx_ref[...].astype(bf16)
    gout[...] = tn(mixed_ref[...], back_attn).astype(bf16)
    send(1, 0, D // BLOCK, 0, D // BLOCK)
    mixed_back[0:rows, :] = nt(back_attn, wout[...]).astype(bf16)
    mixed_back[rows:, :] = jnp.zeros((key_rows - rows, D), bf16)

    @pl.loop(0, HEADS // 2)
    def _(p):
        cols = pl.ds(pl.multiple_of(p * PAIR, PAIR), PAIR)
        low = lax.broadcasted_iota(jnp.int32, (key_rows, PAIR), 1) < HEAD_DIM

        def both(t):
            return (jnp.where(low, t, 0), jnp.where(low, 0, t))

        qp = q_ref[:, cols]
        op = mixed_back[:, cols]
        keys, values, queries, backs = both(k_ref[:, cols]), both(v_ref[:, cols]), both(qp), both(op)
        sums[...] = jnp.zeros(sums.shape, f32)
        for q0, q1 in query_blocks(key_rows):
            kend = q1
            d_query = jnp.zeros((q1 - q0, PAIR), f32)
            d_key = jnp.zeros((kend, PAIR), f32)
            d_value = jnp.zeros((kend, PAIR), f32)
            for h in range(2):
                level = turned[2 * p + h, :, q0:q1]
                soft = jnp.exp(nt(keys[h][:kend], qp[q0:q1]) + bias[:kend, q0:q1] - level)
                d_prob = nt(values[h][:kend], op[q0:q1])
                row_dot = jnp.sum(soft * d_prob, 0, keepdims=True)
                d_score = (soft * (d_prob - row_dot)).astype(bf16)
                d_value += nn(soft.astype(bf16), backs[h][q0:q1])
                d_key += nn(d_score, queries[h][q0:q1])
                d_query += tn(d_score, keys[h][:kend])
            sums[0, q0:q1, :] += d_query * HEAD_DIM ** (-0.5)
            sums[1, :kend, :] += d_key
            sums[2, :kend, :] += d_value
        for part in range(2):
            t = sums[part, 0:rows, :]
            dproj[:, pl.ds(pl.multiple_of(part * D + p * PAIR, PAIR), PAIR)] = (
                t * cos_ref[...] - swap_halves(t) * sin_ref[...]
            ).astype(bf16)
        dproj[:, pl.ds(pl.multiple_of(2 * D + p * PAIR, PAIR), PAIR)] = sums[2, 0:rows, :].astype(bf16)

    arrive(0).wait()
    big[...] = jnp.zeros(big.shape, f32)

    @pl.loop(0, 3)
    def _(part):
        cols = pl.ds(pl.multiple_of(part * D, D), D)
        gqkv[:, cols] = tn(normed_ref[...], dproj[:, cols]).astype(bf16)
        send(0, 0, D // BLOCK, part * (D // BLOCK), D // BLOCK)
        big[...] += nt(dproj[:, cols], wqkv[:, cols])

    step, gain_one = rms_back(big[...], x_ref[...], g_ref[0:1, :])
    gain_ref[0:1, :] = gain_one
    dx_ref[...] += step
    for m in range(4):
        pltpu.make_async_copy(grads[m], grads[m], sem_out.at[m]).wait()
    if spares > 0:

        @pl.loop(0, spares)
        def _(i):
            pltpu.make_async_copy(zero, tiles_out.at[spare[i]], sem_zero).wait()


def weight_shapes():
    return [(r * BLOCK, c * BLOCK) for r, c in GRIDS]


def forward_layer(slots, length, x, gains, cos, sin, gathered):
    rows = x.shape[0]
    key_rows = round_up(rows, BLOCK)
    vmem = pl.BlockSpec(memory_space=pltpu.VMEM)
    smem = pl.BlockSpec(memory_space=pltpu.SMEM)
    hbm = pl.BlockSpec(memory_space=pl.ANY)
    S = jax.ShapeDtypeStruct
    out_shape = [
        S((rows, D), f32),
        S((rows, D), bf16),
        S((key_rows, D), bf16),
        S((key_rows, D), bf16),
        S((key_rows, D), bf16),
        S((key_rows, BLOCK), f32),
        S((rows, D), bf16),
        S((rows, D), f32),
        S((rows, D), bf16),
        S((rows, 2 * FF), bf16),
    ] + [S(s, bf16) for s in weight_shapes()]
    return pl.pallas_call(
        forward_kernel,
        out_shape=out_shape,
        in_specs=[smem, smem, vmem, vmem, vmem, vmem, hbm],
        out_specs=[vmem] * 10 + [hbm] * 4,
        scratch_shapes=[pltpu.VMEM(s, bf16) for s in weight_shapes()]
        + [
            pltpu.VMEM((rows, key_rows), f32),
            pltpu.SemaphoreType.DMA((4,)),
            pltpu.SemaphoreType.DMA((4,)),
        ],
        compiler_params=pltpu.CompilerParams(vmem_limit_bytes=VMEM_BYTES),
        name="forward_block",
    )(slots, length, x, gains, cos, sin, gathered)


def backward_layer(slots, spare, length, back, gains, cos, sin, x, saved, slot_count, tiles):
    rows = x.shape[0]
    key_rows = round_up(rows, BLOCK)
    vmem = pl.BlockSpec(memory_space=pltpu.VMEM)
    smem = pl.BlockSpec(memory_space=pltpu.SMEM)
    hbm = pl.BlockSpec(memory_space=pl.ANY)
    S = jax.ShapeDtypeStruct
    args = (slots, spare, length, back, gains, cos, sin, x) + tuple(saved)
    aliases = {}
    if tiles is not None:
        aliases = {len(args): 2}
        args = args + (tiles,)
    shapes = weight_shapes()
    return pl.pallas_call(
        backward_kernel,
        out_shape=[S((rows, D), f32), S((2, D), f32), S((slot_count, BLOCK, BLOCK), bf16)],
        in_specs=[smem] * 3 + [vmem] * 14 + [hbm] * (len(args) - 17),
        out_specs=[vmem, vmem, hbm],
        input_output_aliases=aliases,
        scratch_shapes=[pltpu.VMEM(s, bf16) for s in shapes]
        + [pltpu.VMEM(s, bf16) for s in shapes]
        + [
            pltpu.VMEM((BLOCK, BLOCK), bf16),
            pltpu.VMEM((key_rows, key_rows), f32),
            pltpu.VMEM((HEADS, 1, key_rows), f32),
            pltpu.VMEM((3, key_rows, PAIR), f32),
            pltpu.VMEM((rows, D), f32),
            pltpu.VMEM((key_rows, D), bf16),
            pltpu.VMEM((rows, 3 * D), bf16),
            pltpu.SemaphoreType.DMA((4,)),
            pltpu.SemaphoreType.DMA((4,)),
            pltpu.SemaphoreType.DMA,
        ],
        compiler_params=pltpu.CompilerParams(vmem_limit_bytes=VMEM_BYTES),
        name="backward_block",
    )(*args)


def optimizer_kernel(factor, g_ref, m_ref, s_ref, r_ref, wg_ref, ns_ref, nm_ref, nc_ref):
    f = factor[0]
    for i in range(g_ref.shape[0]):
        gb = g_ref[i]
        wg_ref[i] = gb.astype(f32) * f
        half = (1.0 - decay_rate) * f * f
        ns_ref[i, 0] = decay_rate * s_ref[i, 0] + half * nt(gb, gb)
        ns_ref[i, 1] = decay_rate * s_ref[i, 1] + half * tn(gb, gb)
        left = nn(r_ref[i, 0].astype(bf16), (gb.astype(f32) * f).astype(bf16)).astype(bf16)
        new = m_ref[i] - step_rate * nn(left, r_ref[i, 1].astype(bf16))
        nm_ref[i] = new
        nc_ref[i] = new.astype(bf16)


def optimizer(factor, owned, master, statistics, inverse_roots):
    count = owned.shape[0]
    per = max(n for n in range(1, 13) if count % n == 0)
    S = jax.ShapeDtypeStruct
    one = pl.BlockSpec((per, BLOCK, BLOCK), lambda i: (i, 0, 0))
    two = pl.BlockSpec((per, 2, BLOCK, BLOCK), lambda i: (i, 0, 0, 0))
    return pl.pallas_call(
        optimizer_kernel,
        grid=(count // per,),
        out_shape=[
            S(master.shape, f32),
            S(statistics.shape, f32),
            S(master.shape, f32),
            S(master.shape, bf16),
        ],
        in_specs=[pl.BlockSpec(memory_space=pltpu.SMEM), one, one, two, two],
        out_specs=[one, two, one, one],
        compiler_params=pltpu.CompilerParams(vmem_limit_bytes=VMEM_BYTES),
        name="optimizer",
    )(factor, owned, master, statistics, inverse_roots)


def to_images(local, bands, band):
    images, band_rows = local.shape[0], local.shape[-2]
    padded = jnp.concatenate([local, jnp.zeros((bands - images,) + local.shape[1:], local.dtype)], 0)
    whole = jnp.zeros((bands,) + local.shape[1:], local.dtype)
    for shift in range(bands):
        block = lax.dynamic_index_in_dim(padded, (band + shift) % bands, 0, keepdims=False)
        if shift > 0:
            pairs = [(b, (b + shift) % bands) for b in range(bands) if (b + shift) % bands < images]
            block = lax.ppermute(block, "band", pairs)
        whole = lax.dynamic_update_index_in_dim(whole, block, (band - shift) % bands, 0)
    return whole


def to_bands(whole, images, bands, band):
    local = jnp.zeros(whole.shape, whole.dtype)
    for shift in range(bands):
        block = lax.dynamic_index_in_dim(whole, (band + shift) % bands, 0, keepdims=False)
        if shift > 0:
            pairs = [(b, (b + shift) % bands) for b in range(images)]
            block = lax.ppermute(block, "band", pairs)
        local = lax.dynamic_update_index_in_dim(local, block, (band - shift) % bands, 0)
    return local[:images]


def rope_tables(rows):
    half = HEAD_DIM // 2
    frequency = rope_base ** (-(jnp.arange(half, dtype=f32) * 2.0 / HEAD_DIM))
    angles = jnp.arange(rows, dtype=jnp.int32).astype(f32)[:, None] * frequency[None, :]
    cosine, sine = jnp.cos(angles), jnp.sin(angles)
    return jnp.tile(cosine, (1, 4)), jnp.tile(jnp.concatenate([-sine, sine], 1), (1, 2))


def shards(
    tokens,
    cotangent,
    lengths,
    slot_of_block,
    master,
    statistics,
    inverse_roots,
    gain_values,
    gain_moments,
):
    images, band_rows, _ = tokens.shape
    band = lax.axis_index("band")
    bands = lax.axis_size("band")
    seq = band_rows * bands
    rows = round_up(seq, 16)
    gathered = lax.all_gather(master.astype(bf16), "dp", axis=0, tiled=True)
    slot_count = gathered.shape[0]

    arrived = to_images(jnp.stack([tokens, cotangent], 1), bands, band)
    token_rows = jnp.pad(arrived[:, 0].reshape(seq, D), ((0, rows - seq), (0, 0)))
    back_rows = jnp.pad(arrived[:, 1].reshape(seq, D), ((0, rows - seq), (0, 0)))
    length = lengths[jnp.minimum(band, images - 1)]
    valid = (jnp.arange(rows, dtype=jnp.int32) < length).astype(f32)
    length = length.reshape(1)
    cos, sin = rope_tables(rows)

    spare_count = slot_count - slot_of_block.shape[0]
    spare = jnp.zeros((1,), jnp.int32)
    if spare_count > 0:
        used = jnp.zeros((slot_count,), jnp.int32).at[slot_of_block].set(1)
        spare = jnp.concatenate([jnp.argsort(used)[:spare_count].astype(jnp.int32), spare])

    hidden = token_rows.astype(f32)
    inputs, saves = [], []
    for layer in range(LAYERS):
        slots = slot_of_block[layer * PER_LAYER : (layer + 1) * PER_LAYER]
        gains = gain_values[2 * layer : 2 * layer + 2]
        inputs.append(hidden)
        hidden, *saved = forward_layer(slots, length, hidden, gains, cos, sin, gathered)
        saves.append(saved)
    layer_output = to_bands(
        hidden[:seq].astype(bf16).reshape(bands, band_rows, D), images, bands, band
    )

    back = back_rows.astype(f32) * valid[:, None]
    tiles = None
    gain_parts = [None] * LAYERS
    for layer in range(LAYERS - 1, -1, -1):
        slots = slot_of_block[layer * PER_LAYER : (layer + 1) * PER_LAYER]
        gains = gain_values[2 * layer : 2 * layer + 2]
        back, gain_parts[layer], tiles = backward_layer(
            slots, spare if layer == LAYERS - 1 else spare[-1:], length, back, gains, cos, sin,
            inputs[layer], saves[layer], slot_count, tiles,
        )
    input_grad = to_bands(back[:seq].astype(bf16).reshape(bands, band_rows, D), images, bands, band)

    owned = lax.psum_scatter(tiles, "dp", scatter_dimension=0, tiled=True)
    owned = lax.psum(owned, "band")
    gain_total = lax.psum(jnp.concatenate(gain_parts, 0), ("dp", "band"))
    owned_f = owned.astype(f32)
    owned_squares = lax.psum(jnp.sum(owned_f * owned_f), "dp")
    grad_norm = jnp.sqrt(owned_squares + jnp.sum(gain_total * gain_total))
    factor = jnp.minimum(1.0, clip_limit / grad_norm)
    weight_grads, new_statistics, new_master, master_copy = optimizer(
        factor.reshape(1), owned, master, statistics, inverse_roots
    )
    gain_grads = gain_total * factor
    new_moments = decay_rate * gain_moments + (1.0 - decay_rate) * gain_grads * gain_grads
    new_gains = gain_values - gain_rate * gain_grads / (jnp.sqrt(new_moments) + epsilon)
    return (
        layer_output,
        input_grad,
        weight_grads,
        grad_norm,
        new_statistics,
        new_master,
        master_copy,
        gain_grads,
        new_moments,
        new_gains,
    )


def solution(mesh):
    return jax.shard_map(
        shards,
        mesh=mesh,
        in_specs=(
            P("dp", "band", None),
            P("dp", "band", None),
            P("dp"),
            P(),
            P("dp", None, None),
            P("dp", None, None, None),
            P("dp", None, None, None),
            P(),
            P(),
        ),
        out_specs=(
            P("dp", "band", None),
            P("dp", "band", None),
            P("dp", None, None),
            P(),
            P("dp", None, None, None),
            P("dp", None, None),
            P("dp", None, None),
            P(),
            P(),
            P(),
        ),
        check_vma=False,
    )
```

time: 2040 us -> 753 us (0.37)
  waiting for transfers between devices: 988 us -> 343 us
  local copies, waits for them, and re-layouts: 618 us -> 19.2 us
  matrix products: 258 us -> 0 us
  Pallas kernels: 0 us -> 218 us
  other arithmetic: 80.5 us -> 15.4 us
  blocking collectives: 59 us -> 102 us
  starting transfers between devices: 0.78 us -> 29.3 us
    unnamed x11 -> x3, waiting for transfers between devices: 316 us -> 0.05 us
    dot_general x38 -> x0, matrix products: 222 us -> none  [the longest x2 20 us: shards(): jnp.einsum('gqhe,gkhe->ghqk', back_mixed, value_heads, preferred_element_...]
    pallas_call x0 -> x5, Pallas kernels: none -> 218 us  [the longest x2 114 us: backward_layer(): pl.pallas_call(backward_kernel, out_shape=[S((rows, D), f32), S((2, D), f...]
    all_gather x5 -> x1, waiting for transfers between devices: 270 us -> 87.7 us  [shards(): gathered = lax.all_gather(master.astype(bf16), 'dp', axis=0, tiled=True)]
    scatter x1 -> x0, local copies, waits for them, and re-layouts: 156 us -> none  [shards(): jnp.zeros((gathered.shape[0], BLOCK, BLOCK), jnp.float32).at[slot_of_block]]
    reduce_scatter x1, waiting for transfers between devices: 319 us -> 173 us  [shards(): owned = lax.psum_scatter(tiles, 'dp', scatter_dimension=0, tiled=True)]
    unnamed x257 -> x16, local copies, waits for them, and re-layouts: 117 us -> 1.21 us
    reshape x18 -> x2, local copies, waits for them, and re-layouts: 85.9 us -> 0.49 us  [the longest x1 0.24 us: shards(): hidden[:seq].astype(bf16).reshape(bands, band_rows, D)]
  transfers between devices with their start and end apart: 9 -> 12, of which waited for: 9 -> 7; matrix products, arithmetic and copies ran while one was open for 16% -> 3% of each run, Pallas kernels for 0% -> 0%
where the time goes in v1:
time: 753 us; the launch traced here: 744 us
  waiting for transfers between devices  343 us (46%)
  Pallas kernels  218 us (29%)
  blocking collectives  102 us (14%)
  starting transfers between devices  29.3 us (4%)
  local copies, waits for them, and re-layouts  19.2 us (3%)
  between operations  16.9 us (2%)
  other arithmetic  15.4 us (2%)
    reduce_scatter x1, waiting for transfers between devices, shards(): owned = lax.psum_scatter(tiles, 'dp', scatter_dimension=0, tiled=True)  173 us
    pallas_call x2, Pallas kernels, backward_layer(): pl.pallas_call(backward_kernel, out_shape=[S((rows, D), f32), S((2, D), f...  114 us
    psum x1, blocking collectives, shards(): gain_total = lax.psum(jnp.concatenate(gain_parts, 0), ('dp', 'band'))  88.1 us
    all_gather x1, waiting for transfers between devices, shards(): gathered = lax.all_gather(master.astype(bf16), 'dp', axis=0, tiled=True)  87.7 us
    pallas_call x2, Pallas kernels, forward_layer(): pl.pallas_call(forward_kernel, out_shape=out_shape, in_specs=[smem, smem,...  70.8 us
    psum x1, waiting for transfers between devices, shards(): owned = lax.psum(owned, 'band')  34.8 us
    pallas_call x1, Pallas kernels, optimizer(): pl.pallas_call(optimizer_kernel, grid=(count // per,), out_shape=[S(maste...  32.6 us
    ppermute x3, waiting for transfers between devices, to_images(): block = lax.ppermute(block, 'band', pairs)  28.2 us
  transfers between devices with their start and end apart: 12, of which 7 were waited for; matrix products, arithmetic and copies ran while one was open for 3% of the time, Pallas kernels for 0%

profile of v1, /device:TPU:16, one launch (start us, length us, event | category | flops | bytes accessed | tf_op | source)
XLA Modules:
  0.0 744.1 jit_solution(8726359229580839612)
XLA Ops:
  7.2 5.6 convert_element_type.43
  15.4 1.4 collective-permute-start
  16.9 4.4 collective-permute-start.1
  21.3 1.9 collective-permute-start.2
  28.0 12.2 %collective-permute-done = bf16[2,145,768]{2,1,0:T(8,128)(2,1)} collective-permute-done((bf16[2,145,768]{2,1,0:T(8,128)(2,1)}, bf16[2,145,768]{2,1,0:T(8,128)(2,1)}, u32[]{:S(2)}, u32[]{:S(2)}) %collective-permute-start) | collective-permute-done | bytes 445472 | tf_op jit(solution)/shard_map/ppermute | solution.py:465
  40.2 1.1 bitcast_dynamic-update-slice_fusion.2
  41.3 7.2 collective-permute-done.1
  48.4 1.1 bitcast_dynamic-update-slice_fusion.1
  49.5 8.9 %collective-permute-done.2 = bf16[2,145,768]{2,1,0:T(8,128)(2,1)} collective-permute-done((bf16[2,145,768]{2,1,0:T(8,128)(2,1)S(1)}, bf16[2,145,768]{2,1,0:T(8,128)(2,1)}, u32[]{:S(2)}, u32[]{:S(2)}) %collective-permute-start.2) | collective-permute-done | bytes 445472 | tf_op jit(solution)/shard_map/ppermute | solution.py:465
  60.5 1.4 reshape_squeeze.6
  62.1 1.4 pad_convert_fusion.x_ref
  63.5 1.5 convert_multiply_fusion.back_ref
  65.0 87.7 %all-gather.2.cloned.1.call-done.w_hbm = bf16[864,128,128]{2,1,0:T(8,128)(2,1)} async-done(((bf16[108,128,128]{2,1,0:T(8,128)(2,1)}), bf16[864,128,128]{2,1,0:T(8,128)(2,1)}) %all-gather.2.cloned.1.call-update) | async-done | bytes 28311568 | tf_op jit(solution)/shard_map/all_gather | solution.py:505
  152.7 35.4 %forward_block.2 = (f32[592,768]{1,0:T(8,128)}, bf16[592,768]{1,0:T(8,128)(2,1)}, bf16[640,768]{1,0:T(8,128)(2,1)}, bf16[640,768]{1,0:T(8,128)(2,1)}, bf16[640,7...) custom-call(s32[432]{0:T(512)} %get-tuple-element.108.slots, ...), custom_call_target="tpu_custom_call" | custom-call | tf_op jit(solution)/shard_map/forward_block/pallas_call | solution.py:367
  188.1 35.4 %forward_block.3 = (f32[592,768]{1,0:T(8,128)}, bf16[592,768]{1,0:T(8,128)(2,1)}, bf16[640,768]{1,0:T(8,128)(2,1)}, bf16[640,768]{1,0:T(8,128)(2,1)}, bf16[640,7...) custom-call(s32[432]{0:T(512)} %get-tuple-element.109.slots, ...), custom_call_target="tpu_custom_call" | custom-call | tf_op jit(solution)/shard_map/forward_block/pallas_call | solution.py:367
  223.5 57.2 %backward_block.2 = (f32[592,768]{1,0:T(8,128)}, f32[2,768]{1,0:T(2,128)}, bf16[864,128,128]{2,1,0:T(8,128)(2,1)}) custom-call(s32[432]{0:T(512)} %get-tuple-element.109.slots, s32[1]{0:T(128)} %constant.161.clone.1.spare, s32[1]{0:T(128)} %dynamic_slice.41.length, f32[592,768]{1,0:T(8,128)} %convert_multiply_fusion.back_ref, ...), custom_call_target="tpu_custom_call" | custom-call | tf_op jit(solution)/shard_map/backward_block/pallas_call | solution.py:396
  280.7 57.0 %backward_block.3 = (f32[592,768]{1,0:T(8,128)}, f32[2,768]{1,0:T(2,128)}, bf16[864,128,128]{2,1,0:T(8,128)(2,1)}) custom-call(s32[432]{0:T(512)} %get-tuple-element.108.slots, s32[1]{0:T(128)} %constant.161.clone.1.spare, s32[1]{0:T(128)} %dynamic_slice.41.length, f32[592,768]{1,0:T(8,128)} %get-tuple-element.63.back_ref, ...), custom_call_target="tpu_custom_call", output_to_operand_aliasing={{2}: (21, {})} | custom-call | tf_op jit(solution)/shard_map/backward_block/pallas_call | solution.py:396
  337.8 173.4 %reduce-scatter.2.cloned.1.call-done = bf16[108,128,128]{2,1,0:T(8,128)(2,1)} async-done(((bf16[864,128,128]{2,1,0:T(8,128)(2,1)}), bf16[108,128,128]{2,1,0:T(8,128)(2,1)}) %reduce-scatter.2.cloned.1.call-update) | async-done | bytes 3538960 | tf_op jit(solution)/shard_map/reduce_scatter | solution.py:546
  511.2 1.6 slice.55
  514.0 3.4 collective-permute-start.3
  517.4 2.4 collective-permute-start.4
  519.8 2.2 collective-permute-start.5
  522.1 1.6 slice.54
  524.9 1.9 collective-permute-start.6
  526.8 6.0 collective-permute-start.7
  532.8 88.1 %psum.23 = f32[4,768]{1,0:T(4,128)S(1)} all-reduce(f32[4,768]{1,0:T(4,128)S(1)} %pad_maximum_fusion.1), channel_id=1, replica_groups=mesh['dp'=8,'band'=4] {'dp','band'}, use_global_device_ids=true, to_apply=%region_4.5 | all-reduce | flops 3072 | bytes 24576 | tf_op jit(solution)/shard_map/psum | solution.py:548
  621.5 5.4 collective-permute-start.8
  628.0 19.3 %collective-permute-done.8 = bf16[145,768]{1,0:T(8,128)(2,1)S(1)} collective-permute-done((bf16[145,768]{1,0:T(8,128)(2,1)}, bf16[145,768]{1,0:T(8,128)(2,1)S(1)}, u32[]{:S(2)}, u32[]{:S(2)}) %collective-permute-start.8) | collective-permute-done | bytes 222752 | tf_op jit(solution)/shard_map/ppermute | solution.py:476
  647.3 34.8 %all-reduce.5.cloned.1.call-done.g_ref = bf16[108,128,128]{2,1,0:T(8,128)(2,1)} async-done(((bf16[108,128,128]{2,1,0:T(8,128)(2,1)}), bf16[108,128,128]{2,1,0:T(8,128)(2,1)}) %all-reduce.5.cloned.1.call-update) | async-done | bytes 3538960 | tf_op jit(solution)/shard_map/psum | solution.py:547
  682.1 4.4 multiply_reduce_fusion
  687.4 14.3 %psum.22 = f32[]{:T(128)} all-reduce(f32[]{:T(128)} %multiply_reduce_fusion), channel_id=1, replica_groups=mesh['dp'=8,'band'=4] {'dp'}, use_global_device_ids=true, to_apply=%region_3.4 | all-reduce | flops 1 | bytes 8 | tf_op jit(solution)/shard_map/psum | solution.py:550
  703.7 32.6 %optimizer.1 = (f32[108,128,128]{2,1,0:T(8,128)}, f32[108,2,128,128]{3,2,1,0:T(8,128)}, f32[108,128,128]{2,1,0:T(8,128)}, bf16[108,128,128]{2,1,0:T(8,128)(2,1)}) custom-call(f32[1]{0:T(128)} %bitcast.23.factor, bf16[108,128,128]{2,1,0:T(8,128)(2,1)} %all-reduce.5.cloned.1.call-done.g_ref, f32[108,128,128]{2,1,0:T(8,128)} %m_ref.1, ...), custom_call_target="tpu_custom_call" | custom-call | tf_op jit(solution)/shard_map/optimizer/pallas_call | solution.py:441
  (62 shorter events, 15.2 us)
Async XLA Ops:
  7.2 145.5 %all-gather.2.cloned.1.call-start = ((), (), s32[]{:S(2)}) async-start(), calls=%async_computation.1 | async-start | bytes 31850496 | tf_op jit(solution)/shard_map/all_gather | solution.py:505
  12.8 1.1 copy-start
  12.8 1.3 copy-start.1
  12.9 498.3 %reduce-scatter.2.cloned.1.call-start = ((), (), s32[]{:S(2)}) async-start(), calls=%async_computation.2 | async-start | bytes 31850496 | tf_op jit(solution)/shard_map/reduce_scatter | solution.py:546
  15.4 10.1 %copy-start.7 = (s32[3]{0:T(128)S(1)}, s32[3]{0:T(128)}, u32[]{:S(2)}) copy-start(s32[3]{0:T(128)} %param.11) | copy-start | bytes 40
  15.4 11.3 %copy-start.2 = (f32[4,768]{1,0:T(4,128)S(1)}, f32[4,768]{1,0:T(4,128)}, u32[]{:S(2)}) copy-start(f32[4,768]{1,0:T(4,128)} %param.16) | copy-start | bytes 36868
  15.4 12.0 %copy-start.6 = (s32[864]{0:T(1024)S(1)}, s32[864]{0:T(1024)}, u32[]{:S(2)}) copy-start(s32[864]{0:T(1024)} %param.12) | copy-start | bytes 10372
  15.4 24.8 %collective-permute-start = (bf16[2,145,768]{2,1,0:T(8,128)(2,1)}, bf16[2,145,768]{2,1,0:T(8,128)(2,1)}, u32[]{:S(2)}, u32[]{:S(2)}) collective-permute-start(bf16[2,145,768]{2,1,0:T(8,128)(2,1)} %get-tuple-element.93), channel_id=1, source_target_pairs={{0,1},{1,2},{3,0},{4,5},{5,6},{7,4},{8,9},{9,10},{11,8},{12,13},{1... | collective-permute-start | bytes 1336328 | tf_op jit(solution)/shard_map/ppermute | solution.py:465
  16.9 31.6 %collective-permute-start.1 = (bf16[2,145,768]{2,1,0:T(8,128)(2,1)S(1)}, bf16[2,145,768]{2,1,0:T(8,128)(2,1)}, u32[]{:S(2)}, u32[]{:S(2)}) collective-permute-start(bf16[2,145,768]{2,1,0:T(8,128)(2,1)S(1)} %get-tuple-element.92), channel_id=1, source_target_pairs={{0,2},{2,0},{3,1},{4,6},{6,4},{7,5},{8,10},{10,8},{11,9},{12,14},{... | collective-permute-start | bytes 1336328 | tf_op jit(solution)/shard_map/ppermute | solution.py:465
  21.3 37.1 %collective-permute-start.2 = (bf16[2,145,768]{2,1,0:T(8,128)(2,1)S(1)}, bf16[2,145,768]{2,1,0:T(8,128)(2,1)}, u32[]{:S(2)}, u32[]{:S(2)}) collective-permute-start(bf16[2,145,768]{2,1,0:T(8,128)(2,1)S(1)} %get-tuple-element.91), channel_id=1, source_target_pairs={{1,0},{2,1},{3,2},{5,4},{6,5},{7,6},{9,8},{10,9},{11,10},{13,12},{... | collective-permute-start | bytes 1336328 | tf_op jit(solution)/shard_map/ppermute | solution.py:465
  337.7 344.4 %all-reduce.5.cloned.1.call-start = ((), (), s32[]{:S(2)}) async-start(), calls=%async_computation.3 | async-start | bytes 7077888 | tf_op jit(solution)/shard_map/psum | solution.py:547
  514.0 107.5 %collective-permute-start.3 = (bf16[145,768]{1,0:T(8,128)(2,1)}, bf16[145,768]{1,0:T(8,128)(2,1)S(1)}, u32[]{:S(2)}, u32[]{:S(2)}) collective-permute-start(bf16[145,768]{1,0:T(8,128)(2,1)} %get-tuple-element.101), channel_id=1, source_target_pairs={{0,1},{1,2},{2,3},{4,5},{5,6},{6,7},{8,9},{9,10},{10,11},{12,13},{... | collective-permute-start | bytes 668168 | tf_op jit(solution)/shard_map/ppermute | solution.py:476
  517.4 109.6 %collective-permute-start.4 = (bf16[145,768]{1,0:T(8,128)(2,1)}, bf16[145,768]{1,0:T(8,128)(2,1)S(1)}, u32[]{:S(2)}, u32[]{:S(2)}) collective-permute-start(bf16[145,768]{1,0:T(8,128)(2,1)} %get-tuple-element.100), channel_id=1, source_target_pairs={{0,2},{1,3},{2,0},{4,6},{5,7},{6,4},{8,10},{9,11},{10,8},{12,14},{... | collective-permute-start | bytes 668168 | tf_op jit(solution)/shard_map/ppermute | solution.py:476
  519.8 107.2 %collective-permute-start.5 = (bf16[145,768]{1,0:T(8,128)(2,1)}, bf16[145,768]{1,0:T(8,128)(2,1)S(1)}, u32[]{:S(2)}, u32[]{:S(2)}) collective-permute-start(bf16[145,768]{1,0:T(8,128)(2,1)} %get-tuple-element.99), channel_id=1, source_target_pairs={{0,3},{1,0},{2,1},{4,7},{5,4},{6,5},{8,11},{9,8},{10,9},{12,15},{1... | collective-permute-start | bytes 668168 | tf_op jit(solution)/shard_map/ppermute | solution.py:476
  523.6 9.1 %copy-start.4 = (f32[2,768]{1,0:T(2,128)S(1)}, f32[2,768]{1,0:T(2,128)}, u32[]{:S(2)}) copy-start(f32[2,768]{1,0:T(2,128)} %get-tuple-element.81) | copy-start | bytes 18436
  523.7 9.1 %copy-start.5 = (f32[2,768]{1,0:T(2,128)S(1)}, f32[2,768]{1,0:T(2,128)}, u32[]{:S(2)}) copy-start(f32[2,768]{1,0:T(2,128)} %get-tuple-element.80) | copy-start | bytes 18436
  524.9 103.1 %collective-permute-start.6 = (bf16[145,768]{1,0:T(8,128)(2,1)}, bf16[145,768]{1,0:T(8,128)(2,1)S(1)}, u32[]{:S(2)}, u32[]{:S(2)}) collective-permute-start(bf16[145,768]{1,0:T(8,128)(2,1)} %get-tuple-element.97), channel_id=1, source_target_pairs={{0,1},{1,2},{2,3},{4,5},{5,6},{6,7},{8,9},{9,10},{10,11},{12,13},{... | collective-permute-start | bytes 668168 | tf_op jit(solution)/shard_map/ppermute | solution.py:476
  526.8 101.2 %collective-permute-start.7 = (bf16[145,768]{1,0:T(8,128)(2,1)}, bf16[145,768]{1,0:T(8,128)(2,1)S(1)}, u32[]{:S(2)}, u32[]{:S(2)}) collective-permute-start(bf16[145,768]{1,0:T(8,128)(2,1)} %get-tuple-element.96), channel_id=1, source_target_pairs={{0,2},{1,3},{2,0},{4,6},{5,7},{6,4},{8,10},{9,11},{10,8},{12,14},{... | collective-permute-start | bytes 668168 | tf_op jit(solution)/shard_map/ppermute | solution.py:476
  621.5 25.8 %collective-permute-start.8 = (bf16[145,768]{1,0:T(8,128)(2,1)}, bf16[145,768]{1,0:T(8,128)(2,1)S(1)}, u32[]{:S(2)}, u32[]{:S(2)}) collective-permute-start(bf16[145,768]{1,0:T(8,128)(2,1)} %get-tuple-element.95), channel_id=1, source_target_pairs={{0,3},{1,0},{2,1},{4,7},{5,4},{6,5},{8,11},{9,8},{10,9},{12,15},{1... | collective-permute-start | bytes 668168 | tf_op jit(solution)/shard_map/ppermute | solution.py:476
  647.3 55.7 %copy-start.3 = (f32[4,768]{1,0:T(4,128)S(1)}, f32[4,768]{1,0:T(4,128)}, u32[]{:S(2)}) copy-start(f32[4,768]{1,0:T(4,128)} %param.17) | copy-start | bytes 36868
Sparse Core Ops, SparseCore 0:
  13.0 139.6 all-gather.1
  337.9 173.2 reduce-scatter.1
  513.6 168.4 all-reduce.4

commit v2 on v1

--- a/solution.py
+++ b/solution.py
@@ -478,6 +478,64 @@
     return local[:images]
 
 
+def add(a, b):
+    return (a.astype(f32) + b.astype(f32)).astype(bf16)
+
+
+def chunk_sizes(per_owner):
+    parts = [per_owner * p // 108 for p in (24, 32, 28, 16)]
+    return parts + [per_owner - sum(parts)]
+
+
+def relative_places(slots, per_owner, me):
+    owner, rank = slots // per_owner, slots % per_owner
+    relative = owner ^ me
+    relative = (relative % 2) * 4 + (relative // 2 % 2) * 2 + relative // 4
+    place = jnp.zeros_like(slots)
+    start = 0
+    for size in chunk_sizes(per_owner):
+        inside = (rank >= start) & (rank < start + size)
+        place = jnp.where(inside, start * 8 + relative * size + rank - start, place)
+        start += size
+    return place
+
+
+def reduce_to_owners(tiles, band):
+    core = [(i, i ^ 1) for i in range(8)]
+    x_pairs = [(i, i ^ 2) for i in range(8)]
+    y_pairs = [(i, i ^ 4) for i in range(8)]
+    sizes = chunk_sizes(tiles.shape[0] // 8)
+    chunks, start = [], 0
+    for size in sizes:
+        chunks.append(tiles[start * 8 : (start + size) * 8].reshape(2, 2, 2, size, BLOCK, BLOCK))
+        start += size
+    from_core = [lax.ppermute(chunk[1], "dp", core) for chunk in chunks]
+    gate, outs = None, []
+    for chunk, received in zip(chunks, from_core):
+        both = add(chunk[0], received)
+        half = both.shape[2] // 2
+        one, two = both[:, :, :half], both[:, :, half:]
+        send_x, send_y = one[1], two[:, 1]
+        if gate is not None:
+            send_x, send_y, _ = lax.optimization_barrier((send_x, send_y, gate))
+        one = add(one[0], lax.ppermute(send_x, "dp", x_pairs))
+        two = add(two[:, 0], lax.ppermute(send_y, "dp", y_pairs))
+        from_y = lax.ppermute(one[1], "dp", y_pairs)
+        from_x = lax.ppermute(two[1], "dp", x_pairs)
+        gate = (from_y, from_x)
+        plane = jnp.concatenate([add(one[0], from_y), add(two[0], from_x)], 0)
+        up = lax.ppermute(plane, "band", [(0, 1)])
+        down = lax.ppermute(plane, "band", [(2, 1)])
+        total = (plane.astype(f32) + up.astype(f32) + down.astype(f32)).astype(bf16)
+        to_first = lax.ppermute(total, "band", [(1, 0)])
+        to_third = lax.ppermute(total, "band", [(1, 2)])
+        to_last = lax.ppermute(to_third, "band", [(2, 3)])
+        total = jnp.where(band == 0, to_first, total)
+        total = jnp.where(band == 2, to_third, total)
+        outs.append(jnp.where(band == 3, to_last, total))
+    return jnp.concatenate(outs, 0)
+
+
 def rope_tables(rows):
     half = HEAD_DIM // 2
     frequency = rope_base ** (-(jnp.arange(half, dtype=f32) * 2.0 / HEAD_DIM))
@@ -532,10 +590,15 @@
     )
 
     back = back_rows.astype(f32) * valid[:, None]
+    by_permutes = lax.axis_size("dp") == 8 and bands == 4 and images == 3
+    places = slot_of_block
+    if by_permutes:
+        places = relative_places(places, master.shape[0], lax.axis_index("dp"))
+        spare = relative_places(spare, master.shape[0], lax.axis_index("dp"))
     tiles = None
     gain_parts = [None] * LAYERS
     for layer in range(LAYERS - 1, -1, -1):
-        slots = slot_of_block[layer * PER_LAYER : (layer + 1) * PER_LAYER]
+        slots = places[layer * PER_LAYER : (layer + 1) * PER_LAYER]
         gains = gain_values[2 * layer : 2 * layer + 2]
         back, gain_parts[layer], tiles = backward_layer(
             slots, spare if layer == LAYERS - 1 else spare[-1:], length, back, gains, cos, sin,
@@ -543,8 +606,11 @@
         )
     input_grad = to_bands(back[:seq].astype(bf16).reshape(bands, band_rows, D), images, bands, band)
 
-    owned = lax.psum_scatter(tiles, "dp", scatter_dimension=0, tiled=True)
-    owned = lax.psum(owned, "band")
+    if by_permutes:
+        owned = reduce_to_owners(tiles, band)
+    else:
+        owned = lax.psum_scatter(tiles, "dp", scatter_dimension=0, tiled=True)
+        owned = lax.psum(owned, "band")
     gain_total = lax.psum(jnp.concatenate(gain_parts, 0), ("dp", "band"))
     owned_f = owned.astype(f32)
     owned_squares = lax.psum(jnp.sum(owned_f * owned_f), "dp")

time: 753 us -> 728 us (0.967)
  waiting for transfers between devices: 343 us -> 225 us
  starting transfers between devices: 29.3 us -> 102 us
  local copies, waits for them, and re-layouts: 19.2 us -> 73.8 us
  blocking collectives: 102 us -> 50.9 us
  other arithmetic: 15.4 us -> 34.6 us
    reduce_scatter x1 -> x0, waiting for transfers between devices: 173 us -> none  [shards(): owned = lax.psum_scatter(tiles, 'dp', scatter_dimension=0, tiled=True)]
    ppermute x0 -> x50, waiting for transfers between devices: none -> 109 us  [the longest x5 49.5 us: reduce_to_owners(): one = add(one[0], lax.ppermute(send_x, 'dp', x_pairs))]
    ppermute x0 -> x50, starting transfers between devices: none -> 76.7 us  [the longest x5 25 us: reduce_to_owners(): down = lax.ppermute(plane, 'band', [(2, 1)])]
    psum x1, blocking collectives: 88.1 us -> 38.5 us  [shards(): gain_total = lax.psum(jnp.concatenate(gain_parts, 0), ('dp', 'band'))]
    psum x1 -> x0, waiting for transfers between devices: 34.8 us -> none  [shards(): owned = lax.psum(owned, 'band')]
    slice x0 -> x6, local copies, waits for them, and re-layouts: none -> 27.5 us  [the longest x5 26.9 us: reduce_to_owners(): from_core = [lax.ppermute(chunk[1], 'dp', core) for chunk in chunks]]
    ppermute x6, waiting for transfers between devices: 19.3 us -> 0.02 us  [to_bands(): block = lax.ppermute(block, 'band', pairs)]
    convert_element_type x0 -> x25, other arithmetic: none -> 18.5 us  [the longest x20 16.9 us: add(): return (a.astype(f32) + b.astype(f32)).astype(bf16)]
  transfers between devices with their start and end apart: 12 -> 60, of which waited for: 7 -> 29; matrix products, arithmetic and copies ran while one was open for 3% -> 12% of each run, Pallas kernels for 0% -> 0%
where the time goes in v2:
time: 728 us; the launch traced here: 722 us
  waiting for transfers between devices  225 us (31%)
  Pallas kernels  218 us (30%)
  starting transfers between devices  102 us (14%)
  local copies, waits for them, and re-layouts  73.8 us (10%)
  blocking collectives  50.9 us (7%)
  other arithmetic  34.6 us (5%)
  between operations  18.3 us (3%)
    pallas_call x2, Pallas kernels, backward_layer(): pl.pallas_call(backward_kernel, out_shape=[S((rows, D), f32), S((2, D), f...  114 us
    all_gather x1, waiting for transfers between devices, shards(): gathered = lax.all_gather(master.astype(bf16), 'dp', axis=0, tiled=True)  87.8 us
    pallas_call x2, Pallas kernels, forward_layer(): pl.pallas_call(forward_kernel, out_shape=out_shape, in_specs=[smem, smem,...  70.8 us
    ppermute x5, waiting for transfers between devices, reduce_to_owners(): one = add(one[0], lax.ppermute(send_x, 'dp', x_pairs))  49.5 us
    psum x1, blocking collectives, shards(): gain_total = lax.psum(jnp.concatenate(gain_parts, 0), ('dp', 'band'))  38.5 us
    pallas_call x1, Pallas kernels, optimizer(): pl.pallas_call(optimizer_kernel, grid=(count // per,), out_shape=[S(maste...  32.6 us
    ppermute x3, waiting for transfers between devices, to_images(): block = lax.ppermute(block, 'band', pairs)  27.5 us
    slice x5, local copies, waits for them, and re-layouts, reduce_to_owners(): from_core = [lax.ppermute(chunk[1], 'dp', core) for chunk in chunks]  26.9 us
  transfers between devices with their start and end apart: 60, of which 29 were waited for; matrix products, arithmetic and copies ran while one was open for 12% of the time, Pallas kernels for 0%

profile of v2, /device:TPU:16, one launch (start us, length us, event | category | flops | bytes accessed | tf_op | source)
XLA Modules:
  0.0 721.7 jit_solution(15777241048914804726)
XLA Ops:
  7.2 5.6 convert_element_type.403
  16.8 4.4 collective-permute-start.1
  28.7 11.4 %collective-permute-done = bf16[2,145,768]{2,1,0:T(8,128)(2,1)} collective-permute-done((bf16[2,145,768]{2,1,0:T(8,128)(2,1)}, bf16[2,145,768]{2,1,0:T(8,128)(2,1)}, u32[]{:S(2)}, u32[]{:S(2)}) %collective-permute-start) | collective-permute-done | bytes 445472 | tf_op jit(solution)/shard_map/ppermute | solution.py:465
  41.2 7.2 collective-permute-done.1
  49.4 8.9 %collective-permute-done.2 = bf16[2,145,768]{2,1,0:T(8,128)(2,1)} collective-permute-done((bf16[2,145,768]{2,1,0:T(8,128)(2,1)S(1)}, bf16[2,145,768]{2,1,0:T(8,128)(2,1)}, u32[]{:S(2)}, u32[]{:S(2)}) %collective-permute-start.2) | collective-permute-done | bytes 445472 | tf_op jit(solution)/shard_map/ppermute | solution.py:465
  64.9 87.8 %all-gather.2.cloned.1.call-done.w_hbm = bf16[864,128,128]{2,1,0:T(8,128)(2,1)} async-done(((bf16[108,128,128]{2,1,0:T(8,128)(2,1)}), bf16[864,128,128]{2,1,0:T(8,128)(2,1)}) %all-gather.2.cloned.1.call-update) | async-done | bytes 28311568 | tf_op jit(solution)/shard_map/all_gather | solution.py:563
  152.7 35.4 %forward_block.2 = (f32[592,768]{1,0:T(8,128)}, bf16[592,768]{1,0:T(8,128)(2,1)}, bf16[640,768]{1,0:T(8,128)(2,1)}, bf16[640,768]{1,0:T(8,128)(2,1)}, bf16[640,7...) custom-call(s32[432]{0:T(512)} %get-tuple-element.146.slots, ...), custom_call_target="tpu_custom_call" | custom-call | tf_op jit(solution)/shard_map/forward_block/pallas_call | solution.py:367
  188.1 35.4 %forward_block.3 = (f32[592,768]{1,0:T(8,128)}, bf16[592,768]{1,0:T(8,128)(2,1)}, bf16[640,768]{1,0:T(8,128)(2,1)}, bf16[640,768]{1,0:T(8,128)(2,1)}, bf16[640,7...) custom-call(s32[432]{0:T(512)} %get-tuple-element.147.slots, ...), custom_call_target="tpu_custom_call" | custom-call | tf_op jit(solution)/shard_map/forward_block/pallas_call | solution.py:367
  226.3 57.2 %backward_block.2 = (f32[592,768]{1,0:T(8,128)}, f32[2,768]{1,0:T(2,128)}, bf16[864,128,128]{2,1,0:T(8,128)(2,1)}) custom-call(s32[432]{0:T(512)} %get-tuple-element.144.slots, s32[1]{0:T(128)S(6)} %mul.152.spare, s32[1]{0:T(128)} %dynamic_slice.41.length, f32[592,768]{1,0:T(8,128)} %convert_multiply_fusion.back_ref, f32[2,768]{1,0:T(2,128)} %get-tuple-element.139.g_ref, ...), custom_call_target="tpu_custom_call" | custom-call | tf_op jit(solution)/shard_map/backward_block/pallas_call | solution.py:396
  283.5 57.0 %backward_block.3 = (f32[592,768]{1,0:T(8,128)}, f32[2,768]{1,0:T(2,128)}, bf16[864,128,128]{2,1,0:T(8,128)(2,1)}) custom-call(s32[432]{0:T(512)} %get-tuple-element.145.slots, s32[1]{0:T(128)S(6)} %mul.152.spare, s32[1]{0:T(128)} %dynamic_slice.41.length, f32[592,768]{1,0:T(8,128)} %get-tuple-element.71.back_ref, ...), custom_call_target="tpu_custom_call", output_to_operand_aliasing={{2}: (21, {})} | custom-call | tf_op jit(solution)/shard_map/backward_block/pallas_call | solution.py:396
  340.5 4.2 fusion.48
  346.9 5.2 fusion.47
  357.8 4.8 fusion.45
  362.6 9.5 %fusion.46 = (bf16[112,128,128]{2,1,0:T(8,128)(2,1)}, bf16[112,128,128]{2,1,0:T(8,128)(2,1)}) fusion(bf16[864,128,128]{2,1,0:T(8,128)(2,1)} %get-tuple-element.87), kind=kLoop, calls=%fused_computation.180 | loop fusion | bytes 14680064 | tf_op jit(solution)/shard_map/slice | solution.py:512
  387.7 4.5 copy.62
  394.9 38.5 %psum.15 = f32[4,768]{1,0:T(4,128)S(1)} all-reduce(f32[4,768]{1,0:T(4,128)S(1)} %pad_maximum_fusion.6), channel_id=1, replica_groups=mesh['dp'=8,'band'=4] {'dp','band'}, use_global_device_ids=true, to_apply=%region_2.3 | all-reduce | flops 3072 | bytes 24576 | tf_op jit(solution)/shard_map/psum | solution.py:614
  458.6 14.0 %collective-permute-done.10 = bf16[2,12,128,128]{3,2,1,0:T(8,128)(2,1)S(1)} collective-permute-done((bf16[2,12,128,128]{3,2,1,0:T(8,128)(2,1)S(1)}, bf16[2,12,128,128]{3,2,1,0:T(8,128)(2,1)S(1)}, u32[]{:S(2)}, u32[]{:S(2)}) %collective-permute-start.10) | collective-permute-done | bytes 786464 | tf_op jit(solution)/shard_map/ppermute | solution.py:521
  478.2 4.1 fusion
  491.4 18.6 %collective-permute-done.20 = bf16[2,16,128,128]{3,2,1,0:T(8,128)(2,1)} collective-permute-done((bf16[2,16,128,128]{3,2,1,0:T(8,128)(2,1)}, bf16[2,16,128,128]{3,2,1,0:T(8,128)(2,1)}, u32[]{:S(2)}, u32[]{:S(2)}) %collective-permute-start.20) | collective-permute-done | bytes 1048608 | tf_op jit(solution)/shard_map/ppermute | solution.py:521
  517.7 5.1 collective-permute-start.15
  529.1 5.8 collective-permute-done.15
  536.7 7.6 %collective-permute-done.30 = bf16[2,14,128,128]{3,2,1,0:T(8,128)(2,1)S(1)} collective-permute-done((bf16[2,14,128,128]{3,2,1,0:T(8,128)(2,1)S(1)}, bf16[2,14,128,128]{3,2,1,0:T(8,128)(2,1)S(1)}, u32[]{:S(2)}, u32[]{:S(2)}) %collective-permute-start.30) | collective-permute-done | bytes 917536 | tf_op jit(solution)/shard_map/ppermute | solution.py:521
  549.5 4.7 collective-permute-start.25
  561.7 6.3 collective-permute-done.40
  568.1 9.0 %collective-permute-start.35 = (bf16[28,128,128]{2,1,0:T(8,128)(2,1)S(1)}, bf16[28,128,128]{2,1,0:T(8,128)(2,1)S(1)}, u32[]{:S(2)}, u32[]{:S(2)}) collective-permute-start(bf16[28,128,128]{2,1,0:T(8,128)(2,1)S(1)} %pad_maximum_fusion.1), channel_id=1, source_target_pairs={{2,1},{6,5},{10,9},{14,13},{18,17},{22,21},{26,25},{30,29}} | collective-permute-start | bytes 2752520 | tf_op jit(solution)/shard_map/ppermute | solution.py:528
  599.4 4.7 collective-permute-start.45
  606.6 8.1 %collective-permute-done.26 = bf16[32,128,128]{2,1,0:T(8,128)(2,1)S(1)} collective-permute-done((bf16[32,128,128]{2,1,0:T(8,128)(2,1)S(1)}, bf16[32,128,128]{2,1,0:T(8,128)(2,1)S(1)}, u32[]{:S(2)}, u32[]{:S(2)}) %collective-permute-start.26) | collective-permute-done | bytes 1048608 | tf_op jit(solution)/shard_map/ppermute | solution.py:531
  624.3 7.8 %collective-permute-done.36 = bf16[28,128,128]{2,1,0:T(8,128)(2,1)S(1)} collective-permute-done((bf16[28,128,128]{2,1,0:T(8,128)(2,1)S(1)}, bf16[28,128,128]{2,1,0:T(8,128)(2,1)S(1)}, u32[]{:S(2)}, u32[]{:S(2)}) %collective-permute-start.36) | collective-permute-done | bytes 917536 | tf_op jit(solution)/shard_map/ppermute | solution.py:531
  634.9 5.5 collective-permute-done.27
  653.2 5.0 collective-permute-done.47
  666.3 12.4 %psum.14 = f32[]{:T(128)} all-reduce(f32[]{:T(128)} %multiply_reduce_fusion), channel_id=1, replica_groups=mesh['dp'=8,'band'=4] {'dp'}, use_global_device_ids=true, to_apply=%region_1.2 | all-reduce | flops 1 | bytes 8 | tf_op jit(solution)/shard_map/psum | solution.py:616
  680.7 32.6 %optimizer.1 = (f32[108,128,128]{2,1,0:T(8,128)}, f32[108,2,128,128]{3,2,1,0:T(8,128)}, f32[108,128,128]{2,1,0:T(8,128)}, bf16[108,128,128]{2,1,0:T(8,128)(2,1)}) custom-call(f32[1]{0:T(128)} %bitcast.74.factor, bf16[108,128,128]{2,1,0:T(8,128)(2,1)} %copy-done, f32[108,128,128]{2,1,0:T(8,128)} %m_ref.1, f32[108,2,128,128]{3,2,1,0:T(8,128)} %s_ref.1, ...), custom_call_target="tpu_custom_call" | custom-call | tf_op jit(solution)/shard_map/optimizer/pallas_call | solution.py:441
  (253 shorter events, 175.0 us)
Async XLA Ops:
  7.2 145.5 %all-gather.2.cloned.1.call-start = ((), (), s32[]{:S(2)}) async-start(), calls=%async_computation | async-start | bytes 31850496 | tf_op jit(solution)/shard_map/all_gather | solution.py:563
  15.5 24.6 %collective-permute-start = (bf16[2,145,768]{2,1,0:T(8,128)(2,1)}, bf16[2,145,768]{2,1,0:T(8,128)(2,1)}, u32[]{:S(2)}, u32[]{:S(2)}) collective-permute-start(bf16[2,145,768]{2,1,0:T(8,128)(2,1)} %get-tuple-element.127), channel_id=1, source_target_pairs={{0,1},{1,2},{3,0},{4,5},{5,6},{7,4},{8,9},{9,10},{11,8},{12,13},{1... | collective-permute-start | bytes 1336328 | tf_op jit(solution)/shard_map/ppermute | solution.py:465
  16.8 31.6 %collective-permute-start.1 = (bf16[2,145,768]{2,1,0:T(8,128)(2,1)S(1)}, bf16[2,145,768]{2,1,0:T(8,128)(2,1)}, u32[]{:S(2)}, u32[]{:S(2)}) collective-permute-start(bf16[2,145,768]{2,1,0:T(8,128)(2,1)S(1)} %get-tuple-element.126), channel_id=1, source_target_pairs={{0,2},{2,0},{3,1},{4,6},{6,4},{7,5},{8,10},{10,8},{11,9},{12,14},{... | collective-permute-start | bytes 1336328 | tf_op jit(solution)/shard_map/ppermute | solution.py:465
  21.2 37.1 %collective-permute-start.2 = (bf16[2,145,768]{2,1,0:T(8,128)(2,1)S(1)}, bf16[2,145,768]{2,1,0:T(8,128)(2,1)}, u32[]{:S(2)}, u32[]{:S(2)}) collective-permute-start(bf16[2,145,768]{2,1,0:T(8,128)(2,1)S(1)} %get-tuple-element.125), channel_id=1, source_target_pairs={{1,0},{2,1},{3,2},{5,4},{6,5},{7,6},{9,8},{10,9},{11,10},{13,12},{... | collective-permute-start | bytes 1336328 | tf_op jit(solution)/shard_map/ppermute | solution.py:465
  346.6 102.0 %collective-permute-start.9 = (bf16[2,2,24,128,128]{4,3,2,0,1:T(8,128)(2,1)}, bf16[2,2,24,128,128]{4,3,2,0,1:T(8,128)(2,1)}, u32[]{:S(2)}, u32[]{:S(2)}) collective-permute-start(bf16[2,2,24,128,128]{4,3,2,0,1:T(8,128)(2,1)} %copy.56), channel_id=1, source_target_pairs={{0,4},{4,0},{8,12},{12,8},{16,20},{20,16},{24,28},{28,24},{1,5},{5... | collective-permute-start | bytes 9437192 | tf_op jit(solution)/shard_map/ppermute | solution.py:512
  354.4 123.8 %collective-permute-start.19 = (bf16[2,2,32,128,128]{4,3,2,0,1:T(8,128)(2,1)}, bf16[2,2,32,128,128]{4,3,2,0,1:T(8,128)(2,1)}, u32[]{:S(2)}, u32[]{:S(2)}) collective-permute-start(bf16[2,2,32,128,128]{4,3,2,0,1:T(8,128)(2,1)} %copy.59), channel_id=1, source_target_pairs={{0,4},{4,0},{8,12},{12,8},{16,20},{20,16},{24,28},{28,24},{1,5},{5... | collective-permute-start | bytes 12582920 | tf_op jit(solution)/shard_map/ppermute | solution.py:512
  374.0 61.7 %collective-permute-start.3 = (bf16[145,768]{1,0:T(8,128)(2,1)}, bf16[145,768]{1,0:T(8,128)(2,1)}, u32[]{:S(2)}, u32[]{:S(2)}) collective-permute-start(bf16[145,768]{1,0:T(8,128)(2,1)} %get-tuple-element.137), channel_id=1, source_target_pairs={{0,1},{1,2},{2,3},{4,5},{5,6},{6,7},{8,9},{9,10},{10,11},{12,13},{... | collective-permute-start | bytes 668168 | tf_op jit(solution)/shard_map/ppermute | solution.py:476
  377.4 63.9 %collective-permute-start.4 = (bf16[145,768]{1,0:T(8,128)(2,1)}, bf16[145,768]{1,0:T(8,128)(2,1)}, u32[]{:S(2)}, u32[]{:S(2)}) collective-permute-start(bf16[145,768]{1,0:T(8,128)(2,1)} %get-tuple-element.136), channel_id=1, source_target_pairs={{0,2},{1,3},{2,0},{4,6},{5,7},{6,4},{8,10},{9,11},{10,8},{12,14},{... | collective-permute-start | bytes 668168 | tf_op jit(solution)/shard_map/ppermute | solution.py:476
  380.5 65.2 %collective-permute-start.5 = (bf16[145,768]{1,0:T(8,128)(2,1)}, bf16[145,768]{1,0:T(8,128)(2,1)S(1)}, u32[]{:S(2)}, u32[]{:S(2)}) collective-permute-start(bf16[145,768]{1,0:T(8,128)(2,1)} %get-tuple-element.135), channel_id=1, source_target_pairs={{0,3},{1,0},{2,1},{4,7},{5,4},{6,5},{8,11},{9,8},{10,9},{12,15},{1... | collective-permute-start | bytes 668168 | tf_op jit(solution)/shard_map/ppermute | solution.py:476
  448.6 41.0 %collective-permute-start.29 = (bf16[2,2,28,128,128]{4,3,2,0,1:T(8,128)(2,1)S(1)}, bf16[2,2,28,128,128]{4,3,2,0,1:T(8,128)(2,1)S(1)}, u32[]{:S(2)}, u32[]{:S(2)}) collective-permute-start(bf16[2,2,28,128,128]{4,3,2,0,1:T(8,128)(2,1)S(1)} %copy-done.8), channel_id=1, source_target_pairs={{0,4},{4,0},{8,12},{12,8},{16,20},{20,16},{24,28},{28,24},{1,5},{5... | collective-permute-start | bytes 11010056 | tf_op jit(solution)/shard_map/ppermute | solution.py:512
  452.5 20.1 %collective-permute-start.10 = (bf16[2,12,128,128]{3,2,1,0:T(8,128)(2,1)S(1)}, bf16[2,12,128,128]{3,2,1,0:T(8,128)(2,1)S(1)}, u32[]{:S(2)}, u32[]{:S(2)}) collective-permute-start(bf16[2,12,128,128]{3,2,1,0:T(8,128)(2,1)S(1)} %slice_bitcast_fusion.10), channel_id=1, source_target_pairs={{0,8},{4,12},{8,0},{12,4},{16,24},{20,28},{24,16},{28,20},{1,9},{5... | collective-permute-start | bytes 2359304 | tf_op jit(solution)/shard_map/ppermute | solution.py:521
  454.9 19.2 %collective-permute-start.12 = (bf16[2,12,128,128]{3,2,1,0:T(8,128)(2,1)S(1)}, bf16[2,12,128,128]{3,2,1,0:T(8,128)(2,1)S(1)}, u32[]{:S(2)}, u32[]{:S(2)}) collective-permute-start(bf16[2,12,128,128]{3,2,1,0:T(8,128)(2,1)S(1)} %slice_bitcast_fusion.8), channel_id=1, source_target_pairs={{0,16},{4,20},{8,24},{12,28},{16,0},{20,4},{24,8},{28,12},{1,17},{... | collective-permute-start | bytes 2359304 | tf_op jit(solution)/shard_map/ppermute | solution.py:522
  457.4 70.8 %collective-permute-start.39 = (bf16[2,2,16,128,128]{4,3,2,0,1:T(8,128)(2,1)S(1)}, bf16[2,2,16,128,128]{4,3,2,0,1:T(8,128)(2,1)S(1)}, u32[]{:S(2)}, u32[]{:S(2)}) collective-permute-start(bf16[2,2,16,128,128]{4,3,2,0,1:T(8,128)(2,1)S(1)} %copy-done.13), channel_id=1, source_target_pairs={{0,4},{4,0},{8,12},{12,8},{16,20},{20,16},{24,28},{28,24},{1,5},{5... | collective-permute-start | bytes 6291464 | tf_op jit(solution)/shard_map/ppermute | solution.py:512
  486.7 23.3 %collective-permute-start.20 = (bf16[2,16,128,128]{3,2,1,0:T(8,128)(2,1)}, bf16[2,16,128,128]{3,2,1,0:T(8,128)(2,1)}, u32[]{:S(2)}, u32[]{:S(2)}) collective-permute-start(bf16[2,16,128,128]{3,2,1,0:T(8,128)(2,1)} %slice_bitcast_fusion.2), channel_id=1, source_target_pairs={{0,8},{4,12},{8,0},{12,4},{16,24},{20,28},{24,16},{28,20},{1,9},{5... | collective-permute-start | bytes 3145736 | tf_op jit(solution)/shard_map/ppermute | solution.py:521
  488.1 22.5 %collective-permute-start.22 = (bf16[2,16,128,128]{3,2,1,0:T(8,128)(2,1)S(1)}, bf16[2,16,128,128]{3,2,1,0:T(8,128)(2,1)}, u32[]{:S(2)}, u32[]{:S(2)}) collective-permute-start(bf16[2,16,128,128]{3,2,1,0:T(8,128)(2,1)S(1)} %slice_bitcast_fusion.1), channel_id=1, source_target_pairs={{0,16},{4,20},{8,24},{12,28},{16,0},{20,4},{24,8},{28,12},{1,17},{... | collective-permute-start | bytes 3145736 | tf_op jit(solution)/shard_map/ppermute | solution.py:522
  517.7 17.3 %collective-permute-start.15 = (bf16[24,128,128]{2,1,0:T(8,128)(2,1)S(1)}, bf16[24,128,128]{2,1,0:T(8,128)(2,1)S(1)}, u32[]{:S(2)}, u32[]{:S(2)}) collective-permute-start(bf16[24,128,128]{2,1,0:T(8,128)(2,1)S(1)} %pad_maximum_fusion.2), channel_id=1, source_target_pairs={{2,1},{6,5},{10,9},{14,13},{18,17},{22,21},{26,25},{30,29}} | collective-permute-start | bytes 2359304 | tf_op jit(solution)/shard_map/ppermute | solution.py:528
  525.7 18.5 %collective-permute-start.30 = (bf16[2,14,128,128]{3,2,1,0:T(8,128)(2,1)S(1)}, bf16[2,14,128,128]{3,2,1,0:T(8,128)(2,1)S(1)}, u32[]{:S(2)}, u32[]{:S(2)}) collective-permute-start(bf16[2,14,128,128]{3,2,1,0:T(8,128)(2,1)S(1)} %slice_bitcast_fusion.6), channel_id=1, source_target_pairs={{0,8},{4,12},{8,0},{12,4},{16,24},{20,28},{24,16},{28,20},{1,9},{5... | collective-permute-start | bytes 2752520 | tf_op jit(solution)/shard_map/ppermute | solution.py:521
  526.2 19.2 %collective-permute-start.32 = (bf16[2,14,128,128]{3,2,1,0:T(8,128)(2,1)S(1)}, bf16[2,14,128,128]{3,2,1,0:T(8,128)(2,1)S(1)}, u32[]{:S(2)}, u32[]{:S(2)}) collective-permute-start(bf16[2,14,128,128]{3,2,1,0:T(8,128)(2,1)S(1)} %slice_bitcast_fusion.5), channel_id=1, source_target_pairs={{0,16},{4,20},{8,24},{12,28},{16,0},{20,4},{24,8},{28,12},{1,17},{... | collective-permute-start | bytes 2752520 | tf_op jit(solution)/shard_map/ppermute | solution.py:522
  535.4 46.8 %collective-permute-start.16 = (bf16[24,128,128]{2,1,0:T(8,128)(2,1)S(1)}, bf16[24,128,128]{2,1,0:T(8,128)(2,1)S(1)}, u32[]{:S(2)}, u32[]{:S(2)}) collective-permute-start(bf16[24,128,128]{2,1,0:T(8,128)(2,1)S(1)} %add_convert_fusion.2), channel_id=1, source_target_pairs={{1,2},{5,6},{9,10},{13,14},{17,18},{21,22},{25,26},{29,30}} | collective-permute-start | bytes 2359304 | tf_op jit(solution)/shard_map/ppermute | solution.py:531
  549.5 28.7 %collective-permute-start.25 = (bf16[32,128,128]{2,1,0:T(8,128)(2,1)S(1)}, bf16[32,128,128]{2,1,0:T(8,128)(2,1)S(1)}, u32[]{:S(2)}, u32[]{:S(2)}) collective-permute-start(bf16[32,128,128]{2,1,0:T(8,128)(2,1)S(1)} %pad_maximum_fusion), channel_id=1, source_target_pairs={{2,1},{6,5},{10,9},{14,13},{18,17},{22,21},{26,25},{30,29}} | collective-permute-start | bytes 3145736 | tf_op jit(solution)/shard_map/ppermute | solution.py:528
  554.2 25.8 %collective-permute-start.24 = (bf16[32,128,128]{2,1,0:T(8,128)(2,1)S(1)}, bf16[32,128,128]{2,1,0:T(8,128)(2,1)S(1)}, u32[]{:S(2)}, u32[]{:S(2)}) collective-permute-start(bf16[32,128,128]{2,1,0:T(8,128)(2,1)S(1)} %pad_maximum_fusion), channel_id=1, source_target_pairs={{0,1},{4,5},{8,9},{12,13},{16,17},{20,21},{24,25},{28,29}} | collective-permute-start | bytes 3145736 | tf_op jit(solution)/shard_map/ppermute | solution.py:527
  568.1 21.7 %collective-permute-start.35 = (bf16[28,128,128]{2,1,0:T(8,128)(2,1)S(1)}, bf16[28,128,128]{2,1,0:T(8,128)(2,1)S(1)}, u32[]{:S(2)}, u32[]{:S(2)}) collective-permute-start(bf16[28,128,128]{2,1,0:T(8,128)(2,1)S(1)} %pad_maximum_fusion.1), channel_id=1, source_target_pairs={{2,1},{6,5},{10,9},{14,13},{18,17},{22,21},{26,25},{30,29}} | collective-permute-start | bytes 2752520 | tf_op jit(solution)/shard_map/ppermute | solution.py:528
  582.2 17.2 %collective-permute-start.18 = (bf16[24,128,128]{2,1,0:T(8,128)(2,1)S(1)}, bf16[24,128,128]{2,1,0:T(8,128)(2,1)S(1)}, u32[]{:S(2)}, u32[]{:S(2)}) collective-permute-start(bf16[24,128,128]{2,1,0:T(8,128)(2,1)S(1)} %add_convert_fusion.2), channel_id=1, source_target_pairs={{1,0},{5,4},{9,8},{13,12},{17,16},{21,20},{25,24},{29,28}} | collective-permute-start | bytes 2359304 | tf_op jit(solution)/shard_map/ppermute | solution.py:530
  588.3 26.5 %collective-permute-start.26 = (bf16[32,128,128]{2,1,0:T(8,128)(2,1)S(1)}, bf16[32,128,128]{2,1,0:T(8,128)(2,1)S(1)}, u32[]{:S(2)}, u32[]{:S(2)}) collective-permute-start(bf16[32,128,128]{2,1,0:T(8,128)(2,1)S(1)} %add_convert_fusion), channel_id=1, source_target_pairs={{1,2},{5,6},{9,10},{13,14},{17,18},{21,22},{25,26},{29,30}} | collective-permute-start | bytes 3145736 | tf_op jit(solution)/shard_map/ppermute | solution.py:531
  596.2 35.9 %collective-permute-start.36 = (bf16[28,128,128]{2,1,0:T(8,128)(2,1)S(1)}, bf16[28,128,128]{2,1,0:T(8,128)(2,1)S(1)}, u32[]{:S(2)}, u32[]{:S(2)}) collective-permute-start(bf16[28,128,128]{2,1,0:T(8,128)(2,1)S(1)} %add_convert_fusion.1), channel_id=1, source_target_pairs={{1,2},{5,6},{9,10},{13,14},{17,18},{21,22},{25,26},{29,30}} | collective-permute-start | bytes 2752520 | tf_op jit(solution)/shard_map/ppermute | solution.py:531
  599.4 17.6 %collective-permute-start.45 = (bf16[16,128,128]{2,1,0:T(8,128)(2,1)S(1)}, bf16[16,128,128]{2,1,0:T(8,128)(2,1)S(1)}, u32[]{:S(2)}, u32[]{:S(2)}) collective-permute-start(bf16[16,128,128]{2,1,0:T(8,128)(2,1)S(1)} %pad_maximum_fusion.3), channel_id=1, source_target_pairs={{2,1},{6,5},{10,9},{14,13},{18,17},{22,21},{26,25},{30,29}} | collective-permute-start | bytes 1572872 | tf_op jit(solution)/shard_map/ppermute | solution.py:528
  614.8 19.4 %collective-permute-start.28 = (bf16[32,128,128]{2,1,0:T(8,128)(2,1)S(1)}, bf16[32,128,128]{2,1,0:T(8,128)(2,1)S(1)}, u32[]{:S(2)}, u32[]{:S(2)}) collective-permute-start(bf16[32,128,128]{2,1,0:T(8,128)(2,1)S(1)} %add_convert_fusion), channel_id=1, source_target_pairs={{1,0},{5,4},{9,8},{13,12},{17,16},{21,20},{25,24},{29,28}} | collective-permute-start | bytes 3145736 | tf_op jit(solution)/shard_map/ppermute | solution.py:530
  615.5 24.9 %collective-permute-start.27 = (bf16[32,128,128]{2,1,0:T(8,128)(2,1)S(1)}, bf16[32,128,128]{2,1,0:T(8,128)(2,1)S(1)}, u32[]{:S(2)}, u32[]{:S(2)}) collective-permute-start(bf16[32,128,128]{2,1,0:T(8,128)(2,1)S(1)} %collective-permute-done.26), channel_id=1, source_target_pairs={{2,3},{6,7},{10,11},{14,15},{18,19},{22,23},{26,27},{30,31}} | collective-permute-start | bytes 3145736 | tf_op jit(solution)/shard_map/ppermute | solution.py:532
  622.3 27.6 %collective-permute-start.38 = (bf16[28,128,128]{2,1,0:T(8,128)(2,1)S(1)}, bf16[28,128,128]{2,1,0:T(8,128)(2,1)S(1)}, u32[]{:S(2)}, u32[]{:S(2)}) collective-permute-start(bf16[28,128,128]{2,1,0:T(8,128)(2,1)S(1)} %add_convert_fusion.1), channel_id=1, source_target_pairs={{1,0},{5,4},{9,8},{13,12},{17,16},{21,20},{25,24},{29,28}} | collective-permute-start | bytes 2752520 | tf_op jit(solution)/shard_map/ppermute | solution.py:530
  623.0 18.7 %collective-permute-start.46 = (bf16[16,128,128]{2,1,0:T(8,128)(2,1)S(1)}, bf16[16,128,128]{2,1,0:T(8,128)(2,1)S(1)}, u32[]{:S(2)}, u32[]{:S(2)}) collective-permute-start(bf16[16,128,128]{2,1,0:T(8,128)(2,1)S(1)} %add_convert_fusion.3), channel_id=1, source_target_pairs={{1,2},{5,6},{9,10},{13,14},{17,18},{21,22},{25,26},{29,30}} | collective-permute-start | bytes 1572872 | tf_op jit(solution)/shard_map/ppermute | solution.py:531
  632.1 20.5 %collective-permute-start.37 = (bf16[28,128,128]{2,1,0:T(8,128)(2,1)S(1)}, bf16[28,128,128]{2,1,0:T(8,128)(2,1)S(1)}, u32[]{:S(2)}, u32[]{:S(2)}) collective-permute-start(bf16[28,128,128]{2,1,0:T(8,128)(2,1)S(1)} %collective-permute-done.36), channel_id=1, source_target_pairs={{2,3},{6,7},{10,11},{14,15},{18,19},{22,23},{26,27},{30,31}} | collective-permute-start | bytes 2752520 | tf_op jit(solution)/shard_map/ppermute | solution.py:532
  634.2 19.1 %collective-permute-start.48 = (bf16[16,128,128]{2,1,0:T(8,128)(2,1)S(1)}, bf16[16,128,128]{2,1,0:T(8,128)(2,1)S(1)}, u32[]{:S(2)}, u32[]{:S(2)}) collective-permute-start(bf16[16,128,128]{2,1,0:T(8,128)(2,1)S(1)} %add_convert_fusion.3), channel_id=1, source_target_pairs={{1,0},{5,4},{9,8},{13,12},{17,16},{21,20},{25,24},{29,28}} | collective-permute-start | bytes 1572872 | tf_op jit(solution)/shard_map/ppermute | solution.py:530
  (51 other events, 490.6 us)
Sparse Core Ops, SparseCore 0:
  13.0 139.6 all-gather.1

commit v3 on v1

--- a/solution.py
+++ b/solution.py
@@ -76,10 +76,14 @@
     return r * t - m * (r * r * r * dot), jnp.sum(u * m * r, 0, keepdims=True)
 
 
+def copies(pairs, sem):
+    return [pltpu.make_async_copy(src, dst, sem.at[i]) for i, (src, dst) in enumerate(pairs)]
+
+
 def forward_kernel(
     slots, length, x_ref, g_ref, cos_ref, sin_ref, w_hbm,
-    xn_ref, normed_ref, q_ref, k_ref, v_ref, st_ref, mixed_ref, mid_ref, n2_ref, gu_ref,
-    wqkv_o, wout_o, wgu_o, wd_o,
+    xn_ref, normed_o, q_o, k_o, v_o, st_o, mixed_o, mid_o, n2_o, gu_o, wqkv_o, wout_o, wgu_o, wd_o,
+    normed_ref, q_ref, k_ref, v_ref, st_ref, mixed_ref, mid_ref, n2_ref, gu_ref,
     wqkv, wout, wgu, wd, bias, sem_in, sem_out,
 ):
     rows = x_ref.shape[0]
@@ -101,21 +105,25 @@
     def arrive(m):
         pltpu.make_async_copy(held[m], held[m], sem_in.at[m]).wait()
 
-    outs = (wqkv_o, wout_o, wgu_o, wd_o)
-
-    def leave(m):
-        return pltpu.make_async_copy(held[m], outs[m], sem_out.at[m])
-
+    saves = copies(
+        [
+            (normed_ref, normed_o), (q_ref, q_o), (k_ref, k_o), (v_ref, v_o), (st_ref, st_o),
+            (mixed_ref, mixed_o), (mid_ref, mid_o), (n2_ref, n2_o), (gu_ref, gu_o),
+            (wqkv, wqkv_o), (wout, wout_o), (wgu, wgu_o), (wd, wd_o),
+        ],
+        sem_out,
+    )
     query = lax.broadcasted_iota(jnp.int32, bias.shape, 0)
     key = lax.broadcasted_iota(jnp.int32, bias.shape, 1)
     bias[...] = jnp.where((key <= query) & (key < length[0]), 0.0, masked_score)
     x = x_ref[...]
     normed_ref[...] = (x * rms(x) * g_ref[0:1, :]).astype(bf16)
+    saves[0].start()
     tail = key_rows - rows
     for ref in (q_ref, k_ref, v_ref):
         ref[rows:, :] = jnp.zeros((tail, D), bf16)
     arrive(0)
-    leave(0).start()
+    saves[9].start()
 
     @pl.loop(0, 2)
     def _(part):
@@ -134,6 +142,8 @@
                 k_ref[0:rows, p * PAIR : (p + 1) * PAIR] = rot
 
     v_ref[0:rows, :] = nn(normed_ref[...], wqkv[:, 2 * D :]).astype(bf16)
+    for i in (1, 2, 3):
+        saves[i].start()
     st_ref[...] = jnp.zeros(st_ref.shape, f32)
 
     @pl.loop(0, HEADS // 2)
@@ -169,15 +179,19 @@
                 lane == 2 * p, first, jnp.where(lane == 2 * p + 1, second, old)
             )
 
+    saves[4].start()
+    saves[5].start()
     arrive(1)
-    leave(1).start()
+    saves[10].start()
     middle = x_ref[...] + nn(mixed_ref[...], wout[...])
     mid_ref[...] = middle
+    saves[6].start()
     n2_ref[...] = (middle * rms(middle) * g_ref[1:2, :]).astype(bf16)
+    saves[7].start()
     arrive(2)
-    leave(2).start()
+    saves[11].start()
     arrive(3)
-    leave(3).start()
+    saves[12].start()
     xn_ref[...] = mid_ref[...]
 
     @pl.loop(0, FF // FF_STEP)
@@ -190,65 +204,56 @@
         gu_ref[:, pl.ds(FF + at, FF_STEP)] = up.astype(bf16)
         xn_ref[...] += nn(act, wd[pl.ds(at, FF_STEP), :])
 
-    for m in range(4):
-        leave(m).wait()
-
-
-def backward_kernel(
-    slots, spare, length, back_ref, g_ref, cos_ref, sin_ref,
-    x_ref, normed_ref, q_ref, k_ref, v_ref, st_ref, mixed_ref, mid_ref, n2_ref, gu_ref,
-    wqkv_i, wout_i, wgu_i, wd_i, *rest,
+    saves[8].start()
+    for save in saves:
+        save.wait()
+
+
+def put_tiles(places, m, grad, zones, outs, sem, i0, i1, j0, count_j):
+    @pl.loop(i0, i1)
+    def _(i):
+        for jj in range(count_j):
+            j = j0 + jj
+            place = places[OFFSETS[m] + i * GRIDS[m][1] + j]
+            tile = grad.at[
+                pl.ds(pl.multiple_of(i * BLOCK, BLOCK), BLOCK),
+                pl.ds(pl.multiple_of(j * BLOCK, BLOCK), BLOCK),
+            ]
+            start = 0
+            for size, out in zip(zones, outs):
+                if len(zones) == 1:
+                    pltpu.make_async_copy(tile, out.at[place], sem).start()
+                else:
+
+                    @pl.when((place >= start) & (place < start + size))
+                    def _(tile=tile, out=out, place=place, start=start):
+                        pltpu.make_async_copy(tile, out.at[place - start], sem).start()
+
+                start += size
+
+
+def back_ffn_kernel(
+    zones, begun, places, spare, back_ref, g_ref, mid_i, n2_i, gu_i, wgu_i, wd_i, *rest
 ):
-    (
-        dx_ref, gain_ref, tiles_out,
-        wqkv, wout, wgu, wd, gqkv, gout, ggu, gd, zero, bias, turned, sums, big, mixed_back, dproj,
-        sem_in, sem_out, sem_zero,
-    ) = rest[-21:]
-    rows = x_ref.shape[0]
-    key_rows = q_ref.shape[0]
-    held = (wqkv, wout, wgu, wd)
-    given = (wqkv_i, wout_i, wgu_i, wd_i)
-
-    def arrive(m):
-        return pltpu.make_async_copy(given[m], held[m], sem_in.at[m])
-
-    for m in (3, 2, 1, 0):
-        arrive(m).start()
-    grads = (gqkv, gout, ggu, gd)
-
-    def send(m, i0, i1, j0, count_j):
-        @pl.loop(i0, i1)
-        def _(i):
-            for jj in range(count_j):
-                j = j0 + jj
-                slot = slots[OFFSETS[m] + i * GRIDS[m][1] + j]
-                pltpu.make_async_copy(
-                    grads[m].at[
-                        pl.ds(pl.multiple_of(i * BLOCK, BLOCK), BLOCK),
-                        pl.ds(pl.multiple_of(j * BLOCK, BLOCK), BLOCK),
-                    ],
-                    tiles_out.at[slot],
-                    sem_out.at[m],
-                ).start()
-
+    rest = rest[begun:]
+    mid_ref_out, gain_ref = rest[:2]
+    outs = rest[2 : 2 + len(zones)]
+    mid_ref, n2_ref, gu_ref, wgu, wd, ggu, gd, big, zero, sem_in, sem_out, sem_zero = rest[2 + len(zones) :]
+    loads = copies([(wd_i, wd), (gu_i, gu_ref), (n2_i, n2_ref), (wgu_i, wgu), (mid_i, mid_ref)], sem_in)
+    for load in loads:
+        load.start()
     spares = spare.shape[0] - 1
     if spares > 0:
         zero[...] = jnp.zeros(zero.shape, bf16)
 
         @pl.loop(0, spares)
         def _(i):
-            pltpu.make_async_copy(zero, tiles_out.at[spare[i]], sem_zero).start()
-
-    key = lax.broadcasted_iota(jnp.int32, bias.shape, 0)
-    query = lax.broadcasted_iota(jnp.int32, bias.shape, 1)
-    bias[...] = jnp.where((key <= query) & (key < length[0]), 0.0, masked_score)
-    levels = st_ref[...].T
-    for h in range(HEADS):
-        turned[h] = levels[h : h + 1, :]
+            pltpu.make_async_copy(zero, outs[0].at[spare[i]], sem_zero).start()
+
     big[...] = jnp.zeros(big.shape, f32)
-    back_b = back_ref[...].astype(bf16)
-    arrive(3).wait()
-    arrive(2).wait()
+    for load in loads[:4]:
+        load.wait()
+    put = functools.partial(put_tiles, places)
 
     @pl.loop(0, FF // FF_STEP)
     def _(t):
@@ -268,20 +273,62 @@
         ggu[:, here] = tn(n2_ref[...], d_gate).astype(bf16)
         ggu[:, there] = tn(n2_ref[...], d_up).astype(bf16)
         per = FF_STEP // BLOCK
-        send(3, t * per, (t + 1) * per, 0, D // BLOCK)
-        send(2, 0, D // BLOCK, t * per, per)
-        send(2, 0, D // BLOCK, FF // BLOCK + t * per, per)
+        put(3, gd, zones, outs, sem_out.at[1], t * per, (t + 1) * per, 0, D // BLOCK)
+        put(2, ggu, zones, outs, sem_out.at[0], 0, D // BLOCK, t * per, per)
+        put(2, ggu, zones, outs, sem_out.at[0], 0, D // BLOCK, FF // BLOCK + t * per, per)
         big[...] += nt(d_gate, wgu[:, here]) + nt(d_up, wgu[:, there])
 
-    step, gain_two = rms_back(big[...], mid_ref[...], g_ref[1:2, :])
-    gain_ref[1:2, :] = gain_two
-    dx_ref[...] = back_ref[...] + step
-    arrive(1).wait()
-    back_attn = dx_ref[...].astype(bf16)
-    gout[...] = tn(mixed_ref[...], back_attn).astype(bf16)
-    send(1, 0, D // BLOCK, 0, D // BLOCK)
+    loads[4].wait()
+    step, gain = rms_back(big[...], mid_ref[...], g_ref[...])
+    gain_ref[...] = gain
+    mid_ref_out[...] = back_ref[...] + step
+    pltpu.make_async_copy(ggu, ggu, sem_out.at[0]).wait()
+    pltpu.make_async_copy(gd, gd, sem_out.at[1]).wait()
+    if spares > 0:
+
+        @pl.loop(0, spares)
+        def _(i):
+            pltpu.make_async_copy(zero, outs[0].at[spare[i]], sem_zero).wait()
+
+
+def back_attention_kernel(
+    zones, begun, places, length, back_ref, cos_ref, sin_ref,
+    q_i, k_i, v_i, st_i, mixed_i, wout_i, *rest
+):
+    rest = rest[begun:]
+    dproj = rest[0]
+    outs = rest[1 : 1 + len(zones)]
+    (
+        q_ref, k_ref, v_ref, st_ref, mixed_ref, wout,
+        gout, bias, turned, sums, mixed_back, sem_in, sem_out,
+    ) = rest[1 + len(zones) :]
+    rows = back_ref.shape[0]
+    key_rows = q_ref.shape[0]
+    loads = copies(
+        [
+            (wout_i, wout), (mixed_i, mixed_ref), (q_i, q_ref), (k_i, k_ref), (v_i, v_ref),
+            (st_i, st_ref),
+        ],
+        sem_in,
+    )
+    for load in loads:
+        load.start()
+    put = functools.partial(put_tiles, places)
+    key = lax.broadcasted_iota(jnp.int32, bias.shape, 0)
+    query = lax.broadcasted_iota(jnp.int32, bias.shape, 1)
+    bias[...] = jnp.where((key <= query) & (key < length[0]), 0.0, masked_score)
+    back_attn = back_ref[...].astype(bf16)
+    loads[0].wait()
     mixed_back[0:rows, :] = nt(back_attn, wout[...]).astype(bf16)
     mixed_back[rows:, :] = jnp.zeros((key_rows - rows, D), bf16)
+    loads[1].wait()
+    gout[...] = tn(mixed_ref[...], back_attn).astype(bf16)
+    put(1, gout, zones, outs, sem_out, 0, D // BLOCK, 0, D // BLOCK)
+    for load in loads[2:]:
+        load.wait()
+    levels = st_ref[...].T
+    for h in range(HEADS):
+        turned[h] = levels[h : h + 1, :]
 
     @pl.loop(0, HEADS // 2)
     def _(p):
@@ -319,41 +366,59 @@
             ).astype(bf16)
         dproj[:, pl.ds(pl.multiple_of(2 * D + p * PAIR, PAIR), PAIR)] = sums[2, 0:rows, :].astype(bf16)
 
-    arrive(0).wait()
+    pltpu.make_async_copy(gout, gout, sem_out).wait()
+
+
+def back_qkv_kernel(zones, begun, places, back_ref, g_ref, dproj, x_i, normed_i, wqkv_i, *rest):
+    rest = rest[begun:]
+    dx_ref, gain_ref = rest[:2]
+    outs = rest[2 : 2 + len(zones)]
+    x_ref, normed_ref, wqkv, gqkv, big, sem_in, sem_out = rest[2 + len(zones) :]
+    loads = copies([(normed_i, normed_ref), (wqkv_i, wqkv), (x_i, x_ref)], sem_in)
+    for load in loads:
+        load.start()
     big[...] = jnp.zeros(big.shape, f32)
+    loads[0].wait()
+    loads[1].wait()
 
     @pl.loop(0, 3)
     def _(part):
         cols = pl.ds(pl.multiple_of(part * D, D), D)
         gqkv[:, cols] = tn(normed_ref[...], dproj[:, cols]).astype(bf16)
-        send(0, 0, D // BLOCK, part * (D // BLOCK), D // BLOCK)
+        put_tiles(
+            places, 0, gqkv, zones, outs, sem_out, 0, D // BLOCK, part * (D // BLOCK), D // BLOCK
+        )
         big[...] += nt(dproj[:, cols], wqkv[:, cols])
 
-    step, gain_one = rms_back(big[...], x_ref[...], g_ref[0:1, :])
-    gain_ref[0:1, :] = gain_one
-    dx_ref[...] += step
-    for m in range(4):
-        pltpu.make_async_copy(grads[m], grads[m], sem_out.at[m]).wait()
-    if spares > 0:
-
-        @pl.loop(0, spares)
-        def _(i):
-            pltpu.make_async_copy(zero, tiles_out.at[spare[i]], sem_zero).wait()
+    loads[2].wait()
+    step, gain = rms_back(big[...], x_ref[...], g_ref[...])
+    gain_ref[...] = gain
+    dx_ref[...] = back_ref[...] + step
+    pltpu.make_async_copy(gqkv, gqkv, sem_out).wait()
 
 
 def weight_shapes():
     return [(r * BLOCK, c * BLOCK) for r, c in GRIDS]
+
+
+VMEM = pl.BlockSpec(memory_space=pltpu.VMEM)
+SMEM = pl.BlockSpec(memory_space=pltpu.SMEM)
+HBM = pl.BlockSpec(memory_space=pl.ANY)
+
+
+def like(struct):
+    return pltpu.VMEM(struct.shape, struct.dtype)
+
+
+def cost(flops, bytes_accessed):
+    return pl.CostEstimate(flops=flops, bytes_accessed=bytes_accessed, transcendentals=0)
 
 
 def forward_layer(slots, length, x, gains, cos, sin, gathered):
     rows = x.shape[0]
     key_rows = round_up(rows, BLOCK)
-    vmem = pl.BlockSpec(memory_space=pltpu.VMEM)
-    smem = pl.BlockSpec(memory_space=pltpu.SMEM)
-    hbm = pl.BlockSpec(memory_space=pl.ANY)
     S = jax.ShapeDtypeStruct
-    out_shape = [
-        S((rows, D), f32),
+    saved = [
         S((rows, D), bf16),
         S((key_rows, D), bf16),
         S((key_rows, D), bf16),
@@ -366,62 +431,109 @@
     ] + [S(s, bf16) for s in weight_shapes()]
     return pl.pallas_call(
         forward_kernel,
-        out_shape=out_shape,
-        in_specs=[smem, smem, vmem, vmem, vmem, vmem, hbm],
-        out_specs=[vmem] * 10 + [hbm] * 4,
-        scratch_shapes=[pltpu.VMEM(s, bf16) for s in weight_shapes()]
+        out_shape=[S((rows, D), f32)] + saved,
+        in_specs=[SMEM, SMEM, VMEM, VMEM, VMEM, VMEM, HBM],
+        out_specs=[VMEM] + [HBM] * 13,
+        scratch_shapes=[like(s) for s in saved]
         + [
             pltpu.VMEM((rows, key_rows), f32),
             pltpu.SemaphoreType.DMA((4,)),
-            pltpu.SemaphoreType.DMA((4,)),
+            pltpu.SemaphoreType.DMA((13,)),
         ],
         compiler_params=pltpu.CompilerParams(vmem_limit_bytes=VMEM_BYTES),
+        cost_estimate=cost(2 * rows * PER_LAYER * BLOCK * BLOCK, 40 * 2**20),
         name="forward_block",
     )(slots, length, x, gains, cos, sin, gathered)
 
 
-def backward_layer(slots, spare, length, back, gains, cos, sin, x, saved, slot_count, tiles):
-    rows = x.shape[0]
+def tile_outputs(zones):
+    return [jax.ShapeDtypeStruct((size, BLOCK, BLOCK), bf16) for size in zones]
+
+
+def back_ffn(places, spare, back, gain, saved, zones, begun):
+    rows = back.shape[0]
+    S = jax.ShapeDtypeStruct
+    args = (places, spare, back, gain) + tuple(saved)
+    first = 2 + len(zones) - len(begun)
+    wgu, wd = saved[3], saved[4]
+    return pl.pallas_call(
+        functools.partial(back_ffn_kernel, zones, len(begun)),
+        out_shape=[S((rows, D), f32), S((1, D), f32)] + tile_outputs(zones),
+        in_specs=[SMEM] * 2 + [VMEM] * 2 + [HBM] * (5 + len(begun)),
+        out_specs=[VMEM, VMEM] + [HBM] * len(zones),
+        input_output_aliases={len(args) + i: first + i for i in range(len(begun))},
+        scratch_shapes=[like(s) for s in saved]
+        + [like(wgu), like(wd)]
+        + [
+            pltpu.VMEM((rows, D), f32),
+            pltpu.VMEM((BLOCK, BLOCK), bf16),
+            pltpu.SemaphoreType.DMA((5,)),
+            pltpu.SemaphoreType.DMA((2,)),
+            pltpu.SemaphoreType.DMA,
+        ],
+        compiler_params=pltpu.CompilerParams(vmem_limit_bytes=VMEM_BYTES),
+        cost_estimate=cost(4 * rows * (COUNTS[2] + COUNTS[3]) * BLOCK * BLOCK, 30 * 2**20),
+        name="backward_feed_forward",
+    )(*args, *begun)
+
+
+def back_attention(places, length, back, cos, sin, saved, zones, begun):
+    rows = back.shape[0]
     key_rows = round_up(rows, BLOCK)
-    vmem = pl.BlockSpec(memory_space=pltpu.VMEM)
-    smem = pl.BlockSpec(memory_space=pltpu.SMEM)
-    hbm = pl.BlockSpec(memory_space=pl.ANY)
     S = jax.ShapeDtypeStruct
-    args = (slots, spare, length, back, gains, cos, sin, x) + tuple(saved)
-    aliases = {}
-    if tiles is not None:
-        aliases = {len(args): 2}
-        args = args + (tiles,)
-    shapes = weight_shapes()
+    args = (places, length, back, cos, sin) + tuple(saved)
+    first = 1 + len(zones) - len(begun)
     return pl.pallas_call(
-        backward_kernel,
-        out_shape=[S((rows, D), f32), S((2, D), f32), S((slot_count, BLOCK, BLOCK), bf16)],
-        in_specs=[smem] * 3 + [vmem] * 14 + [hbm] * (len(args) - 17),
-        out_specs=[vmem, vmem, hbm],
-        input_output_aliases=aliases,
-        scratch_shapes=[pltpu.VMEM(s, bf16) for s in shapes]
-        + [pltpu.VMEM(s, bf16) for s in shapes]
+        functools.partial(back_attention_kernel, zones, len(begun)),
+        out_shape=[S((rows, 3 * D), bf16)] + tile_outputs(zones),
+        in_specs=[SMEM] * 2 + [VMEM] * 3 + [HBM] * (6 + len(begun)),
+        out_specs=[VMEM] + [HBM] * len(zones),
+        input_output_aliases={len(args) + i: first + i for i in range(len(begun))},
+        scratch_shapes=[like(s) for s in saved]
         + [
-            pltpu.VMEM((BLOCK, BLOCK), bf16),
+            like(saved[5]),
             pltpu.VMEM((key_rows, key_rows), f32),
             pltpu.VMEM((HEADS, 1, key_rows), f32),
             pltpu.VMEM((3, key_rows, PAIR), f32),
-            pltpu.VMEM((rows, D), f32),
             pltpu.VMEM((key_rows, D), bf16),
-            pltpu.VMEM((rows, 3 * D), bf16),
-            pltpu.SemaphoreType.DMA((4,)),
-            pltpu.SemaphoreType.DMA((4,)),
+            pltpu.SemaphoreType.DMA((6,)),
             pltpu.SemaphoreType.DMA,
         ],
         compiler_params=pltpu.CompilerParams(vmem_limit_bytes=VMEM_BYTES),
-        name="backward_block",
-    )(*args)
-
-
-def optimizer_kernel(factor, g_ref, m_ref, s_ref, r_ref, wg_ref, ns_ref, nm_ref, nc_ref):
+        cost_estimate=cost(4 * rows * COUNTS[1] * BLOCK * BLOCK + 20 * rows * rows * D, 30 * 2**20),
+        name="backward_attention",
+    )(*args, *begun)
+
+
+def back_qkv(places, back, gain, d_projected, saved, zones, begun):
+    rows = back.shape[0]
+    S = jax.ShapeDtypeStruct
+    args = (places, back, gain, d_projected) + tuple(saved)
+    first = 2 + len(zones) - len(begun)
+    return pl.pallas_call(
+        functools.partial(back_qkv_kernel, zones, len(begun)),
+        out_shape=[S((rows, D), f32), S((1, D), f32)] + tile_outputs(zones),
+        in_specs=[SMEM] + [VMEM] * 3 + [HBM] * (3 + len(begun)),
+        out_specs=[VMEM, VMEM] + [HBM] * len(zones),
+        input_output_aliases={len(args) + i: first + i for i in range(len(begun))},
+        scratch_shapes=[like(s) for s in saved]
+        + [
+            like(saved[2]),
+            pltpu.VMEM((rows, D), f32),
+            pltpu.SemaphoreType.DMA((3,)),
+            pltpu.SemaphoreType.DMA,
+        ],
+        compiler_params=pltpu.CompilerParams(vmem_limit_bytes=VMEM_BYTES),
+        cost_estimate=cost(4 * rows * COUNTS[0] * BLOCK * BLOCK, 20 * 2**20),
+        name="backward_qkv",
+    )(*args, *begun)
+
+
+def optimizer_kernel(factor, rank, g_ref, m_ref, s_ref, r_ref, wg_ref, ns_ref, nm_ref, nc_ref):
     f = factor[0]
-    for i in range(g_ref.shape[0]):
-        gb = g_ref[i]
+    count = m_ref.shape[0]
+    for i in range(count):
+        gb = g_ref[rank[pl.program_id(0) * count + i]]
         wg_ref[i] = gb.astype(f32) * f
         half = (1.0 - decay_rate) * f * f
         ns_ref[i, 0] = decay_rate * s_ref[i, 0] + half * nt(gb, gb)
@@ -432,7 +544,7 @@
         nc_ref[i] = new.astype(bf16)
 
 
-def optimizer(factor, owned, master, statistics, inverse_roots):
+def optimizer(factor, rank, owned, master, statistics, inverse_roots):
     count = owned.shape[0]
     per = max(n for n in range(1, 13) if count % n == 0)
     S = jax.ShapeDtypeStruct
@@ -447,11 +559,11 @@
             S(master.shape, f32),
             S(master.shape, bf16),
         ],
-        in_specs=[pl.BlockSpec(memory_space=pltpu.SMEM), one, one, two, two],
+        in_specs=[SMEM, SMEM, VMEM, one, two, two],
         out_specs=[one, two, one, one],
         compiler_params=pltpu.CompilerParams(vmem_limit_bytes=VMEM_BYTES),
         name="optimizer",
-    )(factor, owned, master, statistics, inverse_roots)
+    )(factor, rank, owned, master, statistics, inverse_roots)
 
 
 def to_images(local, bands, band):
@@ -476,6 +588,86 @@
             block = lax.ppermute(block, "band", pairs)
         local = lax.dynamic_update_index_in_dim(local, block, (band - shift) % bands, 0)
     return local[:images]
+
+
+EARLY = 38
+LATE = (30, 24, 16)
+
+
+def relative_places(slot_of_block, per_owner, me):
+    blocks = slot_of_block.shape[0]
+    block_of_slot = jnp.zeros((blocks,), jnp.int32).at[slot_of_block].set(
+        jnp.arange(blocks, dtype=jnp.int32)
+    )
+    by_owner = block_of_slot.reshape(-1, per_owner)
+    rank = jnp.sum(by_owner[:, None, :] < by_owner[:, :, None], -1, dtype=jnp.int32)
+    early = per_owner - EARLY
+    clean = jnp.all(jnp.where(rank >= early, by_owner >= PER_LAYER, True))
+    relative = (jnp.arange(by_owner.shape[0], dtype=jnp.int32) ^ me)[:, None]
+    core, x, y = relative % 2, relative // 2 % 2, relative // 4
+    place = jnp.zeros_like(rank)
+    zone_sizes = (4 * EARLY, 4 * EARLY, 4 * early, 4 * early)
+    chunks = [(early, EARLY, 0, 0)]
+    start = 0
+    for size in LATE:
+        chunks.append((start, size, 2, 4 * start))
+        start += size
+    for start, size, zone, inside in chunks:
+        half = size // 2
+        at = rank - start
+        spot = jnp.where(at < half, (x * 2 + y) * half + at, 4 * half + (y * 2 + x) * half + at - half)
+        base = jnp.where(core == 0, sum(zone_sizes[:zone]), sum(zone_sizes[: zone + 1]))
+        place = jnp.where((at >= 0) & (at < size), base + inside + spot, place)
+    return place.reshape(-1)[slot_of_block], rank, clean, zone_sizes
+
+
+CORE = [(i, i ^ 1) for i in range(8)]
+ALONG_X = [(i, i ^ 2) for i in range(8)]
+ALONG_Y = [(i, i ^ 4) for i in range(8)]
+
+
+def wide(t, lo, hi):
+    return t[lo:hi].astype(f32)
+
+
+def plane_start(kept, received, gate=None, beside=None):
+    half = kept.shape[0] // 8
+
+    def chip(lo, hi):
+        return wide(kept, lo * half, hi * half) + wide(received, lo * half, hi * half)
+
+    send_x, send_y = chip(2, 4).astype(bf16), chip(6, 8).astype(bf16)
+    if gate is not None:
+        send_x, send_y, _ = lax.optimization_barrier((send_x, send_y, gate))
+    if beside is not None:
+        send_x, send_y, beside = lax.optimization_barrier((send_x, send_y, beside))
+    going = (chip, half, lax.ppermute(send_x, "dp", ALONG_X), lax.ppermute(send_y, "dp", ALONG_Y))
+    return going if beside is None else (going, beside)
+
+
+def plane_turn(chip, half, from_x, from_y):
+    send_y = (chip(1, 2) + wide(from_x, half, 2 * half)).astype(bf16)
+    send_x = (chip(5, 6) + wide(from_y, half, 2 * half)).astype(bf16)
+    return lax.ppermute(send_x, "dp", ALONG_X), lax.ppermute(send_y, "dp", ALONG_Y)
+
+
+def plane_end(chip, half, from_x, from_y, later_x, later_y):
+    one = chip(0, 1) + wide(from_x, 0, half) + later_y.astype(f32)
+    two = chip(4, 5) + wide(from_y, 0, half) + later_x.astype(f32)
+    return jnp.concatenate([one, two], 0).astype(bf16)
+
+
+def sum_bands(plane, band):
+    kind = plane.dtype
+    up = lax.ppermute(plane, "band", [(0, 1)])
+    down = lax.ppermute(plane, "band", [(2, 1)])
+    total = (plane.astype(f32) + up.astype(f32) + down.astype(f32)).astype(kind)
+    to_first = lax.ppermute(total, "band", [(1, 0)])
+    to_third = lax.ppermute(total, "band", [(1, 2)])
+    to_last = lax.ppermute(to_third, "band", [(2, 3)])
+    total = jnp.where(band == 0, to_first, total)
+    total = jnp.where(band == 2, to_third, total)
+    return jnp.where(band == 3, to_last, total)
 
 
 def rope_tables(rows):
@@ -532,26 +724,111 @@
     )
 
     back = back_rows.astype(f32) * valid[:, None]
-    tiles = None
-    gain_parts = [None] * LAYERS
-    for layer in range(LAYERS - 1, -1, -1):
-        slots = slot_of_block[layer * PER_LAYER : (layer + 1) * PER_LAYER]
-        gains = gain_values[2 * layer : 2 * layer + 2]
-        back, gain_parts[layer], tiles = backward_layer(
-            slots, spare if layer == LAYERS - 1 else spare[-1:], length, back, gains, cos, sin,
-            inputs[layer], saves[layer], slot_count, tiles,
+    per_owner = master.shape[0]
+    me = lax.axis_index("dp")
+    by_permutes = (
+        lax.axis_size("dp") == 8
+        and bands == 4
+        and images == 3
+        and slot_count == slot_of_block.shape[0]
+        and per_owner == EARLY + sum(LATE)
+    )
+    if by_permutes:
+        places, ranks, clean, sizes = relative_places(slot_of_block, per_owner, me)
+        rank = lax.dynamic_index_in_dim(ranks, me, 0, keepdims=False)
+        zones_top, zones_bottom = sizes, (sizes[0] + sizes[1],) + sizes[2:]
+    else:
+        places, rank = slot_of_block, jnp.arange(per_owner, dtype=jnp.int32)
+        zones_top = zones_bottom = (slot_count,)
+
+    def backward(layer, back, zones, tiles, ahead=lambda back: back, later=lambda back: back):
+        normed, q, k, v, st, mixed, mid, n2, gu, wqkv, wout, wgu, wd = saves[layer]
+        slots = places[layer * PER_LAYER : (layer + 1) * PER_LAYER]
+        fill = spare if layer == LAYERS - 1 else spare[-1:]
+        back, gain_two, *tiles = back_ffn(
+            slots, fill, back, gain_values[2 * layer + 1 : 2 * layer + 2], (mid, n2, gu, wgu, wd),
+            zones, tiles,
         )
+        back = ahead(back)
+        d_projected, *tiles = back_attention(
+            slots, length, back, cos, sin, (q, k, v, st, mixed, wout), zones, tiles
+        )
+        back = later(back)
+        back, gain_one, *tiles = back_qkv(
+            slots, back, gain_values[2 * layer : 2 * layer + 1], d_projected,
+            (inputs[layer], normed, wqkv), zones, tiles,
+        )
+        return back, [gain_one, gain_two], tiles
+
+    def after(value, *done):
+        return lax.optimization_barrier((value,) + done)[0]
+
+    back, gains_top, tiles = backward(1, back, zones_top, [])
+    if by_permutes:
+        early_kept, early_sent, kept, sent = tiles
+        early = {"output": layer_output}
+        early["core"] = lax.ppermute(early_sent, "dp", CORE)
+
+        def ahead(back):
+            back, early["output"] = lax.optimization_barrier((back, early["output"]))
+            early["plane"], back = plane_start(early_kept, early["core"], beside=back)
+            return back
+
+        def later(back):
+            chip, half, from_x, from_y = early["plane"]
+            back, from_x, from_y = lax.optimization_barrier((back, from_x, from_y))
+            early["plane"] = (chip, half, from_x, from_y)
+            return back
+
+        back, gains_bottom, tiles = backward(0, back, zones_bottom, [kept, sent], ahead, later)
+        layer_output = early["output"]
+        early_late, kept, sent = tiles
+        chunks, start = [], 0
+        for size in LATE:
+            chunks.append((kept[4 * start : 4 * (start + size)], sent[4 * start : 4 * (start + size)]))
+            start += size
+        from_core = [lax.ppermute(chunk[1], "dp", CORE) for chunk in chunks]
+        turned = plane_turn(*early["plane"])
+        gate = turned
+        owned = [None] * len(chunks) + [sum_bands(plane_end(*early["plane"], *turned), band)]
+        gain_total = sum_bands(jnp.concatenate(gains_bottom + gains_top, 0), band)
+        for i, (chunk, received) in enumerate(zip(chunks, from_core)):
+            going = plane_start(chunk[0], received, gate)
+            gate = plane_turn(*going)
+            owned[i] = sum_bands(plane_end(*going, *gate), band)
+            if i == 0:
+                back = after(back, going[2], going[3])
+
+        order = jnp.argsort(places)[: sizes[0] + sizes[1]]
+
+        def again(trip, total):
+            _, late, first, second = lax.optimization_barrier(
+                (trip, early_late, early_kept, early_sent)
+            )
+            mine = (order < PER_LAYER)[:, None, None]
+            first = jnp.where(mine[: sizes[0]], late[: sizes[0]], first)
+            second = jnp.where(mine[sizes[0] :], late[sizes[0] :], second)
+            going = plane_start(first, lax.ppermute(second, "dp", CORE))
+            return sum_bands(plane_end(*going, *plane_turn(*going)), band)
+
+        owned[-1] = lax.fori_loop(0, jnp.where(clean, 0, 1), again, owned[-1])
+        owned = jnp.concatenate(owned, 0)
+    else:
+        back, gains_bottom, tiles = backward(0, back, zones_bottom, tiles)
+        owned = lax.psum_scatter(tiles[0], "dp", scatter_dimension=0, tiled=True)
+        owned = lax.psum(owned, "band")
+        gain_total = lax.psum(jnp.concatenate(gains_bottom + gains_top, 0), "band")
     input_grad = to_bands(back[:seq].astype(bf16).reshape(bands, band_rows, D), images, bands, band)
 
-    owned = lax.psum_scatter(tiles, "dp", scatter_dimension=0, tiled=True)
-    owned = lax.psum(owned, "band")
-    gain_total = lax.psum(jnp.concatenate(gain_parts, 0), ("dp", "band"))
     owned_f = owned.astype(f32)
-    owned_squares = lax.psum(jnp.sum(owned_f * owned_f), "dp")
+    squares = jnp.sum(owned_f * owned_f).reshape(1)
+    summed = lax.psum(jnp.concatenate([gain_total.reshape(-1), squares]), "dp")
+    gain_total = summed[:-1].reshape(gain_values.shape)
+    owned_squares = summed[-1]
     grad_norm = jnp.sqrt(owned_squares + jnp.sum(gain_total * gain_total))
     factor = jnp.minimum(1.0, clip_limit / grad_norm)
     weight_grads, new_statistics, new_master, master_copy = optimizer(
-        factor.reshape(1), owned, master, statistics, inverse_roots
+        factor.reshape(1), rank, owned, master, statistics, inverse_roots
     )
     gain_grads = gain_total * factor
     new_moments = decay_rate * gain_moments + (1.0 - decay_rate) * gain_grads * gain_grads

time: 753 us -> 712 us (0.946)
  waiting for transfers between devices: 343 us -> 223 us
  blocking collectives: 102 us -> 22.3 us
  starting transfers between devices: 29.3 us -> 93.6 us
  other arithmetic: 15.4 us -> 72.7 us
  local copies, waits for them, and re-layouts: 19.2 us -> 41 us
  Pallas kernels: 218 us -> 232 us
    reduce_scatter x1 -> x0, waiting for transfers between devices: 173 us -> none  [shards(): owned = lax.psum_scatter(tiles, 'dp', scatter_dimension=0, tiled=True)]
    ppermute x0 -> x45, waiting for transfers between devices: none -> 107 us  [the longest x4 30.2 us: plane_turn(): lax.ppermute(send_y, 'dp', ALONG_Y)]
    psum x2 -> x1, blocking collectives: 102 us -> 22.3 us  [shards(): summed = lax.psum(jnp.concatenate([gain_total.reshape(-1), squares]), 'dp')]
    ppermute x0 -> x45, starting transfers between devices: none -> 66.3 us  [the longest x5 23.3 us: sum_bands(): down = lax.ppermute(plane, 'band', [(2, 1)])]
    psum x1 -> x0, waiting for transfers between devices: 34.8 us -> none  [shards(): owned = lax.psum(owned, 'band')]
    convert_element_type x0 -> x12, other arithmetic: none -> 23.8 us  [the longest x4 10.6 us: plane_start(): send_x, send_y = (chip(2, 4).astype(bf16), chip(6, 8).astype(bf16))]
    pallas_call x4 -> x8, Pallas kernels: 185 us -> 202 us  [the longest x2 66.4 us: forward_layer(): pl.pallas_call(forward_kernel, out_shape=[S((rows, D), f32)] + saved, in_...]
    ppermute x3, waiting for transfers between devices: 28.2 us -> 16.3 us  [to_images(): block = lax.ppermute(block, 'band', pairs)]
  transfers between devices with their start and end apart: 12 -> 55, of which waited for: 7 -> 23; matrix products, arithmetic and copies ran while one was open for 3% -> 13% of each run, Pallas kernels for 0% -> 7%
where the time goes in v3:
time: 712 us; the launch traced here: 704 us
  Pallas kernels  232 us (33%)
  waiting for transfers between devices  223 us (31%)
  starting transfers between devices  93.6 us (13%)
  other arithmetic  72.7 us (10%)
  local copies, waits for them, and re-layouts  41 us (6%)
  blocking collectives  22.3 us (3%)
  between operations  18.8 us (3%)
    all_gather x1, waiting for transfers between devices, shards(): gathered = lax.all_gather(master.astype(bf16), 'dp', axis=0, tiled=True)  87.2 us
    pallas_call x2, Pallas kernels, forward_layer(): pl.pallas_call(forward_kernel, out_shape=[S((rows, D), f32)] + saved, in_...  66.4 us
    pallas_call x2, Pallas kernels, back_ffn(): pl.pallas_call(functools.partial(back_ffn_kernel, zones, len(begun)), out...  59.9 us
    pallas_call x2, Pallas kernels, back_attention(): pl.pallas_call(functools.partial(back_attention_kernel, zones, len(begun)...  44.4 us
    pallas_call x2, Pallas kernels, back_qkv(): pl.pallas_call(functools.partial(back_qkv_kernel, zones, len(begun)), out...  30.8 us
    pallas_call x1, Pallas kernels, optimizer(): pl.pallas_call(optimizer_kernel, grid=(count // per,), out_shape=[S(maste...  30.7 us
    ppermute x4, waiting for transfers between devices, plane_turn(): lax.ppermute(send_y, 'dp', ALONG_Y)  30.2 us
    ppermute x4, waiting for transfers between devices, plane_start(): lax.ppermute(send_x, 'dp', ALONG_X)  27.8 us
  transfers between devices with their start and end apart: 55, of which 23 were waited for; matrix products, arithmetic and copies ran while one was open for 13% of the time, Pallas kernels for 7%

profile of v3, /device:TPU:16, one launch (start us, length us, event | category | flops | bytes accessed | tf_op | source)
XLA Modules:
  0.0 703.9 jit_solution(10961945608332345731)
XLA Ops:
  7.2 5.6 convert_element_type.498
  21.3 5.3 scatter_custom_fusion
  44.0 13.8 %collective-permute-done.11 = bf16[2,145,768]{2,1,0:T(8,128)(2,1)} collective-permute-done((bf16[2,145,768]{2,1,0:T(8,128)(2,1)S(1)}, bf16[2,145,768]{2,1,0:T(8,128)(2,1)}, u32[]{:S(2)}, u32[]{:S(2)}) %collective-permute-start.11) | collective-permute-done | bytes 445472 | tf_op jit(solution)/shard_map/ppermute | solution.py:577
  65.6 87.2 %all-gather.2.cloned.1.call-done.w_hbm = bf16[864,128,128]{2,1,0:T(8,128)(2,1)} async-done(((bf16[108,128,128]{2,1,0:T(8,128)(2,1)}), bf16[864,128,128]{2,1,0:T(8,128)(2,1)}) %all-gather.2.cloned.1.call-update) | async-done | bytes 28311568 | tf_op jit(solution)/shard_map/all_gather | solution.py:697
  152.7 33.0 %forward_block.2 = (f32[592,768]{1,0:T(8,128)}, bf16[592,768]{1,0:T(8,128)(2,1)}, bf16[640,768]{1,0:T(8,128)(2,1)}, bf16[640,768]{1,0:T(8,128)(2,1)}, bf16[640,7...) custom-call(s32[432]{0:T(512)} %get-tuple-element.349.slots, ...), custom_call_target="tpu_custom_call" | custom-call | flops 8380219392 | bytes 41943040 | tf_op jit(solution)/shard_map/forward_block/pallas_call | solution.py:432
  185.7 33.5 %forward_block.3 = (f32[592,768]{1,0:T(8,128)}, bf16[592,768]{1,0:T(8,128)(2,1)}, bf16[640,768]{1,0:T(8,128)(2,1)}, bf16[640,768]{1,0:T(8,128)(2,1)}, bf16[640,7...) custom-call(s32[432]{0:T(512)} %get-tuple-element.350.slots, ...), custom_call_target="tpu_custom_call" | custom-call | flops 8380219392 | bytes 41943040 | tf_op jit(solution)/shard_map/forward_block/pallas_call | solution.py:432
  219.1 30.2 %backward_feed_forward.2 = (f32[592,768]{1,0:T(8,128)}, f32[1,768]{1,0:T(1,128)}, bf16[152,128,128]{2,1,0:T(8,128)(2,1)}, bf16[152,128,128]{2,1,0:T(8,128)(2,1)}...) custom-call(s32[432]{0:T(512)} %get-tuple-element.351.places, s32[1]{0:T(128)} %constant.277.clone.1.spare, ...), custom_call_target="tpu_custom_call" | custom-call | flops 11173625856 | bytes 31457280 | tf_op jit(solution)/shard_map/backward_feed_forward/pallas_call | solution.py:459
  249.4 22.3 %backward_attention.2 = (bf16[592,2304]{1,0:T(8,128)(2,1)}, bf16[152,128,128]{2,1,0:T(8,128)(2,1)}, bf16[152,128,128]{2,1,0:T(8,128)(2,1)}, bf16[280,128,128]{2,1,0:T(8,128)(2,1)}, bf16[280,128,128]{2,1,0:T(8,128)(2,1)}) custom-call(s32[432]{0:T(512)} %get-tuple-element.351.places, ...), custom_call_target="tpu_custom_call", output_to_operand_aliasing={{1}: (11, {}), {2}: (12, {}), {3}: (13, {}), {4}: (14, {})} | custom-call | flops 6779830272 | bytes 31457280 | tf_op jit(solution)/shard_map/backward_attention/pallas_call | solution.py:486
  271.7 15.4 %backward_qkv.2 = (f32[592,768]{1,0:T(8,128)}, f32[1,768]{1,0:T(1,128)}, bf16[152,128,128]{2,1,0:T(8,128)(2,1)}, bf16[152,128,128]{2,1,0:T(8,128)(2,1)}, bf16[28...) custom-call(s32[432]{0:T(512)} %get-tuple-element.351.places, ...), custom_call_target="tpu_custom_call", output_to_operand_aliasing={{2}: (7, {}), {3}: (8, {}), {4}: (9, {}), {5}: (10, {})} | custom-call | flops 4190109696 | bytes 20971520 | tf_op jit(solution)/shard_map/backward_qkv/pallas_call | solution.py:513
  292.7 5.2 collective-permute-start.14
  299.8 29.7 %backward_feed_forward.3 = (f32[592,768]{1,0:T(8,128)}, f32[1,768]{1,0:T(1,128)}, bf16[304,128,128]{2,1,0:T(8,128)(2,1)}, bf16[280,128,128]{2,1,0:T(8,128)(2,1)}, bf16[280,128,128]{2,1,0:T(8,128)(2,1)}) custom-call(s32[432]{0:T(512)} %get-tuple-element.352.places, s32[1]{0:T(128)} %constant.277.clone.1.spare, ...), custom_call_target="tpu_custom_call", output_to_operand_aliasing={{3}: (9, {}), {4}: (10, {})} | custom-call | flops 11173625856 | bytes 31457280 | tf_op jit(solution)/shard_map/backward_feed_forward/pallas_call | solution.py:459
  330.5 4.8 add_convert_fusion.8
  337.3 22.1 %backward_attention.3 = (bf16[592,2304]{1,0:T(8,128)(2,1)}, bf16[304,128,128]{2,1,0:T(8,128)(2,1)}, bf16[280,128,128]{2,1,0:T(8,128)(2,1)}, bf16[280,128,128]{2,1,0:T(8,128)(2,1)}) custom-call(s32[432]{0:T(512)} %get-tuple-element.352.places, s32[1]{0:T(128)} %dynamic_slice.49.length, ...), custom_call_target="tpu_custom_call", output_to_operand_aliasing={{1}: (11, {}), {2}: (12, {}), {3}: (13, {})} | custom-call | flops 6779830272 | bytes 31457280 | tf_op jit(solution)/shard_map/backward_attention/pallas_call | solution.py:486
  359.5 5.1 collective-permute-done.17
  365.6 15.3 %backward_qkv.3 = (f32[592,768]{1,0:T(8,128)}, f32[1,768]{1,0:T(1,128)}, bf16[304,128,128]{2,1,0:T(8,128)(2,1)}, bf16[280,128,128]{2,1,0:T(8,128)(2,1)}, bf16[280,128,128]{2,1,0:T(8,128)(2,1)}) custom-call(s32[432]{0:T(512)} %get-tuple-element.352.places, ...), custom_call_target="tpu_custom_call", output_to_operand_aliasing={{2}: (7, {}), {3}: (8, {}), {4}: (9, {})} | custom-call | flops 4190109696 | bytes 20971520 | tf_op jit(solution)/shard_map/backward_qkv/pallas_call | solution.py:513
  391.2 13.9 %collective-permute-done.21 = bf16[19,128,128]{2,1,0:T(8,128)(2,1)S(1)} collective-permute-done((bf16[19,128,128]{2,1,0:T(8,128)(2,1)S(1)}, bf16[19,128,128]{2,1,0:T(8,128)(2,1)S(1)}, u32[]{:S(2)}, u32[]{:S(2)}) %collective-permute-start.21) | collective-permute-done | bytes 622624 | tf_op jit(solution)/shard_map/ppermute | solution.py:651
  407.3 20.7 %collective-permute-done.22 = bf16[30,128,128]{2,1,0:T(8,128)(2,1)S(1)} collective-permute-done((bf16[30,128,128]{2,1,0:T(8,128)(2,1)S(1)}, bf16[30,128,128]{2,1,0:T(8,128)(2,1)S(1)}, u32[]{:S(2)}, u32[]{:S(2)}) %collective-permute-start.22) | collective-permute-done | bytes 983072 | tf_op jit(solution)/shard_map/ppermute | solution.py:644
  429.8 9.9 %collective-permute-done.32 = bf16[15,128,128]{2,1,0:T(8,128)(2,1)S(1)} collective-permute-done((bf16[15,128,128]{2,1,0:T(8,128)(2,1)S(1)}, bf16[15,128,128]{2,1,0:T(8,128)(2,1)S(1)}, u32[]{:S(2)}, u32[]{:S(2)}) %collective-permute-start.32) | collective-permute-done | bytes 491552 | tf_op jit(solution)/shard_map/ppermute | solution.py:651
  446.0 5.4 collective-permute-done.33
  454.1 5.3 collective-permute-start.60
  466.6 14.5 %collective-permute-done.28 = f32[4,768]{1,0:T(4,128)S(1)} collective-permute-done((f32[4,768]{1,0:T(4,128)}, f32[4,768]{1,0:T(4,128)S(1)}, u32[]{:S(2)}, u32[]{:S(2)}) %collective-permute-start.28) | collective-permute-done | bytes 12320 | tf_op jit(solution)/shard_map/ppermute | solution.py:663
  491.2 9.2 %collective-permute-done.42 = bf16[24,128,128]{2,1,0:T(8,128)(2,1)S(1)} collective-permute-done((bf16[24,128,128]{2,1,0:T(8,128)(2,1)}, bf16[24,128,128]{2,1,0:T(8,128)(2,1)S(1)}, u32[]{:S(2)}, u32[]{:S(2)}) %collective-permute-start.42) | collective-permute-done | bytes 786464 | tf_op jit(solution)/shard_map/ppermute | solution.py:644
  512.7 5.7 collective-permute-start.35
  539.1 4.9 collective-permute-start.45
  563.8 6.1 collective-permute-start.55
  575.2 7.6 %collective-permute-done.36 = bf16[30,128,128]{2,1,0:T(8,128)(2,1)} collective-permute-done((bf16[30,128,128]{2,1,0:T(8,128)(2,1)}, bf16[30,128,128]{2,1,0:T(8,128)(2,1)}, u32[]{:S(2)}, u32[]{:S(2)}) %collective-permute-start.36) | collective-permute-done | bytes 983072 | tf_op jit(solution)/shard_map/ppermute | solution.py:666
  591.3 8.8 %collective-permute-start.25 = (bf16[145,768]{1,0:T(8,128)(2,1)S(1)}, bf16[145,768]{1,0:T(8,128)(2,1)S(1)}, u32[]{:S(2)}, u32[]{:S(2)}) collective-permute-start(bf16[145,768]{1,0:T(8,128)(2,1)S(1)} %get-tuple-element.333), channel_id=1, source_target_pairs={{0,2},{1,3},{2,0},{4,6},{5,7},{6,4},{8,10},{9,11},{10,8},{12,14},{... | collective-permute-start | bytes 668168 | tf_op jit(solution)/shard_map/ppermute | solution.py:588
  600.1 10.5 %collective-permute-done.24 = bf16[145,768]{1,0:T(8,128)(2,1)S(1)} collective-permute-done((bf16[145,768]{1,0:T(8,128)(2,1)S(1)}, bf16[145,768]{1,0:T(8,128)(2,1)S(1)}, u32[]{:S(2)}, u32[]{:S(2)}) %collective-permute-start.24) | collective-permute-done | bytes 222752 | tf_op jit(solution)/shard_map/ppermute | solution.py:588
  612.7 4.7 collective-permute-start.47
  633.6 5.1 multiply_reduce_fusion
  639.3 22.3 %psum.7 = f32[3073]{0:T(1024)S(1)} all-reduce(f32[3073]{0:T(1024)S(1)} %pad_maximum_fusion.7), channel_id=1, replica_groups=mesh['dp'=8,'band'=4] {'dp'}, use_global_device_ids=true, to_apply=%region_7.8 | all-reduce | flops 3073 | bytes 24584 | tf_op jit(solution)/shard_map/psum | solution.py:825
  664.8 30.7 %optimizer.1 = (f32[108,128,128]{2,1,0:T(8,128)}, f32[108,2,128,128]{3,2,1,0:T(8,128)}, f32[108,128,128]{2,1,0:T(8,128)}, bf16[108,128,128]{2,1,0:T(8,128)(2,1)}) custom-call(f32[1]{0:T(128)} %bitcast.25.factor, s32[108]{0:T(128)} %dynamic-slice_reduce_fusion.rank, bf16[108,128,128]{2,1,0:T(8,128)(2,1)} %get-tuple-element.299.g_ref, f32[108,128,128]{2,1,0:T(8,128)} %m_ref.1, ...), custom_call_target="tpu_custom_call" | custom-call | tf_op jit(solution)/shard_map/optimizer/pallas_call | solution.py:553
  (245 shorter events, 171.4 us)
Async XLA Ops:
  7.2 145.5 %all-gather.2.cloned.1.call-start = ((), (), s32[]{:S(2)}) async-start(), calls=%async_computation | async-start | bytes 31850496 | tf_op jit(solution)/shard_map/all_gather | solution.py:697
  15.4 43.5 %collective-permute-start.12 = (bf16[2,145,768]{2,1,0:T(8,128)(2,1)S(1)}, bf16[2,145,768]{2,1,0:T(8,128)(2,1)}, u32[]{:S(2)}, u32[]{:S(2)}) collective-permute-start(bf16[2,145,768]{2,1,0:T(8,128)(2,1)S(1)} %get-tuple-element.328), channel_id=1, source_target_pairs={{1,0},{2,1},{3,2},{5,4},{6,5},{7,6},{9,8},{10,9},{11,10},{13,12},{... | collective-permute-start | bytes 1336328 | tf_op jit(solution)/shard_map/ppermute | solution.py:577
  17.9 40.0 %collective-permute-start.11 = (bf16[2,145,768]{2,1,0:T(8,128)(2,1)S(1)}, bf16[2,145,768]{2,1,0:T(8,128)(2,1)}, u32[]{:S(2)}, u32[]{:S(2)}) collective-permute-start(bf16[2,145,768]{2,1,0:T(8,128)(2,1)S(1)} %get-tuple-element.329), channel_id=1, source_target_pairs={{0,2},{2,0},{3,1},{4,6},{6,4},{7,5},{8,10},{10,8},{11,9},{12,14},{... | collective-permute-start | bytes 1336328 | tf_op jit(solution)/shard_map/ppermute | solution.py:577
  19.9 23.1 %collective-permute-start.10 = (bf16[2,145,768]{2,1,0:T(8,128)(2,1)}, bf16[2,145,768]{2,1,0:T(8,128)(2,1)}, u32[]{:S(2)}, u32[]{:S(2)}) collective-permute-start(bf16[2,145,768]{2,1,0:T(8,128)(2,1)} %get-tuple-element.330), channel_id=1, source_target_pairs={{0,1},{1,2},{3,0},{4,5},{5,6},{7,4},{8,9},{9,10},{11,8},{12,13},{1... | collective-permute-start | bytes 1336328 | tf_op jit(solution)/shard_map/ppermute | solution.py:577
  287.1 43.4 %collective-permute-start.16 = (bf16[152,128,128]{2,1,0:T(8,128)(2,1)}, bf16[152,128,128]{2,1,0:T(8,128)(2,1)}, u32[]{:S(2)}, u32[]{:S(2)}) collective-permute-start(bf16[152,128,128]{2,1,0:T(8,128)(2,1)} %get-tuple-element.454), channel_id=1, source_target_pairs={{0,4},{4,0},{8,12},{12,8},{16,20},{20,16},{24,28},{28,24},{1,5},{5... | collective-permute-start | bytes 14942216 | tf_op jit(solution)/shard_map/ppermute | solution.py:770
  290.2 39.4 %collective-permute-start.15 = (bf16[145,768]{1,0:T(8,128)(2,1)S(1)}, bf16[145,768]{1,0:T(8,128)(2,1)S(1)}, u32[]{:S(2)}, u32[]{:S(2)}) collective-permute-start(bf16[145,768]{1,0:T(8,128)(2,1)S(1)} %get-tuple-element.336), channel_id=1, source_target_pairs={{0,3},{1,0},{2,1},{4,7},{5,4},{6,5},{8,11},{9,8},{10,9},{12,15},{1... | collective-permute-start | bytes 668168 | tf_op jit(solution)/shard_map/ppermute | solution.py:588
  292.7 36.9 %collective-permute-start.14 = (bf16[145,768]{1,0:T(8,128)(2,1)}, bf16[145,768]{1,0:T(8,128)(2,1)S(1)}, u32[]{:S(2)}, u32[]{:S(2)}) collective-permute-start(bf16[145,768]{1,0:T(8,128)(2,1)} %get-tuple-element.337), channel_id=1, source_target_pairs={{0,2},{1,3},{2,0},{4,6},{5,7},{6,4},{8,10},{9,11},{10,8},{12,14},{... | collective-permute-start | bytes 668168 | tf_op jit(solution)/shard_map/ppermute | solution.py:588
  297.9 31.6 %collective-permute-start.13 = (bf16[145,768]{1,0:T(8,128)(2,1)}, bf16[145,768]{1,0:T(8,128)(2,1)S(1)}, u32[]{:S(2)}, u32[]{:S(2)}) collective-permute-start(bf16[145,768]{1,0:T(8,128)(2,1)} %get-tuple-element.338), channel_id=1, source_target_pairs={{0,1},{1,2},{2,3},{4,5},{5,6},{6,7},{8,9},{9,10},{10,11},{12,13},{... | collective-permute-start | bytes 668168 | tf_op jit(solution)/shard_map/ppermute | solution.py:588
  335.3 29.3 %collective-permute-start.17 = (bf16[38,128,128]{2,1,0:T(8,128)(2,1)}, bf16[38,128,128]{2,1,0:T(8,128)(2,1)}, u32[]{:S(2)}, u32[]{:S(2)}) collective-permute-start(bf16[38,128,128]{2,1,0:T(8,128)(2,1)} %get-tuple-element.235), channel_id=1, source_target_pairs={{0,8},{4,12},{8,0},{12,4},{16,24},{20,28},{24,16},{28,20},{1,9},{5... | collective-permute-start | bytes 3735560 | tf_op jit(solution)/shard_map/ppermute | solution.py:644
  336.8 28.8 %collective-permute-start.18 = (bf16[38,128,128]{2,1,0:T(8,128)(2,1)S(1)}, bf16[38,128,128]{2,1,0:T(8,128)(2,1)}, u32[]{:S(2)}, u32[]{:S(2)}) collective-permute-start(bf16[38,128,128]{2,1,0:T(8,128)(2,1)S(1)} %get-tuple-element.236), channel_id=1, source_target_pairs={{0,16},{4,20},{8,24},{12,28},{16,0},{20,4},{24,8},{28,12},{1,17},{... | collective-permute-start | bytes 3735560 | tf_op jit(solution)/shard_map/ppermute | solution.py:644
  385.9 57.9 %collective-permute-start.39 = (bf16[96,128,128]{2,1,0:T(8,128)(2,1)S(1)}, bf16[96,128,128]{2,1,0:T(8,128)(2,1)S(1)}, u32[]{:S(2)}, u32[]{:S(2)}) collective-permute-start(bf16[96,128,128]{2,1,0:T(8,128)(2,1)S(1)} %slice.427), channel_id=1, source_target_pairs={{0,4},{4,0},{8,12},{12,8},{16,20},{20,16},{24,28},{28,24},{1,5},{5... | collective-permute-start | bytes 9437192 | tf_op jit(solution)/shard_map/ppermute | solution.py:790
  405.3 22.7 %collective-permute-start.22 = (bf16[30,128,128]{2,1,0:T(8,128)(2,1)S(1)}, bf16[30,128,128]{2,1,0:T(8,128)(2,1)S(1)}, u32[]{:S(2)}, u32[]{:S(2)}) collective-permute-start(bf16[30,128,128]{2,1,0:T(8,128)(2,1)S(1)} %get-tuple-element.258), channel_id=1, source_target_pairs={{0,8},{4,12},{8,0},{12,4},{16,24},{20,28},{24,16},{28,20},{1,9},{5... | collective-permute-start | bytes 2949128 | tf_op jit(solution)/shard_map/ppermute | solution.py:644
  405.9 23.9 %collective-permute-start.23 = (bf16[30,128,128]{2,1,0:T(8,128)(2,1)S(1)}, bf16[30,128,128]{2,1,0:T(8,128)(2,1)S(1)}, u32[]{:S(2)}, u32[]{:S(2)}) collective-permute-start(bf16[30,128,128]{2,1,0:T(8,128)(2,1)S(1)} %get-tuple-element.259), channel_id=1, source_target_pairs={{0,16},{4,20},{8,24},{12,28},{16,0},{20,4},{24,8},{28,12},{1,17},{... | collective-permute-start | bytes 2949128 | tf_op jit(solution)/shard_map/ppermute | solution.py:644
  451.4 30.4 %collective-permute-start.40 = (bf16[24,128,128]{2,1,0:T(8,128)(2,1)}, bf16[24,128,128]{2,1,0:T(8,128)(2,1)}, u32[]{:S(2)}, u32[]{:S(2)}) collective-permute-start(bf16[24,128,128]{2,1,0:T(8,128)(2,1)} %get-tuple-element.265), channel_id=1, source_target_pairs={{0,8},{4,12},{8,0},{12,4},{16,24},{20,28},{24,16},{28,20},{1,9},{5... | collective-permute-start | bytes 2359304 | tf_op jit(solution)/shard_map/ppermute | solution.py:644
  453.3 32.8 %collective-permute-start.59 = (bf16[38,128,128]{2,1,0:T(8,128)(2,1)}, bf16[38,128,128]{2,1,0:T(8,128)(2,1)S(1)}, u32[]{:S(2)}, u32[]{:S(2)}) collective-permute-start(bf16[38,128,128]{2,1,0:T(8,128)(2,1)} %pad_maximum_fusion.2), channel_id=1, source_target_pairs={{0,1},{4,5},{8,9},{12,13},{16,17},{20,21},{24,25},{28,29}} | collective-permute-start | bytes 3735560 | tf_op jit(solution)/shard_map/ppermute | solution.py:662
  454.1 33.3 %collective-permute-start.60 = (bf16[38,128,128]{2,1,0:T(8,128)(2,1)}, bf16[38,128,128]{2,1,0:T(8,128)(2,1)}, u32[]{:S(2)}, u32[]{:S(2)}) collective-permute-start(bf16[38,128,128]{2,1,0:T(8,128)(2,1)} %pad_maximum_fusion.2), channel_id=1, source_target_pairs={{2,1},{6,5},{10,9},{14,13},{18,17},{22,21},{26,25},{30,29}} | collective-permute-start | bytes 3735560 | tf_op jit(solution)/shard_map/ppermute | solution.py:663
  462.6 62.2 %collective-permute-start.49 = (bf16[64,128,128]{2,1,0:T(8,128)(2,1)}, bf16[64,128,128]{2,1,0:T(8,128)(2,1)}, u32[]{:S(2)}, u32[]{:S(2)}) collective-permute-start(bf16[64,128,128]{2,1,0:T(8,128)(2,1)} %slice.444), channel_id=1, source_target_pairs={{0,4},{4,0},{8,12},{12,8},{16,20},{20,16},{24,28},{28,24},{1,5},{5... | collective-permute-start | bytes 6291464 | tf_op jit(solution)/shard_map/ppermute | solution.py:790
  484.7 19.9 %collective-permute-start.41 = (bf16[12,128,128]{2,1,0:T(8,128)(2,1)S(1)}, bf16[12,128,128]{2,1,0:T(8,128)(2,1)S(1)}, u32[]{:S(2)}, u32[]{:S(2)}) collective-permute-start(bf16[12,128,128]{2,1,0:T(8,128)(2,1)S(1)} %add_convert_fusion.30), channel_id=1, source_target_pairs={{0,16},{4,20},{8,24},{12,28},{16,0},{20,4},{24,8},{28,12},{1,17},{... | collective-permute-start | bytes 1179656 | tf_op jit(solution)/shard_map/ppermute | solution.py:651
  486.1 25.9 %collective-permute-start.29 = (f32[4,768]{1,0:T(4,128)S(1)}, f32[4,768]{1,0:T(4,128)S(1)}, u32[]{:S(2)}, u32[]{:S(2)}) collective-permute-start(f32[4,768]{1,0:T(4,128)S(1)} %add_add_fusion), channel_id=1, source_target_pairs={{1,2},{5,6},{9,10},{13,14},{17,18},{21,22},{25,26},{29,30}} | collective-permute-start | bytes 36872 | tf_op jit(solution)/shard_map/ppermute | solution.py:666
  489.7 44.5 %collective-permute-start.61 = (bf16[38,128,128]{2,1,0:T(8,128)(2,1)S(1)}, bf16[38,128,128]{2,1,0:T(8,128)(2,1)}, u32[]{:S(2)}, u32[]{:S(2)}) collective-permute-start(bf16[38,128,128]{2,1,0:T(8,128)(2,1)S(1)} %add_convert_fusion.7), channel_id=1, source_target_pairs={{1,2},{5,6},{9,10},{13,14},{17,18},{21,22},{25,26},{29,30}} | collective-permute-start | bytes 3735560 | tf_op jit(solution)/shard_map/ppermute | solution.py:666
  510.4 24.6 %collective-permute-start.34 = (bf16[30,128,128]{2,1,0:T(8,128)(2,1)}, bf16[30,128,128]{2,1,0:T(8,128)(2,1)}, u32[]{:S(2)}, u32[]{:S(2)}) collective-permute-start(bf16[30,128,128]{2,1,0:T(8,128)(2,1)} %pad_maximum_fusion.3), channel_id=1, source_target_pairs={{0,1},{4,5},{8,9},{12,13},{16,17},{20,21},{24,25},{28,29}} | collective-permute-start | bytes 2949128 | tf_op jit(solution)/shard_map/ppermute | solution.py:662
  512.7 23.8 %collective-permute-start.35 = (bf16[30,128,128]{2,1,0:T(8,128)(2,1)}, bf16[30,128,128]{2,1,0:T(8,128)(2,1)}, u32[]{:S(2)}, u32[]{:S(2)}) collective-permute-start(bf16[30,128,128]{2,1,0:T(8,128)(2,1)} %pad_maximum_fusion.3), channel_id=1, source_target_pairs={{2,1},{6,5},{10,9},{14,13},{18,17},{22,21},{26,25},{30,29}} | collective-permute-start | bytes 2949128 | tf_op jit(solution)/shard_map/ppermute | solution.py:663
  534.3 29.6 %collective-permute-start.63 = (bf16[38,128,128]{2,1,0:T(8,128)(2,1)S(1)}, bf16[38,128,128]{2,1,0:T(8,128)(2,1)S(1)}, u32[]{:S(2)}, u32[]{:S(2)}) collective-permute-start(bf16[38,128,128]{2,1,0:T(8,128)(2,1)S(1)} %add_convert_fusion.7), channel_id=1, source_target_pairs={{1,0},{5,4},{9,8},{13,12},{17,16},{21,20},{25,24},{29,28}} | collective-permute-start | bytes 3735560 | tf_op jit(solution)/shard_map/ppermute | solution.py:665
  535.0 34.9 %collective-permute-start.62 = (bf16[38,128,128]{2,1,0:T(8,128)(2,1)}, bf16[38,128,128]{2,1,0:T(8,128)(2,1)S(1)}, u32[]{:S(2)}, u32[]{:S(2)}) collective-permute-start(bf16[38,128,128]{2,1,0:T(8,128)(2,1)} %collective-permute-done.61), channel_id=1, source_target_pairs={{2,3},{6,7},{10,11},{14,15},{18,19},{22,23},{26,27},{30,31}} | collective-permute-start | bytes 3735560 | tf_op jit(solution)/shard_map/ppermute | solution.py:667
  553.1 29.7 %collective-permute-start.36 = (bf16[30,128,128]{2,1,0:T(8,128)(2,1)}, bf16[30,128,128]{2,1,0:T(8,128)(2,1)}, u32[]{:S(2)}, u32[]{:S(2)}) collective-permute-start(bf16[30,128,128]{2,1,0:T(8,128)(2,1)} %add_convert_fusion.10), channel_id=1, source_target_pairs={{1,2},{5,6},{9,10},{13,14},{17,18},{21,22},{25,26},{29,30}} | collective-permute-start | bytes 2949128 | tf_op jit(solution)/shard_map/ppermute | solution.py:666
  557.4 55.4 %collective-permute-start.46 = (bf16[24,128,128]{2,1,0:T(8,128)(2,1)}, bf16[24,128,128]{2,1,0:T(8,128)(2,1)}, u32[]{:S(2)}, u32[]{:S(2)}) collective-permute-start(bf16[24,128,128]{2,1,0:T(8,128)(2,1)} %add_convert_fusion.13), channel_id=1, source_target_pairs={{1,2},{5,6},{9,10},{13,14},{17,18},{21,22},{25,26},{29,30}} | collective-permute-start | bytes 2359304 | tf_op jit(solution)/shard_map/ppermute | solution.py:666
  562.3 22.0 %collective-permute-start.54 = (bf16[16,128,128]{2,1,0:T(8,128)(2,1)S(1)}, bf16[16,128,128]{2,1,0:T(8,128)(2,1)}, u32[]{:S(2)}, u32[]{:S(2)}) collective-permute-start(bf16[16,128,128]{2,1,0:T(8,128)(2,1)S(1)} %pad_maximum_fusion.5), channel_id=1, source_target_pairs={{0,1},{4,5},{8,9},{12,13},{16,17},{20,21},{24,25},{28,29}} | collective-permute-start | bytes 1572872 | tf_op jit(solution)/shard_map/ppermute | solution.py:662
  563.8 21.8 %collective-permute-start.55 = (bf16[16,128,128]{2,1,0:T(8,128)(2,1)S(1)}, bf16[16,128,128]{2,1,0:T(8,128)(2,1)}, u32[]{:S(2)}, u32[]{:S(2)}) collective-permute-start(bf16[16,128,128]{2,1,0:T(8,128)(2,1)S(1)} %pad_maximum_fusion.5), channel_id=1, source_target_pairs={{2,1},{6,5},{10,9},{14,13},{18,17},{22,21},{26,25},{30,29}} | collective-permute-start | bytes 1572872 | tf_op jit(solution)/shard_map/ppermute | solution.py:663
  574.4 43.9 %collective-permute-start.38 = (bf16[30,128,128]{2,1,0:T(8,128)(2,1)}, bf16[30,128,128]{2,1,0:T(8,128)(2,1)S(1)}, u32[]{:S(2)}, u32[]{:S(2)}) collective-permute-start(bf16[30,128,128]{2,1,0:T(8,128)(2,1)} %add_convert_fusion.10), channel_id=1, source_target_pairs={{1,0},{5,4},{9,8},{13,12},{17,16},{21,20},{25,24},{29,28}} | collective-permute-start | bytes 2949128 | tf_op jit(solution)/shard_map/ppermute | solution.py:665
  582.7 40.3 %collective-permute-start.37 = (bf16[30,128,128]{2,1,0:T(8,128)(2,1)}, bf16[30,128,128]{2,1,0:T(8,128)(2,1)S(1)}, u32[]{:S(2)}, u32[]{:S(2)}) collective-permute-start(bf16[30,128,128]{2,1,0:T(8,128)(2,1)} %collective-permute-done.36), channel_id=1, source_target_pairs={{2,3},{6,7},{10,11},{14,15},{18,19},{22,23},{26,27},{30,31}} | collective-permute-start | bytes 2949128 | tf_op jit(solution)/shard_map/ppermute | solution.py:667
  585.6 25.1 %collective-permute-start.24 = (bf16[145,768]{1,0:T(8,128)(2,1)S(1)}, bf16[145,768]{1,0:T(8,128)(2,1)S(1)}, u32[]{:S(2)}, u32[]{:S(2)}) collective-permute-start(bf16[145,768]{1,0:T(8,128)(2,1)S(1)} %get-tuple-element.334), channel_id=1, source_target_pairs={{0,1},{1,2},{2,3},{4,5},{5,6},{6,7},{8,9},{9,10},{10,11},{12,13},{... | collective-permute-start | bytes 668168 | tf_op jit(solution)/shard_map/ppermute | solution.py:588
  591.3 20.6 %collective-permute-start.25 = (bf16[145,768]{1,0:T(8,128)(2,1)S(1)}, bf16[145,768]{1,0:T(8,128)(2,1)S(1)}, u32[]{:S(2)}, u32[]{:S(2)}) collective-permute-start(bf16[145,768]{1,0:T(8,128)(2,1)S(1)} %get-tuple-element.333), channel_id=1, source_target_pairs={{0,2},{1,3},{2,0},{4,6},{5,7},{6,4},{8,10},{9,11},{10,8},{12,14},{... | collective-permute-start | bytes 668168 | tf_op jit(solution)/shard_map/ppermute | solution.py:588
  (46 other events, 553.3 us)
Sparse Core Ops, SparseCore 0:
  13.0 139.6 all-gather.1

commit v4 on v3

--- a/solution.py
+++ b/solution.py
@@ -642,13 +642,14 @@
     if beside is not None:
         send_x, send_y, beside = lax.optimization_barrier((send_x, send_y, beside))
     going = (chip, half, lax.ppermute(send_x, "dp", ALONG_X), lax.ppermute(send_y, "dp", ALONG_Y))
-    return going if beside is None else (going, beside)
+    return (going, beside) if beside is not None else (going, (send_x, send_y))
 
 
 def plane_turn(chip, half, from_x, from_y):
     send_y = (chip(1, 2) + wide(from_x, half, 2 * half)).astype(bf16)
     send_x = (chip(5, 6) + wide(from_y, half, 2 * half)).astype(bf16)
-    return lax.ppermute(send_x, "dp", ALONG_X), lax.ppermute(send_y, "dp", ALONG_Y)
+    turn = lax.ppermute(send_x, "dp", ALONG_X), lax.ppermute(send_y, "dp", ALONG_Y)
+    return turn, (send_x, send_y)
 
 
 def plane_end(chip, half, from_x, from_y, later_x, later_y):
@@ -657,17 +658,32 @@
     return jnp.concatenate([one, two], 0).astype(bf16)
 
 
-def sum_bands(plane, band):
-    kind = plane.dtype
-    up = lax.ppermute(plane, "band", [(0, 1)])
-    down = lax.ppermute(plane, "band", [(2, 1)])
-    total = (plane.astype(f32) + up.astype(f32) + down.astype(f32)).astype(kind)
-    to_first = lax.ppermute(total, "band", [(1, 0)])
-    to_third = lax.ppermute(total, "band", [(1, 2)])
-    to_last = lax.ppermute(to_third, "band", [(2, 3)])
+def bands_meet(plane):
+    return lax.ppermute(plane, "band", [(0, 1)]), lax.ppermute(plane, "band", [(2, 1)])
+
+
+def bands_total(plane, up, down):
+    return (plane.astype(f32) + up.astype(f32) + down.astype(f32)).astype(bf16)
+
+
+def bands_part(total):
+    return lax.ppermute(total, "band", [(1, 0)]), lax.ppermute(total, "band", [(1, 2)])
+
+
+def bands_last(to_third):
+    return lax.ppermute(to_third, "band", [(2, 3)])
+
+
+def bands_choose(band, total, to_first, to_third, to_last):
     total = jnp.where(band == 0, to_first, total)
     total = jnp.where(band == 2, to_third, total)
     return jnp.where(band == 3, to_last, total)
+
+
+def sum_bands(plane, band):
+    total = bands_total(plane, *bands_meet(plane))
+    to_first, to_third = bands_part(total)
+    return bands_choose(band, total, to_first, to_third, bands_last(to_third))
 
 
 def rope_tables(rows):
@@ -760,9 +776,6 @@
         )
         return back, [gain_one, gain_two], tiles
 
-    def after(value, *done):
-        return lax.optimization_barrier((value,) + done)[0]
-
     back, gains_top, tiles = backward(1, back, zones_top, [])
     if by_permutes:
         early_kept, early_sent, kept, sent = tiles
@@ -783,21 +796,86 @@
         back, gains_bottom, tiles = backward(0, back, zones_bottom, [kept, sent], ahead, later)
         layer_output = early["output"]
         early_late, kept, sent = tiles
-        chunks, start = [], 0
+        before = ()
+
+        def group(*arrays):
+            return lax.optimization_barrier(arrays + before)[: len(arrays)]
+
+        from_core, chunks, start = [], [], 0
         for size in LATE:
-            chunks.append((kept[4 * start : 4 * (start + size)], sent[4 * start : 4 * (start + size)]))
+            here = slice(4 * start, 4 * (start + size))
+            from_core.append(lax.ppermute(sent[here], "dp", CORE))
+            chunks.append(kept[here])
             start += size
-        from_core = [lax.ppermute(chunk[1], "dp", CORE) for chunk in chunks]
-        turned = plane_turn(*early["plane"])
-        gate = turned
-        owned = [None] * len(chunks) + [sum_bands(plane_end(*early["plane"], *turned), band)]
-        gain_total = sum_bands(jnp.concatenate(gains_bottom + gains_top, 0), band)
-        for i, (chunk, received) in enumerate(zip(chunks, from_core)):
-            going = plane_start(chunk[0], received, gate)
-            gate = plane_turn(*going)
-            owned[i] = sum_bands(plane_end(*going, *gate), band)
-            if i == 0:
-                back = after(back, going[2], going[3])
+        early_turn, _ = plane_turn(*early["plane"])
+        input_grad = to_bands(
+            back[:seq].astype(bf16).reshape(bands, band_rows, D), images, bands, band
+        )
+        gains = jnp.concatenate(gains_bottom + gains_top, 0).astype(bf16).reshape(-1, BLOCK)
+        gains = jnp.pad(gains, ((0, BLOCK - gains.shape[0]), (0, 0)))[None]
+
+        plane_sums, meets, totals, parts, lasts = {}, {}, {}, {}, {}
+
+        def plane_done(name, going, turn, follow=None):
+            nonlocal before
+            if follow is None:
+                later_x, later_y = group(*turn)
+            else:
+                later_x, later_y, received = group(*turn, from_core[follow])
+            plane = plane_end(*going, later_x, later_y)
+            if name == "early":
+                plane = jnp.concatenate([plane, gains], 0)
+            plane_sums[name] = plane
+            meets[name] = bands_meet(plane)
+            before = (plane,)
+            if follow is not None:
+                going, sends = plane_start(chunks[follow], received)
+                before = (plane,) + sends
+                return going
+
+        def plane_turned(going):
+            nonlocal before
+            from_x, from_y = group(going[2], going[3])
+            going = going[:2] + (from_x, from_y)
+            turn, before = plane_turn(*going)
+            return going, turn
+
+        def met(name, *also):
+            nonlocal before
+            up, down, *also = group(*meets[name], *also)
+            totals[name] = bands_total(plane_sums[name], up, down)
+            parts[name] = bands_part(totals[name])
+            before = (totals[name],)
+            return also
+
+        def parted(name):
+            nonlocal before
+            parts[name] = group(*parts[name])
+            lasts[name] = bands_last(parts[name][1])
+            before = parts[name][1:]
+
+        going = plane_done("early", early["plane"], early_turn, 0)
+        zero, turn = plane_turned(going)
+        (input_grad,) = met("early", input_grad)
+        going = plane_done(0, zero, turn, 1)
+        parted("early")
+        one, turn = plane_turned(going)
+        met(0)
+        going = plane_done(1, one, turn, 2)
+        parted(0)
+        two, turn = plane_turned(going)
+        (lasts["early"],) = met(1, lasts["early"])
+        plane_done(2, two, turn)
+        parted(1)
+        (lasts[0],) = met(2, lasts[0])
+        parted(2)
+        wholes = {}
+        for name in ("early", 0, 1, 2):
+            (last,) = group(lasts[name])
+            wholes[name] = bands_choose(band, totals[name], *parts[name], last)
+            before = (last,)
+        gain_total = wholes["early"][EARLY].astype(f32)[: 2 * LAYERS * D // BLOCK].reshape(-1, D)
+        owned = [wholes[i] for i in range(len(LATE))] + [wholes["early"][:EARLY]]
 
         order = jnp.argsort(places)[: sizes[0] + sizes[1]]
 
@@ -808,8 +886,9 @@
             mine = (order < PER_LAYER)[:, None, None]
             first = jnp.where(mine[: sizes[0]], late[: sizes[0]], first)
             second = jnp.where(mine[sizes[0] :], late[sizes[0] :], second)
-            going = plane_start(first, lax.ppermute(second, "dp", CORE))
-            return sum_bands(plane_end(*going, *plane_turn(*going)), band)
+            going, _ = plane_start(first, lax.ppermute(second, "dp", CORE))
+            turn, _ = plane_turn(*going)
+            return sum_bands(plane_end(*going, *turn), band)
 
         owned[-1] = lax.fori_loop(0, jnp.where(clean, 0, 1), again, owned[-1])
         owned = jnp.concatenate(owned, 0)
@@ -818,7 +897,9 @@
         owned = lax.psum_scatter(tiles[0], "dp", scatter_dimension=0, tiled=True)
         owned = lax.psum(owned, "band")
         gain_total = lax.psum(jnp.concatenate(gains_bottom + gains_top, 0), "band")
-    input_grad = to_bands(back[:seq].astype(bf16).reshape(bands, band_rows, D), images, bands, band)
+        input_grad = to_bands(
+            back[:seq].astype(bf16).reshape(bands, band_rows, D), images, bands, band
+        )
 
     owned_f = owned.astype(f32)
     squares = jnp.sum(owned_f * owned_f).reshape(1)

time: 712 us -> 672 us (0.944)
  starting transfers between devices: 93.6 us -> 66.2 us
  other arithmetic: 72.7 us -> 51.8 us
  waiting for transfers between devices: 223 us -> 232 us
    ppermute x28 -> x23, waiting for transfers between devices: 30.5 us -> 88 us  [the longest x4 39.8 us: bands_part(): lax.ppermute(total, 'band', [(1, 2)])]
    ppermute x4, waiting for transfers between devices: 27.8 us -> 5.35 us  [plane_start(): lax.ppermute(send_x, 'dp', ALONG_X)]
    ppermute x28 -> x23, starting transfers between devices: 49.5 us -> 30 us  [the longest x4 12.5 us: bands_meet(): lax.ppermute(plane, 'band', [(2, 1)])]
    ppermute x4, waiting for transfers between devices: 30.2 us -> 11.7 us  [plane_turn(): lax.ppermute(send_y, 'dp', ALONG_Y)]
    ppermute x6, waiting for transfers between devices: 12.9 us -> 2.51 us  [to_bands(): block = lax.ppermute(block, 'band', pairs)]
  transfers between devices with their start and end apart: 55 -> 50, of which waited for: 23 -> 21; matrix products, arithmetic and copies ran while one was open for 13% -> 10% of each run, Pallas kernels for 7% -> 8%
where the time goes in v4:
time: 672 us; the launch traced here: 666 us
  Pallas kernels  233 us (35%)
  waiting for transfers between devices  232 us (35%)
  starting transfers between devices  66.2 us (10%)
  other arithmetic  51.8 us (8%)
  local copies, waits for them, and re-layouts  43.1 us (6%)
  blocking collectives  22.3 us (3%)
  between operations  18.7 us (3%)
    all_gather x1, waiting for transfers between devices, shards(): gathered = lax.all_gather(master.astype(bf16), 'dp', axis=0, tiled=True)  86.9 us
    pallas_call x2, Pallas kernels, forward_layer(): pl.pallas_call(forward_kernel, out_shape=[S((rows, D), f32)] + saved, in_...  66.5 us
    pallas_call x2, Pallas kernels, back_ffn(): pl.pallas_call(functools.partial(back_ffn_kernel, zones, len(begun)), out...  59.9 us
    pallas_call x2, Pallas kernels, back_attention(): pl.pallas_call(functools.partial(back_attention_kernel, zones, len(begun)...  44.5 us
    ppermute x4, waiting for transfers between devices, bands_part(): lax.ppermute(total, 'band', [(1, 2)])  39.8 us
    ppermute x4, waiting for transfers between devices, bands_meet(): lax.ppermute(plane, 'band', [(2, 1)])  33.2 us
    pallas_call x2, Pallas kernels, back_qkv(): pl.pallas_call(functools.partial(back_qkv_kernel, zones, len(begun)), out...  31 us
    pallas_call x1, Pallas kernels, optimizer(): pl.pallas_call(optimizer_kernel, grid=(count // per,), out_shape=[S(maste...  30.7 us
  transfers between devices with their start and end apart: 50, of which 21 were waited for; matrix products, arithmetic and copies ran while one was open for 10% of the time, Pallas kernels for 8%

profile of v4, /device:TPU:16, one launch (start us, length us, event | category | flops | bytes accessed | tf_op | source)
XLA Modules:
  0.0 666.4 jit_solution(9954456205127429793)
XLA Ops:
  7.2 5.6 convert_element_type.507
  21.4 5.3 scatter_custom_fusion
  44.4 13.7 %collective-permute-done.11 = bf16[2,145,768]{2,1,0:T(8,128)(2,1)} collective-permute-done((bf16[2,145,768]{2,1,0:T(8,128)(2,1)}, bf16[2,145,768]{2,1,0:T(8,128)(2,1)}, u32[]{:S(2)}, u32[]{:S(2)}) %collective-permute-start.11) | collective-permute-done | bytes 445472 | tf_op jit(solution)/shard_map/ppermute | solution.py:577
  65.9 86.9 %all-gather.2.cloned.1.call-done.w_hbm = bf16[864,128,128]{2,1,0:T(8,128)(2,1)} async-done(((bf16[108,128,128]{2,1,0:T(8,128)(2,1)}), bf16[864,128,128]{2,1,0:T(8,128)(2,1)}) %all-gather.2.cloned.1.call-update) | async-done | bytes 28311568 | tf_op jit(solution)/shard_map/all_gather | solution.py:713
  152.7 33.0 %forward_block.2 = (f32[592,768]{1,0:T(8,128)}, bf16[592,768]{1,0:T(8,128)(2,1)}, bf16[640,768]{1,0:T(8,128)(2,1)}, bf16[640,768]{1,0:T(8,128)(2,1)}, bf16[640,7...) custom-call(s32[432]{0:T(512)} %get-tuple-element.421.slots, ...), custom_call_target="tpu_custom_call" | custom-call | flops 8380219392 | bytes 41943040 | tf_op jit(solution)/shard_map/forward_block/pallas_call | solution.py:432
  185.7 33.4 %forward_block.3 = (f32[592,768]{1,0:T(8,128)}, bf16[592,768]{1,0:T(8,128)(2,1)}, bf16[640,768]{1,0:T(8,128)(2,1)}, bf16[640,768]{1,0:T(8,128)(2,1)}, bf16[640,7...) custom-call(s32[432]{0:T(512)} %get-tuple-element.422.slots, ...), custom_call_target="tpu_custom_call" | custom-call | flops 8380219392 | bytes 41943040 | tf_op jit(solution)/shard_map/forward_block/pallas_call | solution.py:432
  219.2 30.2 %backward_feed_forward.2 = (f32[592,768]{1,0:T(8,128)}, f32[1,768]{1,0:T(1,128)}, bf16[152,128,128]{2,1,0:T(8,128)(2,1)}, bf16[152,128,128]{2,1,0:T(8,128)(2,1)}...) custom-call(s32[432]{0:T(512)} %get-tuple-element.423.places, s32[1]{0:T(128)} %constant.277.clone.1.spare, ...), custom_call_target="tpu_custom_call" | custom-call | flops 11173625856 | bytes 31457280 | tf_op jit(solution)/shard_map/backward_feed_forward/pallas_call | solution.py:459
  249.4 22.4 %backward_attention.2 = (bf16[592,2304]{1,0:T(8,128)(2,1)}, bf16[152,128,128]{2,1,0:T(8,128)(2,1)}, bf16[152,128,128]{2,1,0:T(8,128)(2,1)}, bf16[280,128,128]{2,1,0:T(8,128)(2,1)}, bf16[280,128,128]{2,1,0:T(8,128)(2,1)}) custom-call(s32[432]{0:T(512)} %get-tuple-element.423.places, ...), custom_call_target="tpu_custom_call", output_to_operand_aliasing={{1}: (11, {}), {2}: (12, {}), {3}: (13, {}), {4}: (14, {})} | custom-call | flops 6779830272 | bytes 31457280 | tf_op jit(solution)/shard_map/backward_attention/pallas_call | solution.py:486
  271.8 15.5 %backward_qkv.2 = (f32[592,768]{1,0:T(8,128)}, f32[1,768]{1,0:T(1,128)}, bf16[152,128,128]{2,1,0:T(8,128)(2,1)}, bf16[152,128,128]{2,1,0:T(8,128)(2,1)}, bf16[28...) custom-call(s32[432]{0:T(512)} %get-tuple-element.423.places, ...), custom_call_target="tpu_custom_call", output_to_operand_aliasing={{2}: (7, {}), {3}: (8, {}), {4}: (9, {}), {5}: (10, {})} | custom-call | flops 4190109696 | bytes 20971520 | tf_op jit(solution)/shard_map/backward_qkv/pallas_call | solution.py:513
  292.8 5.2 collective-permute-start.14
  299.9 29.7 %backward_feed_forward.3 = (f32[592,768]{1,0:T(8,128)}, f32[1,768]{1,0:T(1,128)}, bf16[304,128,128]{2,1,0:T(8,128)(2,1)}, bf16[280,128,128]{2,1,0:T(8,128)(2,1)}, bf16[280,128,128]{2,1,0:T(8,128)(2,1)}) custom-call(s32[432]{0:T(512)} %get-tuple-element.424.places, s32[1]{0:T(128)} %constant.277.clone.1.spare, ...), custom_call_target="tpu_custom_call", output_to_operand_aliasing={{3}: (9, {}), {4}: (10, {})} | custom-call | flops 11173625856 | bytes 31457280 | tf_op jit(solution)/shard_map/backward_feed_forward/pallas_call | solution.py:459
  330.6 4.8 add_convert_fusion.8
  337.5 22.2 %backward_attention.3 = (bf16[592,2304]{1,0:T(8,128)(2,1)}, bf16[304,128,128]{2,1,0:T(8,128)(2,1)}, bf16[280,128,128]{2,1,0:T(8,128)(2,1)}, bf16[280,128,128]{2,1,0:T(8,128)(2,1)}) custom-call(s32[432]{0:T(512)} %get-tuple-element.424.places, s32[1]{0:T(128)} %dynamic_slice.49.length, ...), custom_call_target="tpu_custom_call", output_to_operand_aliasing={{1}: (11, {}), {2}: (12, {}), {3}: (13, {})} | custom-call | flops 6779830272 | bytes 31457280 | tf_op jit(solution)/shard_map/backward_attention/pallas_call | solution.py:486
  359.7 5.1 collective-permute-done.17
  365.7 15.6 %backward_qkv.3 = (f32[592,768]{1,0:T(8,128)}, f32[1,768]{1,0:T(1,128)}, bf16[304,128,128]{2,1,0:T(8,128)(2,1)}, bf16[280,128,128]{2,1,0:T(8,128)(2,1)}, bf16[280,128,128]{2,1,0:T(8,128)(2,1)}) custom-call(s32[432]{0:T(512)} %get-tuple-element.424.places, ...), custom_call_target="tpu_custom_call", output_to_operand_aliasing={{2}: (7, {}), {3}: (8, {}), {4}: (9, {})} | custom-call | flops 4190109696 | bytes 20971520 | tf_op jit(solution)/shard_map/backward_qkv/pallas_call | solution.py:513
  381.3 4.6 slice.420
  400.7 5.7 collective-permute-done.20
  418.0 4.4 collective-permute-start.23
  426.7 13.4 %collective-permute-done.28 = bf16[30,128,128]{2,1,0:T(8,128)(2,1)S(1)} collective-permute-done((bf16[30,128,128]{2,1,0:T(8,128)(2,1)S(1)}, bf16[30,128,128]{2,1,0:T(8,128)(2,1)S(1)}, u32[]{:S(2)}, u32[]{:S(2)}) %collective-permute-start.28) | collective-permute-done | bytes 983072 | tf_op jit(solution)/shard_map/ppermute | solution.py:644
  442.0 6.3 collective-permute-done.23
  455.8 6.0 collective-permute-done.30
  467.9 15.9 %collective-permute-done.35 = bf16[39,128,128]{2,1,0:T(8,128)(2,1)S(1)} collective-permute-done((bf16[39,128,128]{2,1,0:T(8,128)(2,1)S(1)}, bf16[39,128,128]{2,1,0:T(8,128)(2,1)S(1)}, u32[]{:S(2)}, u32[]{:S(2)}) %collective-permute-start.35) | collective-permute-done | bytes 1277984 | tf_op jit(solution)/shard_map/ppermute | solution.py:670
  488.4 17.1 %collective-permute-done.40 = bf16[30,128,128]{2,1,0:T(8,128)(2,1)S(1)} collective-permute-done((bf16[30,128,128]{2,1,0:T(8,128)(2,1)S(1)}, bf16[30,128,128]{2,1,0:T(8,128)(2,1)S(1)}, u32[]{:S(2)}, u32[]{:S(2)}) %collective-permute-start.40) | collective-permute-done | bytes 983072 | tf_op jit(solution)/shard_map/ppermute | solution.py:662
  512.6 15.6 %collective-permute-done.47 = bf16[30,128,128]{2,1,0:T(8,128)(2,1)S(1)} collective-permute-done((bf16[30,128,128]{2,1,0:T(8,128)(2,1)S(1)}, bf16[30,128,128]{2,1,0:T(8,128)(2,1)S(1)}, u32[]{:S(2)}, u32[]{:S(2)}) %collective-permute-start.47) | collective-permute-done | bytes 983072 | tf_op jit(solution)/shard_map/ppermute | solution.py:670
  532.7 9.9 %collective-permute-done.42 = bf16[24,128,128]{2,1,0:T(8,128)(2,1)S(1)} collective-permute-done((bf16[24,128,128]{2,1,0:T(8,128)(2,1)S(1)}, bf16[24,128,128]{2,1,0:T(8,128)(2,1)S(1)}, u32[]{:S(2)}, u32[]{:S(2)}) %collective-permute-start.42) | collective-permute-done | bytes 786464 | tf_op jit(solution)/shard_map/ppermute | solution.py:662
  549.3 4.4 collective-permute-start.51
  554.4 7.2 %collective-permute-done.54 = bf16[24,128,128]{2,1,0:T(8,128)(2,1)S(1)} collective-permute-done((bf16[24,128,128]{2,1,0:T(8,128)(2,1)S(1)}, bf16[24,128,128]{2,1,0:T(8,128)(2,1)S(1)}, u32[]{:S(2)}, u32[]{:S(2)}) %collective-permute-start.54) | collective-permute-done | bytes 786464 | tf_op jit(solution)/shard_map/ppermute | solution.py:670
  578.3 10.4 %collective-permute-done.57 = bf16[24,128,128]{2,1,0:T(8,128)(2,1)S(1)} collective-permute-done((bf16[24,128,128]{2,1,0:T(8,128)(2,1)}, bf16[24,128,128]{2,1,0:T(8,128)(2,1)S(1)}, u32[]{:S(2)}, u32[]{:S(2)}) %collective-permute-start.57) | collective-permute-done | bytes 786464 | tf_op jit(solution)/shard_map/ppermute | solution.py:674
  589.8 4.5 collective-permute-done.58
  596.4 5.1 multiply_reduce_fusion
  602.1 22.3 %psum.7 = f32[3073]{0:T(1024)S(1)} all-reduce(f32[3073]{0:T(1024)S(1)} %pad_maximum_fusion.7), channel_id=1, replica_groups=mesh['dp'=8,'band'=4] {'dp'}, use_global_device_ids=true, to_apply=%region_7.8 | all-reduce | flops 3073 | bytes 24584 | tf_op jit(solution)/shard_map/psum | solution.py:906
  627.5 30.7 %optimizer.1 = (f32[108,128,128]{2,1,0:T(8,128)}, f32[108,2,128,128]{3,2,1,0:T(8,128)}, f32[108,128,128]{2,1,0:T(8,128)}, bf16[108,128,128]{2,1,0:T(8,128)(2,1)}) custom-call(f32[1]{0:T(128)} %bitcast.27.factor, s32[108]{0:T(128)} %dynamic-slice_reduce_fusion.rank, bf16[108,128,128]{2,1,0:T(8,128)(2,1)} %get-tuple-element.365.g_ref, f32[108,128,128]{2,1,0:T(8,128)} %m_ref.1, ...), custom_call_target="tpu_custom_call" | custom-call | tf_op jit(solution)/shard_map/optimizer/pallas_call | solution.py:553
  (257 shorter events, 135.8 us)
Async XLA Ops:
  7.2 145.5 %all-gather.2.cloned.1.call-start = ((), (), s32[]{:S(2)}) async-start(), calls=%async_computation | async-start | bytes 31850496 | tf_op jit(solution)/shard_map/all_gather | solution.py:713
  15.6 43.6 %collective-permute-start.12 = (bf16[2,145,768]{2,1,0:T(8,128)(2,1)S(1)}, bf16[2,145,768]{2,1,0:T(8,128)(2,1)}, u32[]{:S(2)}, u32[]{:S(2)}) collective-permute-start(bf16[2,145,768]{2,1,0:T(8,128)(2,1)S(1)} %get-tuple-element.400), channel_id=1, source_target_pairs={{1,0},{2,1},{3,2},{5,4},{6,5},{7,6},{9,8},{10,9},{11,10},{13,12},{... | collective-permute-start | bytes 1336328 | tf_op jit(solution)/shard_map/ppermute | solution.py:577
  18.1 40.1 %collective-permute-start.11 = (bf16[2,145,768]{2,1,0:T(8,128)(2,1)}, bf16[2,145,768]{2,1,0:T(8,128)(2,1)}, u32[]{:S(2)}, u32[]{:S(2)}) collective-permute-start(bf16[2,145,768]{2,1,0:T(8,128)(2,1)} %get-tuple-element.401), channel_id=1, source_target_pairs={{0,2},{2,0},{3,1},{4,6},{6,4},{7,5},{8,10},{10,8},{11,9},{12,14},{... | collective-permute-start | bytes 1336328 | tf_op jit(solution)/shard_map/ppermute | solution.py:577
  20.0 23.3 %collective-permute-start.10 = (bf16[2,145,768]{2,1,0:T(8,128)(2,1)}, bf16[2,145,768]{2,1,0:T(8,128)(2,1)}, u32[]{:S(2)}, u32[]{:S(2)}) collective-permute-start(bf16[2,145,768]{2,1,0:T(8,128)(2,1)} %get-tuple-element.402), channel_id=1, source_target_pairs={{0,1},{1,2},{3,0},{4,5},{5,6},{7,4},{8,9},{9,10},{11,8},{12,13},{1... | collective-permute-start | bytes 1336328 | tf_op jit(solution)/shard_map/ppermute | solution.py:577
  287.2 43.4 %collective-permute-start.16 = (bf16[152,128,128]{2,1,0:T(8,128)(2,1)}, bf16[152,128,128]{2,1,0:T(8,128)(2,1)}, u32[]{:S(2)}, u32[]{:S(2)}) collective-permute-start(bf16[152,128,128]{2,1,0:T(8,128)(2,1)} %get-tuple-element.526), channel_id=1, source_target_pairs={{0,4},{4,0},{8,12},{12,8},{16,20},{20,16},{24,28},{28,24},{1,5},{5... | collective-permute-start | bytes 14942216 | tf_op jit(solution)/shard_map/ppermute | solution.py:783
  290.3 39.4 %collective-permute-start.15 = (bf16[145,768]{1,0:T(8,128)(2,1)}, bf16[145,768]{1,0:T(8,128)(2,1)S(1)}, u32[]{:S(2)}, u32[]{:S(2)}) collective-permute-start(bf16[145,768]{1,0:T(8,128)(2,1)} %get-tuple-element.408), channel_id=1, source_target_pairs={{0,3},{1,0},{2,1},{4,7},{5,4},{6,5},{8,11},{9,8},{10,9},{12,15},{1... | collective-permute-start | bytes 668168 | tf_op jit(solution)/shard_map/ppermute | solution.py:588
  292.8 36.9 %collective-permute-start.14 = (bf16[145,768]{1,0:T(8,128)(2,1)}, bf16[145,768]{1,0:T(8,128)(2,1)S(1)}, u32[]{:S(2)}, u32[]{:S(2)}) collective-permute-start(bf16[145,768]{1,0:T(8,128)(2,1)} %get-tuple-element.409), channel_id=1, source_target_pairs={{0,2},{1,3},{2,0},{4,6},{5,7},{6,4},{8,10},{9,11},{10,8},{12,14},{... | collective-permute-start | bytes 668168 | tf_op jit(solution)/shard_map/ppermute | solution.py:588
  298.0 31.6 %collective-permute-start.13 = (bf16[145,768]{1,0:T(8,128)(2,1)}, bf16[145,768]{1,0:T(8,128)(2,1)S(1)}, u32[]{:S(2)}, u32[]{:S(2)}) collective-permute-start(bf16[145,768]{1,0:T(8,128)(2,1)} %get-tuple-element.410), channel_id=1, source_target_pairs={{0,1},{1,2},{2,3},{4,5},{5,6},{6,7},{8,9},{9,10},{10,11},{12,13},{... | collective-permute-start | bytes 668168 | tf_op jit(solution)/shard_map/ppermute | solution.py:588
  335.5 29.3 %collective-permute-start.17 = (bf16[38,128,128]{2,1,0:T(8,128)(2,1)}, bf16[38,128,128]{2,1,0:T(8,128)(2,1)}, u32[]{:S(2)}, u32[]{:S(2)}) collective-permute-start(bf16[38,128,128]{2,1,0:T(8,128)(2,1)} %get-tuple-element.268), channel_id=1, source_target_pairs={{0,8},{4,12},{8,0},{12,4},{16,24},{20,28},{24,16},{28,20},{1,9},{5... | collective-permute-start | bytes 3735560 | tf_op jit(solution)/shard_map/ppermute | solution.py:644
  336.9 28.8 %collective-permute-start.18 = (bf16[38,128,128]{2,1,0:T(8,128)(2,1)S(1)}, bf16[38,128,128]{2,1,0:T(8,128)(2,1)}, u32[]{:S(2)}, u32[]{:S(2)}) collective-permute-start(bf16[38,128,128]{2,1,0:T(8,128)(2,1)S(1)} %get-tuple-element.269), channel_id=1, source_target_pairs={{0,16},{4,20},{8,24},{12,28},{16,0},{20,4},{24,8},{28,12},{1,17},{... | collective-permute-start | bytes 3735560 | tf_op jit(solution)/shard_map/ppermute | solution.py:644
  385.9 24.4 %collective-permute-start.21 = (bf16[120,128,128]{2,1,0:T(8,128)(2,1)}, bf16[120,128,128]{2,1,0:T(8,128)(2,1)}, u32[]{:S(2)}, u32[]{:S(2)}) collective-permute-start(bf16[120,128,128]{2,1,0:T(8,128)(2,1)} %slice.420), channel_id=1, source_target_pairs={{0,4},{4,0},{8,12},{12,8},{16,20},{20,16},{24,28},{28,24},{1,5},{5... | collective-permute-start | bytes 11796488 | tf_op jit(solution)/shard_map/ppermute | solution.py:807
  396.8 58.9 %collective-permute-start.31 = (bf16[96,128,128]{2,1,0:T(8,128)(2,1)}, bf16[96,128,128]{2,1,0:T(8,128)(2,1)S(1)}, u32[]{:S(2)}, u32[]{:S(2)}) collective-permute-start(bf16[96,128,128]{2,1,0:T(8,128)(2,1)} %slice.437), channel_id=1, source_target_pairs={{0,4},{4,0},{8,12},{12,8},{16,20},{20,16},{24,28},{28,24},{1,5},{5... | collective-permute-start | bytes 9437192 | tf_op jit(solution)/shard_map/ppermute | solution.py:807
  397.1 20.2 %collective-permute-start.26 = (bf16[145,768]{1,0:T(8,128)(2,1)S(1)}, bf16[145,768]{1,0:T(8,128)(2,1)S(1)}, u32[]{:S(2)}, u32[]{:S(2)}) collective-permute-start(bf16[145,768]{1,0:T(8,128)(2,1)S(1)} %get-tuple-element.404), channel_id=1, source_target_pairs={{0,3},{1,0},{2,1},{4,7},{5,4},{6,5},{8,11},{9,8},{10,9},{12,15},{1... | collective-permute-start | bytes 668168 | tf_op jit(solution)/shard_map/ppermute | solution.py:588
  416.6 23.4 %collective-permute-start.28 = (bf16[30,128,128]{2,1,0:T(8,128)(2,1)S(1)}, bf16[30,128,128]{2,1,0:T(8,128)(2,1)S(1)}, u32[]{:S(2)}, u32[]{:S(2)}) collective-permute-start(bf16[30,128,128]{2,1,0:T(8,128)(2,1)S(1)} %get-tuple-element.378), channel_id=1, source_target_pairs={{0,16},{4,20},{8,24},{12,28},{16,0},{20,4},{24,8},{28,12},{1,17},{... | collective-permute-start | bytes 2949128 | tf_op jit(solution)/shard_map/ppermute | solution.py:644
  417.3 23.1 %collective-permute-start.27 = (bf16[30,128,128]{2,1,0:T(8,128)(2,1)S(1)}, bf16[30,128,128]{2,1,0:T(8,128)(2,1)S(1)}, u32[]{:S(2)}, u32[]{:S(2)}) collective-permute-start(bf16[30,128,128]{2,1,0:T(8,128)(2,1)S(1)} %get-tuple-element.379), channel_id=1, source_target_pairs={{0,8},{4,12},{8,0},{12,4},{16,24},{20,28},{24,16},{28,20},{1,9},{5... | collective-permute-start | bytes 2949128 | tf_op jit(solution)/shard_map/ppermute | solution.py:644
  418.0 30.3 %collective-permute-start.23 = (bf16[39,128,128]{2,1,0:T(8,128)(2,1)S(1)}, bf16[39,128,128]{2,1,0:T(8,128)(2,1)S(1)}, u32[]{:S(2)}, u32[]{:S(2)}) collective-permute-start(bf16[39,128,128]{2,1,0:T(8,128)(2,1)S(1)} %pad_maximum_fusion.2), channel_id=1, source_target_pairs={{2,1},{6,5},{10,9},{14,13},{18,17},{22,21},{26,25},{30,29}} | collective-permute-start | bytes 3833864 | tf_op jit(solution)/shard_map/ppermute | solution.py:662
  425.0 23.3 %collective-permute-start.22 = (bf16[39,128,128]{2,1,0:T(8,128)(2,1)S(1)}, bf16[39,128,128]{2,1,0:T(8,128)(2,1)S(1)}, u32[]{:S(2)}, u32[]{:S(2)}) collective-permute-start(bf16[39,128,128]{2,1,0:T(8,128)(2,1)S(1)} %pad_maximum_fusion.2), channel_id=1, source_target_pairs={{0,1},{4,5},{8,9},{12,13},{16,17},{20,21},{24,25},{28,29}} | collective-permute-start | bytes 3833864 | tf_op jit(solution)/shard_map/ppermute | solution.py:662
  448.9 34.9 %collective-permute-start.35 = (bf16[39,128,128]{2,1,0:T(8,128)(2,1)S(1)}, bf16[39,128,128]{2,1,0:T(8,128)(2,1)S(1)}, u32[]{:S(2)}, u32[]{:S(2)}) collective-permute-start(bf16[39,128,128]{2,1,0:T(8,128)(2,1)S(1)} %add_convert_fusion.7), channel_id=1, source_target_pairs={{1,2},{5,6},{9,10},{13,14},{17,18},{21,22},{25,26},{29,30}} | collective-permute-start | bytes 3833864 | tf_op jit(solution)/shard_map/ppermute | solution.py:670
  450.2 34.4 %collective-permute-start.34 = (bf16[39,128,128]{2,1,0:T(8,128)(2,1)S(1)}, bf16[39,128,128]{2,1,0:T(8,128)(2,1)S(1)}, u32[]{:S(2)}, u32[]{:S(2)}) collective-permute-start(bf16[39,128,128]{2,1,0:T(8,128)(2,1)S(1)} %add_convert_fusion.7), channel_id=1, source_target_pairs={{1,0},{5,4},{9,8},{13,12},{17,16},{21,20},{25,24},{29,28}} | collective-permute-start | bytes 3833864 | tf_op jit(solution)/shard_map/ppermute | solution.py:670
  455.7 52.2 %collective-permute-start.38 = (bf16[64,128,128]{2,1,0:T(8,128)(2,1)S(1)}, bf16[64,128,128]{2,1,0:T(8,128)(2,1)S(1)}, u32[]{:S(2)}, u32[]{:S(2)}) collective-permute-start(bf16[64,128,128]{2,1,0:T(8,128)(2,1)S(1)} %slice.456), channel_id=1, source_target_pairs={{0,4},{4,0},{8,12},{12,8},{16,20},{20,16},{24,28},{28,24},{1,5},{5... | collective-permute-start | bytes 6291464 | tf_op jit(solution)/shard_map/ppermute | solution.py:807
  463.9 22.9 %collective-permute-start.33 = (bf16[24,128,128]{2,1,0:T(8,128)(2,1)S(1)}, bf16[24,128,128]{2,1,0:T(8,128)(2,1)S(1)}, u32[]{:S(2)}, u32[]{:S(2)}) collective-permute-start(bf16[24,128,128]{2,1,0:T(8,128)(2,1)S(1)} %get-tuple-element.384), channel_id=1, source_target_pairs={{0,16},{4,20},{8,24},{12,28},{16,0},{20,4},{24,8},{28,12},{1,17},{... | collective-permute-start | bytes 2359304 | tf_op jit(solution)/shard_map/ppermute | solution.py:644
  466.1 20.6 %collective-permute-start.32 = (bf16[24,128,128]{2,1,0:T(8,128)(2,1)S(1)}, bf16[24,128,128]{2,1,0:T(8,128)(2,1)S(1)}, u32[]{:S(2)}, u32[]{:S(2)}) collective-permute-start(bf16[24,128,128]{2,1,0:T(8,128)(2,1)S(1)} %get-tuple-element.385), channel_id=1, source_target_pairs={{0,8},{4,12},{8,0},{12,4},{16,24},{20,28},{24,16},{28,20},{1,9},{5... | collective-permute-start | bytes 2359304 | tf_op jit(solution)/shard_map/ppermute | solution.py:644
  484.6 20.8 %collective-permute-start.40 = (bf16[30,128,128]{2,1,0:T(8,128)(2,1)S(1)}, bf16[30,128,128]{2,1,0:T(8,128)(2,1)S(1)}, u32[]{:S(2)}, u32[]{:S(2)}) collective-permute-start(bf16[30,128,128]{2,1,0:T(8,128)(2,1)S(1)} %pad_maximum_fusion.3), channel_id=1, source_target_pairs={{2,1},{6,5},{10,9},{14,13},{18,17},{22,21},{26,25},{30,29}} | collective-permute-start | bytes 2949128 | tf_op jit(solution)/shard_map/ppermute | solution.py:662
  487.2 23.3 %collective-permute-start.37 = (bf16[12,128,128]{2,1,0:T(8,128)(2,1)S(1)}, bf16[12,128,128]{2,1,0:T(8,128)(2,1)S(1)}, u32[]{:S(2)}, u32[]{:S(2)}) collective-permute-start(bf16[12,128,128]{2,1,0:T(8,128)(2,1)S(1)} %get-tuple-element.382), channel_id=1, source_target_pairs={{0,16},{4,20},{8,24},{12,28},{16,0},{20,4},{24,8},{28,12},{1,17},{... | collective-permute-start | bytes 1179656 | tf_op jit(solution)/shard_map/ppermute | solution.py:651
  487.8 22.7 %collective-permute-start.36 = (bf16[12,128,128]{2,1,0:T(8,128)(2,1)S(1)}, bf16[12,128,128]{2,1,0:T(8,128)(2,1)S(1)}, u32[]{:S(2)}, u32[]{:S(2)}) collective-permute-start(bf16[12,128,128]{2,1,0:T(8,128)(2,1)S(1)} %get-tuple-element.383), channel_id=1, source_target_pairs={{0,8},{4,12},{8,0},{12,4},{16,24},{20,28},{24,16},{28,20},{1,9},{5... | collective-permute-start | bytes 1179656 | tf_op jit(solution)/shard_map/ppermute | solution.py:651
  505.9 22.3 %collective-permute-start.47 = (bf16[30,128,128]{2,1,0:T(8,128)(2,1)S(1)}, bf16[30,128,128]{2,1,0:T(8,128)(2,1)S(1)}, u32[]{:S(2)}, u32[]{:S(2)}) collective-permute-start(bf16[30,128,128]{2,1,0:T(8,128)(2,1)S(1)} %add_convert_fusion.10), channel_id=1, source_target_pairs={{1,2},{5,6},{9,10},{13,14},{17,18},{21,22},{25,26},{29,30}} | collective-permute-start | bytes 2949128 | tf_op jit(solution)/shard_map/ppermute | solution.py:670
  507.2 22.5 %collective-permute-start.46 = (bf16[30,128,128]{2,1,0:T(8,128)(2,1)S(1)}, bf16[30,128,128]{2,1,0:T(8,128)(2,1)S(1)}, u32[]{:S(2)}, u32[]{:S(2)}) collective-permute-start(bf16[30,128,128]{2,1,0:T(8,128)(2,1)S(1)} %add_convert_fusion.10), channel_id=1, source_target_pairs={{1,0},{5,4},{9,8},{13,12},{17,16},{21,20},{25,24},{29,28}} | collective-permute-start | bytes 2949128 | tf_op jit(solution)/shard_map/ppermute | solution.py:670
  507.9 35.2 %collective-permute-start.43 = (bf16[39,128,128]{2,1,0:T(8,128)(2,1)S(1)}, bf16[39,128,128]{2,1,0:T(8,128)(2,1)}, u32[]{:S(2)}, u32[]{:S(2)}) collective-permute-start(bf16[39,128,128]{2,1,0:T(8,128)(2,1)S(1)} %collective-permute-done.35), channel_id=1, source_target_pairs={{2,3},{6,7},{10,11},{14,15},{18,19},{22,23},{26,27},{30,31}} | collective-permute-start | bytes 3833864 | tf_op jit(solution)/shard_map/ppermute | solution.py:674
  510.8 19.6 %collective-permute-start.45 = (bf16[16,128,128]{2,1,0:T(8,128)(2,1)S(1)}, bf16[16,128,128]{2,1,0:T(8,128)(2,1)S(1)}, u32[]{:S(2)}, u32[]{:S(2)}) collective-permute-start(bf16[16,128,128]{2,1,0:T(8,128)(2,1)S(1)} %get-tuple-element.390), channel_id=1, source_target_pairs={{0,16},{4,20},{8,24},{12,28},{16,0},{20,4},{24,8},{28,12},{1,17},{... | collective-permute-start | bytes 1572872 | tf_op jit(solution)/shard_map/ppermute | solution.py:644
  511.9 19.9 %collective-permute-start.44 = (bf16[16,128,128]{2,1,0:T(8,128)(2,1)S(1)}, bf16[16,128,128]{2,1,0:T(8,128)(2,1)S(1)}, u32[]{:S(2)}, u32[]{:S(2)}) collective-permute-start(bf16[16,128,128]{2,1,0:T(8,128)(2,1)S(1)} %get-tuple-element.391), channel_id=1, source_target_pairs={{0,8},{4,12},{8,0},{12,4},{16,24},{20,28},{24,16},{28,20},{1,9},{5... | collective-permute-start | bytes 1572872 | tf_op jit(solution)/shard_map/ppermute | solution.py:644
  530.4 31.2 %collective-permute-start.52 = (bf16[30,128,128]{2,1,0:T(8,128)(2,1)S(1)}, bf16[30,128,128]{2,1,0:T(8,128)(2,1)S(1)}, u32[]{:S(2)}, u32[]{:S(2)}) collective-permute-start(bf16[30,128,128]{2,1,0:T(8,128)(2,1)S(1)} %collective-permute-done.47), channel_id=1, source_target_pairs={{2,3},{6,7},{10,11},{14,15},{18,19},{22,23},{26,27},{30,31}} | collective-permute-start | bytes 2949128 | tf_op jit(solution)/shard_map/ppermute | solution.py:674
  573.1 21.2 %collective-permute-start.58 = (bf16[16,128,128]{2,1,0:T(8,128)(2,1)}, bf16[16,128,128]{2,1,0:T(8,128)(2,1)S(1)}, u32[]{:S(2)}, u32[]{:S(2)}) collective-permute-start(bf16[16,128,128]{2,1,0:T(8,128)(2,1)} %collective-permute-done.56), channel_id=1, source_target_pairs={{2,3},{6,7},{10,11},{14,15},{18,19},{22,23},{26,27},{30,31}} | collective-permute-start | bytes 1572872 | tf_op jit(solution)/shard_map/ppermute | solution.py:674
  (51 other events, 643.9 us)
Sparse Core Ops, SparseCore 0:
  13.0 139.6 all-gather.1

commit v5 on v3

--- a/solution.py
+++ b/solution.py
@@ -209,36 +209,26 @@
         save.wait()
 
 
-def put_tiles(places, m, grad, zones, outs, sem, i0, i1, j0, count_j):
+def put_tiles(places, m, grad, tiles_out, sem, i0, i1, j0, count_j):
     @pl.loop(i0, i1)
     def _(i):
         for jj in range(count_j):
             j = j0 + jj
-            place = places[OFFSETS[m] + i * GRIDS[m][1] + j]
-            tile = grad.at[
-                pl.ds(pl.multiple_of(i * BLOCK, BLOCK), BLOCK),
-                pl.ds(pl.multiple_of(j * BLOCK, BLOCK), BLOCK),
-            ]
-            start = 0
-            for size, out in zip(zones, outs):
-                if len(zones) == 1:
-                    pltpu.make_async_copy(tile, out.at[place], sem).start()
-                else:
-
-                    @pl.when((place >= start) & (place < start + size))
-                    def _(tile=tile, out=out, place=place, start=start):
-                        pltpu.make_async_copy(tile, out.at[place - start], sem).start()
-
-                start += size
+            pltpu.make_async_copy(
+                grad.at[
+                    pl.ds(pl.multiple_of(i * BLOCK, BLOCK), BLOCK),
+                    pl.ds(pl.multiple_of(j * BLOCK, BLOCK), BLOCK),
+                ],
+                tiles_out.at[places[OFFSETS[m] + i * GRIDS[m][1] + j]],
+                sem,
+            ).start()
 
 
 def back_ffn_kernel(
-    zones, begun, places, spare, back_ref, g_ref, mid_i, n2_i, gu_i, wgu_i, wd_i, *rest
+    begun, places, spare, back_ref, g_ref, mid_i, n2_i, gu_i, wgu_i, wd_i, *rest
 ):
-    rest = rest[begun:]
-    mid_ref_out, gain_ref = rest[:2]
-    outs = rest[2 : 2 + len(zones)]
-    mid_ref, n2_ref, gu_ref, wgu, wd, ggu, gd, big, zero, sem_in, sem_out, sem_zero = rest[2 + len(zones) :]
+    mid_ref_out, gain_ref, tiles_out, *rest = rest[begun:]
+    mid_ref, n2_ref, gu_ref, wgu, wd, ggu, gd, big, zero, sem_in, sem_out, sem_zero = rest
     loads = copies([(wd_i, wd), (gu_i, gu_ref), (n2_i, n2_ref), (wgu_i, wgu), (mid_i, mid_ref)], sem_in)
     for load in loads:
         load.start()
@@ -248,7 +238,7 @@
 
         @pl.loop(0, spares)
         def _(i):
-            pltpu.make_async_copy(zero, outs[0].at[spare[i]], sem_zero).start()
+            pltpu.make_async_copy(zero, tiles_out.at[spare[i]], sem_zero).start()
 
     big[...] = jnp.zeros(big.shape, f32)
     for load in loads[:4]:
@@ -273,9 +263,9 @@
         ggu[:, here] = tn(n2_ref[...], d_gate).astype(bf16)
         ggu[:, there] = tn(n2_ref[...], d_up).astype(bf16)
         per = FF_STEP // BLOCK
-        put(3, gd, zones, outs, sem_out.at[1], t * per, (t + 1) * per, 0, D // BLOCK)
-        put(2, ggu, zones, outs, sem_out.at[0], 0, D // BLOCK, t * per, per)
-        put(2, ggu, zones, outs, sem_out.at[0], 0, D // BLOCK, FF // BLOCK + t * per, per)
+        put(3, gd, tiles_out, sem_out.at[1], t * per, (t + 1) * per, 0, D // BLOCK)
+        put(2, ggu, tiles_out, sem_out.at[0], 0, D // BLOCK, t * per, per)
+        put(2, ggu, tiles_out, sem_out.at[0], 0, D // BLOCK, FF // BLOCK + t * per, per)
         big[...] += nt(d_gate, wgu[:, here]) + nt(d_up, wgu[:, there])
 
     loads[4].wait()
@@ -288,20 +278,17 @@
 
         @pl.loop(0, spares)
         def _(i):
-            pltpu.make_async_copy(zero, outs[0].at[spare[i]], sem_zero).wait()
+            pltpu.make_async_copy(zero, tiles_out.at[spare[i]], sem_zero).wait()
 
 
 def back_attention_kernel(
-    zones, begun, places, length, back_ref, cos_ref, sin_ref,
+    begun, places, length, back_ref, cos_ref, sin_ref,
     q_i, k_i, v_i, st_i, mixed_i, wout_i, *rest
 ):
-    rest = rest[begun:]
-    dproj = rest[0]
-    outs = rest[1 : 1 + len(zones)]
     (
-        q_ref, k_ref, v_ref, st_ref, mixed_ref, wout,
+        dproj, tiles_out, q_ref, k_ref, v_ref, st_ref, mixed_ref, wout,
         gout, bias, turned, sums, mixed_back, sem_in, sem_out,
-    ) = rest[1 + len(zones) :]
+    ) = rest[begun:]
     rows = back_ref.shape[0]
     key_rows = q_ref.shape[0]
     loads = copies(
@@ -323,7 +310,7 @@
     mixed_back[rows:, :] = jnp.zeros((key_rows - rows, D), bf16)
     loads[1].wait()
     gout[...] = tn(mixed_ref[...], back_attn).astype(bf16)
-    put(1, gout, zones, outs, sem_out, 0, D // BLOCK, 0, D // BLOCK)
+    put(1, gout, tiles_out, sem_out, 0, D // BLOCK, 0, D // BLOCK)
     for load in loads[2:]:
         load.wait()
     levels = st_ref[...].T
@@ -369,11 +356,9 @@
     pltpu.make_async_copy(gout, gout, sem_out).wait()
 
 
-def back_qkv_kernel(zones, begun, places, back_ref, g_ref, dproj, x_i, normed_i, wqkv_i, *rest):
-    rest = rest[begun:]
-    dx_ref, gain_ref = rest[:2]
-    outs = rest[2 : 2 + len(zones)]
-    x_ref, normed_ref, wqkv, gqkv, big, sem_in, sem_out = rest[2 + len(zones) :]
+def back_qkv_kernel(begun, places, back_ref, g_ref, dproj, x_i, normed_i, wqkv_i, *rest):
+    dx_ref, gain_ref, tiles_out, *rest = rest[begun:]
+    x_ref, normed_ref, wqkv, gqkv, big, sem_in, sem_out = rest
     loads = copies([(normed_i, normed_ref), (wqkv_i, wqkv), (x_i, x_ref)], sem_in)
     for load in loads:
         load.start()
@@ -385,9 +370,7 @@
     def _(part):
         cols = pl.ds(pl.multiple_of(part * D, D), D)
         gqkv[:, cols] = tn(normed_ref[...], dproj[:, cols]).astype(bf16)
-        put_tiles(
-            places, 0, gqkv, zones, outs, sem_out, 0, D // BLOCK, part * (D // BLOCK), D // BLOCK
-        )
+        put_tiles(places, 0, gqkv, tiles_out, sem_out, 0, D // BLOCK, part * (D // BLOCK), D // BLOCK)
         big[...] += nt(dproj[:, cols], wqkv[:, cols])
 
     loads[2].wait()
@@ -446,22 +429,17 @@
     )(slots, length, x, gains, cos, sin, gathered)
 
 
-def tile_outputs(zones):
-    return [jax.ShapeDtypeStruct((size, BLOCK, BLOCK), bf16) for size in zones]
-
-
-def back_ffn(places, spare, back, gain, saved, zones, begun):
+def back_ffn(places, spare, back, gain, saved, slot_count, begun):
     rows = back.shape[0]
     S = jax.ShapeDtypeStruct
     args = (places, spare, back, gain) + tuple(saved)
-    first = 2 + len(zones) - len(begun)
     wgu, wd = saved[3], saved[4]
     return pl.pallas_call(
-        functools.partial(back_ffn_kernel, zones, len(begun)),
-        out_shape=[S((rows, D), f32), S((1, D), f32)] + tile_outputs(zones),
+        functools.partial(back_ffn_kernel, len(begun)),
+        out_shape=[S((rows, D), f32), S((1, D), f32), S((slot_count, BLOCK, BLOCK), bf16)],
         in_specs=[SMEM] * 2 + [VMEM] * 2 + [HBM] * (5 + len(begun)),
-        out_specs=[VMEM, VMEM] + [HBM] * len(zones),
-        input_output_aliases={len(args) + i: first + i for i in range(len(begun))},
+        out_specs=[VMEM, VMEM, HBM],
+        input_output_aliases={len(args): 2} if begun else {},
         scratch_shapes=[like(s) for s in saved]
         + [like(wgu), like(wd)]
         + [
@@ -477,18 +455,17 @@
     )(*args, *begun)
 
 
-def back_attention(places, length, back, cos, sin, saved, zones, begun):
+def back_attention(places, length, back, cos, sin, saved, slot_count, begun):
     rows = back.shape[0]
     key_rows = round_up(rows, BLOCK)
     S = jax.ShapeDtypeStruct
     args = (places, length, back, cos, sin) + tuple(saved)
-    first = 1 + len(zones) - len(begun)
     return pl.pallas_call(
-        functools.partial(back_attention_kernel, zones, len(begun)),
-        out_shape=[S((rows, 3 * D), bf16)] + tile_outputs(zones),
+        functools.partial(back_attention_kernel, len(begun)),
+        out_shape=[S((rows, 3 * D), bf16), S((slot_count, BLOCK, BLOCK), bf16)],
         in_specs=[SMEM] * 2 + [VMEM] * 3 + [HBM] * (6 + len(begun)),
-        out_specs=[VMEM] + [HBM] * len(zones),
-        input_output_aliases={len(args) + i: first + i for i in range(len(begun))},
+        out_specs=[VMEM, HBM],
+        input_output_aliases={len(args): 1} if begun else {},
         scratch_shapes=[like(s) for s in saved]
         + [
             like(saved[5]),
@@ -505,17 +482,16 @@
     )(*args, *begun)
 
 
-def back_qkv(places, back, gain, d_projected, saved, zones, begun):
+def back_qkv(places, back, gain, d_projected, saved, slot_count, begun):
     rows = back.shape[0]
     S = jax.ShapeDtypeStruct
     args = (places, back, gain, d_projected) + tuple(saved)
-    first = 2 + len(zones) - len(begun)
     return pl.pallas_call(
-        functools.partial(back_qkv_kernel, zones, len(begun)),
-        out_shape=[S((rows, D), f32), S((1, D), f32)] + tile_outputs(zones),
+        functools.partial(back_qkv_kernel, len(begun)),
+        out_shape=[S((rows, D), f32), S((1, D), f32), S((slot_count, BLOCK, BLOCK), bf16)],
         in_specs=[SMEM] + [VMEM] * 3 + [HBM] * (3 + len(begun)),
-        out_specs=[VMEM, VMEM] + [HBM] * len(zones),
-        input_output_aliases={len(args) + i: first + i for i in range(len(begun))},
+        out_specs=[VMEM, VMEM, HBM],
+        input_output_aliases={len(args): 2} if begun else {},
         scratch_shapes=[like(s) for s in saved]
         + [
             like(saved[2]),
@@ -579,19 +555,29 @@
     return whole
 
 
-def to_bands(whole, images, bands, band):
-    local = jnp.zeros(whole.shape, whole.dtype)
+def send_to_bands(whole, images, bands, band):
+    blocks = []
     for shift in range(bands):
         block = lax.dynamic_index_in_dim(whole, (band + shift) % bands, 0, keepdims=False)
         if shift > 0:
             pairs = [(b, (b + shift) % bands) for b in range(images)]
             block = lax.ppermute(block, "band", pairs)
+        blocks.append(block)
+    return tuple(blocks)
+
+
+def at_bands(blocks, images, bands, band):
+    local = jnp.zeros((bands,) + blocks[0].shape, blocks[0].dtype)
+    for shift, block in enumerate(blocks):
         local = lax.dynamic_update_index_in_dim(local, block, (band - shift) % bands, 0)
     return local[:images]
 
 
-EARLY = 38
-LATE = (30, 24, 16)
+CHUNKS = (22, 18, 20, 18, 18, 12)
+FFN_FIRST = OFFSETS[2]
+LEAST = (PER_LAYER + FFN_FIRST, PER_LAYER, FFN_FIRST, FFN_FIRST, 0, 0)
+GAIN_CHUNK = 4
+STARTS = tuple(sum(CHUNKS[:i]) for i in range(len(CHUNKS)))
 
 
 def relative_places(slot_of_block, per_owner, me):
@@ -600,25 +586,19 @@
         jnp.arange(blocks, dtype=jnp.int32)
     )
     by_owner = block_of_slot.reshape(-1, per_owner)
-    rank = jnp.sum(by_owner[:, None, :] < by_owner[:, :, None], -1, dtype=jnp.int32)
-    early = per_owner - EARLY
-    clean = jnp.all(jnp.where(rank >= early, by_owner >= PER_LAYER, True))
+    rank = jnp.sum(by_owner[:, None, :] > by_owner[:, :, None], -1, dtype=jnp.int32)
     relative = (jnp.arange(by_owner.shape[0], dtype=jnp.int32) ^ me)[:, None]
     core, x, y = relative % 2, relative // 2 % 2, relative // 4
     place = jnp.zeros_like(rank)
-    zone_sizes = (4 * EARLY, 4 * EARLY, 4 * early, 4 * early)
-    chunks = [(early, EARLY, 0, 0)]
-    start = 0
-    for size in LATE:
-        chunks.append((start, size, 2, 4 * start))
-        start += size
-    for start, size, zone, inside in chunks:
+    clean = jnp.bool_(True)
+    for start, size, least in zip(STARTS, CHUNKS, LEAST):
         half = size // 2
         at = rank - start
+        here = (at >= 0) & (at < size)
         spot = jnp.where(at < half, (x * 2 + y) * half + at, 4 * half + (y * 2 + x) * half + at - half)
-        base = jnp.where(core == 0, sum(zone_sizes[:zone]), sum(zone_sizes[: zone + 1]))
-        place = jnp.where((at >= 0) & (at < size), base + inside + spot, place)
-    return place.reshape(-1)[slot_of_block], rank, clean, zone_sizes
+        place = jnp.where(here, 8 * start + core * 4 * size + spot, place)
+        clean = clean & jnp.all(jnp.where(here, by_owner >= least, True))
+    return place.reshape(-1)[slot_of_block], rank, clean
 
 
 CORE = [(i, i ^ 1) for i in range(8)]
@@ -630,44 +610,149 @@
     return t[lo:hi].astype(f32)
 
 
-def plane_start(kept, received, gate=None, beside=None):
-    half = kept.shape[0] // 8
-
-    def chip(lo, hi):
-        return wide(kept, lo * half, hi * half) + wide(received, lo * half, hi * half)
-
-    send_x, send_y = chip(2, 4).astype(bf16), chip(6, 8).astype(bf16)
-    if gate is not None:
-        send_x, send_y, _ = lax.optimization_barrier((send_x, send_y, gate))
-    if beside is not None:
-        send_x, send_y, beside = lax.optimization_barrier((send_x, send_y, beside))
-    going = (chip, half, lax.ppermute(send_x, "dp", ALONG_X), lax.ppermute(send_y, "dp", ALONG_Y))
-    return going if beside is None else (going, beside)
-
-
-def plane_turn(chip, half, from_x, from_y):
-    send_y = (chip(1, 2) + wide(from_x, half, 2 * half)).astype(bf16)
-    send_x = (chip(5, 6) + wide(from_y, half, 2 * half)).astype(bf16)
-    return lax.ppermute(send_x, "dp", ALONG_X), lax.ppermute(send_y, "dp", ALONG_Y)
-
-
-def plane_end(chip, half, from_x, from_y, later_x, later_y):
-    one = chip(0, 1) + wide(from_x, 0, half) + later_y.astype(f32)
-    two = chip(4, 5) + wide(from_y, 0, half) + later_x.astype(f32)
-    return jnp.concatenate([one, two], 0).astype(bf16)
-
-
-def sum_bands(plane, band):
-    kind = plane.dtype
-    up = lax.ppermute(plane, "band", [(0, 1)])
-    down = lax.ppermute(plane, "band", [(2, 1)])
-    total = (plane.astype(f32) + up.astype(f32) + down.astype(f32)).astype(kind)
-    to_first = lax.ppermute(total, "band", [(1, 0)])
-    to_third = lax.ppermute(total, "band", [(1, 2)])
-    to_last = lax.ppermute(to_third, "band", [(2, 3)])
-    total = jnp.where(band == 0, to_first, total)
-    total = jnp.where(band == 2, to_third, total)
-    return jnp.where(band == 3, to_last, total)
+def split_wide(t):
+    high = lax.reduce_precision(t, 8, 7)
+    both = jnp.concatenate([high, t - high], 0)
+    return jnp.pad(both, ((0, BLOCK - both.shape[0]), (0, 0))).astype(bf16)[None]
+
+
+def join_wide(tile, rows):
+    return tile[0, :rows].astype(f32) + tile[0, rows : 2 * rows].astype(f32)
+
+
+def with_tile(t, extra):
+    return t if extra is None else jnp.concatenate([t, split_wide(extra)], 0)
+
+
+class Chunk:
+    def __init__(self, index, extra=None):
+        self.index, self.extra = index, extra
+        self.half = CHUNKS[index] // 2
+
+    def begin(self, tiles):
+        size, at = CHUNKS[self.index], 8 * STARTS[self.index]
+        self.kept = tiles[at : at + 4 * size]
+        self.sent = tiles[at + 4 * size : at + 8 * size]
+
+    def own(self):
+        return join_wide(split_wide(self.extra), self.extra.shape[0])
+
+    def take(self, arrived):
+        if self.extra is not None:
+            self.extra = self.own() + join_wide(arrived[-1:], self.extra.shape[0])
+
+    def chip(self, lo, hi):
+        lo, hi = lo * self.half, hi * self.half
+        return wide(self.kept, lo, hi) + wide(self.received, lo, hi)
+
+    def to_core(self):
+        return (with_tile(self.sent, self.extra),)
+
+    def go_core(self, send):
+        return (lax.ppermute(send, "dp", CORE),)
+
+    def to_plane(self, received):
+        self.received = received
+        self.take(received)
+        return with_tile(self.chip(2, 4).astype(bf16), self.extra), self.chip(6, 8).astype(bf16)
+
+    def go_plane(self, send_x, send_y):
+        return lax.ppermute(send_x, "dp", ALONG_X), lax.ppermute(send_y, "dp", ALONG_Y)
+
+    def to_turn(self, from_x, from_y):
+        self.from_x, self.from_y = from_x, from_y
+        self.take(from_x)
+        half = self.half
+        send_y = (self.chip(1, 2) + wide(from_x, half, 2 * half)).astype(bf16)
+        send_x = (self.chip(5, 6) + wide(from_y, half, 2 * half)).astype(bf16)
+        return send_x, with_tile(send_y, self.extra)
+
+    def to_meet(self, from_x, from_y):
+        self.take(from_y)
+        half = self.half
+        one = self.chip(0, 1) + wide(self.from_x, 0, half) + wide(from_y, 0, half)
+        two = self.chip(4, 5) + wide(self.from_y, 0, half) + wide(from_x, 0, half)
+        self.plane = with_tile(jnp.concatenate([one, two], 0).astype(bf16), self.extra)
+        return (self.plane,)
+
+    def go_meet(self, plane):
+        return lax.ppermute(plane, "band", [(0, 1)]), lax.ppermute(plane, "band", [(2, 1)])
+
+    def to_part(self, up, down):
+        total = self.plane.astype(f32) + up.astype(f32) + down.astype(f32)
+        if self.extra is not None:
+            total = total[:-1]
+            rows = self.extra.shape[0]
+            self.extra = self.own() + join_wide(up[-1:], rows) + join_wide(down[-1:], rows)
+        self.total = with_tile(total.astype(bf16), self.extra)
+        return (self.total,)
+
+    def go_part(self, total):
+        return lax.ppermute(total, "band", [(1, 0)]), lax.ppermute(total, "band", [(1, 2)])
+
+    def to_last(self, to_first, to_third):
+        self.to_first, self.to_third = to_first, to_third
+        return (to_third,)
+
+    def go_last(self, to_third):
+        return (lax.ppermute(to_third, "band", [(2, 3)]),)
+
+    def to_end(self, to_last):
+        band = lax.axis_index("band")
+        total = jnp.where(band == 0, self.to_first, self.total)
+        total = jnp.where(band == 2, self.to_third, total)
+        self.total = jnp.where(band == 3, to_last, total)
+        return ()
+
+    STEPS = ("core", "plane", "turn", "meet", "part", "last", "end")
+
+    def step(self, name, arrived=()):
+        return getattr(self, "to_" + name)(*arrived)
+
+    def go(self, name, sends):
+        way = {"turn": "plane"}.get(name, name)
+        return getattr(self, "go_" + way)(*sends) if way != "end" else ()
+
+
+class Sequence:
+    def __init__(self):
+        self.before = ()
+        self.arrived = {}
+
+    def round(self, steps, *beside):
+        counts = [len(self.arrived.get(id(chunk), ())) for chunk, _ in steps]
+        arrays = sum((tuple(self.arrived.get(id(chunk), ())) for chunk, _ in steps), ())
+        taken = len(arrays)
+        arrays = lax.optimization_barrier(arrays + self.before + beside)
+        beside = arrays[len(arrays) - len(beside) :]
+        new = [chunk for chunk, name in steps if name == "core"]
+        for chunk in new:
+            chunk.begin(*beside[:1])
+        sends, at = [], 0
+        for (chunk, name), count in zip(steps, counts):
+            sends.append(chunk.step(name, arrays[:taken][at : at + count]))
+            at += count
+        flat = sum((tuple(s) for s in sends), ())
+        if beside:
+            kept = tuple(chunk.kept for chunk in new)
+            together = lax.optimization_barrier(flat + kept + beside)
+            beside = together[len(together) - len(beside) :]
+            for chunk, piece in zip(new, together[len(flat) :]):
+                chunk.kept = piece
+            flat = together[: len(flat)]
+        at = 0
+        for (chunk, name), s in zip(steps, sends):
+            self.arrived[id(chunk)] = chunk.go(name, flat[at : at + len(s)])
+            at += len(s)
+        self.before = flat
+        return beside
+
+
+def reduce_all(chunks, tiles):
+    sequence = Sequence()
+    for chunk in chunks:
+        for name in Chunk.STEPS:
+            (tiles,) = sequence.round([(chunk, name)], tiles)
 
 
 def rope_tables(rows):
@@ -719,9 +804,11 @@
         inputs.append(hidden)
         hidden, *saved = forward_layer(slots, length, hidden, gains, cos, sin, gathered)
         saves.append(saved)
-    layer_output = to_bands(
-        hidden[:seq].astype(bf16).reshape(bands, band_rows, D), images, bands, band
-    )
+
+    def send_rows(t):
+        return send_to_bands(t[:seq].astype(bf16).reshape(bands, band_rows, D), images, bands, band)
+
+    output_blocks = send_rows(hidden)
 
     back = back_rows.astype(f32) * valid[:, None]
     per_owner = master.shape[0]
@@ -731,100 +818,113 @@
         and bands == 4
         and images == 3
         and slot_count == slot_of_block.shape[0]
-        and per_owner == EARLY + sum(LATE)
+        and per_owner == sum(CHUNKS)
     )
     if by_permutes:
-        places, ranks, clean, sizes = relative_places(slot_of_block, per_owner, me)
+        places, ranks, clean = relative_places(slot_of_block, per_owner, me)
         rank = lax.dynamic_index_in_dim(ranks, me, 0, keepdims=False)
-        zones_top, zones_bottom = sizes, (sizes[0] + sizes[1],) + sizes[2:]
     else:
         places, rank = slot_of_block, jnp.arange(per_owner, dtype=jnp.int32)
-        zones_top = zones_bottom = (slot_count,)
-
-    def backward(layer, back, zones, tiles, ahead=lambda back: back, later=lambda back: back):
+
+    def same(layer, part, back, tiles, *others):
+        return (back, tiles) + others
+
+    def backward(layer, back, tiles, between=same):
         normed, q, k, v, st, mixed, mid, n2, gu, wqkv, wout, wgu, wd = saves[layer]
         slots = places[layer * PER_LAYER : (layer + 1) * PER_LAYER]
         fill = spare if layer == LAYERS - 1 else spare[-1:]
         back, gain_two, *tiles = back_ffn(
             slots, fill, back, gain_values[2 * layer + 1 : 2 * layer + 2], (mid, n2, gu, wgu, wd),
-            zones, tiles,
+            slot_count, tiles,
         )
-        back = ahead(back)
+        back, tiles = between(layer, 0, back, tiles[0])
         d_projected, *tiles = back_attention(
-            slots, length, back, cos, sin, (q, k, v, st, mixed, wout), zones, tiles
+            slots, length, back, cos, sin, (q, k, v, st, mixed, wout), slot_count, [tiles]
         )
-        back = later(back)
+        back, tiles, d_projected = between(layer, 1, back, tiles[0], d_projected)
         back, gain_one, *tiles = back_qkv(
             slots, back, gain_values[2 * layer : 2 * layer + 1], d_projected,
-            (inputs[layer], normed, wqkv), zones, tiles,
+            (inputs[layer], normed, wqkv), slot_count, [tiles],
         )
-        return back, [gain_one, gain_two], tiles
-
-    def after(value, *done):
-        return lax.optimization_barrier((value,) + done)[0]
-
-    back, gains_top, tiles = backward(1, back, zones_top, [])
+        back, tiles = between(layer, 2, back, tiles[0])
+        return back, [gain_one, gain_two], [tiles]
+
     if by_permutes:
-        early_kept, early_sent, kept, sent = tiles
-        early = {"output": layer_output}
-        early["core"] = lax.ppermute(early_sent, "dp", CORE)
-
-        def ahead(back):
-            back, early["output"] = lax.optimization_barrier((back, early["output"]))
-            early["plane"], back = plane_start(early_kept, early["core"], beside=back)
-            return back
-
-        def later(back):
-            chip, half, from_x, from_y = early["plane"]
-            back, from_x, from_y = lax.optimization_barrier((back, from_x, from_y))
-            early["plane"] = (chip, half, from_x, from_y)
-            return back
-
-        back, gains_bottom, tiles = backward(0, back, zones_bottom, [kept, sent], ahead, later)
-        layer_output = early["output"]
-        early_late, kept, sent = tiles
-        chunks, start = [], 0
-        for size in LATE:
-            chunks.append((kept[4 * start : 4 * (start + size)], sent[4 * start : 4 * (start + size)]))
-            start += size
-        from_core = [lax.ppermute(chunk[1], "dp", CORE) for chunk in chunks]
-        turned = plane_turn(*early["plane"])
-        gate = turned
-        owned = [None] * len(chunks) + [sum_bands(plane_end(*early["plane"], *turned), band)]
-        gain_total = sum_bands(jnp.concatenate(gains_bottom + gains_top, 0), band)
-        for i, (chunk, received) in enumerate(zip(chunks, from_core)):
-            going = plane_start(chunk[0], received, gate)
-            gate = plane_turn(*going)
-            owned[i] = sum_bands(plane_end(*going, *gate), band)
-            if i == 0:
-                back = after(back, going[2], going[3])
-
-        order = jnp.argsort(places)[: sizes[0] + sizes[1]]
+        sequence = Sequence()
+        chunk = [Chunk(i) for i in range(len(CHUNKS))]
+        rounds = [
+            [(0, "core")],
+            [(0, "plane")],
+            [(0, "turn"), (1, "core")],
+            [(0, "meet"), (1, "plane"), (2, "core"), (3, "core")],
+            [(0, "part"), (1, "turn"), (2, "plane")],
+        ]
+
+        def between(layer, part, back, tiles, *others):
+            nonlocal output_blocks
+            after = 3 * (LAYERS - 1 - layer) + part
+            if after == len(rounds):
+                return (back, tiles) + others
+            if after == 3:
+                *output_blocks, back = lax.optimization_barrier(output_blocks + (back,))
+            tiles, back, *others = sequence.round(
+                [(chunk[i], name) for i, name in rounds[after]], tiles, back, *others
+            )
+            return (back, tiles) + tuple(others)
+
+        back, gains_top, tiles = backward(1, back, [], between)
+        back, gains_bottom, tiles = backward(0, back, tiles, between)
+        gains = jnp.concatenate(gains_bottom + gains_top, 0).reshape(-1, BLOCK)
+        chunk[GAIN_CHUNK].extra = gains
+        for steps in (
+            [(4, "core"), (1, "meet"), (0, "last")],
+            [(2, "turn"), (3, "plane"), (5, "core")],
+            [(2, "meet"), (4, "plane")],
+            [(1, "part")],
+            [(3, "turn")],
+            [(0, "end"), (2, "part"), (1, "last")],
+            [(3, "meet"), (5, "plane")],
+            [(4, "turn")],
+            [(2, "last"), (1, "end")],
+            [(4, "meet"), (5, "turn")],
+            [(3, "part")],
+            [(5, "meet")],
+            [(4, "part")],
+            [(3, "last"), (2, "end")],
+            [(5, "part")],
+            [(4, "last"), (3, "end")],
+            [(5, "last")],
+            [(4, "end")],
+            [(5, "end")],
+        ):
+            tiles = sequence.round([(chunk[i], name) for i, name in steps], *tiles)
+            if steps[0] == (4, "core"):
+                input_blocks = send_rows(back)
+            if steps[0] == (2, "meet"):
+                input_blocks = lax.optimization_barrier(input_blocks + sequence.before)
+                sequence.before = sequence.before + input_blocks[:bands]
+        whole = jnp.concatenate([chunk[i].total[: CHUNKS[i]] for i in range(len(CHUNKS))], 0)
 
         def again(trip, total):
-            _, late, first, second = lax.optimization_barrier(
-                (trip, early_late, early_kept, early_sent)
-            )
-            mine = (order < PER_LAYER)[:, None, None]
-            first = jnp.where(mine[: sizes[0]], late[: sizes[0]], first)
-            second = jnp.where(mine[sizes[0] :], late[sizes[0] :], second)
-            going = plane_start(first, lax.ppermute(second, "dp", CORE))
-            return sum_bands(plane_end(*going, *plane_turn(*going)), band)
-
-        owned[-1] = lax.fori_loop(0, jnp.where(clean, 0, 1), again, owned[-1])
-        owned = jnp.concatenate(owned, 0)
+            _, everything = lax.optimization_barrier((trip, tiles[0]))
+            parts = [Chunk(i) for i in range(GAIN_CHUNK)]
+            reduce_all(parts, everything)
+            return jnp.concatenate([part.total for part in parts] + [total[STARTS[GAIN_CHUNK] :]], 0)
+
+        owned = lax.fori_loop(0, jnp.where(clean, 0, 1), again, whole)
+        gain_total = join_wide(chunk[GAIN_CHUNK].total[-1:], gains.shape[0]).reshape(-1, D)
     else:
-        back, gains_bottom, tiles = backward(0, back, zones_bottom, tiles)
+        back, gains_top, tiles = backward(1, back, [])
+        back, gains_bottom, tiles = backward(0, back, tiles)
         owned = lax.psum_scatter(tiles[0], "dp", scatter_dimension=0, tiled=True)
         owned = lax.psum(owned, "band")
-        gain_total = lax.psum(jnp.concatenate(gains_bottom + gains_top, 0), "band")
-    input_grad = to_bands(back[:seq].astype(bf16).reshape(bands, band_rows, D), images, bands, band)
-
+        gain_total = lax.psum(jnp.concatenate(gains_bottom + gains_top, 0), ("dp", "band"))
+        input_blocks = send_rows(back)
+
+    layer_output = at_bands(output_blocks, images, bands, band)
+    input_grad = at_bands(input_blocks[:bands], images, bands, band)
     owned_f = owned.astype(f32)
-    squares = jnp.sum(owned_f * owned_f).reshape(1)
-    summed = lax.psum(jnp.concatenate([gain_total.reshape(-1), squares]), "dp")
-    gain_total = summed[:-1].reshape(gain_values.shape)
-    owned_squares = summed[-1]
+    owned_squares = lax.psum(jnp.sum(owned_f * owned_f), "dp")
     grad_norm = jnp.sqrt(owned_squares + jnp.sum(gain_total * gain_total))
     factor = jnp.minimum(1.0, clip_limit / grad_norm)
     weight_grads, new_statistics, new_master, master_copy = optimizer(

time: 712 us -> 717 us (level)
  local copies, waits for them, and re-layouts: 41 us -> 75.8 us
  waiting for transfers between devices: 223 us -> 209 us
  blocking collectives: 22.3 us -> 12.4 us
  other arithmetic: 72.7 us -> 64.9 us
    slice x10 -> x11, local copies, waits for them, and re-layouts: 14.5 us -> 43.9 us  [the longest x6 37 us: begin(): self.kept = tiles[at:at + 4 * size]]
    ppermute x51 -> x66, waiting for transfers between devices: 120 us -> 108 us  [the longest x12 26.5 us: go_plane(): lax.ppermute(send_y, 'dp', ALONG_Y)]
    psum x1, blocking collectives: 22.3 us -> 12.4 us  [shards(): owned_squares = lax.psum(jnp.sum(owned_f * owned_f), 'dp')]
    select_n x7 -> x2, other arithmetic: 7.98 us -> 0.12 us  [the longest x1 0.11 us: to_end(): self.total = jnp.where(band == 3, to_last, total)]
    convert_element_type x12 -> x17, other arithmetic: 23.8 us -> 27.4 us  [the longest x6 14.5 us: to_plane(): self.chip(6, 8).astype(bf16)]
    ppermute x51 -> x66, starting transfers between devices: 87.9 us -> 86.3 us  [the longest x6 18.6 us: send_to_bands(): block = lax.ppermute(block, 'band', pairs)]
  transfers between devices with their start and end apart: 55 -> 70, of which waited for: 23 -> 25; matrix products, arithmetic and copies ran while one was open for 13% -> 12% of each run, Pallas kernels for 7% -> 14%
where the time goes in v5:
time: 717 us; the launch traced here: 710 us
  Pallas kernels  228 us (32%)
  waiting for transfers between devices  209 us (29%)
  starting transfers between devices  94.1 us (13%)
  local copies, waits for them, and re-layouts  75.8 us (11%)
  other arithmetic  64.9 us (9%)
  between operations  22.7 us (3%)
  blocking collectives  12.4 us (2%)
    all_gather x1, waiting for transfers between devices, shards(): gathered = lax.all_gather(master.astype(bf16), 'dp', axis=0, tiled=True)  87.7 us
    pallas_call x2, Pallas kernels, forward_layer(): pl.pallas_call(forward_kernel, out_shape=[S((rows, D), f32)] + saved, in_...  66.6 us
    pallas_call x2, Pallas kernels, back_ffn(): pl.pallas_call(functools.partial(back_ffn_kernel, len(begun)), out_shape=...  56.4 us
    pallas_call x2, Pallas kernels, back_attention(): pl.pallas_call(functools.partial(back_attention_kernel, len(begun)), out_...  44.6 us
    slice x6, local copies, waits for them, and re-layouts, begin(): self.kept = tiles[at:at + 4 * size]  37 us
    pallas_call x1, Pallas kernels, optimizer(): pl.pallas_call(optimizer_kernel, grid=(count // per,), out_shape=[S(maste...  30.7 us
    pallas_call x2, Pallas kernels, back_qkv(): pl.pallas_call(functools.partial(back_qkv_kernel, len(begun)), out_shape=...  29.3 us
    ppermute x12, waiting for transfers between devices, go_plane(): lax.ppermute(send_y, 'dp', ALONG_Y)  26.5 us
  transfers between devices with their start and end apart: 70, of which 25 were waited for; matrix products, arithmetic and copies ran while one was open for 12% of the time, Pallas kernels for 14%

profile of v5, /device:TPU:16, one launch (start us, length us, event | category | flops | bytes accessed | tf_op | source)
XLA Modules:
  0.0 709.6 jit_solution(13354132208800048994)
XLA Ops:
  7.2 5.6 convert_element_type.937
  25.6 5.3 scatter_custom_fusion
  43.3 5.2 collective-permute-done.41
  49.5 8.9 %collective-permute-done.42 = bf16[2,145,768]{2,1,0:T(8,128)(2,1)} collective-permute-done((bf16[2,145,768]{2,1,0:T(8,128)(2,1)S(1)}, bf16[2,145,768]{2,1,0:T(8,128)(2,1)}, u32[]{:S(2)}, u32[]{:S(2)}) %collective-permute-start.42) | collective-permute-done | bytes 445472 | tf_op jit(solution)/shard_map/ppermute | solution.py:553
  65.0 87.7 %all-gather.2.cloned.1.call-done.w_hbm = bf16[864,128,128]{2,1,0:T(8,128)(2,1)} async-done(((bf16[108,128,128]{2,1,0:T(8,128)(2,1)}), bf16[864,128,128]{2,1,0:T(8,128)(2,1)}) %all-gather.2.cloned.1.call-update) | async-done | bytes 28311568 | tf_op jit(solution)/shard_map/all_gather | solution.py:782
  152.7 33.1 %forward_block.2 = (f32[592,768]{1,0:T(8,128)}, bf16[592,768]{1,0:T(8,128)(2,1)}, bf16[640,768]{1,0:T(8,128)(2,1)}, bf16[640,768]{1,0:T(8,128)(2,1)}, bf16[640,7...) custom-call(s32[432]{0:T(512)} %get-tuple-element.753.slots, ...), custom_call_target="tpu_custom_call" | custom-call | flops 8380219392 | bytes 41943040 | tf_op jit(solution)/shard_map/forward_block/pallas_call | solution.py:415
  185.8 33.5 %forward_block.3 = (f32[592,768]{1,0:T(8,128)}, bf16[592,768]{1,0:T(8,128)(2,1)}, bf16[640,768]{1,0:T(8,128)(2,1)}, bf16[640,768]{1,0:T(8,128)(2,1)}, bf16[640,7...) custom-call(s32[432]{0:T(512)} %get-tuple-element.754.slots, ...), custom_call_target="tpu_custom_call" | custom-call | flops 8380219392 | bytes 41943040 | tf_op jit(solution)/shard_map/forward_block/pallas_call | solution.py:415
  219.3 28.1 %backward_feed_forward.2 = (f32[592,768]{1,0:T(8,128)}, f32[1,768]{1,0:T(1,128)}, bf16[864,128,128]{2,1,0:T(8,128)(2,1)}) custom-call(s32[432]{0:T(512)} %get-tuple-element.742.places, s32[1]{0:T(128)} %constant.302.clone.1.spare, f32[592,768]{1,0:T(8,128)} %convert_multiply_fusion.back_ref, f32[1,768]{1,0:T(1,128)} %get-tuple-element.729.g_ref, ...), custom_call_target="tpu_custom_call" | custom-call | flops 11173625856 | bytes 31457280 | tf_op jit(solution)/shard_map/backward_feed_forward/pallas_call | solution.py:437
  247.4 7.6 %fusion.47 = (bf16[88,128,128]{2,1,0:T(8,128)(2,1)}, bf16[88,128,128]{2,1,0:T(8,128)(2,1)}) fusion(bf16[864,128,128]{2,1,0:T(8,128)(2,1)} %get-tuple-element.394.rest_0_), kind=kLoop, calls=%fused_computation.253 | loop fusion | bytes 11534336 | tf_op jit(solution)/shard_map/slice | solution.py:634
  255.2 22.2 %backward_attention.2 = (bf16[592,2304]{1,0:T(8,128)(2,1)}, bf16[864,128,128]{2,1,0:T(8,128)(2,1)}) custom-call(s32[432]{0:T(512)} %get-tuple-element.742.places, s32[1]{0:T(128)} %dynamic_slice.45.length, f32[592,768]{1,0:T(8,128)} %get-tuple-element.403.back_ref, f32[592,128]{1,0:T(8,128)} %copy.70.cos_ref, ...), custom_call_target="tpu_custom_call", output_to_operand_aliasing={{1}: (11, {})} | custom-call | flops 6779830272 | bytes 31457280 | tf_op jit(solution)/shard_map/backward_attention/pallas_call | solution.py:463
  283.1 14.7 %backward_qkv.2 = (f32[592,768]{1,0:T(8,128)}, f32[1,768]{1,0:T(1,128)}, bf16[864,128,128]{2,1,0:T(8,128)(2,1)}) custom-call(s32[432]{0:T(512)} %get-tuple-element.742.places, f32[592,768]{1,0:T(8,128)} %get-tuple-element.403.back_ref, f32[1,768]{1,0:T(1,128)} %get-tuple-element.728.g_ref, ...), custom_call_target="tpu_custom_call", output_to_operand_aliasing={{2}: (7, {})} | custom-call | flops 4190109696 | bytes 20971520 | tf_op jit(solution)/shard_map/backward_qkv/pallas_call | solution.py:489
  300.7 6.6 fusion.46
  322.0 11.1 %collective-permute-done.43 = bf16[145,768]{1,0:T(8,128)(2,1)} collective-permute-done((bf16[145,768]{1,0:T(8,128)(2,1)S(1)}, bf16[145,768]{1,0:T(8,128)(2,1)}, u32[]{:S(2)}, u32[]{:S(2)}) %collective-permute-start.43) | collective-permute-done | bytes 222752 | tf_op jit(solution)/shard_map/ppermute | solution.py:564
  333.7 28.3 %backward_feed_forward.3 = (f32[592,768]{1,0:T(8,128)}, f32[1,768]{1,0:T(1,128)}, bf16[864,128,128]{2,1,0:T(8,128)(2,1)}) custom-call(s32[432]{0:T(512)} %get-tuple-element.743.places, s32[1]{0:T(128)} %constant.302.clone.1.spare, f32[592,768]{1,0:T(8,128)} %get-tuple-element.414.back_ref, ...), custom_call_target="tpu_custom_call", output_to_operand_aliasing={{2}: (9, {})} | custom-call | flops 11173625856 | bytes 31457280 | tf_op jit(solution)/shard_map/backward_feed_forward/pallas_call | solution.py:437
  362.0 7.3 %fusion.45 = (bf16[80,128,128]{2,1,0:T(8,128)(2,1)}, bf16[80,128,128]{2,1,0:T(8,128)(2,1)}) fusion(bf16[864,128,128]{2,1,0:T(8,128)(2,1)} %get-tuple-element.449.rest_0_), kind=kLoop, calls=%fused_computation.251 | loop fusion | bytes 10485760 | tf_op jit(solution)/shard_map/slice | solution.py:634
  369.4 6.5 fusion.44
  386.3 22.4 %backward_attention.3 = (bf16[592,2304]{1,0:T(8,128)(2,1)}, bf16[864,128,128]{2,1,0:T(8,128)(2,1)}) custom-call(s32[432]{0:T(512)} %get-tuple-element.743.places, s32[1]{0:T(128)} %dynamic_slice.45.length, f32[592,768]{1,0:T(8,128)} %get-tuple-element.461.back_ref, f32[592,128]{1,0:T(8,128)} %copy.70.cos_ref, ...), custom_call_target="tpu_custom_call", output_to_operand_aliasing={{1}: (11, {})} | custom-call | flops 6779830272 | bytes 31457280 | tf_op jit(solution)/shard_map/backward_attention/pallas_call | solution.py:463
  419.9 14.6 %backward_qkv.3 = (f32[592,768]{1,0:T(8,128)}, f32[1,768]{1,0:T(1,128)}, bf16[864,128,128]{2,1,0:T(8,128)(2,1)}) custom-call(s32[432]{0:T(512)} %get-tuple-element.743.places, f32[592,768]{1,0:T(8,128)} %get-tuple-element.461.back_ref, f32[1,768]{1,0:T(1,128)} %get-tuple-element.726.g_ref, ...), custom_call_target="tpu_custom_call", output_to_operand_aliasing={{2}: (7, {})} | custom-call | flops 4190109696 | bytes 20971520 | tf_op jit(solution)/shard_map/backward_qkv/pallas_call | solution.py:489
  435.9 8.5 %collective-permute-done.64 = bf16[9,128,128]{2,1,0:T(8,128)(2,1)S(1)} collective-permute-done((bf16[9,128,128]{2,1,0:T(8,128)(2,1)S(1)}, bf16[9,128,128]{2,1,0:T(8,128)(2,1)S(1)}, u32[]{:S(2)}, u32[]{:S(2)}) %collective-permute-start.64) | collective-permute-done | bytes 294944 | tf_op jit(solution)/shard_map/ppermute | solution.py:660
  448.3 5.1 fusion.43
  462.3 10.3 %collective-permute-done.60 = bf16[20,128,128]{2,1,0:T(8,128)(2,1)} collective-permute-done((bf16[20,128,128]{2,1,0:T(8,128)(2,1)}, bf16[20,128,128]{2,1,0:T(8,128)(2,1)}, u32[]{:S(2)}, u32[]{:S(2)}) %collective-permute-start.60) | collective-permute-done | bytes 655392 | tf_op jit(solution)/shard_map/ppermute | solution.py:660
  491.9 6.5 collective-permute-start.58
  513.2 6.6 collective-permute-done.59
  524.8 7.9 %collective-permute-done.78 = bf16[18,128,128]{2,1,0:T(8,128)(2,1)S(1)} collective-permute-done((bf16[18,128,128]{2,1,0:T(8,128)(2,1)S(1)}, bf16[18,128,128]{2,1,0:T(8,128)(2,1)S(1)}, u32[]{:S(2)}, u32[]{:S(2)}) %collective-permute-start.78) | collective-permute-done | bytes 589856 | tf_op jit(solution)/shard_map/ppermute | solution.py:660
  556.4 7.5 %collective-permute-done.83 = bf16[18,128,128]{2,1,0:T(8,128)(2,1)S(1)} collective-permute-done((bf16[18,128,128]{2,1,0:T(8,128)(2,1)S(1)}, bf16[18,128,128]{2,1,0:T(8,128)(2,1)S(1)}, u32[]{:S(2)}, u32[]{:S(2)}) %collective-permute-start.83) | collective-permute-done | bytes 589856 | tf_op jit(solution)/shard_map/ppermute | solution.py:660
  570.2 9.2 %collective-permute-done.89 = bf16[9,128,128]{2,1,0:T(8,128)(2,1)S(1)} collective-permute-done((bf16[9,128,128]{2,1,0:T(8,128)(2,1)S(1)}, bf16[9,128,128]{2,1,0:T(8,128)(2,1)S(1)}, u32[]{:S(2)}, u32[]{:S(2)}) %collective-permute-start.89) | collective-permute-done | bytes 294944 | tf_op jit(solution)/shard_map/ppermute | solution.py:660
  587.4 7.0 collective-permute-done.88
  599.1 5.1 collective-permute-done.97
  621.8 6.4 collective-permute-done.101
  634.7 5.6 collective-permute-done.105
  655.3 12.4 %psum.7 = f32[]{:T(128)} all-reduce(f32[]{:T(128)} %multiply_reduce_fusion), channel_id=1, replica_groups=mesh['dp'=8,'band'=4] {'dp'}, use_global_device_ids=true, to_apply=%region_11.12 | all-reduce | flops 1 | bytes 8 | tf_op jit(solution)/shard_map/psum | solution.py:927
  670.5 30.7 %optimizer.1 = (f32[108,128,128]{2,1,0:T(8,128)}, f32[108,2,128,128]{3,2,1,0:T(8,128)}, f32[108,128,128]{2,1,0:T(8,128)}, bf16[108,128,128]{2,1,0:T(8,128)(2,1)}) custom-call(f32[1]{0:T(128)} %bitcast.36.factor, s32[108]{0:T(128)} %dynamic-slice_reduce_fusion.rank, bf16[108,128,128]{2,1,0:T(8,128)(2,1)} %get-tuple-element.601.g_ref, f32[108,128,128]{2,1,0:T(8,128)} %m_ref.1, ...), custom_call_target="tpu_custom_call" | custom-call | tf_op jit(solution)/shard_map/optimizer/pallas_call | solution.py:529
  (362 shorter events, 209.5 us)
Async XLA Ops:
  7.2 145.5 %all-gather.2.cloned.1.call-start = ((), (), s32[]{:S(2)}) async-start(), calls=%async_computation | async-start | bytes 31850496 | tf_op jit(solution)/shard_map/all_gather | solution.py:782
  15.4 26.7 %collective-permute-start.40 = (bf16[2,145,768]{2,1,0:T(8,128)(2,1)}, bf16[2,145,768]{2,1,0:T(8,128)(2,1)}, u32[]{:S(2)}, u32[]{:S(2)}) collective-permute-start(bf16[2,145,768]{2,1,0:T(8,128)(2,1)} %get-tuple-element.708), channel_id=1, source_target_pairs={{0,1},{1,2},{3,0},{4,5},{5,6},{7,4},{8,9},{9,10},{11,8},{12,13},{1... | collective-permute-start | bytes 1336328 | tf_op jit(solution)/shard_map/ppermute | solution.py:553
  16.9 31.6 %collective-permute-start.41 = (bf16[2,145,768]{2,1,0:T(8,128)(2,1)S(1)}, bf16[2,145,768]{2,1,0:T(8,128)(2,1)}, u32[]{:S(2)}, u32[]{:S(2)}) collective-permute-start(bf16[2,145,768]{2,1,0:T(8,128)(2,1)S(1)} %get-tuple-element.707), channel_id=1, source_target_pairs={{0,2},{2,0},{3,1},{4,6},{6,4},{7,5},{8,10},{10,8},{11,9},{12,14},{... | collective-permute-start | bytes 1336328 | tf_op jit(solution)/shard_map/ppermute | solution.py:553
  21.3 37.1 %collective-permute-start.42 = (bf16[2,145,768]{2,1,0:T(8,128)(2,1)S(1)}, bf16[2,145,768]{2,1,0:T(8,128)(2,1)}, u32[]{:S(2)}, u32[]{:S(2)}) collective-permute-start(bf16[2,145,768]{2,1,0:T(8,128)(2,1)S(1)} %get-tuple-element.706), channel_id=1, source_target_pairs={{1,0},{2,1},{3,2},{5,4},{6,5},{7,6},{9,8},{10,9},{11,10},{13,12},{... | collective-permute-start | bytes 1336328 | tf_op jit(solution)/shard_map/ppermute | solution.py:553
  255.0 22.5 %collective-permute-start.46 = (bf16[88,128,128]{2,1,0:T(8,128)(2,1)}, bf16[88,128,128]{2,1,0:T(8,128)(2,1)}, u32[]{:S(2)}, u32[]{:S(2)}) collective-permute-start(bf16[88,128,128]{2,1,0:T(8,128)(2,1)} %get-tuple-element.386), channel_id=1, source_target_pairs={{0,4},{4,0},{8,12},{12,8},{16,20},{20,16},{24,28},{28,24},{1,5},{5... | collective-permute-start | bytes 8650760 | tf_op jit(solution)/shard_map/ppermute | solution.py:652
  281.0 18.5 %collective-permute-start.47 = (bf16[22,128,128]{2,1,0:T(8,128)(2,1)}, bf16[22,128,128]{2,1,0:T(8,128)(2,1)S(1)}, u32[]{:S(2)}, u32[]{:S(2)}) collective-permute-start(bf16[22,128,128]{2,1,0:T(8,128)(2,1)} %get-tuple-element.401), channel_id=1, source_target_pairs={{0,8},{4,12},{8,0},{12,4},{16,24},{20,28},{24,16},{28,20},{1,9},{5... | collective-permute-start | bytes 2162696 | tf_op jit(solution)/shard_map/ppermute | solution.py:660
  282.5 18.2 %collective-permute-start.48 = (bf16[22,128,128]{2,1,0:T(8,128)(2,1)}, bf16[22,128,128]{2,1,0:T(8,128)(2,1)S(1)}, u32[]{:S(2)}, u32[]{:S(2)}) collective-permute-start(bf16[22,128,128]{2,1,0:T(8,128)(2,1)} %get-tuple-element.402), channel_id=1, source_target_pairs={{0,16},{4,20},{8,24},{12,28},{16,0},{20,4},{24,8},{28,12},{1,17},{... | collective-permute-start | bytes 2162696 | tf_op jit(solution)/shard_map/ppermute | solution.py:660
  309.9 52.1 %collective-permute-start.51 = (bf16[72,128,128]{2,1,0:T(8,128)(2,1)}, bf16[72,128,128]{2,1,0:T(8,128)(2,1)}, u32[]{:S(2)}, u32[]{:S(2)}) collective-permute-start(bf16[72,128,128]{2,1,0:T(8,128)(2,1)} %get-tuple-element.428), channel_id=1, source_target_pairs={{0,4},{4,0},{8,12},{12,8},{16,20},{20,16},{24,28},{28,24},{1,5},{5... | collective-permute-start | bytes 7077896 | tf_op jit(solution)/shard_map/ppermute | solution.py:652
  312.6 20.5 %collective-permute-start.43 = (bf16[145,768]{1,0:T(8,128)(2,1)S(1)}, bf16[145,768]{1,0:T(8,128)(2,1)}, u32[]{:S(2)}, u32[]{:S(2)}) collective-permute-start(bf16[145,768]{1,0:T(8,128)(2,1)S(1)} %get-tuple-element.718), channel_id=1, source_target_pairs={{0,1},{1,2},{2,3},{4,5},{5,6},{6,7},{8,9},{9,10},{10,11},{12,13},{... | collective-permute-start | bytes 668168 | tf_op jit(solution)/shard_map/ppermute | solution.py:564
  316.0 45.9 %collective-permute-start.44 = (bf16[145,768]{1,0:T(8,128)(2,1)}, bf16[145,768]{1,0:T(8,128)(2,1)}, u32[]{:S(2)}, u32[]{:S(2)}) collective-permute-start(bf16[145,768]{1,0:T(8,128)(2,1)} %get-tuple-element.717), channel_id=1, source_target_pairs={{0,2},{1,3},{2,0},{4,6},{5,7},{6,4},{8,10},{9,11},{10,8},{12,14},{... | collective-permute-start | bytes 668168 | tf_op jit(solution)/shard_map/ppermute | solution.py:564
  319.1 42.8 %collective-permute-start.45 = (bf16[145,768]{1,0:T(8,128)(2,1)}, bf16[145,768]{1,0:T(8,128)(2,1)S(1)}, u32[]{:S(2)}, u32[]{:S(2)}) collective-permute-start(bf16[145,768]{1,0:T(8,128)(2,1)} %get-tuple-element.716), channel_id=1, source_target_pairs={{0,3},{1,0},{2,1},{4,7},{5,4},{6,5},{8,11},{9,8},{10,9},{12,15},{1... | collective-permute-start | bytes 668168 | tf_op jit(solution)/shard_map/ppermute | solution.py:564
  321.4 40.6 %collective-permute-start.49 = (bf16[11,128,128]{2,1,0:T(8,128)(2,1)}, bf16[11,128,128]{2,1,0:T(8,128)(2,1)S(1)}, u32[]{:S(2)}, u32[]{:S(2)}) collective-permute-start(bf16[11,128,128]{2,1,0:T(8,128)(2,1)} %get-tuple-element.426), channel_id=1, source_target_pairs={{0,8},{4,12},{8,0},{12,4},{16,24},{20,28},{24,16},{28,20},{1,9},{5... | collective-permute-start | bytes 1081352 | tf_op jit(solution)/shard_map/ppermute | solution.py:660
  333.1 28.9 %collective-permute-start.50 = (bf16[11,128,128]{2,1,0:T(8,128)(2,1)}, bf16[11,128,128]{2,1,0:T(8,128)(2,1)S(1)}, u32[]{:S(2)}, u32[]{:S(2)}) collective-permute-start(bf16[11,128,128]{2,1,0:T(8,128)(2,1)} %get-tuple-element.427), channel_id=1, source_target_pairs={{0,16},{4,20},{8,24},{12,28},{16,0},{20,4},{24,8},{28,12},{1,17},{... | collective-permute-start | bytes 1081352 | tf_op jit(solution)/shard_map/ppermute | solution.py:660
  380.5 28.4 %collective-permute-start.56 = (bf16[80,128,128]{2,1,0:T(8,128)(2,1)}, bf16[80,128,128]{2,1,0:T(8,128)(2,1)}, u32[]{:S(2)}, u32[]{:S(2)}) collective-permute-start(bf16[80,128,128]{2,1,0:T(8,128)(2,1)} %get-tuple-element.440), channel_id=1, source_target_pairs={{0,4},{4,0},{8,12},{12,8},{16,20},{20,16},{24,28},{28,24},{1,5},{5... | collective-permute-start | bytes 7864328 | tf_op jit(solution)/shard_map/ppermute | solution.py:652
  380.6 28.3 %collective-permute-start.52 = (bf16[22,128,128]{2,1,0:T(8,128)(2,1)S(1)}, bf16[22,128,128]{2,1,0:T(8,128)(2,1)}, u32[]{:S(2)}, u32[]{:S(2)}) collective-permute-start(bf16[22,128,128]{2,1,0:T(8,128)(2,1)S(1)} %pad_maximum_fusion.5), channel_id=1, source_target_pairs={{0,1},{4,5},{8,9},{12,13},{16,17},{20,21},{24,25},{28,29}} | collective-permute-start | bytes 2162696 | tf_op jit(solution)/shard_map/ppermute | solution.py:679
  382.1 26.7 %collective-permute-start.53 = (bf16[22,128,128]{2,1,0:T(8,128)(2,1)S(1)}, bf16[22,128,128]{2,1,0:T(8,128)(2,1)}, u32[]{:S(2)}, u32[]{:S(2)}) collective-permute-start(bf16[22,128,128]{2,1,0:T(8,128)(2,1)S(1)} %pad_maximum_fusion.5), channel_id=1, source_target_pairs={{2,1},{6,5},{10,9},{14,13},{18,17},{22,21},{26,25},{30,29}} | collective-permute-start | bytes 2162696 | tf_op jit(solution)/shard_map/ppermute | solution.py:679
  384.3 24.5 %collective-permute-start.54 = (bf16[18,128,128]{2,1,0:T(8,128)(2,1)}, bf16[18,128,128]{2,1,0:T(8,128)(2,1)}, u32[]{:S(2)}, u32[]{:S(2)}) collective-permute-start(bf16[18,128,128]{2,1,0:T(8,128)(2,1)} %get-tuple-element.438), channel_id=1, source_target_pairs={{0,8},{4,12},{8,0},{12,4},{16,24},{20,28},{24,16},{28,20},{1,9},{5... | collective-permute-start | bytes 1769480 | tf_op jit(solution)/shard_map/ppermute | solution.py:660
  384.8 24.0 %collective-permute-start.55 = (bf16[18,128,128]{2,1,0:T(8,128)(2,1)}, bf16[18,128,128]{2,1,0:T(8,128)(2,1)}, u32[]{:S(2)}, u32[]{:S(2)}) collective-permute-start(bf16[18,128,128]{2,1,0:T(8,128)(2,1)} %get-tuple-element.439), channel_id=1, source_target_pairs={{0,16},{4,20},{8,24},{12,28},{16,0},{20,4},{24,8},{28,12},{1,17},{... | collective-permute-start | bytes 1769480 | tf_op jit(solution)/shard_map/ppermute | solution.py:660
  408.7 53.6 %collective-permute-start.62 = (bf16[72,128,128]{2,1,0:T(8,128)(2,1)}, bf16[72,128,128]{2,1,0:T(8,128)(2,1)}, u32[]{:S(2)}, u32[]{:S(2)}) collective-permute-start(bf16[72,128,128]{2,1,0:T(8,128)(2,1)} %get-tuple-element.441), channel_id=1, source_target_pairs={{0,4},{4,0},{8,12},{12,8},{16,20},{20,16},{24,28},{28,24},{1,5},{5... | collective-permute-start | bytes 7077896 | tf_op jit(solution)/shard_map/ppermute | solution.py:652
  416.3 28.1 %collective-permute-start.65 = (bf16[22,128,128]{2,1,0:T(8,128)(2,1)S(1)}, bf16[22,128,128]{2,1,0:T(8,128)(2,1)S(1)}, u32[]{:S(2)}, u32[]{:S(2)}) collective-permute-start(bf16[22,128,128]{2,1,0:T(8,128)(2,1)S(1)} %add_convert_fusion.28), channel_id=1, source_target_pairs={{1,0},{5,4},{9,8},{13,12},{17,16},{21,20},{25,24},{29,28}} | collective-permute-start | bytes 2162696 | tf_op jit(solution)/shard_map/ppermute | solution.py:691
  417.1 27.4 %collective-permute-start.66 = (bf16[22,128,128]{2,1,0:T(8,128)(2,1)S(1)}, bf16[22,128,128]{2,1,0:T(8,128)(2,1)}, u32[]{:S(2)}, u32[]{:S(2)}) collective-permute-start(bf16[22,128,128]{2,1,0:T(8,128)(2,1)S(1)} %add_convert_fusion.28), channel_id=1, source_target_pairs={{1,2},{5,6},{9,10},{13,14},{17,18},{21,22},{25,26},{29,30}} | collective-permute-start | bytes 2162696 | tf_op jit(solution)/shard_map/ppermute | solution.py:691
  455.2 45.6 %collective-permute-start.69 = (bf16[73,128,128]{2,1,0:T(8,128)(2,1)}, bf16[73,128,128]{2,1,0:T(8,128)(2,1)}, u32[]{:S(2)}, u32[]{:S(2)}) collective-permute-start(bf16[73,128,128]{2,1,0:T(8,128)(2,1)} %pad_maximum_fusion.4), channel_id=1, source_target_pairs={{0,4},{4,0},{8,12},{12,8},{16,20},{20,16},{24,28},{28,24},{1,5},{5... | collective-permute-start | bytes 7176200 | tf_op jit(solution)/shard_map/ppermute | solution.py:652
  498.5 22.8 %collective-permute-start.73 = (bf16[18,128,128]{2,1,0:T(8,128)(2,1)}, bf16[18,128,128]{2,1,0:T(8,128)(2,1)S(1)}, u32[]{:S(2)}, u32[]{:S(2)}) collective-permute-start(bf16[18,128,128]{2,1,0:T(8,128)(2,1)} %pad_maximum_fusion.10), channel_id=1, source_target_pairs={{0,1},{4,5},{8,9},{12,13},{16,17},{20,21},{24,25},{28,29}} | collective-permute-start | bytes 1769480 | tf_op jit(solution)/shard_map/ppermute | solution.py:679
  499.2 22.1 %collective-permute-start.74 = (bf16[18,128,128]{2,1,0:T(8,128)(2,1)}, bf16[18,128,128]{2,1,0:T(8,128)(2,1)S(1)}, u32[]{:S(2)}, u32[]{:S(2)}) collective-permute-start(bf16[18,128,128]{2,1,0:T(8,128)(2,1)} %pad_maximum_fusion.10), channel_id=1, source_target_pairs={{2,1},{6,5},{10,9},{14,13},{18,17},{22,21},{26,25},{30,29}} | collective-permute-start | bytes 1769480 | tf_op jit(solution)/shard_map/ppermute | solution.py:679
  508.2 25.2 %collective-permute-start.70 = (bf16[22,128,128]{2,1,0:T(8,128)(2,1)}, bf16[22,128,128]{2,1,0:T(8,128)(2,1)S(1)}, u32[]{:S(2)}, u32[]{:S(2)}) collective-permute-start(bf16[22,128,128]{2,1,0:T(8,128)(2,1)} %collective-permute-done.66), channel_id=1, source_target_pairs={{2,3},{6,7},{10,11},{14,15},{18,19},{22,23},{26,27},{30,31}} | collective-permute-start | bytes 2162696 | tf_op jit(solution)/shard_map/ppermute | solution.py:698
  521.3 29.9 %collective-permute-start.86 = (bf16[48,128,128]{2,1,0:T(8,128)(2,1)S(1)}, bf16[48,128,128]{2,1,0:T(8,128)(2,1)S(1)}, u32[]{:S(2)}, u32[]{:S(2)}) collective-permute-start(bf16[48,128,128]{2,1,0:T(8,128)(2,1)S(1)} %copy-done.25), channel_id=1, source_target_pairs={{0,4},{4,0},{8,12},{12,8},{16,20},{20,16},{24,28},{28,24},{1,5},{5... | collective-permute-start | bytes 4718600 | tf_op jit(solution)/shard_map/ppermute | solution.py:652
  521.7 19.0 %collective-permute-start.75 = (bf16[18,128,128]{2,1,0:T(8,128)(2,1)S(1)}, bf16[18,128,128]{2,1,0:T(8,128)(2,1)S(1)}, u32[]{:S(2)}, u32[]{:S(2)}) collective-permute-start(bf16[18,128,128]{2,1,0:T(8,128)(2,1)S(1)} %add_convert_fusion.36), channel_id=1, source_target_pairs={{1,0},{5,4},{9,8},{13,12},{17,16},{21,20},{25,24},{29,28}} | collective-permute-start | bytes 1769480 | tf_op jit(solution)/shard_map/ppermute | solution.py:691
  522.5 20.1 %collective-permute-start.76 = (bf16[18,128,128]{2,1,0:T(8,128)(2,1)S(1)}, bf16[18,128,128]{2,1,0:T(8,128)(2,1)S(1)}, u32[]{:S(2)}, u32[]{:S(2)}) collective-permute-start(bf16[18,128,128]{2,1,0:T(8,128)(2,1)S(1)} %add_convert_fusion.36), channel_id=1, source_target_pairs={{1,2},{5,6},{9,10},{13,14},{17,18},{21,22},{25,26},{29,30}} | collective-permute-start | bytes 1769480 | tf_op jit(solution)/shard_map/ppermute | solution.py:691
  543.3 21.2 %collective-permute-start.82 = (bf16[19,128,128]{2,1,0:T(8,128)(2,1)S(1)}, bf16[19,128,128]{2,1,0:T(8,128)(2,1)S(1)}, u32[]{:S(2)}, u32[]{:S(2)}) collective-permute-start(bf16[19,128,128]{2,1,0:T(8,128)(2,1)S(1)} %pad_maximum_fusion.7), channel_id=1, source_target_pairs={{0,8},{4,12},{8,0},{12,4},{16,24},{20,28},{24,16},{28,20},{1,9},{5... | collective-permute-start | bytes 1867784 | tf_op jit(solution)/shard_map/ppermute | solution.py:660
  563.9 17.8 %collective-permute-start.91 = (bf16[12,128,128]{2,1,0:T(8,128)(2,1)S(1)}, bf16[12,128,128]{2,1,0:T(8,128)(2,1)S(1)}, u32[]{:S(2)}, u32[]{:S(2)}) collective-permute-start(bf16[12,128,128]{2,1,0:T(8,128)(2,1)S(1)} %get-tuple-element.535), channel_id=1, source_target_pairs={{0,8},{4,12},{8,0},{12,4},{16,24},{20,28},{24,16},{28,20},{1,9},{5... | collective-permute-start | bytes 1179656 | tf_op jit(solution)/shard_map/ppermute | solution.py:660
  584.2 20.0 %collective-permute-start.97 = (bf16[19,128,128]{2,1,0:T(8,128)(2,1)S(1)}, bf16[19,128,128]{2,1,0:T(8,128)(2,1)S(1)}, u32[]{:S(2)}, u32[]{:S(2)}) collective-permute-start(bf16[19,128,128]{2,1,0:T(8,128)(2,1)S(1)} %pad_maximum_fusion.8), channel_id=1, source_target_pairs={{2,1},{6,5},{10,9},{14,13},{18,17},{22,21},{26,25},{30,29}} | collective-permute-start | bytes 1867784 | tf_op jit(solution)/shard_map/ppermute | solution.py:679
  609.9 18.3 %collective-permute-start.101 = (bf16[19,128,128]{2,1,0:T(8,128)(2,1)S(1)}, bf16[19,128,128]{2,1,0:T(8,128)(2,1)S(1)}, u32[]{:S(2)}, u32[]{:S(2)}) collective-permute-start(bf16[19,128,128]{2,1,0:T(8,128)(2,1)S(1)} %pad_maximum_fusion.9), channel_id=1, source_target_pairs={{1,2},{5,6},{9,10},{13,14},{17,18},{21,22},{25,26},{29,30}} | collective-permute-start | bytes 1867784 | tf_op jit(solution)/shard_map/ppermute | solution.py:691
  (88 other events, 1036.1 us)
Sparse Core Ops, SparseCore 0:
  13.0 139.6 all-gather.1

commit v6 on v3

--- a/solution.py
+++ b/solution.py
@@ -209,7 +209,7 @@
         save.wait()
 
 
-def put_tiles(places, m, grad, zones, outs, sem, i0, i1, j0, count_j):
+def put_tiles(places, zones, m, grad, outs, sem, i0, i1, j0, count_j):
     @pl.loop(i0, i1)
     def _(i):
         for jj in range(count_j):
@@ -219,26 +219,22 @@
                 pl.ds(pl.multiple_of(i * BLOCK, BLOCK), BLOCK),
                 pl.ds(pl.multiple_of(j * BLOCK, BLOCK), BLOCK),
             ]
-            start = 0
-            for size, out in zip(zones, outs):
-                if len(zones) == 1:
-                    pltpu.make_async_copy(tile, out.at[place], sem).start()
-                else:
-
-                    @pl.when((place >= start) & (place < start + size))
-                    def _(tile=tile, out=out, place=place, start=start):
-                        pltpu.make_async_copy(tile, out.at[place - start], sem).start()
-
-                start += size
+            if len(outs) == 1:
+                pltpu.make_async_copy(tile, outs[0].at[place], sem).start()
+                continue
+            for out, (low, high, _) in zip(outs, zones):
+
+                @pl.when((place >= low) & (place < high))
+                def _(tile=tile, out=out, place=place, low=low):
+                    pltpu.make_async_copy(tile, out.at[place - low], sem).start()
 
 
 def back_ffn_kernel(
-    zones, begun, places, spare, back_ref, g_ref, mid_i, n2_i, gu_i, wgu_i, wd_i, *rest
+    begun, zones, places, spare, back_ref, g_ref, mid_i, n2_i, gu_i, wgu_i, wd_i, *rest
 ):
-    rest = rest[begun:]
-    mid_ref_out, gain_ref = rest[:2]
-    outs = rest[2 : 2 + len(zones)]
-    mid_ref, n2_ref, gu_ref, wgu, wd, ggu, gd, big, zero, sem_in, sem_out, sem_zero = rest[2 + len(zones) :]
+    mid_ref_out, gain_ref, *rest = rest[begun:]
+    tiles_out, rest = rest[: len(zones)], rest[len(zones) :]
+    mid_ref, n2_ref, gu_ref, wgu, wd, ggu, gd, big, zero, sem_in, sem_out, sem_zero = rest
     loads = copies([(wd_i, wd), (gu_i, gu_ref), (n2_i, n2_ref), (wgu_i, wgu), (mid_i, mid_ref)], sem_in)
     for load in loads:
         load.start()
@@ -248,12 +244,12 @@
 
         @pl.loop(0, spares)
         def _(i):
-            pltpu.make_async_copy(zero, outs[0].at[spare[i]], sem_zero).start()
+            pltpu.make_async_copy(zero, tiles_out[0].at[spare[i]], sem_zero).start()
 
     big[...] = jnp.zeros(big.shape, f32)
     for load in loads[:4]:
         load.wait()
-    put = functools.partial(put_tiles, places)
+    put = functools.partial(put_tiles, places, zones)
 
     @pl.loop(0, FF // FF_STEP)
     def _(t):
@@ -273,9 +269,9 @@
         ggu[:, here] = tn(n2_ref[...], d_gate).astype(bf16)
         ggu[:, there] = tn(n2_ref[...], d_up).astype(bf16)
         per = FF_STEP // BLOCK
-        put(3, gd, zones, outs, sem_out.at[1], t * per, (t + 1) * per, 0, D // BLOCK)
-        put(2, ggu, zones, outs, sem_out.at[0], 0, D // BLOCK, t * per, per)
-        put(2, ggu, zones, outs, sem_out.at[0], 0, D // BLOCK, FF // BLOCK + t * per, per)
+        put(3, gd, tiles_out, sem_out.at[1], t * per, (t + 1) * per, 0, D // BLOCK)
+        put(2, ggu, tiles_out, sem_out.at[0], 0, D // BLOCK, t * per, per)
+        put(2, ggu, tiles_out, sem_out.at[0], 0, D // BLOCK, FF // BLOCK + t * per, per)
         big[...] += nt(d_gate, wgu[:, here]) + nt(d_up, wgu[:, there])
 
     loads[4].wait()
@@ -288,20 +284,19 @@
 
         @pl.loop(0, spares)
         def _(i):
-            pltpu.make_async_copy(zero, outs[0].at[spare[i]], sem_zero).wait()
+            pltpu.make_async_copy(zero, tiles_out[0].at[spare[i]], sem_zero).wait()
 
 
 def back_attention_kernel(
-    zones, begun, places, length, back_ref, cos_ref, sin_ref,
+    begun, zones, places, length, back_ref, cos_ref, sin_ref,
     q_i, k_i, v_i, st_i, mixed_i, wout_i, *rest
 ):
-    rest = rest[begun:]
-    dproj = rest[0]
-    outs = rest[1 : 1 + len(zones)]
+    dproj, *rest = rest[begun:]
+    tiles_out, rest = rest[: len(zones)], rest[len(zones) :]
     (
         q_ref, k_ref, v_ref, st_ref, mixed_ref, wout,
         gout, bias, turned, sums, mixed_back, sem_in, sem_out,
-    ) = rest[1 + len(zones) :]
+    ) = rest
     rows = back_ref.shape[0]
     key_rows = q_ref.shape[0]
     loads = copies(
@@ -313,7 +308,7 @@
     )
     for load in loads:
         load.start()
-    put = functools.partial(put_tiles, places)
+    put = functools.partial(put_tiles, places, zones)
     key = lax.broadcasted_iota(jnp.int32, bias.shape, 0)
     query = lax.broadcasted_iota(jnp.int32, bias.shape, 1)
     bias[...] = jnp.where((key <= query) & (key < length[0]), 0.0, masked_score)
@@ -323,7 +318,7 @@
     mixed_back[rows:, :] = jnp.zeros((key_rows - rows, D), bf16)
     loads[1].wait()
     gout[...] = tn(mixed_ref[...], back_attn).astype(bf16)
-    put(1, gout, zones, outs, sem_out, 0, D // BLOCK, 0, D // BLOCK)
+    put(1, gout, tiles_out, sem_out, 0, D // BLOCK, 0, D // BLOCK)
     for load in loads[2:]:
         load.wait()
     levels = st_ref[...].T
@@ -369,11 +364,10 @@
     pltpu.make_async_copy(gout, gout, sem_out).wait()
 
 
-def back_qkv_kernel(zones, begun, places, back_ref, g_ref, dproj, x_i, normed_i, wqkv_i, *rest):
-    rest = rest[begun:]
-    dx_ref, gain_ref = rest[:2]
-    outs = rest[2 : 2 + len(zones)]
-    x_ref, normed_ref, wqkv, gqkv, big, sem_in, sem_out = rest[2 + len(zones) :]
+def back_qkv_kernel(begun, zones, places, back_ref, g_ref, dproj, x_i, normed_i, wqkv_i, *rest):
+    dx_ref, gain_ref, *rest = rest[begun:]
+    tiles_out, rest = rest[: len(zones)], rest[len(zones) :]
+    x_ref, normed_ref, wqkv, gqkv, big, sem_in, sem_out = rest
     loads = copies([(normed_i, normed_ref), (wqkv_i, wqkv), (x_i, x_ref)], sem_in)
     for load in loads:
         load.start()
@@ -385,9 +379,7 @@
     def _(part):
         cols = pl.ds(pl.multiple_of(part * D, D), D)
         gqkv[:, cols] = tn(normed_ref[...], dproj[:, cols]).astype(bf16)
-        put_tiles(
-            places, 0, gqkv, zones, outs, sem_out, 0, D // BLOCK, part * (D // BLOCK), D // BLOCK
-        )
+        put_tiles(places, zones, 0, gqkv, tiles_out, sem_out, 0, D // BLOCK, part * (D // BLOCK), D // BLOCK)
         big[...] += nt(dproj[:, cols], wqkv[:, cols])
 
     loads[2].wait()
@@ -446,22 +438,26 @@
     )(slots, length, x, gains, cos, sin, gathered)
 
 
-def tile_outputs(zones):
-    return [jax.ShapeDtypeStruct((size, BLOCK, BLOCK), bf16) for size in zones]
+def tile_arrays(zones):
+    return [jax.ShapeDtypeStruct((size, BLOCK, BLOCK), bf16) for _, _, size in zones]
+
+
+def in_place(args, begun, zones, first):
+    late = first + len(zones) - len(begun)
+    return {len(args) + i: late + i for i in range(len(begun))}
 
 
 def back_ffn(places, spare, back, gain, saved, zones, begun):
     rows = back.shape[0]
     S = jax.ShapeDtypeStruct
     args = (places, spare, back, gain) + tuple(saved)
-    first = 2 + len(zones) - len(begun)
     wgu, wd = saved[3], saved[4]
     return pl.pallas_call(
-        functools.partial(back_ffn_kernel, zones, len(begun)),
-        out_shape=[S((rows, D), f32), S((1, D), f32)] + tile_outputs(zones),
+        functools.partial(back_ffn_kernel, len(begun), zones),
+        out_shape=[S((rows, D), f32), S((1, D), f32)] + tile_arrays(zones),
         in_specs=[SMEM] * 2 + [VMEM] * 2 + [HBM] * (5 + len(begun)),
         out_specs=[VMEM, VMEM] + [HBM] * len(zones),
-        input_output_aliases={len(args) + i: first + i for i in range(len(begun))},
+        input_output_aliases=in_place(args, begun, zones, 2),
         scratch_shapes=[like(s) for s in saved]
         + [like(wgu), like(wd)]
         + [
@@ -482,13 +478,12 @@
     key_rows = round_up(rows, BLOCK)
     S = jax.ShapeDtypeStruct
     args = (places, length, back, cos, sin) + tuple(saved)
-    first = 1 + len(zones) - len(begun)
     return pl.pallas_call(
-        functools.partial(back_attention_kernel, zones, len(begun)),
-        out_shape=[S((rows, 3 * D), bf16)] + tile_outputs(zones),
+        functools.partial(back_attention_kernel, len(begun), zones),
+        out_shape=[S((rows, 3 * D), bf16)] + tile_arrays(zones),
         in_specs=[SMEM] * 2 + [VMEM] * 3 + [HBM] * (6 + len(begun)),
         out_specs=[VMEM] + [HBM] * len(zones),
-        input_output_aliases={len(args) + i: first + i for i in range(len(begun))},
+        input_output_aliases=in_place(args, begun, zones, 1),
         scratch_shapes=[like(s) for s in saved]
         + [
             like(saved[5]),
@@ -509,13 +504,12 @@
     rows = back.shape[0]
     S = jax.ShapeDtypeStruct
     args = (places, back, gain, d_projected) + tuple(saved)
-    first = 2 + len(zones) - len(begun)
     return pl.pallas_call(
-        functools.partial(back_qkv_kernel, zones, len(begun)),
-        out_shape=[S((rows, D), f32), S((1, D), f32)] + tile_outputs(zones),
+        functools.partial(back_qkv_kernel, len(begun), zones),
+        out_shape=[S((rows, D), f32), S((1, D), f32)] + tile_arrays(zones),
         in_specs=[SMEM] + [VMEM] * 3 + [HBM] * (3 + len(begun)),
         out_specs=[VMEM, VMEM] + [HBM] * len(zones),
-        input_output_aliases={len(args) + i: first + i for i in range(len(begun))},
+        input_output_aliases=in_place(args, begun, zones, 2),
         scratch_shapes=[like(s) for s in saved]
         + [
             like(saved[2]),
@@ -579,46 +573,60 @@
     return whole
 
 
-def to_bands(whole, images, bands, band):
-    local = jnp.zeros(whole.shape, whole.dtype)
+def send_to_bands(whole, images, bands, band):
+    blocks = []
     for shift in range(bands):
         block = lax.dynamic_index_in_dim(whole, (band + shift) % bands, 0, keepdims=False)
         if shift > 0:
             pairs = [(b, (b + shift) % bands) for b in range(images)]
             block = lax.ppermute(block, "band", pairs)
+        blocks.append(block)
+    return tuple(blocks)
+
+
+def at_bands(blocks, images, bands, band):
+    local = jnp.zeros((bands,) + blocks[0].shape, blocks[0].dtype)
+    for shift, block in enumerate(blocks):
         local = lax.dynamic_update_index_in_dim(local, block, (band - shift) % bands, 0)
     return local[:images]
 
 
-EARLY = 38
-LATE = (30, 24, 16)
-
-
-def relative_places(slot_of_block, per_owner, me):
+EARLY = (22, 18, 38)
+LATE = (18, 12)
+FFN_FIRST = OFFSETS[2]
+LEAST = (PER_LAYER + FFN_FIRST, PER_LAYER, FFN_FIRST)
+
+
+def chunk_places(slot_of_block, per_owner, me):
     blocks = slot_of_block.shape[0]
     block_of_slot = jnp.zeros((blocks,), jnp.int32).at[slot_of_block].set(
         jnp.arange(blocks, dtype=jnp.int32)
     )
     by_owner = block_of_slot.reshape(-1, per_owner)
-    rank = jnp.sum(by_owner[:, None, :] < by_owner[:, :, None], -1, dtype=jnp.int32)
-    early = per_owner - EARLY
-    clean = jnp.all(jnp.where(rank >= early, by_owner >= PER_LAYER, True))
-    relative = (jnp.arange(by_owner.shape[0], dtype=jnp.int32) ^ me)[:, None]
+    rank = jnp.sum(by_owner[:, None, :] > by_owner[:, :, None], -1, dtype=jnp.int32)
+    owner = jnp.arange(by_owner.shape[0], dtype=jnp.int32)
+    relative = (owner ^ me)[:, None]
+    owner = owner[:, None]
     core, x, y = relative % 2, relative // 2 % 2, relative // 4
     place = jnp.zeros_like(rank)
-    zone_sizes = (4 * EARLY, 4 * EARLY, 4 * early, 4 * early)
-    chunks = [(early, EARLY, 0, 0)]
+    clean = jnp.bool_(True)
     start = 0
+    for size, least in zip(EARLY, LEAST):
+        at = rank - start
+        here = (at >= 0) & (at < size)
+        place = jnp.where(here, 8 * start + owner * size + at, place)
+        clean = clean & jnp.all(jnp.where(here, by_owner >= least, True))
+        start += size
+    base = 8 * start + core * 4 * sum(LATE)
     for size in LATE:
-        chunks.append((start, size, 2, 4 * start))
-        start += size
-    for start, size, zone, inside in chunks:
         half = size // 2
         at = rank - start
+        here = (at >= 0) & (at < size)
         spot = jnp.where(at < half, (x * 2 + y) * half + at, 4 * half + (y * 2 + x) * half + at - half)
-        base = jnp.where(core == 0, sum(zone_sizes[:zone]), sum(zone_sizes[: zone + 1]))
-        place = jnp.where((at >= 0) & (at < size), base + inside + spot, place)
-    return place.reshape(-1)[slot_of_block], rank, clean, zone_sizes
+        place = jnp.where(here, base + spot, place)
+        start += size
+        base += 4 * size
+    return place.reshape(-1)[slot_of_block], rank, clean
 
 
 CORE = [(i, i ^ 1) for i in range(8)]
@@ -630,44 +638,99 @@
     return t[lo:hi].astype(f32)
 
 
-def plane_start(kept, received, gate=None, beside=None):
-    half = kept.shape[0] // 8
-
-    def chip(lo, hi):
-        return wide(kept, lo * half, hi * half) + wide(received, lo * half, hi * half)
-
-    send_x, send_y = chip(2, 4).astype(bf16), chip(6, 8).astype(bf16)
-    if gate is not None:
-        send_x, send_y, _ = lax.optimization_barrier((send_x, send_y, gate))
-    if beside is not None:
-        send_x, send_y, beside = lax.optimization_barrier((send_x, send_y, beside))
-    going = (chip, half, lax.ppermute(send_x, "dp", ALONG_X), lax.ppermute(send_y, "dp", ALONG_Y))
-    return going if beside is None else (going, beside)
-
-
-def plane_turn(chip, half, from_x, from_y):
-    send_y = (chip(1, 2) + wide(from_x, half, 2 * half)).astype(bf16)
-    send_x = (chip(5, 6) + wide(from_y, half, 2 * half)).astype(bf16)
-    return lax.ppermute(send_x, "dp", ALONG_X), lax.ppermute(send_y, "dp", ALONG_Y)
-
-
-def plane_end(chip, half, from_x, from_y, later_x, later_y):
-    one = chip(0, 1) + wide(from_x, 0, half) + later_y.astype(f32)
-    two = chip(4, 5) + wide(from_y, 0, half) + later_x.astype(f32)
-    return jnp.concatenate([one, two], 0).astype(bf16)
-
-
-def sum_bands(plane, band):
-    kind = plane.dtype
-    up = lax.ppermute(plane, "band", [(0, 1)])
-    down = lax.ppermute(plane, "band", [(2, 1)])
-    total = (plane.astype(f32) + up.astype(f32) + down.astype(f32)).astype(kind)
-    to_first = lax.ppermute(total, "band", [(1, 0)])
-    to_third = lax.ppermute(total, "band", [(1, 2)])
-    to_last = lax.ppermute(to_third, "band", [(2, 3)])
-    total = jnp.where(band == 0, to_first, total)
-    total = jnp.where(band == 2, to_third, total)
-    return jnp.where(band == 3, to_last, total)
+class Bands:
+    def to_meet(self, plane):
+        self.plane = plane
+        return (plane,)
+
+    def go_meet(self, plane):
+        return lax.ppermute(plane, "band", [(0, 1)]), lax.ppermute(plane, "band", [(2, 1)])
+
+    def to_part(self, up, down):
+        self.total = (self.plane.astype(f32) + up.astype(f32) + down.astype(f32)).astype(bf16)
+        return (self.total,)
+
+    def go_part(self, total):
+        return lax.ppermute(total, "band", [(1, 0)]), lax.ppermute(total, "band", [(1, 2)])
+
+    def to_last(self, to_first, to_third):
+        self.to_first, self.to_third = to_first, to_third
+        return (to_third,)
+
+    def go_last(self, to_third):
+        return (lax.ppermute(to_third, "band", [(2, 3)]),)
+
+    def to_end(self, to_last):
+        band = lax.axis_index("band")
+        total = jnp.where(band == 0, self.to_first, self.total)
+        total = jnp.where(band == 2, self.to_third, total)
+        self.total = jnp.where(band == 3, to_last, total)
+        return ()
+
+    def go_end(self):
+        return ()
+
+
+class Chunk(Bands):
+    def __init__(self, index, kept, sent):
+        size, at = LATE[index], 4 * sum(LATE[:index])
+        self.half = size // 2
+        self.kept, self.sent = kept[at : at + 4 * size], sent[at : at + 4 * size]
+
+    def chip(self, lo, hi):
+        lo, hi = lo * self.half, hi * self.half
+        return wide(self.kept, lo, hi) + wide(self.received, lo, hi)
+
+    def to_core(self):
+        return (self.sent,)
+
+    def go_core(self, send):
+        return (lax.ppermute(send, "dp", CORE),)
+
+    def to_plane(self, received):
+        self.received = received
+        return self.chip(2, 4).astype(bf16), self.chip(6, 8).astype(bf16)
+
+    def go_plane(self, send_x, send_y):
+        return lax.ppermute(send_x, "dp", ALONG_X), lax.ppermute(send_y, "dp", ALONG_Y)
+
+    go_turn = go_plane
+
+    def to_turn(self, from_x, from_y):
+        self.from_x, self.from_y = from_x, from_y
+        half = self.half
+        send_y = (self.chip(1, 2) + wide(from_x, half, 2 * half)).astype(bf16)
+        send_x = (self.chip(5, 6) + wide(from_y, half, 2 * half)).astype(bf16)
+        return send_x, send_y
+
+    def to_meet(self, from_x, from_y):
+        half = self.half
+        one = self.chip(0, 1) + wide(self.from_x, 0, half) + wide(from_y, 0, half)
+        two = self.chip(4, 5) + wide(self.from_y, 0, half) + wide(from_x, 0, half)
+        self.plane = jnp.concatenate([one, two], 0).astype(bf16)
+        return (self.plane,)
+
+
+class Sequence:
+    def __init__(self):
+        self.before = ()
+        self.arrived = {}
+
+    def round(self, *steps):
+        arrived = [tuple(self.arrived.get(chunk, ())) for chunk, _ in steps]
+        flat = sum(arrived, ())
+        flat = lax.optimization_barrier(flat + self.before)
+        at, self.before = 0, ()
+        for (chunk, name), had in zip(steps, arrived):
+            sends = getattr(chunk, "to_" + name)(*flat[at : at + len(had)])
+            at += len(had)
+            self.arrived[chunk] = getattr(chunk, "go_" + name)(*sends)
+            self.before = self.before + tuple(sends)
+
+    def wait_for(self, *arrays):
+        arrays = lax.optimization_barrier(arrays + self.before)[: len(arrays)]
+        self.before = self.before + arrays
+        return arrays
 
 
 def rope_tables(rows):
@@ -719,9 +782,11 @@
         inputs.append(hidden)
         hidden, *saved = forward_layer(slots, length, hidden, gains, cos, sin, gathered)
         saves.append(saved)
-    layer_output = to_bands(
-        hidden[:seq].astype(bf16).reshape(bands, band_rows, D), images, bands, band
-    )
+
+    def send_rows(t):
+        return send_to_bands(t[:seq].astype(bf16).reshape(bands, band_rows, D), images, bands, band)
+
+    output_blocks = send_rows(hidden)
 
     back = back_rows.astype(f32) * valid[:, None]
     per_owner = master.shape[0]
@@ -731,100 +796,111 @@
         and bands == 4
         and images == 3
         and slot_count == slot_of_block.shape[0]
-        and per_owner == EARLY + sum(LATE)
+        and per_owner == sum(EARLY) + sum(LATE)
     )
     if by_permutes:
-        places, ranks, clean, sizes = relative_places(slot_of_block, per_owner, me)
+        places, ranks, clean = chunk_places(slot_of_block, per_owner, me)
         rank = lax.dynamic_index_in_dim(ranks, me, 0, keepdims=False)
-        zones_top, zones_bottom = sizes, (sizes[0] + sizes[1],) + sizes[2:]
+        ends = [8 * sum(EARLY[: i + 1]) for i in range(len(EARLY))]
+        late = 4 * sum(LATE)
+        bounds = [0] + ends + [ends[-1] + late, ends[-1] + 2 * late]
+        zones = tuple((low, high, high - low) for low, high in zip(bounds, bounds[1:]))
     else:
         places, rank = slot_of_block, jnp.arange(per_owner, dtype=jnp.int32)
-        zones_top = zones_bottom = (slot_count,)
-
-    def backward(layer, back, zones, tiles, ahead=lambda back: back, later=lambda back: back):
+        zones = ((0, slot_count, slot_count),)
+
+    def backward(layer, back, tiles, zones, freeze=lambda kernel, tiles, zones: (tiles, zones)):
         normed, q, k, v, st, mixed, mid, n2, gu, wqkv, wout, wgu, wd = saves[layer]
         slots = places[layer * PER_LAYER : (layer + 1) * PER_LAYER]
         fill = spare if layer == LAYERS - 1 else spare[-1:]
+        first = 3 * (LAYERS - 1 - layer)
         back, gain_two, *tiles = back_ffn(
             slots, fill, back, gain_values[2 * layer + 1 : 2 * layer + 2], (mid, n2, gu, wgu, wd),
             zones, tiles,
         )
-        back = ahead(back)
+        tiles, zones = freeze(first, tiles, zones)
         d_projected, *tiles = back_attention(
             slots, length, back, cos, sin, (q, k, v, st, mixed, wout), zones, tiles
         )
-        back = later(back)
+        tiles, zones = freeze(first + 1, tiles, zones)
         back, gain_one, *tiles = back_qkv(
             slots, back, gain_values[2 * layer : 2 * layer + 1], d_projected,
             (inputs[layer], normed, wqkv), zones, tiles,
         )
-        return back, [gain_one, gain_two], tiles
-
-    def after(value, *done):
-        return lax.optimization_barrier((value,) + done)[0]
-
-    back, gains_top, tiles = backward(1, back, zones_top, [])
+        tiles, zones = freeze(first + 2, tiles, zones)
+        return back, [gain_one, gain_two], tiles, zones
+
     if by_permutes:
-        early_kept, early_sent, kept, sent = tiles
-        early = {"output": layer_output}
-        early["core"] = lax.ppermute(early_sent, "dp", CORE)
-
-        def ahead(back):
-            back, early["output"] = lax.optimization_barrier((back, early["output"]))
-            early["plane"], back = plane_start(early_kept, early["core"], beside=back)
-            return back
-
-        def later(back):
-            chip, half, from_x, from_y = early["plane"]
-            back, from_x, from_y = lax.optimization_barrier((back, from_x, from_y))
-            early["plane"] = (chip, half, from_x, from_y)
-            return back
-
-        back, gains_bottom, tiles = backward(0, back, zones_bottom, [kept, sent], ahead, later)
-        layer_output = early["output"]
-        early_late, kept, sent = tiles
-        chunks, start = [], 0
-        for size in LATE:
-            chunks.append((kept[4 * start : 4 * (start + size)], sent[4 * start : 4 * (start + size)]))
-            start += size
-        from_core = [lax.ppermute(chunk[1], "dp", CORE) for chunk in chunks]
-        turned = plane_turn(*early["plane"])
-        gate = turned
-        owned = [None] * len(chunks) + [sum_bands(plane_end(*early["plane"], *turned), band)]
-        gain_total = sum_bands(jnp.concatenate(gains_bottom + gains_top, 0), band)
-        for i, (chunk, received) in enumerate(zip(chunks, from_core)):
-            going = plane_start(chunk[0], received, gate)
-            gate = plane_turn(*going)
-            owned[i] = sum_bands(plane_end(*going, *gate), band)
-            if i == 0:
-                back = after(back, going[2], going[3])
-
-        order = jnp.argsort(places)[: sizes[0] + sizes[1]]
+        early, early_sums = [], []
+
+        def freeze(kernel, tiles, zones):
+            if kernel not in (0, 2, 3):
+                return tiles, zones
+            at = 0 if kernel == 0 else 1
+            nonlocal output_blocks
+            early.append(tiles[at])
+            ready, *early_sums[:] = lax.optimization_barrier((tiles[at], *early_sums))
+            if kernel == 0:
+                ready, *output_blocks = lax.optimization_barrier((ready, *output_blocks))
+            early_sums.append(lax.psum_scatter(ready, "dp", scatter_dimension=0, tiled=True))
+            missed = (0, zones[at][1], ends[-1])
+            return tiles[:at] + tiles[at + 1 :], (missed,) + zones[at + 1 :]
+
+        back, gains_top, tiles, zones = backward(1, back, [], zones, freeze)
+        back, gains_bottom, tiles, zones = backward(0, back, tiles, zones, freeze)
+        missed, kept, sent = tiles
+        gains = jnp.concatenate(gains_bottom + gains_top, 0).astype(bf16).reshape(-1, BLOCK)
+        gains = jnp.pad(gains, ((0, BLOCK - gains.shape[0]), (0, 0)))[None]
+        sequence = Sequence()
+        one, two = [Chunk(i, kept, sent) for i in range(len(LATE))]
+        top, bottom = Bands(), Bands()
+        sequence.arrived[top] = (jnp.concatenate(early_sums[:2] + [gains], 0),)
+        sequence.arrived[bottom] = (early_sums[2],)
+        input_blocks = send_rows(back)
+        sequence.round((one, "core"), (two, "core"), (top, "meet"))
+        sequence.round((one, "plane"))
+        sequence.round((one, "turn"))
+        input_blocks = sequence.wait_for(*input_blocks)
+        sequence.round((top, "part"))
+        sequence.round((bottom, "meet"))
+        sequence.round((one, "meet"), (two, "plane"))
+        sequence.round((two, "turn"))
+        sequence.round((top, "last"), (bottom, "part"))
+        sequence.round((two, "meet"))
+        sequence.round((one, "part"))
+        sequence.round((bottom, "last"), (top, "end"))
+        sequence.round((two, "part"), (one, "last"))
+        sequence.round((two, "last"), (bottom, "end"))
+        sequence.round((one, "end"), (two, "end"))
+        early_total = jnp.concatenate([top.total[:-1], bottom.total], 0)
 
         def again(trip, total):
-            _, late, first, second = lax.optimization_barrier(
-                (trip, early_late, early_kept, early_sent)
-            )
-            mine = (order < PER_LAYER)[:, None, None]
-            first = jnp.where(mine[: sizes[0]], late[: sizes[0]], first)
-            second = jnp.where(mine[sizes[0] :], late[sizes[0] :], second)
-            going = plane_start(first, lax.ppermute(second, "dp", CORE))
-            return sum_bands(plane_end(*going, *plane_turn(*going)), band)
-
-        owned[-1] = lax.fori_loop(0, jnp.where(clean, 0, 1), again, owned[-1])
-        owned = jnp.concatenate(owned, 0)
+            _, spare_tiles, *parts = lax.optimization_barrier((trip, missed, *early))
+            block_at = jnp.argsort(places)
+            sums, start = [], 0
+            for part, end, least in zip(parts, ends, LEAST):
+                late_here = (block_at[start:end] < least)[:, None, None]
+                whole = jnp.where(late_here, spare_tiles[start:end], part)
+                sums.append(lax.psum_scatter(whole, "dp", scatter_dimension=0, tiled=True))
+                start = end
+            return lax.psum(jnp.concatenate(sums, 0), "band")
+
+        early_total = lax.fori_loop(0, jnp.where(clean, 0, 1), again, early_total)
+        owned = jnp.concatenate([early_total, one.total, two.total], 0)
+        gain_total = top.total[-1].astype(f32)[: gain_values.size // BLOCK].reshape(-1, D)
+        gain_total = lax.psum(gain_total, "dp")
     else:
-        back, gains_bottom, tiles = backward(0, back, zones_bottom, tiles)
+        back, gains_top, tiles, _ = backward(1, back, [], zones)
+        back, gains_bottom, tiles, _ = backward(0, back, tiles, zones)
         owned = lax.psum_scatter(tiles[0], "dp", scatter_dimension=0, tiled=True)
         owned = lax.psum(owned, "band")
-        gain_total = lax.psum(jnp.concatenate(gains_bottom + gains_top, 0), "band")
-    input_grad = to_bands(back[:seq].astype(bf16).reshape(bands, band_rows, D), images, bands, band)
-
+        gain_total = lax.psum(jnp.concatenate(gains_bottom + gains_top, 0), ("dp", "band"))
+        input_blocks = send_rows(back)
+
+    layer_output = at_bands(output_blocks, images, bands, band)
+    input_grad = at_bands(input_blocks[:bands], images, bands, band)
     owned_f = owned.astype(f32)
-    squares = jnp.sum(owned_f * owned_f).reshape(1)
-    summed = lax.psum(jnp.concatenate([gain_total.reshape(-1), squares]), "dp")
-    gain_total = summed[:-1].reshape(gain_values.shape)
-    owned_squares = summed[-1]
+    owned_squares = lax.psum(jnp.sum(owned_f * owned_f), "dp")
     grad_norm = jnp.sqrt(owned_squares + jnp.sum(gain_total * gain_total))
     factor = jnp.minimum(1.0, clip_limit / grad_norm)
     weight_grads, new_statistics, new_master, master_copy = optimizer(

time: 712 us -> 670 us (0.941)
  other arithmetic: 72.7 us -> 42.6 us
  starting transfers between devices: 93.6 us -> 79.8 us
    ppermute x51 -> x36, waiting for transfers between devices: 120 us -> 68.6 us  [the longest x4 16.8 us: go_last(): return (lax.ppermute(to_third, 'band', [(2, 3)]),)]
    reduce_scatter x0 -> x3, waiting for transfers between devices: none -> 47.1 us  [freeze(): lax.psum_scatter(ready, 'dp', scatter_dimension=0, tiled=True)]
    ppermute x51 -> x36, starting transfers between devices: 87.9 us -> 72 us  [the longest x4 19.8 us: go_meet(): lax.ppermute(plane, 'band', [(2, 1)])]
    convert_element_type x12 -> x8, other arithmetic: 23.8 us -> 12.9 us  [the longest x2 4.8 us: to_plane(): return (self.chip(2, 4).astype(bf16), self.chip(6, 8).astype(bf16))]
    another operation x7 -> x6, other arithmetic: 11.7 us -> 3.36 us
  transfers between devices with their start and end apart: 55 -> 43, of which waited for: 23 -> 19; matrix products, arithmetic and copies ran while one was open for 13% -> 10% of each run, Pallas kernels for 7% -> 21%
where the time goes in v6:
time: 670 us; the launch traced here: 663 us
  Pallas kernels  235 us (35%)
  waiting for transfers between devices  218 us (33%)
  starting transfers between devices  79.8 us (12%)
  local copies, waits for them, and re-layouts  44.7 us (7%)
  other arithmetic  42.6 us (6%)
  blocking collectives  23.4 us (3%)
  between operations  19.8 us (3%)
    all_gather x1, waiting for transfers between devices, shards(): gathered = lax.all_gather(master.astype(bf16), 'dp', axis=0, tiled=True)  87.8 us
    pallas_call x2, Pallas kernels, forward_layer(): pl.pallas_call(forward_kernel, out_shape=[S((rows, D), f32)] + saved, in_...  66.6 us
    pallas_call x2, Pallas kernels, back_ffn(): pl.pallas_call(functools.partial(back_ffn_kernel, len(begun), zones), out...  60.9 us
    reduce_scatter x3, waiting for transfers between devices, freeze(): lax.psum_scatter(ready, 'dp', scatter_dimension=0, tiled=True)  47.1 us
    pallas_call x2, Pallas kernels, back_attention(): pl.pallas_call(functools.partial(back_attention_kernel, len(begun), zones...  44.8 us
    pallas_call x2, Pallas kernels, back_qkv(): pl.pallas_call(functools.partial(back_qkv_kernel, len(begun), zones), out...  31.9 us
    pallas_call x1, Pallas kernels, optimizer(): pl.pallas_call(optimizer_kernel, grid=(count // per,), out_shape=[S(maste...  30.7 us
    psum x1, blocking collectives, shards(): owned_squares = lax.psum(jnp.sum(owned_f * owned_f), 'dp')  23.4 us
  transfers between devices with their start and end apart: 43, of which 19 were waited for; matrix products, arithmetic and copies ran while one was open for 10% of the time, Pallas kernels for 21%

profile of v6, /device:TPU:16, one launch (start us, length us, event | category | flops | bytes accessed | tf_op | source)
XLA Modules:
  0.0 663.3 jit_solution(966993308442107618)
XLA Ops:
  7.2 5.6 convert_element_type.240
  16.7 4.4 collective-permute-start.1
  23.2 5.3 scatter_custom_fusion
  42.8 5.5 collective-permute-done.1
  49.4 8.9 %collective-permute-done.2 = bf16[2,145,768]{2,1,0:T(8,128)(2,1)} collective-permute-done((bf16[2,145,768]{2,1,0:T(8,128)(2,1)S(1)}, bf16[2,145,768]{2,1,0:T(8,128)(2,1)}, u32[]{:S(2)}, u32[]{:S(2)}) %collective-permute-start.2) | collective-permute-done | bytes 445472 | tf_op jit(solution)/shard_map/ppermute | solution.py:571
  64.9 87.8 %all-gather.2.cloned.1.call-done.w_hbm = bf16[864,128,128]{2,1,0:T(8,128)(2,1)} async-done(((bf16[108,128,128]{2,1,0:T(8,128)(2,1)}), bf16[864,128,128]{2,1,0:T(8,128)(2,1)}) %all-gather.2.cloned.1.call-update) | async-done | bytes 28311568 | tf_op jit(solution)/shard_map/all_gather | solution.py:760
  152.7 33.0 %forward_block.2 = (f32[592,768]{1,0:T(8,128)}, bf16[592,768]{1,0:T(8,128)(2,1)}, bf16[640,768]{1,0:T(8,128)(2,1)}, bf16[640,768]{1,0:T(8,128)(2,1)}, bf16[640,7...) custom-call(s32[432]{0:T(512)} %get-tuple-element.345.slots, ...), custom_call_target="tpu_custom_call" | custom-call | flops 8380219392 | bytes 41943040 | tf_op jit(solution)/shard_map/forward_block/pallas_call | solution.py:424
  185.7 33.5 %forward_block.3 = (f32[592,768]{1,0:T(8,128)}, bf16[592,768]{1,0:T(8,128)(2,1)}, bf16[640,768]{1,0:T(8,128)(2,1)}, bf16[640,768]{1,0:T(8,128)(2,1)}, bf16[640,7...) custom-call(s32[432]{0:T(512)} %get-tuple-element.346.slots, ...), custom_call_target="tpu_custom_call" | custom-call | flops 8380219392 | bytes 41943040 | tf_op jit(solution)/shard_map/forward_block/pallas_call | solution.py:424
  229.3 30.8 %backward_feed_forward.2 = (f32[592,768]{1,0:T(8,128)}, f32[1,768]{1,0:T(1,128)}, bf16[176,128,128]{2,1,0:T(8,128)(2,1)}, bf16[144,128,128]{2,1,0:T(8,128)(2,1)}...) custom-call(s32[432]{0:T(512)} %get-tuple-element.344.places, ...), custom_call_target="tpu_custom_call" | custom-call | flops 11173625856 | bytes 31457280 | tf_op jit(solution)/shard_map/backward_feed_forward/pallas_call | solution.py:455
  260.9 22.6 %backward_attention.2 = (bf16[592,2304]{1,0:T(8,128)(2,1)}, bf16[624,128,128]{2,1,0:T(8,128)(2,1)}, bf16[144,128,128]{2,1,0:T(8,128)(2,1)}, bf16[304,128,128]{2,...) custom-call(s32[432]{0:T(512)} %get-tuple-element.344.places, ...), custom_call_target="tpu_custom_call", output_to_operand_aliasing={{2}: (11, {}), {3}: (12, {}), {4}: (13, {}), {5}: (14, {})} | custom-call | flops 6779830272 | bytes 31457280 | tf_op jit(solution)/shard_map/backward_attention/pallas_call | solution.py:481
  283.5 16.5 %backward_qkv.2 = (f32[592,768]{1,0:T(8,128)}, f32[1,768]{1,0:T(1,128)}, bf16[624,128,128]{2,1,0:T(8,128)(2,1)}, bf16[144,128,128]{2,1,0:T(8,128)(2,1)}, bf16[30...) custom-call(s32[432]{0:T(512)} %get-tuple-element.344.places, ...), custom_call_target="tpu_custom_call", output_to_operand_aliasing={{2}: (7, {}), {3}: (8, {}), {4}: (9, {}), {5}: (10, {}), {6... | custom-call | flops 4190109696 | bytes 20971520 | tf_op jit(solution)/shard_map/backward_qkv/pallas_call | solution.py:507
  300.0 19.6 %reduce-scatter.7.cloned.1.call-done = bf16[22,128,128]{2,1,0:T(8,128)(2,1)} async-done(((bf16[176,128,128]{2,1,0:T(8,128)(2,1)}), bf16[22,128,128]{2,1,0:T(8,128)(2,1)}) %reduce-scatter.7.cloned.1.call-update) | async-done | bytes 720912 | tf_op jit(solution)/shard_map/reduce_scatter | solution.py:845
  319.7 30.2 %backward_feed_forward.3 = (f32[592,768]{1,0:T(8,128)}, f32[1,768]{1,0:T(1,128)}, bf16[624,128,128]{2,1,0:T(8,128)(2,1)}, bf16[304,128,128]{2,1,0:T(8,128)(2,1)}...) custom-call(s32[432]{0:T(512)} %get-tuple-element.343.places, ...), custom_call_target="tpu_custom_call", output_to_operand_aliasing={{2}: (9, {}), {3}: (10, {}), {4}: (11, {}), {5}: (12, {})} | custom-call | flops 11173625856 | bytes 31457280 | tf_op jit(solution)/shard_map/backward_feed_forward/pallas_call | solution.py:455
  349.9 27.5 %reduce-scatter.9.cloned.1.call-done = bf16[18,128,128]{2,1,0:T(8,128)(2,1)} async-done(((bf16[144,128,128]{2,1,0:T(8,128)(2,1)}), bf16[18,128,128]{2,1,0:T(8,128)(2,1)}) %reduce-scatter.9.cloned.1.call-update) | async-done | bytes 589840 | tf_op jit(solution)/shard_map/reduce_scatter | solution.py:845
  377.4 22.2 %backward_attention.3 = (bf16[592,2304]{1,0:T(8,128)(2,1)}, bf16[624,128,128]{2,1,0:T(8,128)(2,1)}, bf16[120,128,128]{2,1,0:T(8,128)(2,1)}, bf16[120,128,128]{2,1,0:T(8,128)(2,1)}) custom-call(s32[432]{0:T(512)} %get-tuple-element.343.places, s32[1]{0:T(128)} %dynamic_slice.49.length, ...), custom_call_target="tpu_custom_call", output_to_operand_aliasing={{1}: (11, {}), {2}: (12, {}), {3}: (13, {})} | custom-call | flops 6779830272 | bytes 31457280 | tf_op jit(solution)/shard_map/backward_attention/pallas_call | solution.py:481
  399.7 15.4 %backward_qkv.3 = (f32[592,768]{1,0:T(8,128)}, f32[1,768]{1,0:T(1,128)}, bf16[624,128,128]{2,1,0:T(8,128)(2,1)}, bf16[120,128,128]{2,1,0:T(8,128)(2,1)}, bf16[120,128,128]{2,1,0:T(8,128)(2,1)}) custom-call(s32[432]{0:T(512)} %get-tuple-element.343.places, ...), custom_call_target="tpu_custom_call", output_to_operand_aliasing={{2}: (7, {}), {3}: (8, {}), {4}: (9, {})} | custom-call | flops 4190109696 | bytes 20971520 | tf_op jit(solution)/shard_map/backward_qkv/pallas_call | solution.py:507
  439.7 9.3 %collective-permute-done.10 = bf16[18,128,128]{2,1,0:T(8,128)(2,1)} collective-permute-done((bf16[18,128,128]{2,1,0:T(8,128)(2,1)}, bf16[18,128,128]{2,1,0:T(8,128)(2,1)}, u32[]{:S(2)}, u32[]{:S(2)}) %collective-permute-start.10) | collective-permute-done | bytes 589856 | tf_op jit(solution)/shard_map/ppermute | solution.py:695
  459.9 4.6 collective-permute-start.8
  475.1 9.4 %collective-permute-start.17 = (bf16[38,128,128]{2,1,0:T(8,128)(2,1)}, bf16[38,128,128]{2,1,0:T(8,128)(2,1)S(1)}, u32[]{:S(2)}, u32[]{:S(2)}) collective-permute-start(bf16[38,128,128]{2,1,0:T(8,128)(2,1)} %reduce-scatter.11.cloned.1.call-done), channel_id=1, source_target_pairs={{2,1},{6,5},{10,9},{14,13},{18,17},{22,21},{26,25},{30,29}} | collective-permute-start | bytes 3735560 | tf_op jit(solution)/shard_map/ppermute | solution.py:647
  489.1 6.5 collective-permute-done.21
  498.5 5.7 collective-permute-done.22
  517.7 6.0 collective-permute-start.27
  525.3 8.7 %collective-permute-done.27 = bf16[18,128,128]{2,1,0:T(8,128)(2,1)S(1)} collective-permute-done((bf16[18,128,128]{2,1,0:T(8,128)(2,1)S(1)}, bf16[18,128,128]{2,1,0:T(8,128)(2,1)S(1)}, u32[]{:S(2)}, u32[]{:S(2)}) %collective-permute-start.27) | collective-permute-done | bytes 589856 | tf_op jit(solution)/shard_map/ppermute | solution.py:647
  537.2 7.0 %collective-permute-done.24 = bf16[38,128,128]{2,1,0:T(8,128)(2,1)} collective-permute-done((bf16[38,128,128]{2,1,0:T(8,128)(2,1)S(1)}, bf16[38,128,128]{2,1,0:T(8,128)(2,1)}, u32[]{:S(2)}, u32[]{:S(2)}) %collective-permute-start.24) | collective-permute-done | bytes 1245216 | tf_op jit(solution)/shard_map/ppermute | solution.py:654
  561.3 5.1 collective-permute-done.35
  566.4 8.6 %collective-permute-done.36 = bf16[38,128,128]{2,1,0:T(8,128)(2,1)} collective-permute-done((bf16[38,128,128]{2,1,0:T(8,128)(2,1)}, bf16[38,128,128]{2,1,0:T(8,128)(2,1)}, u32[]{:S(2)}, u32[]{:S(2)}) %collective-permute-start.36) | collective-permute-done | bytes 1245216 | tf_op jit(solution)/shard_map/ppermute | solution.py:661
  575.0 4.4 collective-permute-start.38
  582.6 4.0 collective-permute-done.37
  586.6 4.2 collective-permute-done.38
  593.5 5.1 multiply_reduce_fusion
  598.6 23.4 %all-reduce.4 = (f32[]{:T(128)}, f32[4,768]{1,0:T(4,128)S(1)}) all-reduce(f32[]{:T(128)} %get-tuple-element.306, f32[4,768]{1,0:T(4,128)S(1)} %reshape.321), channel_id=1, replica_groups=mesh['dp'=8,'band'=4] {'dp'}, use_global_device_ids=true, to_apply=%region_16.17 | all-reduce | flops 3073 | bytes 24584 | tf_op jit(solution)/shard_map/psum | solution.py:903
  624.6 30.7 %optimizer.1 = (f32[108,128,128]{2,1,0:T(8,128)}, f32[108,2,128,128]{3,2,1,0:T(8,128)}, f32[108,128,128]{2,1,0:T(8,128)}, bf16[108,128,128]{2,1,0:T(8,128)(2,1)}) custom-call(f32[1]{0:T(128)} %bitcast.28.factor, s32[108]{0:T(128)} %dynamic-slice_reduce_fusion.rank, bf16[108,128,128]{2,1,0:T(8,128)(2,1)} %get-tuple-element.307.g_ref, f32[108,128,128]{2,1,0:T(8,128)} %m_ref.1, ...), custom_call_target="tpu_custom_call" | custom-call | tf_op jit(solution)/shard_map/optimizer/pallas_call | solution.py:547
  (237 shorter events, 132.2 us)
Async XLA Ops:
  7.2 145.5 %all-gather.2.cloned.1.call-start = ((), (), s32[]{:S(2)}) async-start(), calls=%async_computation.6 | async-start | bytes 31850496 | tf_op jit(solution)/shard_map/all_gather | solution.py:760
  12.9 306.8 %reduce-scatter.7.cloned.1.call-start = ((), (), s32[]{:S(2)}) async-start(), calls=%async_computation.7 | async-start | bytes 6488064 | tf_op jit(solution)/shard_map/reduce_scatter | solution.py:845
  15.4 26.3 %collective-permute-start = (bf16[2,145,768]{2,1,0:T(8,128)(2,1)}, bf16[2,145,768]{2,1,0:T(8,128)(2,1)}, u32[]{:S(2)}, u32[]{:S(2)}) collective-permute-start(bf16[2,145,768]{2,1,0:T(8,128)(2,1)} %get-tuple-element.324), channel_id=1, source_target_pairs={{0,1},{1,2},{3,0},{4,5},{5,6},{7,4},{8,9},{9,10},{11,8},{12,13},{1... | collective-permute-start | bytes 1336328 | tf_op jit(solution)/shard_map/ppermute | solution.py:571
  16.7 31.6 %collective-permute-start.1 = (bf16[2,145,768]{2,1,0:T(8,128)(2,1)S(1)}, bf16[2,145,768]{2,1,0:T(8,128)(2,1)}, u32[]{:S(2)}, u32[]{:S(2)}) collective-permute-start(bf16[2,145,768]{2,1,0:T(8,128)(2,1)S(1)} %get-tuple-element.323), channel_id=1, source_target_pairs={{0,2},{2,0},{3,1},{4,6},{6,4},{7,5},{8,10},{10,8},{11,9},{12,14},{... | collective-permute-start | bytes 1336328 | tf_op jit(solution)/shard_map/ppermute | solution.py:571
  21.2 37.1 %collective-permute-start.2 = (bf16[2,145,768]{2,1,0:T(8,128)(2,1)S(1)}, bf16[2,145,768]{2,1,0:T(8,128)(2,1)}, u32[]{:S(2)}, u32[]{:S(2)}) collective-permute-start(bf16[2,145,768]{2,1,0:T(8,128)(2,1)S(1)} %get-tuple-element.322), channel_id=1, source_target_pairs={{1,0},{2,1},{3,2},{5,4},{6,5},{7,6},{9,8},{10,9},{11,10},{13,12},{... | collective-permute-start | bytes 1336328 | tf_op jit(solution)/shard_map/ppermute | solution.py:571
  221.2 38.9 %collective-permute-start.3 = (bf16[145,768]{1,0:T(8,128)(2,1)S(1)}, bf16[145,768]{1,0:T(8,128)(2,1)S(1)}, u32[]{:S(2)}, u32[]{:S(2)}) collective-permute-start(bf16[145,768]{1,0:T(8,128)(2,1)S(1)} %get-tuple-element.332), channel_id=1, source_target_pairs={{0,1},{1,2},{2,3},{4,5},{5,6},{6,7},{8,9},{9,10},{10,11},{12,13},{... | collective-permute-start | bytes 668168 | tf_op jit(solution)/shard_map/ppermute | solution.py:582
  224.6 35.5 %collective-permute-start.4 = (bf16[145,768]{1,0:T(8,128)(2,1)S(1)}, bf16[145,768]{1,0:T(8,128)(2,1)S(1)}, u32[]{:S(2)}, u32[]{:S(2)}) collective-permute-start(bf16[145,768]{1,0:T(8,128)(2,1)S(1)} %get-tuple-element.331), channel_id=1, source_target_pairs={{0,2},{1,3},{2,0},{4,6},{5,7},{6,4},{8,10},{9,11},{10,8},{12,14},{... | collective-permute-start | bytes 668168 | tf_op jit(solution)/shard_map/ppermute | solution.py:582
  227.0 33.1 %collective-permute-start.5 = (bf16[145,768]{1,0:T(8,128)(2,1)S(1)}, bf16[145,768]{1,0:T(8,128)(2,1)S(1)}, u32[]{:S(2)}, u32[]{:S(2)}) collective-permute-start(bf16[145,768]{1,0:T(8,128)(2,1)S(1)} %get-tuple-element.330), channel_id=1, source_target_pairs={{0,3},{1,0},{2,1},{4,7},{5,4},{6,5},{8,11},{9,8},{10,9},{12,15},{1... | collective-permute-start | bytes 668168 | tf_op jit(solution)/shard_map/ppermute | solution.py:582
  260.9 116.4 %reduce-scatter.9.cloned.1.call-start = ((), (), s32[]{:S(2)}) async-start(), calls=%async_computation.8 | async-start | bytes 5308416 | tf_op jit(solution)/shard_map/reduce_scatter | solution.py:845
  319.6 154.6 %reduce-scatter.11.cloned.1.call-start = ((), (), s32[]{:S(2)}) async-start(), calls=%async_computation.9 | async-start | bytes 11206656 | tf_op jit(solution)/shard_map/reduce_scatter | solution.py:845
  421.5 52.7 %collective-permute-start.20 = (bf16[48,128,128]{2,1,0:T(8,128)(2,1)}, bf16[48,128,128]{2,1,0:T(8,128)(2,1)}, u32[]{:S(2)}, u32[]{:S(2)}) collective-permute-start(bf16[48,128,128]{2,1,0:T(8,128)(2,1)} %slice.211), channel_id=1, source_target_pairs={{0,4},{4,0},{8,12},{12,8},{16,20},{20,16},{24,28},{28,24},{1,5},{5... | collective-permute-start | bytes 4718600 | tf_op jit(solution)/shard_map/ppermute | solution.py:688
  422.2 47.4 %collective-permute-start.12 = (bf16[41,128,128]{2,1,0:T(8,128)(2,1)S(1)}, bf16[41,128,128]{2,1,0:T(8,128)(2,1)}, u32[]{:S(2)}, u32[]{:S(2)}) collective-permute-start(bf16[41,128,128]{2,1,0:T(8,128)(2,1)S(1)} %pad_maximum_fusion.3), channel_id=1, source_target_pairs={{0,1},{4,5},{8,9},{12,13},{16,17},{20,21},{24,25},{28,29}} | collective-permute-start | bytes 4030472 | tf_op jit(solution)/shard_map/ppermute | solution.py:647
  423.9 45.7 %collective-permute-start.13 = (bf16[41,128,128]{2,1,0:T(8,128)(2,1)S(1)}, bf16[41,128,128]{2,1,0:T(8,128)(2,1)}, u32[]{:S(2)}, u32[]{:S(2)}) collective-permute-start(bf16[41,128,128]{2,1,0:T(8,128)(2,1)S(1)} %pad_maximum_fusion.3), channel_id=1, source_target_pairs={{2,1},{6,5},{10,9},{14,13},{18,17},{22,21},{26,25},{30,29}} | collective-permute-start | bytes 4030472 | tf_op jit(solution)/shard_map/ppermute | solution.py:647
  430.2 18.8 %collective-permute-start.10 = (bf16[18,128,128]{2,1,0:T(8,128)(2,1)}, bf16[18,128,128]{2,1,0:T(8,128)(2,1)}, u32[]{:S(2)}, u32[]{:S(2)}) collective-permute-start(bf16[18,128,128]{2,1,0:T(8,128)(2,1)} %get-tuple-element.313), channel_id=1, source_target_pairs={{0,8},{4,12},{8,0},{12,4},{16,24},{20,28},{24,16},{28,20},{1,9},{5... | collective-permute-start | bytes 1769480 | tf_op jit(solution)/shard_map/ppermute | solution.py:695
  431.6 22.5 %collective-permute-start.11 = (bf16[18,128,128]{2,1,0:T(8,128)(2,1)}, bf16[18,128,128]{2,1,0:T(8,128)(2,1)}, u32[]{:S(2)}, u32[]{:S(2)}) collective-permute-start(bf16[18,128,128]{2,1,0:T(8,128)(2,1)} %get-tuple-element.312), channel_id=1, source_target_pairs={{0,16},{4,20},{8,24},{12,28},{16,0},{20,4},{24,8},{28,12},{1,17},{... | collective-permute-start | bytes 1769480 | tf_op jit(solution)/shard_map/ppermute | solution.py:695
  454.1 13.0 %collective-permute-start.7 = (bf16[145,768]{1,0:T(8,128)(2,1)S(1)}, bf16[145,768]{1,0:T(8,128)(2,1)S(1)}, u32[]{:S(2)}, u32[]{:S(2)}) collective-permute-start(bf16[145,768]{1,0:T(8,128)(2,1)S(1)} %get-tuple-element.327), channel_id=1, source_target_pairs={{0,2},{1,3},{2,0},{4,6},{5,7},{6,4},{8,10},{9,11},{10,8},{12,14},{... | collective-permute-start | bytes 668168 | tf_op jit(solution)/shard_map/ppermute | solution.py:582
  468.6 16.0 %collective-permute-start.19 = (bf16[9,128,128]{2,1,0:T(8,128)(2,1)}, bf16[9,128,128]{2,1,0:T(8,128)(2,1)}, u32[]{:S(2)}, u32[]{:S(2)}) collective-permute-start(bf16[9,128,128]{2,1,0:T(8,128)(2,1)} %get-tuple-element.310), channel_id=1, source_target_pairs={{0,16},{4,20},{8,24},{12,28},{16,0},{20,4},{24,8},{28,12},{1,17},{... | collective-permute-start | bytes 884744 | tf_op jit(solution)/shard_map/ppermute | solution.py:695
  472.0 35.0 %collective-permute-start.14 = (bf16[41,128,128]{2,1,0:T(8,128)(2,1)S(1)}, bf16[41,128,128]{2,1,0:T(8,128)(2,1)S(1)}, u32[]{:S(2)}, u32[]{:S(2)}) collective-permute-start(bf16[41,128,128]{2,1,0:T(8,128)(2,1)S(1)} %add_convert_fusion), channel_id=1, source_target_pairs={{1,0},{5,4},{9,8},{13,12},{17,16},{21,20},{25,24},{29,28}} | collective-permute-start | bytes 4030472 | tf_op jit(solution)/shard_map/ppermute | solution.py:654
  472.9 35.5 %collective-permute-start.15 = (bf16[41,128,128]{2,1,0:T(8,128)(2,1)S(1)}, bf16[41,128,128]{2,1,0:T(8,128)(2,1)}, u32[]{:S(2)}, u32[]{:S(2)}) collective-permute-start(bf16[41,128,128]{2,1,0:T(8,128)(2,1)S(1)} %add_convert_fusion), channel_id=1, source_target_pairs={{1,2},{5,6},{9,10},{13,14},{17,18},{21,22},{25,26},{29,30}} | collective-permute-start | bytes 4030472 | tf_op jit(solution)/shard_map/ppermute | solution.py:654
  474.3 34.2 %collective-permute-start.16 = (bf16[38,128,128]{2,1,0:T(8,128)(2,1)}, bf16[38,128,128]{2,1,0:T(8,128)(2,1)S(1)}, u32[]{:S(2)}, u32[]{:S(2)}) collective-permute-start(bf16[38,128,128]{2,1,0:T(8,128)(2,1)} %reduce-scatter.11.cloned.1.call-done), channel_id=1, source_target_pairs={{0,1},{4,5},{8,9},{12,13},{16,17},{20,21},{24,25},{28,29}} | collective-permute-start | bytes 3735560 | tf_op jit(solution)/shard_map/ppermute | solution.py:647
  475.1 35.1 %collective-permute-start.17 = (bf16[38,128,128]{2,1,0:T(8,128)(2,1)}, bf16[38,128,128]{2,1,0:T(8,128)(2,1)S(1)}, u32[]{:S(2)}, u32[]{:S(2)}) collective-permute-start(bf16[38,128,128]{2,1,0:T(8,128)(2,1)} %reduce-scatter.11.cloned.1.call-done), channel_id=1, source_target_pairs={{2,1},{6,5},{10,9},{14,13},{18,17},{22,21},{26,25},{30,29}} | collective-permute-start | bytes 3735560 | tf_op jit(solution)/shard_map/ppermute | solution.py:647
  505.5 11.4 %collective-permute-start.28 = (bf16[6,128,128]{2,1,0:T(8,128)(2,1)S(1)}, bf16[6,128,128]{2,1,0:T(8,128)(2,1)S(1)}, u32[]{:S(2)}, u32[]{:S(2)}) collective-permute-start(bf16[6,128,128]{2,1,0:T(8,128)(2,1)S(1)} %get-tuple-element.317), channel_id=1, source_target_pairs={{0,8},{4,12},{8,0},{12,4},{16,24},{20,28},{24,16},{28,20},{1,9},{5... | collective-permute-start | bytes 589832 | tf_op jit(solution)/shard_map/ppermute | solution.py:695
  510.8 25.7 %collective-permute-start.23 = (bf16[38,128,128]{2,1,0:T(8,128)(2,1)S(1)}, bf16[38,128,128]{2,1,0:T(8,128)(2,1)S(1)}, u32[]{:S(2)}, u32[]{:S(2)}) collective-permute-start(bf16[38,128,128]{2,1,0:T(8,128)(2,1)S(1)} %add_convert_fusion.1), channel_id=1, source_target_pairs={{1,0},{5,4},{9,8},{13,12},{17,16},{21,20},{25,24},{29,28}} | collective-permute-start | bytes 3735560 | tf_op jit(solution)/shard_map/ppermute | solution.py:654
  511.5 32.7 %collective-permute-start.24 = (bf16[38,128,128]{2,1,0:T(8,128)(2,1)S(1)}, bf16[38,128,128]{2,1,0:T(8,128)(2,1)}, u32[]{:S(2)}, u32[]{:S(2)}) collective-permute-start(bf16[38,128,128]{2,1,0:T(8,128)(2,1)S(1)} %add_convert_fusion.1), channel_id=1, source_target_pairs={{1,2},{5,6},{9,10},{13,14},{17,18},{21,22},{25,26},{29,30}} | collective-permute-start | bytes 3735560 | tf_op jit(solution)/shard_map/ppermute | solution.py:654
  512.8 32.7 %collective-permute-start.25 = (bf16[41,128,128]{2,1,0:T(8,128)(2,1)}, bf16[41,128,128]{2,1,0:T(8,128)(2,1)S(1)}, u32[]{:S(2)}, u32[]{:S(2)}) collective-permute-start(bf16[41,128,128]{2,1,0:T(8,128)(2,1)} %collective-permute-done.15), channel_id=1, source_target_pairs={{2,3},{6,7},{10,11},{14,15},{18,19},{22,23},{26,27},{30,31}} | collective-permute-start | bytes 4030472 | tf_op jit(solution)/shard_map/ppermute | solution.py:661
  517.7 16.4 %collective-permute-start.27 = (bf16[18,128,128]{2,1,0:T(8,128)(2,1)S(1)}, bf16[18,128,128]{2,1,0:T(8,128)(2,1)S(1)}, u32[]{:S(2)}, u32[]{:S(2)}) collective-permute-start(bf16[18,128,128]{2,1,0:T(8,128)(2,1)S(1)} %pad_maximum_fusion.4), channel_id=1, source_target_pairs={{2,1},{6,5},{10,9},{14,13},{18,17},{22,21},{26,25},{30,29}} | collective-permute-start | bytes 1769480 | tf_op jit(solution)/shard_map/ppermute | solution.py:647
  534.3 16.5 %collective-permute-start.32 = (bf16[18,128,128]{2,1,0:T(8,128)(2,1)S(1)}, bf16[18,128,128]{2,1,0:T(8,128)(2,1)S(1)}, u32[]{:S(2)}, u32[]{:S(2)}) collective-permute-start(bf16[18,128,128]{2,1,0:T(8,128)(2,1)S(1)} %add_convert_fusion.2), channel_id=1, source_target_pairs={{1,0},{5,4},{9,8},{13,12},{17,16},{21,20},{25,24},{29,28}} | collective-permute-start | bytes 1769480 | tf_op jit(solution)/shard_map/ppermute | solution.py:654
  535.2 18.6 %collective-permute-start.33 = (bf16[18,128,128]{2,1,0:T(8,128)(2,1)S(1)}, bf16[18,128,128]{2,1,0:T(8,128)(2,1)}, u32[]{:S(2)}, u32[]{:S(2)}) collective-permute-start(bf16[18,128,128]{2,1,0:T(8,128)(2,1)S(1)} %add_convert_fusion.2), channel_id=1, source_target_pairs={{1,2},{5,6},{9,10},{13,14},{17,18},{21,22},{25,26},{29,30}} | collective-permute-start | bytes 1769480 | tf_op jit(solution)/shard_map/ppermute | solution.py:654
  536.5 12.4 %collective-permute-start.30 = (bf16[12,128,128]{2,1,0:T(8,128)(2,1)S(1)}, bf16[12,128,128]{2,1,0:T(8,128)(2,1)S(1)}, u32[]{:S(2)}, u32[]{:S(2)}) collective-permute-start(bf16[12,128,128]{2,1,0:T(8,128)(2,1)S(1)} %pad_maximum_fusion.5), channel_id=1, source_target_pairs={{0,1},{4,5},{8,9},{12,13},{16,17},{20,21},{24,25},{28,29}} | collective-permute-start | bytes 1179656 | tf_op jit(solution)/shard_map/ppermute | solution.py:647
  545.6 29.4 %collective-permute-start.36 = (bf16[38,128,128]{2,1,0:T(8,128)(2,1)}, bf16[38,128,128]{2,1,0:T(8,128)(2,1)}, u32[]{:S(2)}, u32[]{:S(2)}) collective-permute-start(bf16[38,128,128]{2,1,0:T(8,128)(2,1)} %collective-permute-done.24), channel_id=1, source_target_pairs={{2,3},{6,7},{10,11},{14,15},{18,19},{22,23},{26,27},{30,31}} | collective-permute-start | bytes 3735560 | tf_op jit(solution)/shard_map/ppermute | solution.py:661
  557.4 29.2 %collective-permute-start.37 = (bf16[18,128,128]{2,1,0:T(8,128)(2,1)}, bf16[18,128,128]{2,1,0:T(8,128)(2,1)}, u32[]{:S(2)}, u32[]{:S(2)}) collective-permute-start(bf16[18,128,128]{2,1,0:T(8,128)(2,1)} %collective-permute-done.33), channel_id=1, source_target_pairs={{2,3},{6,7},{10,11},{14,15},{18,19},{22,23},{26,27},{30,31}} | collective-permute-start | bytes 1769480 | tf_op jit(solution)/shard_map/ppermute | solution.py:661
  575.0 15.8 %collective-permute-start.38 = (bf16[12,128,128]{2,1,0:T(8,128)(2,1)}, bf16[12,128,128]{2,1,0:T(8,128)(2,1)S(1)}, u32[]{:S(2)}, u32[]{:S(2)}) collective-permute-start(bf16[12,128,128]{2,1,0:T(8,128)(2,1)} %collective-permute-done.35), channel_id=1, source_target_pairs={{2,3},{6,7},{10,11},{14,15},{18,19},{22,23},{26,27},{30,31}} | collective-permute-start | bytes 1179656 | tf_op jit(solution)/shard_map/ppermute | solution.py:661
  (42 other events, 380.5 us)
Sparse Core Ops, SparseCore 0:
  13.0 139.6 all-gather.1
  260.3 59.3 reduce-scatter.6
  323.5 53.8 reduce-scatter.8
  381.4 83.3 reduce-scatter.10

commit v7 on v6

--- a/solution.py
+++ b/solution.py
@@ -37,6 +37,7 @@
 OFFSETS = [sum(COUNTS[:i]) for i in range(4)]
 PER_LAYER = sum(COUNTS)
 FF_STEP = 512
+TOGETHER = 4
 
 
 def round_up(n, m):
@@ -146,38 +147,31 @@
         saves[i].start()
     st_ref[...] = jnp.zeros(st_ref.shape, f32)
 
-    @pl.loop(0, HEADS // 2)
-    def _(p):
-        cols = pl.ds(pl.multiple_of(p * PAIR, PAIR), PAIR)
-        kp = k_ref[:, cols]
-        vp = v_ref[:, cols]
-        low = lax.broadcasted_iota(jnp.int32, kp.shape, 1) < HEAD_DIM
-        keys = (jnp.where(low, kp, 0), jnp.where(low, 0, kp))
-        values = (jnp.where(low, vp, 1), jnp.where(low, 1, vp))
+    @pl.loop(0, HEADS // TOGETHER)
+    def _(g):
+        width = TOGETHER * HEAD_DIM
+        cols = pl.ds(pl.multiple_of(g * width, width), width)
         for q0, q1 in query_blocks(rows):
+            count = q1 - q0
             kend = min(round_up(q1, BLOCK), key_rows)
             qp = q_ref[q0:q1, cols]
-            mask = bias[q0:q1, :kend]
-            parts = []
-            tops = []
-            for h in range(2):
-                s = nt(qp, keys[h][:kend]) + mask
-                top = jnp.max(s, -1, keepdims=True)
-                e = jnp.exp(s - top).astype(bf16)
-                parts.append(nn(e, values[h][:kend]))
-                tops.append(top)
-            lane = lax.broadcasted_iota(jnp.int32, parts[0].shape, 1)
-            low_q = lane < HEAD_DIM
-            total = pltpu.roll(jnp.where(low_q, parts[1], parts[0]), HEAD_DIM, 1)
-            mixed_ref[q0:q1, cols] = (jnp.where(low_q, parts[0], parts[1]) / total).astype(bf16)
-            log_total = jnp.log(total)
-            other = pltpu.roll(log_total, HEAD_DIM, 1)
-            first = tops[0] + jnp.where(low_q, log_total, other)
-            second = tops[1] + jnp.where(low_q, other, log_total)
-            old = st_ref[q0:q1, :]
-            st_ref[q0:q1, :] = jnp.where(
-                lane == 2 * p, first, jnp.where(lane == 2 * p + 1, second, old)
-            )
+            head = lax.broadcasted_iota(jnp.int32, qp.shape, 1) // HEAD_DIM
+            stacked = jnp.concatenate([jnp.where(head == h, qp, 0) for h in range(TOGETHER)], 0)
+            s = nt(stacked, k_ref[:kend, cols]).reshape(TOGETHER, count, kend) + bias[q0:q1, :kend][None]
+            top = jnp.max(s, -1, keepdims=True)
+            e = jnp.exp(s - top)
+            total = jnp.sum(e, -1, keepdims=True)
+            out = nn(e.astype(bf16).reshape(TOGETHER * count, kend), v_ref[:kend, cols])
+            out = out.reshape(TOGETHER, count, width) / total
+            level = top + jnp.log(total)
+            mixed = out[0]
+            lane = lax.broadcasted_iota(jnp.int32, (count, BLOCK), 1)
+            levels = st_ref[q0:q1, :]
+            for h in range(TOGETHER):
+                mixed = jnp.where(head == h, out[h], mixed)
+                levels = jnp.where(lane == g * TOGETHER + h, level[h], levels)
+            mixed_ref[q0:q1, cols] = mixed.astype(bf16)
+            st_ref[q0:q1, :] = levels
 
     saves[4].start()
     saves[5].start()
@@ -229,15 +223,48 @@
                     pltpu.make_async_copy(tile, out.at[place - low], sem).start()
 
 
-def back_ffn_kernel(
-    begun, zones, places, spare, back_ref, g_ref, mid_i, n2_i, gu_i, wgu_i, wd_i, *rest
+def backward_kernel(
+    begun, zones, places, spare, length, back_ref, g_ref, cos_ref, sin_ref,
+    x_i, normed_i, q_i, k_i, v_i, st_i, mixed_i, mid_i, n2_i, gu_i, wqkv_i, wout_i, wgu_i, wd_i, *rest
 ):
-    mid_ref_out, gain_ref, *rest = rest[begun:]
+    dx_ref, gain_ref, *rest = rest[begun:]
     tiles_out, rest = rest[: len(zones)], rest[len(zones) :]
-    mid_ref, n2_ref, gu_ref, wgu, wd, ggu, gd, big, zero, sem_in, sem_out, sem_zero = rest
-    loads = copies([(wd_i, wd), (gu_i, gu_ref), (n2_i, n2_ref), (wgu_i, wgu), (mid_i, mid_ref)], sem_in)
-    for load in loads:
-        load.start()
+    (
+        x_ref, normed_ref, q_ref, k_ref, v_ref, st_ref, mixed_ref, mid_ref, n2_ref, gu_ref,
+        wqkv, wout, wgu, wd, gqkv, gout, ggu, gd,
+        turned, bias, levels, sums, big, mixed_back, dproj, zero, sem_in, sem_ffn, sem_out, sem_zero,
+    ) = rest
+    rows = back_ref.shape[0]
+    key_rows = q_ref.shape[0]
+    loads = dict(
+        zip(
+            ("n2", "mid", "wout", "mixed", "q", "k", "v", "st", "normed", "wqkv", "x"),
+            copies(
+                [
+                    (n2_i, n2_ref), (mid_i, mid_ref), (wout_i, wout), (mixed_i, mixed_ref), (q_i, q_ref), (k_i, k_ref), (v_i, v_ref),
+                    (st_i, st_ref), (normed_i, normed_ref), (wqkv_i, wqkv), (x_i, x_ref),
+                ],
+                sem_in,
+            ),
+        )
+    )
+
+    def ffn_loads(t):
+        here = pl.ds(pl.multiple_of(t * FF_STEP, FF_STEP), FF_STEP)
+        there = pl.ds(pl.multiple_of(FF + t * FF_STEP, FF_STEP), FF_STEP)
+        parts = [(wd_i.at[here, :], wd.at[here, :])]
+        for cols in (here, there):
+            parts += [(gu_i.at[:, cols], gu_ref.at[:, cols]), (wgu_i.at[:, cols], wgu.at[:, cols])]
+        return [pltpu.make_async_copy(src, dst, sem_ffn.at[t, i]) for i, (src, dst) in enumerate(parts)]
+
+    loads["n2"].start()
+    for t in range(FF // FF_STEP):
+        for load in ffn_loads(t):
+            load.start()
+    for name, load in loads.items():
+        if name != "n2":
+            load.start()
+    put = functools.partial(put_tiles, places, zones)
     spares = spare.shape[0] - 1
     if spares > 0:
         zero[...] = jnp.zeros(zero.shape, bf16)
@@ -246,13 +273,17 @@
         def _(i):
             pltpu.make_async_copy(zero, tiles_out[0].at[spare[i]], sem_zero).start()
 
+    key = lax.broadcasted_iota(jnp.int32, bias.shape, 0)
+    query = lax.broadcasted_iota(jnp.int32, bias.shape, 1)
+    bias[...] = jnp.where((key <= query) & (key < length[0]), 0.0, masked_score)
     big[...] = jnp.zeros(big.shape, f32)
-    for load in loads[:4]:
-        load.wait()
-    put = functools.partial(put_tiles, places, zones)
+    loads["n2"].wait()
+    turned[...] = n2_ref[...].T
 
     @pl.loop(0, FF // FF_STEP)
     def _(t):
+        for load in ffn_loads(t):
+            load.wait()
         at = pl.multiple_of(t * FF_STEP, FF_STEP)
         here = pl.ds(at, FF_STEP)
         there = pl.ds(FF + at, FF_STEP)
@@ -266,94 +297,61 @@
         d_gate = (d_act * up * (sig * (1.0 + gate * (1.0 - sig)))).astype(bf16)
         d_up = (d_act * silu).astype(bf16)
         gd[here, :] = tn(act, back_ffn).astype(bf16)
-        ggu[:, here] = tn(n2_ref[...], d_gate).astype(bf16)
-        ggu[:, there] = tn(n2_ref[...], d_up).astype(bf16)
+        ggu[:, here] = nn(turned[...], d_gate).astype(bf16)
+        ggu[:, there] = nn(turned[...], d_up).astype(bf16)
         per = FF_STEP // BLOCK
-        put(3, gd, tiles_out, sem_out.at[1], t * per, (t + 1) * per, 0, D // BLOCK)
-        put(2, ggu, tiles_out, sem_out.at[0], 0, D // BLOCK, t * per, per)
-        put(2, ggu, tiles_out, sem_out.at[0], 0, D // BLOCK, FF // BLOCK + t * per, per)
+        put(3, gd, tiles_out, sem_out.at[3], t * per, (t + 1) * per, 0, D // BLOCK)
+        put(2, ggu, tiles_out, sem_out.at[2], 0, D // BLOCK, t * per, per)
+        put(2, ggu, tiles_out, sem_out.at[2], 0, D // BLOCK, FF // BLOCK + t * per, per)
         big[...] += nt(d_gate, wgu[:, here]) + nt(d_up, wgu[:, there])
 
-    loads[4].wait()
-    step, gain = rms_back(big[...], mid_ref[...], g_ref[...])
-    gain_ref[...] = gain
-    mid_ref_out[...] = back_ref[...] + step
-    pltpu.make_async_copy(ggu, ggu, sem_out.at[0]).wait()
-    pltpu.make_async_copy(gd, gd, sem_out.at[1]).wait()
-    if spares > 0:
-
-        @pl.loop(0, spares)
-        def _(i):
-            pltpu.make_async_copy(zero, tiles_out[0].at[spare[i]], sem_zero).wait()
-
-
-def back_attention_kernel(
-    begun, zones, places, length, back_ref, cos_ref, sin_ref,
-    q_i, k_i, v_i, st_i, mixed_i, wout_i, *rest
-):
-    dproj, *rest = rest[begun:]
-    tiles_out, rest = rest[: len(zones)], rest[len(zones) :]
-    (
-        q_ref, k_ref, v_ref, st_ref, mixed_ref, wout,
-        gout, bias, turned, sums, mixed_back, sem_in, sem_out,
-    ) = rest
-    rows = back_ref.shape[0]
-    key_rows = q_ref.shape[0]
-    loads = copies(
-        [
-            (wout_i, wout), (mixed_i, mixed_ref), (q_i, q_ref), (k_i, k_ref), (v_i, v_ref),
-            (st_i, st_ref),
-        ],
-        sem_in,
-    )
-    for load in loads:
-        load.start()
-    put = functools.partial(put_tiles, places, zones)
-    key = lax.broadcasted_iota(jnp.int32, bias.shape, 0)
-    query = lax.broadcasted_iota(jnp.int32, bias.shape, 1)
-    bias[...] = jnp.where((key <= query) & (key < length[0]), 0.0, masked_score)
-    back_attn = back_ref[...].astype(bf16)
-    loads[0].wait()
+    loads["mid"].wait()
+    step, gain = rms_back(big[...], mid_ref[...], g_ref[1:2, :])
+    gain_ref[1:2, :] = gain
+    dx_ref[...] = back_ref[...] + step
+    back_attn = dx_ref[...].astype(bf16)
+    loads["wout"].wait()
     mixed_back[0:rows, :] = nt(back_attn, wout[...]).astype(bf16)
     mixed_back[rows:, :] = jnp.zeros((key_rows - rows, D), bf16)
-    loads[1].wait()
+    loads["mixed"].wait()
     gout[...] = tn(mixed_ref[...], back_attn).astype(bf16)
-    put(1, gout, tiles_out, sem_out, 0, D // BLOCK, 0, D // BLOCK)
-    for load in loads[2:]:
-        load.wait()
-    levels = st_ref[...].T
+    put(1, gout, tiles_out, sem_out.at[1], 0, D // BLOCK, 0, D // BLOCK)
+    for name in ("q", "k", "v", "st"):
+        loads[name].wait()
+    by_head = st_ref[...].T
     for h in range(HEADS):
-        turned[h] = levels[h : h + 1, :]
+        levels[h] = by_head[h : h + 1, :]
 
     @pl.loop(0, HEADS // 2)
     def _(p):
         cols = pl.ds(pl.multiple_of(p * PAIR, PAIR), PAIR)
         low = lax.broadcasted_iota(jnp.int32, (key_rows, PAIR), 1) < HEAD_DIM
 
-        def both(t):
-            return (jnp.where(low, t, 0), jnp.where(low, 0, t))
-
-        qp = q_ref[:, cols]
-        op = mixed_back[:, cols]
-        keys, values, queries, backs = both(k_ref[:, cols]), both(v_ref[:, cols]), both(qp), both(op)
-        sums[...] = jnp.zeros(sums.shape, f32)
+        def stacked(t, n):
+            return jnp.concatenate([jnp.where(low[:n], t[:n], 0), jnp.where(low[:n], 0, t[:n])], 0)
+
+        def chosen(t, n):
+            return jnp.where(low[:n], t[:n], t[n:])
+
         for q0, q1 in query_blocks(key_rows):
-            kend = q1
-            d_query = jnp.zeros((q1 - q0, PAIR), f32)
-            d_key = jnp.zeros((kend, PAIR), f32)
-            d_value = jnp.zeros((kend, PAIR), f32)
-            for h in range(2):
-                level = turned[2 * p + h, :, q0:q1]
-                soft = jnp.exp(nt(keys[h][:kend], qp[q0:q1]) + bias[:kend, q0:q1] - level)
-                d_prob = nt(values[h][:kend], op[q0:q1])
-                row_dot = jnp.sum(soft * d_prob, 0, keepdims=True)
-                d_score = (soft * (d_prob - row_dot)).astype(bf16)
-                d_value += nn(soft.astype(bf16), backs[h][q0:q1])
-                d_key += nn(d_score, queries[h][q0:q1])
-                d_query += tn(d_score, keys[h][:kend])
-            sums[0, q0:q1, :] += d_query * HEAD_DIM ** (-0.5)
-            sums[1, :kend, :] += d_key
-            sums[2, :kend, :] += d_value
+            kend, count = q1, q1 - q0
+            keys, values = k_ref[:kend, cols], v_ref[:kend, cols]
+            queries, backs = q_ref[q0:q1, cols], mixed_back[q0:q1, cols]
+            level = jnp.stack([levels[2 * p + h, :, q0:q1] for h in range(2)], 0)
+            scores = nt(stacked(keys, kend), queries).reshape(2, kend, count)
+            soft = jnp.exp(scores + bias[:kend, q0:q1][None] - level)
+            d_prob = nt(stacked(values, kend), backs).reshape(2, kend, count)
+            row_dot = jnp.sum(soft * d_prob, 1, keepdims=True)
+            d_score = (soft * (d_prob - row_dot)).astype(bf16)
+            d_value = chosen(nn(soft.astype(bf16).reshape(2 * kend, count), backs), kend)
+            d_key = chosen(nn(d_score.reshape(2 * kend, count), queries), kend)
+            d_query = jnp.where(low[:count], tn(d_score[0], keys), tn(d_score[1], keys))
+            sums[0, q0:q1, :] = d_query * HEAD_DIM ** (-0.5)
+            if q0 > 0:
+                sums[1, :q0, :] += d_key[:q0]
+                sums[2, :q0, :] += d_value[:q0]
+            sums[1, q0:kend, :] = d_key[q0:]
+            sums[2, q0:kend, :] = d_value[q0:]
         for part in range(2):
             t = sums[part, 0:rows, :]
             dproj[:, pl.ds(pl.multiple_of(part * D + p * PAIR, PAIR), PAIR)] = (
@@ -361,32 +359,29 @@
             ).astype(bf16)
         dproj[:, pl.ds(pl.multiple_of(2 * D + p * PAIR, PAIR), PAIR)] = sums[2, 0:rows, :].astype(bf16)
 
-    pltpu.make_async_copy(gout, gout, sem_out).wait()
-
-
-def back_qkv_kernel(begun, zones, places, back_ref, g_ref, dproj, x_i, normed_i, wqkv_i, *rest):
-    dx_ref, gain_ref, *rest = rest[begun:]
-    tiles_out, rest = rest[: len(zones)], rest[len(zones) :]
-    x_ref, normed_ref, wqkv, gqkv, big, sem_in, sem_out = rest
-    loads = copies([(normed_i, normed_ref), (wqkv_i, wqkv), (x_i, x_ref)], sem_in)
-    for load in loads:
-        load.start()
-    big[...] = jnp.zeros(big.shape, f32)
-    loads[0].wait()
-    loads[1].wait()
-
-    @pl.loop(0, 3)
-    def _(part):
-        cols = pl.ds(pl.multiple_of(part * D, D), D)
-        gqkv[:, cols] = tn(normed_ref[...], dproj[:, cols]).astype(bf16)
-        put_tiles(places, zones, 0, gqkv, tiles_out, sem_out, 0, D // BLOCK, part * (D // BLOCK), D // BLOCK)
-        big[...] += nt(dproj[:, cols], wqkv[:, cols])
-
-    loads[2].wait()
-    step, gain = rms_back(big[...], x_ref[...], g_ref[...])
-    gain_ref[...] = gain
-    dx_ref[...] = back_ref[...] + step
-    pltpu.make_async_copy(gqkv, gqkv, sem_out).wait()
+    loads["normed"].wait()
+    turned[...] = normed_ref[...].T
+    loads["wqkv"].wait()
+    for part in range(3):
+        cols = slice(part * D, (part + 1) * D)
+        gqkv[:, cols] = nn(turned[...], dproj[:, cols]).astype(bf16)
+        put(0, gqkv, tiles_out, sem_out.at[0], 0, D // BLOCK, part * (D // BLOCK), D // BLOCK)
+        if part == 0:
+            big[...] = nt(dproj[:, cols], wqkv[:, cols])
+        else:
+            big[...] += nt(dproj[:, cols], wqkv[:, cols])
+
+    loads["x"].wait()
+    step, gain = rms_back(big[...], x_ref[...], g_ref[0:1, :])
+    gain_ref[0:1, :] = gain
+    dx_ref[...] += step
+    for m, grad in enumerate((gqkv, gout, ggu, gd)):
+        pltpu.make_async_copy(grad, grad, sem_out.at[m]).wait()
+    if spares > 0:
+
+        @pl.loop(0, spares)
+        def _(i):
+            pltpu.make_async_copy(zero, tiles_out[0].at[spare[i]], sem_zero).wait()
 
 
 def weight_shapes():
@@ -442,84 +437,37 @@
     return [jax.ShapeDtypeStruct((size, BLOCK, BLOCK), bf16) for _, _, size in zones]
 
 
-def in_place(args, begun, zones, first):
-    late = first + len(zones) - len(begun)
-    return {len(args) + i: late + i for i in range(len(begun))}
-
-
-def back_ffn(places, spare, back, gain, saved, zones, begun):
+def backward_layer(places, spare, length, back, gains, cos, sin, saved, zones, begun):
     rows = back.shape[0]
+    key_rows = round_up(rows, BLOCK)
     S = jax.ShapeDtypeStruct
-    args = (places, spare, back, gain) + tuple(saved)
-    wgu, wd = saved[3], saved[4]
+    args = (places, spare, length, back, gains, cos, sin) + tuple(saved)
+    late = 2 + len(zones) - len(begun)
     return pl.pallas_call(
-        functools.partial(back_ffn_kernel, len(begun), zones),
-        out_shape=[S((rows, D), f32), S((1, D), f32)] + tile_arrays(zones),
-        in_specs=[SMEM] * 2 + [VMEM] * 2 + [HBM] * (5 + len(begun)),
+        functools.partial(backward_kernel, len(begun), zones),
+        out_shape=[S((rows, D), f32), S((2, D), f32)] + tile_arrays(zones),
+        in_specs=[SMEM] * 3 + [VMEM] * 4 + [HBM] * (14 + len(begun)),
         out_specs=[VMEM, VMEM] + [HBM] * len(zones),
-        input_output_aliases=in_place(args, begun, zones, 2),
+        input_output_aliases={len(args) + i: late + i for i in range(len(begun))},
         scratch_shapes=[like(s) for s in saved]
-        + [like(wgu), like(wd)]
+        + [pltpu.VMEM(s, bf16) for s in weight_shapes()]
         + [
+            pltpu.VMEM((D, rows), bf16),
+            pltpu.VMEM((key_rows, key_rows), f32),
+            pltpu.VMEM((HEADS, 1, key_rows), f32),
+            pltpu.VMEM((3, key_rows, PAIR), f32),
             pltpu.VMEM((rows, D), f32),
+            pltpu.VMEM((key_rows, D), bf16),
+            pltpu.VMEM((rows, 3 * D), bf16),
             pltpu.VMEM((BLOCK, BLOCK), bf16),
-            pltpu.SemaphoreType.DMA((5,)),
-            pltpu.SemaphoreType.DMA((2,)),
+            pltpu.SemaphoreType.DMA((11,)),
+            pltpu.SemaphoreType.DMA((FF // FF_STEP, 5)),
+            pltpu.SemaphoreType.DMA((4,)),
             pltpu.SemaphoreType.DMA,
         ],
         compiler_params=pltpu.CompilerParams(vmem_limit_bytes=VMEM_BYTES),
-        cost_estimate=cost(4 * rows * (COUNTS[2] + COUNTS[3]) * BLOCK * BLOCK, 30 * 2**20),
-        name="backward_feed_forward",
-    )(*args, *begun)
-
-
-def back_attention(places, length, back, cos, sin, saved, zones, begun):
-    rows = back.shape[0]
-    key_rows = round_up(rows, BLOCK)
-    S = jax.ShapeDtypeStruct
-    args = (places, length, back, cos, sin) + tuple(saved)
-    return pl.pallas_call(
-        functools.partial(back_attention_kernel, len(begun), zones),
-        out_shape=[S((rows, 3 * D), bf16)] + tile_arrays(zones),
-        in_specs=[SMEM] * 2 + [VMEM] * 3 + [HBM] * (6 + len(begun)),
-        out_specs=[VMEM] + [HBM] * len(zones),
-        input_output_aliases=in_place(args, begun, zones, 1),
-        scratch_shapes=[like(s) for s in saved]
-        + [
-            like(saved[5]),
-            pltpu.VMEM((key_rows, key_rows), f32),
-            pltpu.VMEM((HEADS, 1, key_rows), f32),
-            pltpu.VMEM((3, key_rows, PAIR), f32),
-            pltpu.VMEM((key_rows, D), bf16),
-            pltpu.SemaphoreType.DMA((6,)),
-            pltpu.SemaphoreType.DMA,
-        ],
-        compiler_params=pltpu.CompilerParams(vmem_limit_bytes=VMEM_BYTES),
-        cost_estimate=cost(4 * rows * COUNTS[1] * BLOCK * BLOCK + 20 * rows * rows * D, 30 * 2**20),
-        name="backward_attention",
-    )(*args, *begun)
-
-
-def back_qkv(places, back, gain, d_projected, saved, zones, begun):
-    rows = back.shape[0]
-    S = jax.ShapeDtypeStruct
-    args = (places, back, gain, d_projected) + tuple(saved)
-    return pl.pallas_call(
-        functools.partial(back_qkv_kernel, len(begun), zones),
-        out_shape=[S((rows, D), f32), S((1, D), f32)] + tile_arrays(zones),
-        in_specs=[SMEM] + [VMEM] * 3 + [HBM] * (3 + len(begun)),
-        out_specs=[VMEM, VMEM] + [HBM] * len(zones),
-        input_output_aliases=in_place(args, begun, zones, 2),
-        scratch_shapes=[like(s) for s in saved]
-        + [
-            like(saved[2]),
-            pltpu.VMEM((rows, D), f32),
-            pltpu.SemaphoreType.DMA((3,)),
-            pltpu.SemaphoreType.DMA,
-        ],
-        compiler_params=pltpu.CompilerParams(vmem_limit_bytes=VMEM_BYTES),
-        cost_estimate=cost(4 * rows * COUNTS[0] * BLOCK * BLOCK, 20 * 2**20),
-        name="backward_qkv",
+        cost_estimate=cost(4 * rows * PER_LAYER * BLOCK * BLOCK + 20 * rows * rows * D, 60 * 2**20),
+        name="backward_block",
     )(*args, *begun)
 
 
@@ -591,10 +539,9 @@
     return local[:images]
 
 
-EARLY = (22, 18, 38)
-LATE = (18, 12)
-FFN_FIRST = OFFSETS[2]
-LEAST = (PER_LAYER + FFN_FIRST, PER_LAYER, FFN_FIRST)
+EARLY = (36,)
+LATE = (30, 26, 16)
+LEAST = (PER_LAYER,)
 
 
 def chunk_places(slot_of_block, per_owner, me):
@@ -617,15 +564,13 @@
         place = jnp.where(here, 8 * start + owner * size + at, place)
         clean = clean & jnp.all(jnp.where(here, by_owner >= least, True))
         start += size
-    base = 8 * start + core * 4 * sum(LATE)
     for size in LATE:
         half = size // 2
         at = rank - start
         here = (at >= 0) & (at < size)
         spot = jnp.where(at < half, (x * 2 + y) * half + at, 4 * half + (y * 2 + x) * half + at - half)
-        place = jnp.where(here, base + spot, place)
+        place = jnp.where(here, 8 * start + core * 4 * size + spot, place)
         start += size
-        base += 4 * size
     return place.reshape(-1)[slot_of_block], rank, clean
 
 
@@ -672,10 +617,9 @@
 
 
 class Chunk(Bands):
-    def __init__(self, index, kept, sent):
-        size, at = LATE[index], 4 * sum(LATE[:index])
-        self.half = size // 2
-        self.kept, self.sent = kept[at : at + 4 * size], sent[at : at + 4 * size]
+    def __init__(self, kept, sent):
+        self.half = kept.shape[0] // 8
+        self.kept, self.sent = kept, sent
 
     def chip(self, lo, hi):
         lo, hi = lo * self.half, hi * self.half
@@ -802,77 +746,55 @@
         places, ranks, clean = chunk_places(slot_of_block, per_owner, me)
         rank = lax.dynamic_index_in_dim(ranks, me, 0, keepdims=False)
         ends = [8 * sum(EARLY[: i + 1]) for i in range(len(EARLY))]
-        late = 4 * sum(LATE)
-        bounds = [0] + ends + [ends[-1] + late, ends[-1] + 2 * late]
+        bounds = [0] + ends
+        for size in LATE:
+            bounds += [bounds[-1] + 4 * size, bounds[-1] + 8 * size]
         zones = tuple((low, high, high - low) for low, high in zip(bounds, bounds[1:]))
     else:
         places, rank = slot_of_block, jnp.arange(per_owner, dtype=jnp.int32)
         zones = ((0, slot_count, slot_count),)
 
-    def backward(layer, back, tiles, zones, freeze=lambda kernel, tiles, zones: (tiles, zones)):
-        normed, q, k, v, st, mixed, mid, n2, gu, wqkv, wout, wgu, wd = saves[layer]
-        slots = places[layer * PER_LAYER : (layer + 1) * PER_LAYER]
+    def backward(layer, back, tiles, zones):
         fill = spare if layer == LAYERS - 1 else spare[-1:]
-        first = 3 * (LAYERS - 1 - layer)
-        back, gain_two, *tiles = back_ffn(
-            slots, fill, back, gain_values[2 * layer + 1 : 2 * layer + 2], (mid, n2, gu, wgu, wd),
-            zones, tiles,
+        back, gains, *tiles = backward_layer(
+            places[layer * PER_LAYER : (layer + 1) * PER_LAYER], fill, length, back,
+            gain_values[2 * layer : 2 * layer + 2], cos, sin, (inputs[layer], *saves[layer]), zones, tiles,
         )
-        tiles, zones = freeze(first, tiles, zones)
-        d_projected, *tiles = back_attention(
-            slots, length, back, cos, sin, (q, k, v, st, mixed, wout), zones, tiles
-        )
-        tiles, zones = freeze(first + 1, tiles, zones)
-        back, gain_one, *tiles = back_qkv(
-            slots, back, gain_values[2 * layer : 2 * layer + 1], d_projected,
-            (inputs[layer], normed, wqkv), zones, tiles,
-        )
-        tiles, zones = freeze(first + 2, tiles, zones)
-        return back, [gain_one, gain_two], tiles, zones
+        return back, gains, tiles
 
     if by_permutes:
-        early, early_sums = [], []
-
-        def freeze(kernel, tiles, zones):
-            if kernel not in (0, 2, 3):
-                return tiles, zones
-            at = 0 if kernel == 0 else 1
-            nonlocal output_blocks
-            early.append(tiles[at])
-            ready, *early_sums[:] = lax.optimization_barrier((tiles[at], *early_sums))
-            if kernel == 0:
-                ready, *output_blocks = lax.optimization_barrier((ready, *output_blocks))
-            early_sums.append(lax.psum_scatter(ready, "dp", scatter_dimension=0, tiled=True))
-            missed = (0, zones[at][1], ends[-1])
-            return tiles[:at] + tiles[at + 1 :], (missed,) + zones[at + 1 :]
-
-        back, gains_top, tiles, zones = backward(1, back, [], zones, freeze)
-        back, gains_bottom, tiles, zones = backward(0, back, tiles, zones, freeze)
-        missed, kept, sent = tiles
-        gains = jnp.concatenate(gains_bottom + gains_top, 0).astype(bf16).reshape(-1, BLOCK)
+        back, gains_top, tiles = backward(1, back, [], zones)
+        early = tiles[:1]
+        ready, *output_blocks = lax.optimization_barrier((tiles[0], *output_blocks))
+        early_sums = [lax.psum_scatter(ready, "dp", scatter_dimension=0, tiled=True)]
+        back, gains_bottom, tiles = backward(0, back, tiles[1:], zones)
+        missed, *late = tiles
+        gains = jnp.concatenate([gains_bottom, gains_top], 0).astype(bf16).reshape(-1, BLOCK)
         gains = jnp.pad(gains, ((0, BLOCK - gains.shape[0]), (0, 0)))[None]
         sequence = Sequence()
-        one, two = [Chunk(i, kept, sent) for i in range(len(LATE))]
-        top, bottom = Bands(), Bands()
-        sequence.arrived[top] = (jnp.concatenate(early_sums[:2] + [gains], 0),)
-        sequence.arrived[bottom] = (early_sums[2],)
-        input_blocks = send_rows(back)
-        sequence.round((one, "core"), (two, "core"), (top, "meet"))
+        chunks = [Chunk(*late[2 * i : 2 * i + 2]) for i in range(len(LATE))]
+        one, two, three = chunks
+        top = Bands()
+        sequence.arrived[top] = (jnp.concatenate([early_sums[0], gains], 0),)
+        sequence.round((one, "core"), (two, "core"), (three, "core"))
         sequence.round((one, "plane"))
+        sequence.round((top, "meet"))
         sequence.round((one, "turn"))
-        input_blocks = sequence.wait_for(*input_blocks)
         sequence.round((top, "part"))
-        sequence.round((bottom, "meet"))
         sequence.round((one, "meet"), (two, "plane"))
         sequence.round((two, "turn"))
-        sequence.round((top, "last"), (bottom, "part"))
-        sequence.round((two, "meet"))
-        sequence.round((one, "part"))
-        sequence.round((bottom, "last"), (top, "end"))
+        sequence.round((one, "part"), (top, "last"))
+        sequence.round((two, "meet"), (three, "plane"))
+        sequence.round((three, "turn"))
         sequence.round((two, "part"), (one, "last"))
-        sequence.round((two, "last"), (bottom, "end"))
-        sequence.round((one, "end"), (two, "end"))
-        early_total = jnp.concatenate([top.total[:-1], bottom.total], 0)
+        sequence.round((three, "meet"), (top, "end"))
+        sequence.round((two, "last"), (three, "part"))
+        (back,) = sequence.wait_for(back)
+        input_blocks = send_rows(back)
+        sequence.round((three, "last"), (one, "end"))
+        sequence.round((two, "end"))
+        sequence.round((three, "end"))
+        early_total = top.total[:-1]
 
         def again(trip, total):
             _, spare_tiles, *parts = lax.optimization_barrier((trip, missed, *early))
@@ -886,21 +808,27 @@
             return lax.psum(jnp.concatenate(sums, 0), "band")
 
         early_total = lax.fori_loop(0, jnp.where(clean, 0, 1), again, early_total)
-        owned = jnp.concatenate([early_total, one.total, two.total], 0)
+        owned = jnp.concatenate([early_total] + [chunk.total for chunk in chunks], 0)
         gain_total = top.total[-1].astype(f32)[: gain_values.size // BLOCK].reshape(-1, D)
-        gain_total = lax.psum(gain_total, "dp")
     else:
-        back, gains_top, tiles, _ = backward(1, back, [], zones)
-        back, gains_bottom, tiles, _ = backward(0, back, tiles, zones)
+        back, gains_top, tiles = backward(1, back, [], zones)
+        back, gains_bottom, tiles = backward(0, back, tiles, zones)
         owned = lax.psum_scatter(tiles[0], "dp", scatter_dimension=0, tiled=True)
         owned = lax.psum(owned, "band")
-        gain_total = lax.psum(jnp.concatenate(gains_bottom + gains_top, 0), ("dp", "band"))
+        gain_total = lax.psum(jnp.concatenate([gains_bottom, gains_top], 0), ("dp", "band"))
         input_blocks = send_rows(back)
 
     layer_output = at_bands(output_blocks, images, bands, band)
     input_grad = at_bands(input_blocks[:bands], images, bands, band)
     owned_f = owned.astype(f32)
-    owned_squares = lax.psum(jnp.sum(owned_f * owned_f), "dp")
+    owned_squares = jnp.sum(owned_f * owned_f)
+    if by_permutes:
+        last = jnp.concatenate([gain_total.reshape(-1, BLOCK), jnp.broadcast_to(owned_squares, (1, BLOCK))], 0)
+        for pairs in (CORE, ALONG_X, ALONG_Y):
+            last = last + lax.ppermute(last, "dp", pairs)
+        gain_total, owned_squares = last[:-1].reshape(gain_values.shape), last[-1, 0]
+    else:
+        owned_squares = lax.psum(owned_squares, "dp")
     grad_norm = jnp.sqrt(owned_squares + jnp.sum(gain_total * gain_total))
     factor = jnp.minimum(1.0, clip_limit / grad_norm)
     weight_grads, new_statistics, new_master, master_copy = optimizer(

time: 670 us -> 614 us (0.916)
  Pallas kernels: 235 us -> 198 us
  blocking collectives: 23.4 us -> 0 us
  other arithmetic: 42.6 us -> 50.6 us
  local copies, waits for them, and re-layouts: 44.7 us -> 38 us
    reduce_scatter x3 -> x1, waiting for transfers between devices: 47.1 us -> 9.47 us  [shards(): lax.psum_scatter(ready, 'dp', scatter_dimension=0, tiled=True)]
    ppermute x4, waiting for transfers between devices: 12.4 us -> 36.8 us  [go_meet(): lax.ppermute(plane, 'band', [(2, 1)])]
    pallas_call x6 -> x2, Pallas kernels: 138 us -> 114 us  [backward_layer(): pl.pallas_call(functools.partial(backward_kernel, len(begun), zones), out...]
    psum x1 -> x0, blocking collectives: 23.4 us -> none  [shards(): owned_squares = lax.psum(jnp.sum(owned_f * owned_f), 'dp')]
    ppermute x4, waiting for transfers between devices: 15.2 us -> 0.11 us  [go_part(): lax.ppermute(total, 'band', [(1, 2)])]
    pallas_call x2, Pallas kernels: 66.6 us -> 53.9 us  [forward_layer(): pl.pallas_call(forward_kernel, out_shape=[S((rows, D), f32)] + saved, in_...]
    ppermute x4 -> x6, waiting for transfers between devices: 15.8 us -> 27.1 us  [go_plane(): lax.ppermute(send_x, 'dp', ALONG_X)]
  transfers between devices with their start and end apart: 43 -> 49, of which waited for: 19 -> 22; matrix products, arithmetic and copies ran while one was open for 10% -> 12% of each run, Pallas kernels for 21% -> 19%
where the time goes in v7:
time: 614 us; the launch traced here: 607 us
  waiting for transfers between devices  216 us (35%)
  Pallas kernels  198 us (32%)
  starting transfers between devices  84.8 us (14%)
  other arithmetic  50.6 us (8%)
  local copies, waits for them, and re-layouts  38 us (6%)
  between operations  18.7 us (3%)
    pallas_call x2, Pallas kernels, backward_layer(): pl.pallas_call(functools.partial(backward_kernel, len(begun), zones), out...  114 us
    all_gather x1, waiting for transfers between devices, shards(): gathered = lax.all_gather(master.astype(bf16), 'dp', axis=0, tiled=True)  87.7 us
    pallas_call x2, Pallas kernels, forward_layer(): pl.pallas_call(forward_kernel, out_shape=[S((rows, D), f32)] + saved, in_...  53.9 us
    ppermute x4, waiting for transfers between devices, go_meet(): lax.ppermute(plane, 'band', [(2, 1)])  36.8 us
    pallas_call x1, Pallas kernels, optimizer(): pl.pallas_call(optimizer_kernel, grid=(count // per,), out_shape=[S(maste...  30.7 us
    ppermute x6, waiting for transfers between devices, go_plane(): lax.ppermute(send_x, 'dp', ALONG_X)  27.1 us
    ppermute x4, waiting for transfers between devices, go_last(): return (lax.ppermute(to_third, 'band', [(2, 3)]),)  22.3 us
    ppermute x6, starting transfers between devices, send_to_bands(): block = lax.ppermute(block, 'band', pairs)  21.7 us
  transfers between devices with their start and end apart: 49, of which 22 were waited for; matrix products, arithmetic and copies ran while one was open for 12% of the time, Pallas kernels for 19%

profile of v7, /device:TPU:16, one launch (start us, length us, event | category | flops | bytes accessed | tf_op | source)
XLA Modules:
  0.0 606.7 jit_solution(12182568512834198823)
XLA Ops:
  7.2 5.6 convert_element_type.307
  16.9 4.4 collective-permute-start.1
  25.5 5.3 scatter_custom_fusion
  34.6 3.9 gather_fusion
  42.0 6.4 %collective-permute-done.1 = bf16[2,145,768]{2,1,0:T(8,128)(2,1)} collective-permute-done((bf16[2,145,768]{2,1,0:T(8,128)(2,1)S(1)}, bf16[2,145,768]{2,1,0:T(8,128)(2,1)}, u32[]{:S(2)}, u32[]{:S(2)}) %collective-permute-start.1) | collective-permute-done | bytes 445472 | tf_op jit(solution)/shard_map/ppermute | solution.py:519
  49.5 8.9 %collective-permute-done.2 = bf16[2,145,768]{2,1,0:T(8,128)(2,1)} collective-permute-done((bf16[2,145,768]{2,1,0:T(8,128)(2,1)S(1)}, bf16[2,145,768]{2,1,0:T(8,128)(2,1)}, u32[]{:S(2)}, u32[]{:S(2)}) %collective-permute-start.2) | collective-permute-done | bytes 445472 | tf_op jit(solution)/shard_map/ppermute | solution.py:519
  65.0 87.7 %all-gather.2.cloned.1.call-done.w_hbm = bf16[864,128,128]{2,1,0:T(8,128)(2,1)} async-done(((bf16[108,128,128]{2,1,0:T(8,128)(2,1)}), bf16[864,128,128]{2,1,0:T(8,128)(2,1)}) %all-gather.2.cloned.1.call-update) | async-done | bytes 28311568 | tf_op jit(solution)/shard_map/all_gather | solution.py:704
  152.7 26.7 %forward_block.2 = (f32[592,768]{1,0:T(8,128)}, bf16[592,768]{1,0:T(8,128)(2,1)}, bf16[640,768]{1,0:T(8,128)(2,1)}, bf16[640,768]{1,0:T(8,128)(2,1)}, bf16[640,7...) custom-call(s32[432]{0:T(512)} %get-tuple-element.284.slots, ...), custom_call_target="tpu_custom_call" | custom-call | flops 8380219392 | bytes 41943040 | tf_op jit(solution)/shard_map/forward_block/pallas_call | solution.py:419
  179.4 27.2 %forward_block.3 = (f32[592,768]{1,0:T(8,128)}, bf16[592,768]{1,0:T(8,128)(2,1)}, bf16[640,768]{1,0:T(8,128)(2,1)}, bf16[640,768]{1,0:T(8,128)(2,1)}, bf16[640,7...) custom-call(s32[432]{0:T(512)} %get-tuple-element.283.slots, ...), custom_call_target="tpu_custom_call" | custom-call | flops 8380219392 | bytes 41943040 | tf_op jit(solution)/shard_map/forward_block/pallas_call | solution.py:419
  209.2 3.4 collective-permute-start.3
  217.3 56.9 %backward_block.2 = (f32[592,768]{1,0:T(8,128)}, f32[2,768]{1,0:T(2,128)}, bf16[288,128,128]{2,1,0:T(8,128)(2,1)}, bf16[120,128,128]{2,1,0:T(8,128)(2,1)}, bf16[...) custom-call(s32[432]{0:T(512)} %get-tuple-element.282.places, ...), custom_call_target="tpu_custom_call" | custom-call | flops 22143565824 | bytes 62914560 | tf_op jit(solution)/shard_map/backward_block/pallas_call | solution.py:446
  275.1 56.9 %backward_block.3 = (f32[592,768]{1,0:T(8,128)}, f32[2,768]{1,0:T(2,128)}, bf16[288,128,128]{2,1,0:T(8,128)(2,1)}, bf16[120,128,128]{2,1,0:T(8,128)(2,1)}, bf16[...) custom-call(s32[432]{0:T(512)} %get-tuple-element.281.places, ...), custom_call_target="tpu_custom_call", output_to_operand_aliasing={{3}: (21, {}), {4}: (22, {}), {5}: (23, {}), {6}: (24, {}),... | custom-call | flops 22143565824 | bytes 62914560 | tf_op jit(solution)/shard_map/backward_block/pallas_call | solution.py:446
  333.3 5.9 collective-permute-done.6
  339.2 3.9 add_convert_fusion.2
  345.1 9.5 %reduce-scatter.3.cloned.1.call-done = bf16[36,128,128]{2,1,0:T(8,128)(2,1)} async-done(((bf16[288,128,128]{2,1,0:T(8,128)(2,1)}), bf16[36,128,128]{2,1,0:T(8,128)(2,1)}) %reduce-scatter.3.cloned.1.call-update) | async-done | bytes 1179664 | tf_op jit(solution)/shard_map/reduce_scatter | solution.py:769
  358.1 12.5 %collective-permute-done.7 = bf16[30,128,128]{2,1,0:T(8,128)(2,1)S(1)} collective-permute-done((bf16[30,128,128]{2,1,0:T(8,128)(2,1)}, bf16[30,128,128]{2,1,0:T(8,128)(2,1)S(1)}, u32[]{:S(2)}, u32[]{:S(2)}) %collective-permute-start.7) | collective-permute-done | bytes 983072 | tf_op jit(solution)/shard_map/ppermute | solution.py:639
  374.6 9.1 %collective-permute-done.13 = bf16[37,128,128]{2,1,0:T(8,128)(2,1)S(1)} collective-permute-done((bf16[37,128,128]{2,1,0:T(8,128)(2,1)S(1)}, bf16[37,128,128]{2,1,0:T(8,128)(2,1)S(1)}, u32[]{:S(2)}, u32[]{:S(2)}) %collective-permute-start.13) | collective-permute-done | bytes 1212448 | tf_op jit(solution)/shard_map/ppermute | solution.py:592
  395.2 13.4 %collective-permute-done.14 = bf16[26,128,128]{2,1,0:T(8,128)(2,1)S(1)} collective-permute-done((bf16[26,128,128]{2,1,0:T(8,128)(2,1)S(1)}, bf16[26,128,128]{2,1,0:T(8,128)(2,1)S(1)}, u32[]{:S(2)}, u32[]{:S(2)}) %collective-permute-start.14) | collective-permute-done | bytes 852000 | tf_op jit(solution)/shard_map/ppermute | solution.py:639
  409.3 3.3 collective-permute-start.20
  415.2 15.9 %collective-permute-done.20 = bf16[30,128,128]{2,1,0:T(8,128)(2,1)S(1)} collective-permute-done((bf16[30,128,128]{2,1,0:T(8,128)(2,1)S(1)}, bf16[30,128,128]{2,1,0:T(8,128)(2,1)S(1)}, u32[]{:S(2)}, u32[]{:S(2)}) %collective-permute-start.20) | collective-permute-done | bytes 983072 | tf_op jit(solution)/shard_map/ppermute | solution.py:592
  433.8 6.7 %collective-permute-done.17 = bf16[13,128,128]{2,1,0:T(8,128)(2,1)S(1)} collective-permute-done((bf16[13,128,128]{2,1,0:T(8,128)(2,1)S(1)}, bf16[13,128,128]{2,1,0:T(8,128)(2,1)S(1)}, u32[]{:S(2)}, u32[]{:S(2)}) %collective-permute-start.17) | collective-permute-done | bytes 426016 | tf_op jit(solution)/shard_map/ppermute | solution.py:639
  452.7 6.2 %collective-permute-start.24 = (bf16[26,128,128]{2,1,0:T(8,128)(2,1)}, bf16[26,128,128]{2,1,0:T(8,128)(2,1)}, u32[]{:S(2)}, u32[]{:S(2)}) collective-permute-start(bf16[26,128,128]{2,1,0:T(8,128)(2,1)} %pad_maximum_fusion.3), channel_id=1, source_target_pairs={{2,1},{6,5},{10,9},{14,13},{18,17},{22,21},{26,25},{30,29}} | collective-permute-start | bytes 2555912 | tf_op jit(solution)/shard_map/ppermute | solution.py:592
  464.1 7.8 %collective-permute-done.24 = bf16[26,128,128]{2,1,0:T(8,128)(2,1)} collective-permute-done((bf16[26,128,128]{2,1,0:T(8,128)(2,1)}, bf16[26,128,128]{2,1,0:T(8,128)(2,1)}, u32[]{:S(2)}, u32[]{:S(2)}) %collective-permute-start.24) | collective-permute-done | bytes 852000 | tf_op jit(solution)/shard_map/ppermute | solution.py:592
  480.8 5.1 collective-permute-start.35
  488.5 4.0 collective-permute-done.35
  502.2 2.5 slice.338
  510.1 4.9 collective-permute-start.37
  515.0 6.8 %collective-permute-start.38 = (bf16[145,768]{1,0:T(8,128)(2,1)}, bf16[145,768]{1,0:T(8,128)(2,1)}, u32[]{:S(2)}, u32[]{:S(2)}) collective-permute-start(bf16[145,768]{1,0:T(8,128)(2,1)} %get-tuple-element.268), channel_id=1, source_target_pairs={{0,3},{1,0},{2,1},{4,7},{5,4},{6,5},{8,11},{9,8},{10,9},{12,15},{1... | collective-permute-start | bytes 668168 | tf_op jit(solution)/shard_map/ppermute | solution.py:530
  524.6 13.8 %collective-permute-done.42 = bf16[26,128,128]{2,1,0:T(8,128)(2,1)} collective-permute-done((bf16[26,128,128]{2,1,0:T(8,128)(2,1)}, bf16[26,128,128]{2,1,0:T(8,128)(2,1)}, u32[]{:S(2)}, u32[]{:S(2)}) %collective-permute-start.42) | collective-permute-done | bytes 852000 | tf_op jit(solution)/shard_map/ppermute | solution.py:606
  539.8 7.4 %collective-permute-done.43 = bf16[16,128,128]{2,1,0:T(8,128)(2,1)S(1)} collective-permute-done((bf16[16,128,128]{2,1,0:T(8,128)(2,1)}, bf16[16,128,128]{2,1,0:T(8,128)(2,1)S(1)}, u32[]{:S(2)}, u32[]{:S(2)}) %collective-permute-start.43) | collective-permute-done | bytes 524320 | tf_op jit(solution)/shard_map/ppermute | solution.py:606
  549.3 5.0 multiply_reduce_fusion
  567.6 30.7 %optimizer.1 = (f32[108,128,128]{2,1,0:T(8,128)}, f32[108,2,128,128]{3,2,1,0:T(8,128)}, f32[108,128,128]{2,1,0:T(8,128)}, bf16[108,128,128]{2,1,0:T(8,128)(2,1)}) custom-call(f32[1]{0:T(128)} %bitcast.28.factor, s32[108]{0:T(128)} %dynamic-slice_reduce_fusion.rank, bf16[108,128,128]{2,1,0:T(8,128)(2,1)} %get-tuple-element.243.g_ref, f32[108,128,128]{2,1,0:T(8,128)} %m_ref.1, ...), custom_call_target="tpu_custom_call" | custom-call | tf_op jit(solution)/shard_map/optimizer/pallas_call | solution.py:495
  (238 shorter events, 120.7 us)
Async XLA Ops:
  7.2 145.5 %all-gather.2.cloned.1.call-start = ((), (), s32[]{:S(2)}) async-start(), calls=%async_computation.2 | async-start | bytes 31850496 | tf_op jit(solution)/shard_map/all_gather | solution.py:704
  12.9 341.7 %reduce-scatter.3.cloned.1.call-start = ((), (), s32[]{:S(2)}) async-start(), calls=%async_computation.3 | async-start | bytes 10616832 | tf_op jit(solution)/shard_map/reduce_scatter | solution.py:769
  15.4 25.5 %collective-permute-start = (bf16[2,145,768]{2,1,0:T(8,128)(2,1)}, bf16[2,145,768]{2,1,0:T(8,128)(2,1)}, u32[]{:S(2)}, u32[]{:S(2)}) collective-permute-start(bf16[2,145,768]{2,1,0:T(8,128)(2,1)} %get-tuple-element.266), channel_id=1, source_target_pairs={{0,1},{1,2},{3,0},{4,5},{5,6},{7,4},{8,9},{9,10},{11,8},{12,13},{1... | collective-permute-start | bytes 1336328 | tf_op jit(solution)/shard_map/ppermute | solution.py:519
  16.9 31.6 %collective-permute-start.1 = (bf16[2,145,768]{2,1,0:T(8,128)(2,1)S(1)}, bf16[2,145,768]{2,1,0:T(8,128)(2,1)}, u32[]{:S(2)}, u32[]{:S(2)}) collective-permute-start(bf16[2,145,768]{2,1,0:T(8,128)(2,1)S(1)} %get-tuple-element.265), channel_id=1, source_target_pairs={{0,2},{2,0},{3,1},{4,6},{6,4},{7,5},{8,10},{10,8},{11,9},{12,14},{... | collective-permute-start | bytes 1336328 | tf_op jit(solution)/shard_map/ppermute | solution.py:519
  21.3 37.1 %collective-permute-start.2 = (bf16[2,145,768]{2,1,0:T(8,128)(2,1)S(1)}, bf16[2,145,768]{2,1,0:T(8,128)(2,1)}, u32[]{:S(2)}, u32[]{:S(2)}) collective-permute-start(bf16[2,145,768]{2,1,0:T(8,128)(2,1)S(1)} %get-tuple-element.264), channel_id=1, source_target_pairs={{1,0},{2,1},{3,2},{5,4},{6,5},{7,6},{9,8},{10,9},{11,10},{13,12},{... | collective-permute-start | bytes 1336328 | tf_op jit(solution)/shard_map/ppermute | solution.py:519
  209.2 65.0 %collective-permute-start.3 = (bf16[145,768]{1,0:T(8,128)(2,1)S(1)}, bf16[145,768]{1,0:T(8,128)(2,1)S(1)}, u32[]{:S(2)}, u32[]{:S(2)}) collective-permute-start(bf16[145,768]{1,0:T(8,128)(2,1)S(1)} %get-tuple-element.274), channel_id=1, source_target_pairs={{0,1},{1,2},{2,3},{4,5},{5,6},{6,7},{8,9},{9,10},{10,11},{12,13},{... | collective-permute-start | bytes 668168 | tf_op jit(solution)/shard_map/ppermute | solution.py:530
  212.6 61.6 %collective-permute-start.4 = (bf16[145,768]{1,0:T(8,128)(2,1)S(1)}, bf16[145,768]{1,0:T(8,128)(2,1)S(1)}, u32[]{:S(2)}, u32[]{:S(2)}) collective-permute-start(bf16[145,768]{1,0:T(8,128)(2,1)S(1)} %get-tuple-element.273), channel_id=1, source_target_pairs={{0,2},{1,3},{2,0},{4,6},{5,7},{6,4},{8,10},{9,11},{10,8},{12,14},{... | collective-permute-start | bytes 668168 | tf_op jit(solution)/shard_map/ppermute | solution.py:530
  215.1 59.2 %collective-permute-start.5 = (bf16[145,768]{1,0:T(8,128)(2,1)S(1)}, bf16[145,768]{1,0:T(8,128)(2,1)S(1)}, u32[]{:S(2)}, u32[]{:S(2)}) collective-permute-start(bf16[145,768]{1,0:T(8,128)(2,1)S(1)} %get-tuple-element.272), channel_id=1, source_target_pairs={{0,3},{1,0},{2,1},{4,7},{5,4},{6,5},{8,11},{9,8},{10,9},{12,15},{1... | collective-permute-start | bytes 668168 | tf_op jit(solution)/shard_map/ppermute | solution.py:530
  332.1 52.2 %collective-permute-start.11 = (bf16[104,128,128]{2,1,0:T(8,128)(2,1)}, bf16[104,128,128]{2,1,0:T(8,128)(2,1)}, u32[]{:S(2)}, u32[]{:S(2)}) collective-permute-start(bf16[104,128,128]{2,1,0:T(8,128)(2,1)} %get-tuple-element.180), channel_id=1, source_target_pairs={{0,4},{4,0},{8,12},{12,8},{16,20},{20,16},{24,28},{28,24},{1,5},{5... | collective-permute-start | bytes 10223624 | tf_op jit(solution)/shard_map/ppermute | solution.py:632
  343.1 27.5 %collective-permute-start.7 = (bf16[30,128,128]{2,1,0:T(8,128)(2,1)}, bf16[30,128,128]{2,1,0:T(8,128)(2,1)S(1)}, u32[]{:S(2)}, u32[]{:S(2)}) collective-permute-start(bf16[30,128,128]{2,1,0:T(8,128)(2,1)} %get-tuple-element.249), channel_id=1, source_target_pairs={{0,8},{4,12},{8,0},{12,4},{16,24},{20,28},{24,16},{28,20},{1,9},{5... | collective-permute-start | bytes 2949128 | tf_op jit(solution)/shard_map/ppermute | solution.py:639
  344.5 26.1 %collective-permute-start.8 = (bf16[30,128,128]{2,1,0:T(8,128)(2,1)S(1)}, bf16[30,128,128]{2,1,0:T(8,128)(2,1)S(1)}, u32[]{:S(2)}, u32[]{:S(2)}) collective-permute-start(bf16[30,128,128]{2,1,0:T(8,128)(2,1)S(1)} %get-tuple-element.248), channel_id=1, source_target_pairs={{0,16},{4,20},{8,24},{12,28},{16,0},{20,4},{24,8},{28,12},{1,17},{... | collective-permute-start | bytes 2949128 | tf_op jit(solution)/shard_map/ppermute | solution.py:639
  355.9 18.7 %collective-permute-start.12 = (bf16[37,128,128]{2,1,0:T(8,128)(2,1)S(1)}, bf16[37,128,128]{2,1,0:T(8,128)(2,1)S(1)}, u32[]{:S(2)}, u32[]{:S(2)}) collective-permute-start(bf16[37,128,128]{2,1,0:T(8,128)(2,1)S(1)} %pad_maximum_fusion.1), channel_id=1, source_target_pairs={{0,1},{4,5},{8,9},{12,13},{16,17},{20,21},{24,25},{28,29}} | collective-permute-start | bytes 3637256 | tf_op jit(solution)/shard_map/ppermute | solution.py:592
  356.7 27.0 %collective-permute-start.13 = (bf16[37,128,128]{2,1,0:T(8,128)(2,1)S(1)}, bf16[37,128,128]{2,1,0:T(8,128)(2,1)S(1)}, u32[]{:S(2)}, u32[]{:S(2)}) collective-permute-start(bf16[37,128,128]{2,1,0:T(8,128)(2,1)S(1)} %pad_maximum_fusion.1), channel_id=1, source_target_pairs={{2,1},{6,5},{10,9},{14,13},{18,17},{22,21},{26,25},{30,29}} | collective-permute-start | bytes 3637256 | tf_op jit(solution)/shard_map/ppermute | solution.py:592
  389.0 19.6 %collective-permute-start.14 = (bf16[26,128,128]{2,1,0:T(8,128)(2,1)S(1)}, bf16[26,128,128]{2,1,0:T(8,128)(2,1)S(1)}, u32[]{:S(2)}, u32[]{:S(2)}) collective-permute-start(bf16[26,128,128]{2,1,0:T(8,128)(2,1)S(1)} %get-tuple-element.255), channel_id=1, source_target_pairs={{0,8},{4,12},{8,0},{12,4},{16,24},{20,28},{24,16},{28,20},{1,9},{5... | collective-permute-start | bytes 2555912 | tf_op jit(solution)/shard_map/ppermute | solution.py:639
  389.6 19.7 %collective-permute-start.15 = (bf16[26,128,128]{2,1,0:T(8,128)(2,1)S(1)}, bf16[26,128,128]{2,1,0:T(8,128)(2,1)S(1)}, u32[]{:S(2)}, u32[]{:S(2)}) collective-permute-start(bf16[26,128,128]{2,1,0:T(8,128)(2,1)S(1)} %get-tuple-element.254), channel_id=1, source_target_pairs={{0,16},{4,20},{8,24},{12,28},{16,0},{20,4},{24,8},{28,12},{1,17},{... | collective-permute-start | bytes 2555912 | tf_op jit(solution)/shard_map/ppermute | solution.py:639
  391.0 42.9 %collective-permute-start.18 = (bf16[64,128,128]{2,1,0:T(8,128)(2,1)S(1)}, bf16[64,128,128]{2,1,0:T(8,128)(2,1)S(1)}, u32[]{:S(2)}, u32[]{:S(2)}) collective-permute-start(bf16[64,128,128]{2,1,0:T(8,128)(2,1)S(1)} %copy-done.27), channel_id=1, source_target_pairs={{0,4},{4,0},{8,12},{12,8},{16,20},{20,16},{24,28},{28,24},{1,5},{5... | collective-permute-start | bytes 6291464 | tf_op jit(solution)/shard_map/ppermute | solution.py:632
  391.0 42.4 %collective-permute-start.21 = (bf16[37,128,128]{2,1,0:T(8,128)(2,1)S(1)}, bf16[37,128,128]{2,1,0:T(8,128)(2,1)S(1)}, u32[]{:S(2)}, u32[]{:S(2)}) collective-permute-start(bf16[37,128,128]{2,1,0:T(8,128)(2,1)S(1)} %add_convert_fusion), channel_id=1, source_target_pairs={{1,0},{5,4},{9,8},{13,12},{17,16},{21,20},{25,24},{29,28}} | collective-permute-start | bytes 3637256 | tf_op jit(solution)/shard_map/ppermute | solution.py:599
  391.7 41.6 %collective-permute-start.22 = (bf16[37,128,128]{2,1,0:T(8,128)(2,1)S(1)}, bf16[37,128,128]{2,1,0:T(8,128)(2,1)}, u32[]{:S(2)}, u32[]{:S(2)}) collective-permute-start(bf16[37,128,128]{2,1,0:T(8,128)(2,1)S(1)} %add_convert_fusion), channel_id=1, source_target_pairs={{1,2},{5,6},{9,10},{13,14},{17,18},{21,22},{25,26},{29,30}} | collective-permute-start | bytes 3637256 | tf_op jit(solution)/shard_map/ppermute | solution.py:599
  409.3 21.8 %collective-permute-start.20 = (bf16[30,128,128]{2,1,0:T(8,128)(2,1)S(1)}, bf16[30,128,128]{2,1,0:T(8,128)(2,1)S(1)}, u32[]{:S(2)}, u32[]{:S(2)}) collective-permute-start(bf16[30,128,128]{2,1,0:T(8,128)(2,1)S(1)} %pad_maximum_fusion.2), channel_id=1, source_target_pairs={{2,1},{6,5},{10,9},{14,13},{18,17},{22,21},{26,25},{30,29}} | collective-permute-start | bytes 2949128 | tf_op jit(solution)/shard_map/ppermute | solution.py:592
  414.1 19.7 %collective-permute-start.16 = (bf16[13,128,128]{2,1,0:T(8,128)(2,1)S(1)}, bf16[13,128,128]{2,1,0:T(8,128)(2,1)S(1)}, u32[]{:S(2)}, u32[]{:S(2)}) collective-permute-start(bf16[13,128,128]{2,1,0:T(8,128)(2,1)S(1)} %get-tuple-element.253), channel_id=1, source_target_pairs={{0,8},{4,12},{8,0},{12,4},{16,24},{20,28},{24,16},{28,20},{1,9},{5... | collective-permute-start | bytes 1277960 | tf_op jit(solution)/shard_map/ppermute | solution.py:639
  443.2 29.0 %collective-permute-start.25 = (bf16[30,128,128]{2,1,0:T(8,128)(2,1)S(1)}, bf16[30,128,128]{2,1,0:T(8,128)(2,1)}, u32[]{:S(2)}, u32[]{:S(2)}) collective-permute-start(bf16[30,128,128]{2,1,0:T(8,128)(2,1)S(1)} %add_convert_fusion.1), channel_id=1, source_target_pairs={{1,0},{5,4},{9,8},{13,12},{17,16},{21,20},{25,24},{29,28}} | collective-permute-start | bytes 2949128 | tf_op jit(solution)/shard_map/ppermute | solution.py:599
  444.8 27.4 %collective-permute-start.26 = (bf16[30,128,128]{2,1,0:T(8,128)(2,1)S(1)}, bf16[30,128,128]{2,1,0:T(8,128)(2,1)}, u32[]{:S(2)}, u32[]{:S(2)}) collective-permute-start(bf16[30,128,128]{2,1,0:T(8,128)(2,1)S(1)} %add_convert_fusion.1), channel_id=1, source_target_pairs={{1,2},{5,6},{9,10},{13,14},{17,18},{21,22},{25,26},{29,30}} | collective-permute-start | bytes 2949128 | tf_op jit(solution)/shard_map/ppermute | solution.py:599
  446.1 32.1 %collective-permute-start.33 = (bf16[37,128,128]{2,1,0:T(8,128)(2,1)}, bf16[37,128,128]{2,1,0:T(8,128)(2,1)}, u32[]{:S(2)}, u32[]{:S(2)}) collective-permute-start(bf16[37,128,128]{2,1,0:T(8,128)(2,1)} %collective-permute-done.22), channel_id=1, source_target_pairs={{2,3},{6,7},{10,11},{14,15},{18,19},{22,23},{26,27},{30,31}} | collective-permute-start | bytes 3637256 | tf_op jit(solution)/shard_map/ppermute | solution.py:606
  452.7 19.1 %collective-permute-start.24 = (bf16[26,128,128]{2,1,0:T(8,128)(2,1)}, bf16[26,128,128]{2,1,0:T(8,128)(2,1)}, u32[]{:S(2)}, u32[]{:S(2)}) collective-permute-start(bf16[26,128,128]{2,1,0:T(8,128)(2,1)} %pad_maximum_fusion.3), channel_id=1, source_target_pairs={{2,1},{6,5},{10,9},{14,13},{18,17},{22,21},{26,25},{30,29}} | collective-permute-start | bytes 2555912 | tf_op jit(solution)/shard_map/ppermute | solution.py:592
  486.1 24.0 %collective-permute-start.41 = (bf16[30,128,128]{2,1,0:T(8,128)(2,1)}, bf16[30,128,128]{2,1,0:T(8,128)(2,1)}, u32[]{:S(2)}, u32[]{:S(2)}) collective-permute-start(bf16[30,128,128]{2,1,0:T(8,128)(2,1)} %collective-permute-done.26), channel_id=1, source_target_pairs={{2,3},{6,7},{10,11},{14,15},{18,19},{22,23},{26,27},{30,31}} | collective-permute-start | bytes 2949128 | tf_op jit(solution)/shard_map/ppermute | solution.py:606
  493.7 21.3 %collective-permute-start.39 = (bf16[16,128,128]{2,1,0:T(8,128)(2,1)}, bf16[16,128,128]{2,1,0:T(8,128)(2,1)}, u32[]{:S(2)}, u32[]{:S(2)}) collective-permute-start(bf16[16,128,128]{2,1,0:T(8,128)(2,1)} %add_convert_fusion.7), channel_id=1, source_target_pairs={{1,0},{5,4},{9,8},{13,12},{17,16},{21,20},{25,24},{29,28}} | collective-permute-start | bytes 1572872 | tf_op jit(solution)/shard_map/ppermute | solution.py:599
  495.1 26.7 %collective-permute-start.40 = (bf16[16,128,128]{2,1,0:T(8,128)(2,1)}, bf16[16,128,128]{2,1,0:T(8,128)(2,1)}, u32[]{:S(2)}, u32[]{:S(2)}) collective-permute-start(bf16[16,128,128]{2,1,0:T(8,128)(2,1)} %add_convert_fusion.7), channel_id=1, source_target_pairs={{1,2},{5,6},{9,10},{13,14},{17,18},{21,22},{25,26},{29,30}} | collective-permute-start | bytes 1572872 | tf_op jit(solution)/shard_map/ppermute | solution.py:599
  497.4 41.0 %collective-permute-start.42 = (bf16[26,128,128]{2,1,0:T(8,128)(2,1)}, bf16[26,128,128]{2,1,0:T(8,128)(2,1)}, u32[]{:S(2)}, u32[]{:S(2)}) collective-permute-start(bf16[26,128,128]{2,1,0:T(8,128)(2,1)} %collective-permute-done.30), channel_id=1, source_target_pairs={{2,3},{6,7},{10,11},{14,15},{18,19},{22,23},{26,27},{30,31}} | collective-permute-start | bytes 2555912 | tf_op jit(solution)/shard_map/ppermute | solution.py:606
  507.0 48.0 %collective-permute-start.36 = (bf16[145,768]{1,0:T(8,128)(2,1)}, bf16[145,768]{1,0:T(8,128)(2,1)}, u32[]{:S(2)}, u32[]{:S(2)}) collective-permute-start(bf16[145,768]{1,0:T(8,128)(2,1)} %get-tuple-element.270), channel_id=1, source_target_pairs={{0,1},{1,2},{2,3},{4,5},{5,6},{6,7},{8,9},{9,10},{10,11},{12,13},{... | collective-permute-start | bytes 668168 | tf_op jit(solution)/shard_map/ppermute | solution.py:530
  510.1 48.4 %collective-permute-start.37 = (bf16[145,768]{1,0:T(8,128)(2,1)}, bf16[145,768]{1,0:T(8,128)(2,1)}, u32[]{:S(2)}, u32[]{:S(2)}) collective-permute-start(bf16[145,768]{1,0:T(8,128)(2,1)} %get-tuple-element.269), channel_id=1, source_target_pairs={{0,2},{1,3},{2,0},{4,6},{5,7},{6,4},{8,10},{9,11},{10,8},{12,14},{... | collective-permute-start | bytes 668168 | tf_op jit(solution)/shard_map/ppermute | solution.py:530
  515.0 47.3 %collective-permute-start.38 = (bf16[145,768]{1,0:T(8,128)(2,1)}, bf16[145,768]{1,0:T(8,128)(2,1)}, u32[]{:S(2)}, u32[]{:S(2)}) collective-permute-start(bf16[145,768]{1,0:T(8,128)(2,1)} %get-tuple-element.268), channel_id=1, source_target_pairs={{0,3},{1,0},{2,1},{4,7},{5,4},{6,5},{8,11},{9,8},{10,9},{12,15},{1... | collective-permute-start | bytes 668168 | tf_op jit(solution)/shard_map/ppermute | solution.py:530
  521.8 25.3 %collective-permute-start.43 = (bf16[16,128,128]{2,1,0:T(8,128)(2,1)}, bf16[16,128,128]{2,1,0:T(8,128)(2,1)S(1)}, u32[]{:S(2)}, u32[]{:S(2)}) collective-permute-start(bf16[16,128,128]{2,1,0:T(8,128)(2,1)} %collective-permute-done.40), channel_id=1, source_target_pairs={{2,3},{6,7},{10,11},{14,15},{18,19},{22,23},{26,27},{30,31}} | collective-permute-start | bytes 1572872 | tf_op jit(solution)/shard_map/ppermute | solution.py:606
  (46 other events, 511.6 us)
Sparse Core Ops, SparseCore 0:
  13.0 139.6 all-gather.1
  274.4 80.1 reduce-scatter.2

commit v8 on v7

--- a/solution.py
+++ b/solution.py
@@ -540,7 +540,7 @@
 
 
 EARLY = (36,)
-LATE = (30, 26, 16)
+LATE = (24, 28, 20)
 LEAST = (PER_LAYER,)
 
 
@@ -610,9 +610,9 @@
         total = jnp.where(band == 0, self.to_first, self.total)
         total = jnp.where(band == 2, self.to_third, total)
         self.total = jnp.where(band == 3, to_last, total)
-        return ()
-
-    def go_end(self):
+        return (self.total,)
+
+    def go_end(self, total):
         return ()
 
 
@@ -780,18 +780,22 @@
         sequence.round((one, "plane"))
         sequence.round((top, "meet"))
         sequence.round((one, "turn"))
+        sequence.round((two, "plane"))
+        sequence.round((one, "meet"))
         sequence.round((top, "part"))
-        sequence.round((one, "meet"), (two, "plane"))
         sequence.round((two, "turn"))
-        sequence.round((one, "part"), (top, "last"))
-        sequence.round((two, "meet"), (three, "plane"))
+        sequence.round((three, "plane"))
+        sequence.round((one, "part"))
+        sequence.round((two, "meet"))
+        sequence.round((top, "last"))
         sequence.round((three, "turn"))
-        sequence.round((two, "part"), (one, "last"))
-        sequence.round((three, "meet"), (top, "end"))
-        sequence.round((two, "last"), (three, "part"))
-        (back,) = sequence.wait_for(back)
-        input_blocks = send_rows(back)
-        sequence.round((three, "last"), (one, "end"))
+        sequence.round((three, "meet"))
+        sequence.round((two, "part"))
+        sequence.round((one, "last"))
+        sequence.round((three, "part"), (top, "end"))
+        sequence.round((two, "last"))
+        sequence.round((three, "last"))
+        sequence.round((one, "end"))
         sequence.round((two, "end"))
         sequence.round((three, "end"))
         early_total = top.total[:-1]
@@ -816,10 +820,8 @@
         owned = lax.psum_scatter(tiles[0], "dp", scatter_dimension=0, tiled=True)
         owned = lax.psum(owned, "band")
         gain_total = lax.psum(jnp.concatenate([gains_bottom, gains_top], 0), ("dp", "band"))
-        input_blocks = send_rows(back)
 
     layer_output = at_bands(output_blocks, images, bands, band)
-    input_grad = at_bands(input_blocks[:bands], images, bands, band)
     owned_f = owned.astype(f32)
     owned_squares = jnp.sum(owned_f * owned_f)
     if by_permutes:
@@ -831,6 +833,8 @@
         owned_squares = lax.psum(owned_squares, "dp")
     grad_norm = jnp.sqrt(owned_squares + jnp.sum(gain_total * gain_total))
     factor = jnp.minimum(1.0, clip_limit / grad_norm)
+    back, factor = lax.optimization_barrier((back, factor))
+    input_grad = at_bands(send_rows(back), images, bands, band)
     weight_grads, new_statistics, new_master, master_copy = optimizer(
         factor.reshape(1), rank, owned, master, statistics, inverse_roots
     )

time: 614 us -> 597 us (0.972)
  waiting for transfers between devices: 216 us -> 195 us
    ppermute x4, waiting for transfers between devices: 0.11 us -> 23.9 us  [go_part(): lax.ppermute(total, 'band', [(1, 2)])]
    ppermute x4, waiting for transfers between devices: 36.8 us -> 14.1 us  [go_meet(): lax.ppermute(plane, 'band', [(2, 1)])]
    ppermute x6, waiting for transfers between devices: 27.1 us -> 9.99 us  [go_plane(): lax.ppermute(send_x, 'dp', ALONG_X)]
    ppermute x4, waiting for transfers between devices: 22.3 us -> 13.8 us  [go_last(): return (lax.ppermute(to_third, 'band', [(2, 3)]),)]
    ppermute x4, starting transfers between devices: 15.9 us -> 23.2 us  [go_meet(): lax.ppermute(plane, 'band', [(2, 1)])]
  transfers between devices with their start and end apart: 49 -> 49, of which waited for: 22 -> 24; matrix products, arithmetic and copies ran while one was open for 12% -> 11% of each run, Pallas kernels for 19% -> 25%
where the time goes in v8:
time: 597 us; the launch traced here: 588 us
  Pallas kernels  199 us (33%)
  waiting for transfers between devices  195 us (33%)
  starting transfers between devices  84.5 us (14%)
  other arithmetic  50.1 us (8%)
  local copies, waits for them, and re-layouts  40.8 us (7%)
  between operations  18.7 us (3%)
    pallas_call x2, Pallas kernels, backward_layer(): pl.pallas_call(functools.partial(backward_kernel, len(begun), zones), out...  114 us
    all_gather x1, waiting for transfers between devices, shards(): gathered = lax.all_gather(master.astype(bf16), 'dp', axis=0, tiled=True)  87.7 us
    pallas_call x2, Pallas kernels, forward_layer(): pl.pallas_call(forward_kernel, out_shape=[S((rows, D), f32)] + saved, in_...  54.1 us
    pallas_call x1, Pallas kernels, optimizer(): pl.pallas_call(optimizer_kernel, grid=(count // per,), out_shape=[S(maste...  30.7 us
    ppermute x4, waiting for transfers between devices, go_part(): lax.ppermute(total, 'band', [(1, 2)])  23.9 us
    ppermute x4, starting transfers between devices, go_meet(): lax.ppermute(plane, 'band', [(2, 1)])  23.2 us
    ppermute x6, starting transfers between devices, send_to_bands(): block = lax.ppermute(block, 'band', pairs)  16.8 us
    ppermute x3, waiting for transfers between devices, to_images(): block = lax.ppermute(block, 'band', pairs)  15.1 us
  transfers between devices with their start and end apart: 49, of which 24 were waited for; matrix products, arithmetic and copies ran while one was open for 11% of the time, Pallas kernels for 25%

profile of v8, /device:TPU:16, one launch (start us, length us, event | category | flops | bytes accessed | tf_op | source)
XLA Modules:
  0.0 587.7 jit_solution(16896667196946732096)
XLA Ops:
  7.2 5.6 convert_element_type.307
  16.9 4.4 collective-permute-start.1
  25.5 5.3 scatter_custom_fusion
  34.7 3.9 gather_fusion
  42.2 6.2 %collective-permute-done.1 = bf16[2,145,768]{2,1,0:T(8,128)(2,1)} collective-permute-done((bf16[2,145,768]{2,1,0:T(8,128)(2,1)S(1)}, bf16[2,145,768]{2,1,0:T(8,128)(2,1)}, u32[]{:S(2)}, u32[]{:S(2)}) %collective-permute-start.1) | collective-permute-done | bytes 445472 | tf_op jit(solution)/shard_map/ppermute | solution.py:519
  49.5 8.9 %collective-permute-done.2 = bf16[2,145,768]{2,1,0:T(8,128)(2,1)} collective-permute-done((bf16[2,145,768]{2,1,0:T(8,128)(2,1)S(1)}, bf16[2,145,768]{2,1,0:T(8,128)(2,1)}, u32[]{:S(2)}, u32[]{:S(2)}) %collective-permute-start.2) | collective-permute-done | bytes 445472 | tf_op jit(solution)/shard_map/ppermute | solution.py:519
  65.0 87.7 %all-gather.2.cloned.1.call-done.w_hbm = bf16[864,128,128]{2,1,0:T(8,128)(2,1)} async-done(((bf16[108,128,128]{2,1,0:T(8,128)(2,1)}), bf16[864,128,128]{2,1,0:T(8,128)(2,1)}) %all-gather.2.cloned.1.call-update) | async-done | bytes 28311568 | tf_op jit(solution)/shard_map/all_gather | solution.py:704
  152.7 26.8 %forward_block.2 = (f32[592,768]{1,0:T(8,128)}, bf16[592,768]{1,0:T(8,128)(2,1)}, bf16[640,768]{1,0:T(8,128)(2,1)}, bf16[640,768]{1,0:T(8,128)(2,1)}, bf16[640,7...) custom-call(s32[432]{0:T(512)} %get-tuple-element.288.slots, ...), custom_call_target="tpu_custom_call" | custom-call | flops 8380219392 | bytes 41943040 | tf_op jit(solution)/shard_map/forward_block/pallas_call | solution.py:419
  179.5 27.3 %forward_block.3 = (f32[592,768]{1,0:T(8,128)}, bf16[592,768]{1,0:T(8,128)(2,1)}, bf16[640,768]{1,0:T(8,128)(2,1)}, bf16[640,768]{1,0:T(8,128)(2,1)}, bf16[640,7...) custom-call(s32[432]{0:T(512)} %get-tuple-element.287.slots, ...), custom_call_target="tpu_custom_call" | custom-call | flops 8380219392 | bytes 41943040 | tf_op jit(solution)/shard_map/forward_block/pallas_call | solution.py:419
  209.4 3.4 collective-permute-start.3
  217.5 57.0 %backward_block.2 = (f32[592,768]{1,0:T(8,128)}, f32[2,768]{1,0:T(2,128)}, bf16[288,128,128]{2,1,0:T(8,128)(2,1)}, bf16[96,128,128]{2,1,0:T(8,128)(2,1)}, bf16[9...) custom-call(s32[432]{0:T(512)} %get-tuple-element.286.places, ...), custom_call_target="tpu_custom_call" | custom-call | flops 22143565824 | bytes 62914560 | tf_op jit(solution)/shard_map/backward_block/pallas_call | solution.py:446
  275.3 57.1 %backward_block.3 = (f32[592,768]{1,0:T(8,128)}, f32[2,768]{1,0:T(2,128)}, bf16[288,128,128]{2,1,0:T(8,128)(2,1)}, bf16[96,128,128]{2,1,0:T(8,128)(2,1)}, bf16[9...) custom-call(s32[432]{0:T(512)} %get-tuple-element.285.places, ...), custom_call_target="tpu_custom_call", output_to_operand_aliasing={{3}: (21, {}), {4}: (22, {}), {5}: (23, {}), {6}: (24, {}),... | custom-call | flops 22143565824 | bytes 62914560 | tf_op jit(solution)/shard_map/backward_block/pallas_call | solution.py:446
  333.0 9.1 %collective-permute-done.8 = bf16[96,128,128]{2,1,0:T(8,128)(2,1)S(1)} collective-permute-done((bf16[96,128,128]{2,1,0:T(8,128)(2,1)}, bf16[96,128,128]{2,1,0:T(8,128)(2,1)S(1)}, u32[]{:S(2)}, u32[]{:S(2)}) %collective-permute-start.8) | collective-permute-done | bytes 3145760 | tf_op jit(solution)/shard_map/ppermute | solution.py:632
  342.1 3.1 add_convert_fusion.5
  347.2 5.8 reduce-scatter.3.cloned.1.call-done
  355.3 11.5 %collective-permute-done.10 = bf16[24,128,128]{2,1,0:T(8,128)(2,1)} collective-permute-done((bf16[24,128,128]{2,1,0:T(8,128)(2,1)}, bf16[24,128,128]{2,1,0:T(8,128)(2,1)}, u32[]{:S(2)}, u32[]{:S(2)}) %collective-permute-start.10) | collective-permute-done | bytes 786464 | tf_op jit(solution)/shard_map/ppermute | solution.py:639
  366.8 4.0 collective-permute-start.14
  376.5 6.1 %collective-permute-done.15 = bf16[12,128,128]{2,1,0:T(8,128)(2,1)S(1)} collective-permute-done((bf16[12,128,128]{2,1,0:T(8,128)(2,1)S(1)}, bf16[12,128,128]{2,1,0:T(8,128)(2,1)S(1)}, u32[]{:S(2)}, u32[]{:S(2)}) %collective-permute-start.15) | collective-permute-done | bytes 393248 | tf_op jit(solution)/shard_map/ppermute | solution.py:639
  387.1 8.9 %collective-permute-done.14 = bf16[37,128,128]{2,1,0:T(8,128)(2,1)S(1)} collective-permute-done((bf16[37,128,128]{2,1,0:T(8,128)(2,1)S(1)}, bf16[37,128,128]{2,1,0:T(8,128)(2,1)S(1)}, u32[]{:S(2)}, u32[]{:S(2)}) %collective-permute-start.14) | collective-permute-done | bytes 1212448 | tf_op jit(solution)/shard_map/ppermute | solution.py:592
  396.1 4.4 collective-permute-start.24
  410.7 5.1 collective-permute-done.24
  421.4 8.5 %collective-permute-start.33 = (bf16[28,128,128]{2,1,0:T(8,128)(2,1)S(1)}, bf16[28,128,128]{2,1,0:T(8,128)(2,1)S(1)}, u32[]{:S(2)}, u32[]{:S(2)}) collective-permute-start(bf16[28,128,128]{2,1,0:T(8,128)(2,1)S(1)} %pad_maximum_fusion.2), channel_id=1, source_target_pairs={{2,1},{6,5},{10,9},{14,13},{18,17},{22,21},{26,25},{30,29}} | collective-permute-start | bytes 2752520 | tf_op jit(solution)/shard_map/ppermute | solution.py:592
  435.0 3.7 collective-permute-start.29
  446.7 6.2 %collective-permute-start.28 = (bf16[20,128,128]{2,1,0:T(8,128)(2,1)}, bf16[20,128,128]{2,1,0:T(8,128)(2,1)}, u32[]{:S(2)}, u32[]{:S(2)}) collective-permute-start(bf16[20,128,128]{2,1,0:T(8,128)(2,1)} %pad_maximum_fusion.4), channel_id=1, source_target_pairs={{2,1},{6,5},{10,9},{14,13},{18,17},{22,21},{26,25},{30,29}} | collective-permute-start | bytes 1966088 | tf_op jit(solution)/shard_map/ppermute | solution.py:592
  455.1 5.5 collective-permute-done.31
  471.9 15.8 %collective-permute-done.38 = bf16[28,128,128]{2,1,0:T(8,128)(2,1)} collective-permute-done((bf16[28,128,128]{2,1,0:T(8,128)(2,1)S(1)}, bf16[28,128,128]{2,1,0:T(8,128)(2,1)}, u32[]{:S(2)}, u32[]{:S(2)}) %collective-permute-start.38) | collective-permute-done | bytes 917536 | tf_op jit(solution)/shard_map/ppermute | solution.py:599
  499.0 7.8 %collective-permute-done.39 = bf16[28,128,128]{2,1,0:T(8,128)(2,1)} collective-permute-done((bf16[28,128,128]{2,1,0:T(8,128)(2,1)}, bf16[28,128,128]{2,1,0:T(8,128)(2,1)}, u32[]{:S(2)}, u32[]{:S(2)}) %collective-permute-start.39) | collective-permute-done | bytes 917536 | tf_op jit(solution)/shard_map/ppermute | solution.py:606
  508.2 6.0 %collective-permute-done.40 = bf16[20,128,128]{2,1,0:T(8,128)(2,1)S(1)} collective-permute-done((bf16[20,128,128]{2,1,0:T(8,128)(2,1)}, bf16[20,128,128]{2,1,0:T(8,128)(2,1)S(1)}, u32[]{:S(2)}, u32[]{:S(2)}) %collective-permute-start.40) | collective-permute-done | bytes 655392 | tf_op jit(solution)/shard_map/ppermute | solution.py:606
  517.7 5.0 multiply_reduce_fusion
  538.1 4.1 collective-permute-start.44
  544.1 2.8 collective-permute-start.46
  546.9 30.7 %optimizer.1 = (f32[108,128,128]{2,1,0:T(8,128)}, f32[108,2,128,128]{3,2,1,0:T(8,128)}, f32[108,128,128]{2,1,0:T(8,128)}, bf16[108,128,128]{2,1,0:T(8,128)(2,1)}) custom-call(f32[1]{0:T(128)} %bitcast.28.factor, s32[108]{0:T(128)} %dynamic-slice_reduce_fusion.rank, bf16[108,128,128]{2,1,0:T(8,128)(2,1)} %get-tuple-element.247.g_ref, f32[108,128,128]{2,1,0:T(8,128)} %m_ref.1, ...), custom_call_target="tpu_custom_call" | custom-call | tf_op jit(solution)/shard_map/optimizer/pallas_call | solution.py:495
  (236 shorter events, 121.3 us)
Async XLA Ops:
  7.2 145.5 %all-gather.2.cloned.1.call-start = ((), (), s32[]{:S(2)}) async-start(), calls=%async_computation.2 | async-start | bytes 31850496 | tf_op jit(solution)/shard_map/all_gather | solution.py:704
  12.9 340.1 %reduce-scatter.3.cloned.1.call-start = ((), (), s32[]{:S(2)}) async-start(), calls=%async_computation.3 | async-start | bytes 10616832 | tf_op jit(solution)/shard_map/reduce_scatter | solution.py:769
  15.4 25.8 %collective-permute-start = (bf16[2,145,768]{2,1,0:T(8,128)(2,1)}, bf16[2,145,768]{2,1,0:T(8,128)(2,1)}, u32[]{:S(2)}, u32[]{:S(2)}) collective-permute-start(bf16[2,145,768]{2,1,0:T(8,128)(2,1)} %get-tuple-element.270), channel_id=1, source_target_pairs={{0,1},{1,2},{3,0},{4,5},{5,6},{7,4},{8,9},{9,10},{11,8},{12,13},{1... | collective-permute-start | bytes 1336328 | tf_op jit(solution)/shard_map/ppermute | solution.py:519
  16.9 31.6 %collective-permute-start.1 = (bf16[2,145,768]{2,1,0:T(8,128)(2,1)S(1)}, bf16[2,145,768]{2,1,0:T(8,128)(2,1)}, u32[]{:S(2)}, u32[]{:S(2)}) collective-permute-start(bf16[2,145,768]{2,1,0:T(8,128)(2,1)S(1)} %get-tuple-element.269), channel_id=1, source_target_pairs={{0,2},{2,0},{3,1},{4,6},{6,4},{7,5},{8,10},{10,8},{11,9},{12,14},{... | collective-permute-start | bytes 1336328 | tf_op jit(solution)/shard_map/ppermute | solution.py:519
  21.3 37.1 %collective-permute-start.2 = (bf16[2,145,768]{2,1,0:T(8,128)(2,1)S(1)}, bf16[2,145,768]{2,1,0:T(8,128)(2,1)}, u32[]{:S(2)}, u32[]{:S(2)}) collective-permute-start(bf16[2,145,768]{2,1,0:T(8,128)(2,1)S(1)} %get-tuple-element.268), channel_id=1, source_target_pairs={{1,0},{2,1},{3,2},{5,4},{6,5},{7,6},{9,8},{10,9},{11,10},{13,12},{... | collective-permute-start | bytes 1336328 | tf_op jit(solution)/shard_map/ppermute | solution.py:519
  209.4 65.1 %collective-permute-start.3 = (bf16[145,768]{1,0:T(8,128)(2,1)S(1)}, bf16[145,768]{1,0:T(8,128)(2,1)S(1)}, u32[]{:S(2)}, u32[]{:S(2)}) collective-permute-start(bf16[145,768]{1,0:T(8,128)(2,1)S(1)} %get-tuple-element.278), channel_id=1, source_target_pairs={{0,1},{1,2},{2,3},{4,5},{5,6},{6,7},{8,9},{9,10},{10,11},{12,13},{... | collective-permute-start | bytes 668168 | tf_op jit(solution)/shard_map/ppermute | solution.py:530
  212.8 61.7 %collective-permute-start.4 = (bf16[145,768]{1,0:T(8,128)(2,1)S(1)}, bf16[145,768]{1,0:T(8,128)(2,1)S(1)}, u32[]{:S(2)}, u32[]{:S(2)}) collective-permute-start(bf16[145,768]{1,0:T(8,128)(2,1)S(1)} %get-tuple-element.277), channel_id=1, source_target_pairs={{0,2},{1,3},{2,0},{4,6},{5,7},{6,4},{8,10},{9,11},{10,8},{12,14},{... | collective-permute-start | bytes 668168 | tf_op jit(solution)/shard_map/ppermute | solution.py:530
  215.3 59.3 %collective-permute-start.5 = (bf16[145,768]{1,0:T(8,128)(2,1)S(1)}, bf16[145,768]{1,0:T(8,128)(2,1)S(1)}, u32[]{:S(2)}, u32[]{:S(2)}) collective-permute-start(bf16[145,768]{1,0:T(8,128)(2,1)S(1)} %get-tuple-element.276), channel_id=1, source_target_pairs={{0,3},{1,0},{2,1},{4,7},{5,4},{6,5},{8,11},{9,8},{10,9},{12,15},{1... | collective-permute-start | bytes 668168 | tf_op jit(solution)/shard_map/ppermute | solution.py:530
  332.5 41.5 %collective-permute-start.7 = (bf16[112,128,128]{2,1,0:T(8,128)(2,1)}, bf16[112,128,128]{2,1,0:T(8,128)(2,1)}, u32[]{:S(2)}, u32[]{:S(2)}) collective-permute-start(bf16[112,128,128]{2,1,0:T(8,128)(2,1)} %get-tuple-element.182), channel_id=1, source_target_pairs={{0,4},{4,0},{8,12},{12,8},{16,20},{20,16},{24,28},{28,24},{1,5},{5... | collective-permute-start | bytes 11010056 | tf_op jit(solution)/shard_map/ppermute | solution.py:632
  345.2 21.6 %collective-permute-start.10 = (bf16[24,128,128]{2,1,0:T(8,128)(2,1)}, bf16[24,128,128]{2,1,0:T(8,128)(2,1)}, u32[]{:S(2)}, u32[]{:S(2)}) collective-permute-start(bf16[24,128,128]{2,1,0:T(8,128)(2,1)} %get-tuple-element.258), channel_id=1, source_target_pairs={{0,16},{4,20},{8,24},{12,28},{16,0},{20,4},{24,8},{28,12},{1,17},{... | collective-permute-start | bytes 2359304 | tf_op jit(solution)/shard_map/ppermute | solution.py:639
  345.8 25.0 %collective-permute-start.9 = (bf16[24,128,128]{2,1,0:T(8,128)(2,1)}, bf16[24,128,128]{2,1,0:T(8,128)(2,1)}, u32[]{:S(2)}, u32[]{:S(2)}) collective-permute-start(bf16[24,128,128]{2,1,0:T(8,128)(2,1)} %get-tuple-element.259), channel_id=1, source_target_pairs={{0,8},{4,12},{8,0},{12,4},{16,24},{20,28},{24,16},{28,20},{1,9},{5... | collective-permute-start | bytes 2359304 | tf_op jit(solution)/shard_map/ppermute | solution.py:639
  347.1 60.2 %collective-permute-start.6 = (bf16[80,128,128]{2,1,0:T(8,128)(2,1)}, bf16[80,128,128]{2,1,0:T(8,128)(2,1)}, u32[]{:S(2)}, u32[]{:S(2)}) collective-permute-start(bf16[80,128,128]{2,1,0:T(8,128)(2,1)} %get-tuple-element.180), channel_id=1, source_target_pairs={{0,4},{4,0},{8,12},{12,8},{16,20},{20,16},{24,28},{28,24},{1,5},{5... | collective-permute-start | bytes 7864328 | tf_op jit(solution)/shard_map/ppermute | solution.py:632
  354.5 31.9 %collective-permute-start.13 = (bf16[37,128,128]{2,1,0:T(8,128)(2,1)S(1)}, bf16[37,128,128]{2,1,0:T(8,128)(2,1)S(1)}, u32[]{:S(2)}, u32[]{:S(2)}) collective-permute-start(bf16[37,128,128]{2,1,0:T(8,128)(2,1)S(1)} %pad_maximum_fusion.1), channel_id=1, source_target_pairs={{0,1},{4,5},{8,9},{12,13},{16,17},{20,21},{24,25},{28,29}} | collective-permute-start | bytes 3637256 | tf_op jit(solution)/shard_map/ppermute | solution.py:592
  366.8 29.3 %collective-permute-start.14 = (bf16[37,128,128]{2,1,0:T(8,128)(2,1)S(1)}, bf16[37,128,128]{2,1,0:T(8,128)(2,1)S(1)}, u32[]{:S(2)}, u32[]{:S(2)}) collective-permute-start(bf16[37,128,128]{2,1,0:T(8,128)(2,1)S(1)} %pad_maximum_fusion.1), channel_id=1, source_target_pairs={{2,1},{6,5},{10,9},{14,13},{18,17},{22,21},{26,25},{30,29}} | collective-permute-start | bytes 3637256 | tf_op jit(solution)/shard_map/ppermute | solution.py:592
  382.6 20.4 %collective-permute-start.11 = (bf16[28,128,128]{2,1,0:T(8,128)(2,1)S(1)}, bf16[28,128,128]{2,1,0:T(8,128)(2,1)S(1)}, u32[]{:S(2)}, u32[]{:S(2)}) collective-permute-start(bf16[28,128,128]{2,1,0:T(8,128)(2,1)S(1)} %get-tuple-element.253), channel_id=1, source_target_pairs={{0,8},{4,12},{8,0},{12,4},{16,24},{20,28},{24,16},{28,20},{1,9},{5... | collective-permute-start | bytes 2752520 | tf_op jit(solution)/shard_map/ppermute | solution.py:639
  384.1 20.1 %collective-permute-start.12 = (bf16[28,128,128]{2,1,0:T(8,128)(2,1)S(1)}, bf16[28,128,128]{2,1,0:T(8,128)(2,1)S(1)}, u32[]{:S(2)}, u32[]{:S(2)}) collective-permute-start(bf16[28,128,128]{2,1,0:T(8,128)(2,1)S(1)} %get-tuple-element.252), channel_id=1, source_target_pairs={{0,16},{4,20},{8,24},{12,28},{16,0},{20,4},{24,8},{28,12},{1,17},{... | collective-permute-start | bytes 2752520 | tf_op jit(solution)/shard_map/ppermute | solution.py:639
  386.4 22.0 %collective-permute-start.23 = (bf16[24,128,128]{2,1,0:T(8,128)(2,1)S(1)}, bf16[24,128,128]{2,1,0:T(8,128)(2,1)S(1)}, u32[]{:S(2)}, u32[]{:S(2)}) collective-permute-start(bf16[24,128,128]{2,1,0:T(8,128)(2,1)S(1)} %pad_maximum_fusion.3), channel_id=1, source_target_pairs={{0,1},{4,5},{8,9},{12,13},{16,17},{20,21},{24,25},{28,29}} | collective-permute-start | bytes 2359304 | tf_op jit(solution)/shard_map/ppermute | solution.py:592
  396.1 19.7 %collective-permute-start.24 = (bf16[24,128,128]{2,1,0:T(8,128)(2,1)S(1)}, bf16[24,128,128]{2,1,0:T(8,128)(2,1)S(1)}, u32[]{:S(2)}, u32[]{:S(2)}) collective-permute-start(bf16[24,128,128]{2,1,0:T(8,128)(2,1)S(1)} %pad_maximum_fusion.3), channel_id=1, source_target_pairs={{2,1},{6,5},{10,9},{14,13},{18,17},{22,21},{26,25},{30,29}} | collective-permute-start | bytes 2359304 | tf_op jit(solution)/shard_map/ppermute | solution.py:592
  404.2 27.5 %collective-permute-start.20 = (bf16[37,128,128]{2,1,0:T(8,128)(2,1)S(1)}, bf16[37,128,128]{2,1,0:T(8,128)(2,1)}, u32[]{:S(2)}, u32[]{:S(2)}) collective-permute-start(bf16[37,128,128]{2,1,0:T(8,128)(2,1)S(1)} %add_convert_fusion), channel_id=1, source_target_pairs={{1,2},{5,6},{9,10},{13,14},{17,18},{21,22},{25,26},{29,30}} | collective-permute-start | bytes 3637256 | tf_op jit(solution)/shard_map/ppermute | solution.py:599
  420.6 24.6 %collective-permute-start.32 = (bf16[28,128,128]{2,1,0:T(8,128)(2,1)S(1)}, bf16[28,128,128]{2,1,0:T(8,128)(2,1)S(1)}, u32[]{:S(2)}, u32[]{:S(2)}) collective-permute-start(bf16[28,128,128]{2,1,0:T(8,128)(2,1)S(1)} %pad_maximum_fusion.2), channel_id=1, source_target_pairs={{0,1},{4,5},{8,9},{12,13},{16,17},{20,21},{24,25},{28,29}} | collective-permute-start | bytes 2752520 | tf_op jit(solution)/shard_map/ppermute | solution.py:592
  421.4 25.4 %collective-permute-start.33 = (bf16[28,128,128]{2,1,0:T(8,128)(2,1)S(1)}, bf16[28,128,128]{2,1,0:T(8,128)(2,1)S(1)}, u32[]{:S(2)}, u32[]{:S(2)}) collective-permute-start(bf16[28,128,128]{2,1,0:T(8,128)(2,1)S(1)} %pad_maximum_fusion.2), channel_id=1, source_target_pairs={{2,1},{6,5},{10,9},{14,13},{18,17},{22,21},{26,25},{30,29}} | collective-permute-start | bytes 2752520 | tf_op jit(solution)/shard_map/ppermute | solution.py:592
  435.0 30.1 %collective-permute-start.29 = (bf16[37,128,128]{2,1,0:T(8,128)(2,1)}, bf16[37,128,128]{2,1,0:T(8,128)(2,1)}, u32[]{:S(2)}, u32[]{:S(2)}) collective-permute-start(bf16[37,128,128]{2,1,0:T(8,128)(2,1)} %collective-permute-done.20), channel_id=1, source_target_pairs={{2,3},{6,7},{10,11},{14,15},{18,19},{22,23},{26,27},{30,31}} | collective-permute-start | bytes 3637256 | tf_op jit(solution)/shard_map/ppermute | solution.py:606
  441.5 19.0 %collective-permute-start.31 = (bf16[24,128,128]{2,1,0:T(8,128)(2,1)S(1)}, bf16[24,128,128]{2,1,0:T(8,128)(2,1)S(1)}, u32[]{:S(2)}, u32[]{:S(2)}) collective-permute-start(bf16[24,128,128]{2,1,0:T(8,128)(2,1)S(1)} %add_convert_fusion.4), channel_id=1, source_target_pairs={{1,2},{5,6},{9,10},{13,14},{17,18},{21,22},{25,26},{29,30}} | collective-permute-start | bytes 2359304 | tf_op jit(solution)/shard_map/ppermute | solution.py:599
  453.4 18.5 %collective-permute-start.37 = (bf16[28,128,128]{2,1,0:T(8,128)(2,1)S(1)}, bf16[28,128,128]{2,1,0:T(8,128)(2,1)}, u32[]{:S(2)}, u32[]{:S(2)}) collective-permute-start(bf16[28,128,128]{2,1,0:T(8,128)(2,1)S(1)} %add_convert_fusion.1), channel_id=1, source_target_pairs={{1,0},{5,4},{9,8},{13,12},{17,16},{21,20},{25,24},{29,28}} | collective-permute-start | bytes 2752520 | tf_op jit(solution)/shard_map/ppermute | solution.py:599
  461.5 26.2 %collective-permute-start.38 = (bf16[28,128,128]{2,1,0:T(8,128)(2,1)S(1)}, bf16[28,128,128]{2,1,0:T(8,128)(2,1)}, u32[]{:S(2)}, u32[]{:S(2)}) collective-permute-start(bf16[28,128,128]{2,1,0:T(8,128)(2,1)S(1)} %add_convert_fusion.1), channel_id=1, source_target_pairs={{1,2},{5,6},{9,10},{13,14},{17,18},{21,22},{25,26},{29,30}} | collective-permute-start | bytes 2752520 | tf_op jit(solution)/shard_map/ppermute | solution.py:599
  462.8 35.1 %collective-permute-start.34 = (bf16[24,128,128]{2,1,0:T(8,128)(2,1)}, bf16[24,128,128]{2,1,0:T(8,128)(2,1)}, u32[]{:S(2)}, u32[]{:S(2)}) collective-permute-start(bf16[24,128,128]{2,1,0:T(8,128)(2,1)} %copy-done.9), channel_id=1, source_target_pairs={{2,3},{6,7},{10,11},{14,15},{18,19},{22,23},{26,27},{30,31}} | collective-permute-start | bytes 2359304 | tf_op jit(solution)/shard_map/ppermute | solution.py:606
  467.5 28.1 %collective-permute-start.35 = (bf16[20,128,128]{2,1,0:T(8,128)(2,1)}, bf16[20,128,128]{2,1,0:T(8,128)(2,1)}, u32[]{:S(2)}, u32[]{:S(2)}) collective-permute-start(bf16[20,128,128]{2,1,0:T(8,128)(2,1)} %add_convert_fusion.7), channel_id=1, source_target_pairs={{1,0},{5,4},{9,8},{13,12},{17,16},{21,20},{25,24},{29,28}} | collective-permute-start | bytes 1966088 | tf_op jit(solution)/shard_map/ppermute | solution.py:599
  469.1 27.5 %collective-permute-start.36 = (bf16[20,128,128]{2,1,0:T(8,128)(2,1)}, bf16[20,128,128]{2,1,0:T(8,128)(2,1)}, u32[]{:S(2)}, u32[]{:S(2)}) collective-permute-start(bf16[20,128,128]{2,1,0:T(8,128)(2,1)} %add_convert_fusion.7), channel_id=1, source_target_pairs={{1,2},{5,6},{9,10},{13,14},{17,18},{21,22},{25,26},{29,30}} | collective-permute-start | bytes 1966088 | tf_op jit(solution)/shard_map/ppermute | solution.py:599
  487.7 19.2 %collective-permute-start.39 = (bf16[28,128,128]{2,1,0:T(8,128)(2,1)}, bf16[28,128,128]{2,1,0:T(8,128)(2,1)}, u32[]{:S(2)}, u32[]{:S(2)}) collective-permute-start(bf16[28,128,128]{2,1,0:T(8,128)(2,1)} %collective-permute-done.38), channel_id=1, source_target_pairs={{2,3},{6,7},{10,11},{14,15},{18,19},{22,23},{26,27},{30,31}} | collective-permute-start | bytes 2752520 | tf_op jit(solution)/shard_map/ppermute | solution.py:606
  538.1 40.1 %collective-permute-start.44 = (bf16[145,768]{1,0:T(8,128)(2,1)}, bf16[145,768]{1,0:T(8,128)(2,1)S(1)}, u32[]{:S(2)}, u32[]{:S(2)}) collective-permute-start(bf16[145,768]{1,0:T(8,128)(2,1)} %get-tuple-element.274), channel_id=1, source_target_pairs={{0,1},{1,2},{2,3},{4,5},{5,6},{6,7},{8,9},{9,10},{10,11},{12,13},{... | collective-permute-start | bytes 668168 | tf_op jit(solution)/shard_map/ppermute | solution.py:530
  542.2 36.1 %collective-permute-start.45 = (bf16[145,768]{1,0:T(8,128)(2,1)}, bf16[145,768]{1,0:T(8,128)(2,1)S(1)}, u32[]{:S(2)}, u32[]{:S(2)}) collective-permute-start(bf16[145,768]{1,0:T(8,128)(2,1)} %get-tuple-element.273), channel_id=1, source_target_pairs={{0,2},{1,3},{2,0},{4,6},{5,7},{6,4},{8,10},{9,11},{10,8},{12,14},{... | collective-permute-start | bytes 668168 | tf_op jit(solution)/shard_map/ppermute | solution.py:530
  544.1 34.2 %collective-permute-start.46 = (bf16[145,768]{1,0:T(8,128)(2,1)S(1)}, bf16[145,768]{1,0:T(8,128)(2,1)S(1)}, u32[]{:S(2)}, u32[]{:S(2)}) collective-permute-start(bf16[145,768]{1,0:T(8,128)(2,1)S(1)} %get-tuple-element.272), channel_id=1, source_target_pairs={{0,3},{1,0},{2,1},{4,7},{5,4},{6,5},{8,11},{9,8},{10,9},{12,15},{1... | collective-permute-start | bytes 668168 | tf_op jit(solution)/shard_map/ppermute | solution.py:530
  (45 other events, 481.6 us)
Sparse Core Ops, SparseCore 0:
  13.0 139.6 all-gather.1
  274.7 78.2 reduce-scatter.2

commit v9 on v8

--- a/solution.py
+++ b/solution.py
@@ -488,7 +488,7 @@
 
 def optimizer(factor, rank, owned, master, statistics, inverse_roots):
     count = owned.shape[0]
-    per = max(n for n in range(1, 13) if count % n == 0)
+    per = max(n for n in range(1, 19) if count % n == 0)
     S = jax.ShapeDtypeStruct
     one = pl.BlockSpec((per, BLOCK, BLOCK), lambda i: (i, 0, 0))
     two = pl.BlockSpec((per, 2, BLOCK, BLOCK), lambda i: (i, 0, 0, 0))
@@ -790,9 +790,9 @@
         sequence.round((top, "last"))
         sequence.round((three, "turn"))
         sequence.round((three, "meet"))
-        sequence.round((two, "part"))
+        sequence.round((two, "part"), (top, "end"))
         sequence.round((one, "last"))
-        sequence.round((three, "part"), (top, "end"))
+        sequence.round((three, "part"))
         sequence.round((two, "last"))
         sequence.round((three, "last"))
         sequence.round((one, "end"))

time: 597 us -> 594 us (level)
  waiting for transfers between devices: 195 us -> 206 us
  starting transfers between devices: 84.5 us -> 74.6 us
    ppermute x6, waiting for transfers between devices: 9.99 us -> 25.7 us  [go_plane(): lax.ppermute(send_x, 'dp', ALONG_X)]
    ppermute x6, waiting for transfers between devices: 12.6 us -> 1.1 us  [go_plane(): lax.ppermute(send_y, 'dp', ALONG_Y)]
    ppermute x4, starting transfers between devices: 23.2 us -> 15.2 us  [go_meet(): lax.ppermute(plane, 'band', [(2, 1)])]
  transfers between devices with their start and end apart: 49 -> 49, of which waited for: 24 -> 24; matrix products, arithmetic and copies ran while one was open for 11% -> 10% of each run, Pallas kernels for 25% -> 25%
where the time goes in v9:
time: 594 us; the launch traced here: 585 us
  waiting for transfers between devices  206 us (35%)
  Pallas kernels  198 us (33%)
  starting transfers between devices  74.6 us (13%)
  other arithmetic  52.2 us (9%)
  local copies, waits for them, and re-layouts  35.2 us (6%)
  between operations  18.8 us (3%)
    pallas_call x2, Pallas kernels, backward_layer(): pl.pallas_call(functools.partial(backward_kernel, len(begun), zones), out...  114 us
    all_gather x1, waiting for transfers between devices, shards(): gathered = lax.all_gather(master.astype(bf16), 'dp', axis=0, tiled=True)  87.7 us
    pallas_call x2, Pallas kernels, forward_layer(): pl.pallas_call(forward_kernel, out_shape=[S((rows, D), f32)] + saved, in_...  53.9 us
    pallas_call x1, Pallas kernels, optimizer(): pl.pallas_call(optimizer_kernel, grid=(count // per,), out_shape=[S(maste...  29.9 us
    ppermute x4, waiting for transfers between devices, go_part(): lax.ppermute(total, 'band', [(1, 2)])  29.1 us
    ppermute x6, waiting for transfers between devices, go_plane(): lax.ppermute(send_x, 'dp', ALONG_X)  25.7 us
    ppermute x6, starting transfers between devices, send_to_bands(): block = lax.ppermute(block, 'band', pairs)  16.8 us
    ppermute x4, waiting for transfers between devices, go_meet(): lax.ppermute(plane, 'band', [(2, 1)])  15.4 us
  transfers between devices with their start and end apart: 49, of which 24 were waited for; matrix products, arithmetic and copies ran while one was open for 10% of the time, Pallas kernels for 25%

profile of v9, /device:TPU:16, one launch (start us, length us, event | category | flops | bytes accessed | tf_op | source)
XLA Modules:
  0.0 584.8 jit_solution(4179799403748796263)
XLA Ops:
  7.2 5.6 convert_element_type.307
  16.9 4.4 collective-permute-start.1
  25.5 5.3 scatter_custom_fusion
  34.6 3.9 gather_fusion
  42.1 6.3 %collective-permute-done.1 = bf16[2,145,768]{2,1,0:T(8,128)(2,1)} collective-permute-done((bf16[2,145,768]{2,1,0:T(8,128)(2,1)S(1)}, bf16[2,145,768]{2,1,0:T(8,128)(2,1)}, u32[]{:S(2)}, u32[]{:S(2)}) %collective-permute-start.1) | collective-permute-done | bytes 445472 | tf_op jit(solution)/shard_map/ppermute | solution.py:519
  49.5 8.9 %collective-permute-done.2 = bf16[2,145,768]{2,1,0:T(8,128)(2,1)} collective-permute-done((bf16[2,145,768]{2,1,0:T(8,128)(2,1)S(1)}, bf16[2,145,768]{2,1,0:T(8,128)(2,1)}, u32[]{:S(2)}, u32[]{:S(2)}) %collective-permute-start.2) | collective-permute-done | bytes 445472 | tf_op jit(solution)/shard_map/ppermute | solution.py:519
  65.0 87.7 %all-gather.2.cloned.1.call-done.w_hbm = bf16[864,128,128]{2,1,0:T(8,128)(2,1)} async-done(((bf16[108,128,128]{2,1,0:T(8,128)(2,1)}), bf16[864,128,128]{2,1,0:T(8,128)(2,1)}) %all-gather.2.cloned.1.call-update) | async-done | bytes 28311568 | tf_op jit(solution)/shard_map/all_gather | solution.py:704
  152.7 26.7 %forward_block.2 = (f32[592,768]{1,0:T(8,128)}, bf16[592,768]{1,0:T(8,128)(2,1)}, bf16[640,768]{1,0:T(8,128)(2,1)}, bf16[640,768]{1,0:T(8,128)(2,1)}, bf16[640,7...) custom-call(s32[432]{0:T(512)} %get-tuple-element.288.slots, ...), custom_call_target="tpu_custom_call" | custom-call | flops 8380219392 | bytes 41943040 | tf_op jit(solution)/shard_map/forward_block/pallas_call | solution.py:419
  179.4 27.2 %forward_block.3 = (f32[592,768]{1,0:T(8,128)}, bf16[592,768]{1,0:T(8,128)(2,1)}, bf16[640,768]{1,0:T(8,128)(2,1)}, bf16[640,768]{1,0:T(8,128)(2,1)}, bf16[640,7...) custom-call(s32[432]{0:T(512)} %get-tuple-element.287.slots, ...), custom_call_target="tpu_custom_call" | custom-call | flops 8380219392 | bytes 41943040 | tf_op jit(solution)/shard_map/forward_block/pallas_call | solution.py:419
  209.3 3.4 collective-permute-start.3
  217.4 56.9 %backward_block.2 = (f32[592,768]{1,0:T(8,128)}, f32[2,768]{1,0:T(2,128)}, bf16[288,128,128]{2,1,0:T(8,128)(2,1)}, bf16[96,128,128]{2,1,0:T(8,128)(2,1)}, bf16[9...) custom-call(s32[432]{0:T(512)} %get-tuple-element.286.places, ...), custom_call_target="tpu_custom_call" | custom-call | flops 22143565824 | bytes 62914560 | tf_op jit(solution)/shard_map/backward_block/pallas_call | solution.py:446
  275.1 57.0 %backward_block.3 = (f32[592,768]{1,0:T(8,128)}, f32[2,768]{1,0:T(2,128)}, bf16[288,128,128]{2,1,0:T(8,128)(2,1)}, bf16[96,128,128]{2,1,0:T(8,128)(2,1)}, bf16[9...) custom-call(s32[432]{0:T(512)} %get-tuple-element.285.places, ...), custom_call_target="tpu_custom_call", output_to_operand_aliasing={{3}: (21, {}), {4}: (22, {}), {5}: (23, {}), {6}: (24, {}),... | custom-call | flops 22143565824 | bytes 62914560 | tf_op jit(solution)/shard_map/backward_block/pallas_call | solution.py:446
  332.7 9.1 %collective-permute-done.7 = bf16[96,128,128]{2,1,0:T(8,128)(2,1)S(1)} collective-permute-done((bf16[96,128,128]{2,1,0:T(8,128)(2,1)}, bf16[96,128,128]{2,1,0:T(8,128)(2,1)S(1)}, u32[]{:S(2)}, u32[]{:S(2)}) %collective-permute-start.7) | collective-permute-done | bytes 3145760 | tf_op jit(solution)/shard_map/ppermute | solution.py:632
  341.8 3.1 add_convert_fusion.5
  347.0 5.8 reduce-scatter.3.cloned.1.call-done
  355.1 11.5 %collective-permute-done.8 = bf16[24,128,128]{2,1,0:T(8,128)(2,1)} collective-permute-done((bf16[24,128,128]{2,1,0:T(8,128)(2,1)}, bf16[24,128,128]{2,1,0:T(8,128)(2,1)}, u32[]{:S(2)}, u32[]{:S(2)}) %collective-permute-start.8) | collective-permute-done | bytes 786464 | tf_op jit(solution)/shard_map/ppermute | solution.py:639
  366.6 3.9 collective-permute-start.13
  376.1 6.2 %collective-permute-done.14 = bf16[12,128,128]{2,1,0:T(8,128)(2,1)S(1)} collective-permute-done((bf16[12,128,128]{2,1,0:T(8,128)(2,1)S(1)}, bf16[12,128,128]{2,1,0:T(8,128)(2,1)S(1)}, u32[]{:S(2)}, u32[]{:S(2)}) %collective-permute-start.14) | collective-permute-done | bytes 393248 | tf_op jit(solution)/shard_map/ppermute | solution.py:639
  386.6 9.2 %collective-permute-done.13 = bf16[37,128,128]{2,1,0:T(8,128)(2,1)S(1)} collective-permute-done((bf16[37,128,128]{2,1,0:T(8,128)(2,1)S(1)}, bf16[37,128,128]{2,1,0:T(8,128)(2,1)S(1)}, u32[]{:S(2)}, u32[]{:S(2)}) %collective-permute-start.13) | collective-permute-done | bytes 1212448 | tf_op jit(solution)/shard_map/ppermute | solution.py:592
  395.8 4.4 collective-permute-start.19
  410.0 5.5 collective-permute-done.19
  420.9 10.4 %collective-permute-done.24 = bf16[37,128,128]{2,1,0:T(8,128)(2,1)S(1)} collective-permute-done((bf16[37,128,128]{2,1,0:T(8,128)(2,1)S(1)}, bf16[37,128,128]{2,1,0:T(8,128)(2,1)S(1)}, u32[]{:S(2)}, u32[]{:S(2)}) %collective-permute-start.24) | collective-permute-done | bytes 1212448 | tf_op jit(solution)/shard_map/ppermute | solution.py:599
  437.7 5.8 collective-permute-done.28
  450.7 5.4 collective-permute-start.34
  463.2 3.4 collective-permute-start.32
  471.8 13.5 %collective-permute-done.38 = bf16[28,128,128]{2,1,0:T(8,128)(2,1)} collective-permute-done((bf16[28,128,128]{2,1,0:T(8,128)(2,1)S(1)}, bf16[28,128,128]{2,1,0:T(8,128)(2,1)}, u32[]{:S(2)}, u32[]{:S(2)}) %collective-permute-start.38) | collective-permute-done | bytes 917536 | tf_op jit(solution)/shard_map/ppermute | solution.py:599
  490.7 4.1 collective-permute-done.36
  498.7 4.9 collective-permute-done.39
  504.9 7.1 %collective-permute-done.40 = bf16[20,128,128]{2,1,0:T(8,128)(2,1)S(1)} collective-permute-done((bf16[20,128,128]{2,1,0:T(8,128)(2,1)}, bf16[20,128,128]{2,1,0:T(8,128)(2,1)S(1)}, u32[]{:S(2)}, u32[]{:S(2)}) %collective-permute-start.40) | collective-permute-done | bytes 655392 | tf_op jit(solution)/shard_map/ppermute | solution.py:606
  515.5 5.1 multiply_reduce_fusion
  536.0 4.1 collective-permute-start.44
  544.8 29.9 %optimizer.1 = (f32[108,128,128]{2,1,0:T(8,128)}, f32[108,2,128,128]{3,2,1,0:T(8,128)}, f32[108,128,128]{2,1,0:T(8,128)}, bf16[108,128,128]{2,1,0:T(8,128)(2,1)}) custom-call(f32[1]{0:T(128)} %bitcast.28.factor, s32[108]{0:T(128)} %dynamic-slice_reduce_fusion.rank, bf16[108,128,128]{2,1,0:T(8,128)(2,1)} %get-tuple-element.247.g_ref, f32[108,128,128]{2,1,0:T(8,128)} %m_ref.1, ...), custom_call_target="tpu_custom_call" | custom-call | tf_op jit(solution)/shard_map/optimizer/pallas_call | solution.py:495
  (244 shorter events, 120.3 us)
Async XLA Ops:
  7.2 145.5 %all-gather.2.cloned.1.call-start = ((), (), s32[]{:S(2)}) async-start(), calls=%async_computation.2 | async-start | bytes 31850496 | tf_op jit(solution)/shard_map/all_gather | solution.py:704
  12.9 340.0 %reduce-scatter.3.cloned.1.call-start = ((), (), s32[]{:S(2)}) async-start(), calls=%async_computation.3 | async-start | bytes 10616832 | tf_op jit(solution)/shard_map/reduce_scatter | solution.py:769
  15.4 25.6 %collective-permute-start = (bf16[2,145,768]{2,1,0:T(8,128)(2,1)}, bf16[2,145,768]{2,1,0:T(8,128)(2,1)}, u32[]{:S(2)}, u32[]{:S(2)}) collective-permute-start(bf16[2,145,768]{2,1,0:T(8,128)(2,1)} %get-tuple-element.270), channel_id=1, source_target_pairs={{0,1},{1,2},{3,0},{4,5},{5,6},{7,4},{8,9},{9,10},{11,8},{12,13},{1... | collective-permute-start | bytes 1336328 | tf_op jit(solution)/shard_map/ppermute | solution.py:519
  16.9 31.6 %collective-permute-start.1 = (bf16[2,145,768]{2,1,0:T(8,128)(2,1)S(1)}, bf16[2,145,768]{2,1,0:T(8,128)(2,1)}, u32[]{:S(2)}, u32[]{:S(2)}) collective-permute-start(bf16[2,145,768]{2,1,0:T(8,128)(2,1)S(1)} %get-tuple-element.269), channel_id=1, source_target_pairs={{0,2},{2,0},{3,1},{4,6},{6,4},{7,5},{8,10},{10,8},{11,9},{12,14},{... | collective-permute-start | bytes 1336328 | tf_op jit(solution)/shard_map/ppermute | solution.py:519
  21.3 37.1 %collective-permute-start.2 = (bf16[2,145,768]{2,1,0:T(8,128)(2,1)S(1)}, bf16[2,145,768]{2,1,0:T(8,128)(2,1)}, u32[]{:S(2)}, u32[]{:S(2)}) collective-permute-start(bf16[2,145,768]{2,1,0:T(8,128)(2,1)S(1)} %get-tuple-element.268), channel_id=1, source_target_pairs={{1,0},{2,1},{3,2},{5,4},{6,5},{7,6},{9,8},{10,9},{11,10},{13,12},{... | collective-permute-start | bytes 1336328 | tf_op jit(solution)/shard_map/ppermute | solution.py:519
  209.3 65.0 %collective-permute-start.3 = (bf16[145,768]{1,0:T(8,128)(2,1)S(1)}, bf16[145,768]{1,0:T(8,128)(2,1)S(1)}, u32[]{:S(2)}, u32[]{:S(2)}) collective-permute-start(bf16[145,768]{1,0:T(8,128)(2,1)S(1)} %get-tuple-element.278), channel_id=1, source_target_pairs={{0,1},{1,2},{2,3},{4,5},{5,6},{6,7},{8,9},{9,10},{10,11},{12,13},{... | collective-permute-start | bytes 668168 | tf_op jit(solution)/shard_map/ppermute | solution.py:530
  212.7 61.6 %collective-permute-start.4 = (bf16[145,768]{1,0:T(8,128)(2,1)S(1)}, bf16[145,768]{1,0:T(8,128)(2,1)S(1)}, u32[]{:S(2)}, u32[]{:S(2)}) collective-permute-start(bf16[145,768]{1,0:T(8,128)(2,1)S(1)} %get-tuple-element.277), channel_id=1, source_target_pairs={{0,2},{1,3},{2,0},{4,6},{5,7},{6,4},{8,10},{9,11},{10,8},{12,14},{... | collective-permute-start | bytes 668168 | tf_op jit(solution)/shard_map/ppermute | solution.py:530
  215.1 59.2 %collective-permute-start.5 = (bf16[145,768]{1,0:T(8,128)(2,1)S(1)}, bf16[145,768]{1,0:T(8,128)(2,1)S(1)}, u32[]{:S(2)}, u32[]{:S(2)}) collective-permute-start(bf16[145,768]{1,0:T(8,128)(2,1)S(1)} %get-tuple-element.276), channel_id=1, source_target_pairs={{0,3},{1,0},{2,1},{4,7},{5,4},{6,5},{8,11},{9,8},{10,9},{12,15},{1... | collective-permute-start | bytes 668168 | tf_op jit(solution)/shard_map/ppermute | solution.py:530
  332.2 41.6 %collective-permute-start.6 = (bf16[112,128,128]{2,1,0:T(8,128)(2,1)}, bf16[112,128,128]{2,1,0:T(8,128)(2,1)}, u32[]{:S(2)}, u32[]{:S(2)}) collective-permute-start(bf16[112,128,128]{2,1,0:T(8,128)(2,1)} %get-tuple-element.180), channel_id=1, source_target_pairs={{0,4},{4,0},{8,12},{12,8},{16,20},{20,16},{24,28},{28,24},{1,5},{5... | collective-permute-start | bytes 11010056 | tf_op jit(solution)/shard_map/ppermute | solution.py:632
  344.9 21.6 %collective-permute-start.8 = (bf16[24,128,128]{2,1,0:T(8,128)(2,1)}, bf16[24,128,128]{2,1,0:T(8,128)(2,1)}, u32[]{:S(2)}, u32[]{:S(2)}) collective-permute-start(bf16[24,128,128]{2,1,0:T(8,128)(2,1)} %get-tuple-element.259), channel_id=1, source_target_pairs={{0,8},{4,12},{8,0},{12,4},{16,24},{20,28},{24,16},{28,20},{1,9},{5... | collective-permute-start | bytes 2359304 | tf_op jit(solution)/shard_map/ppermute | solution.py:639
  346.4 24.1 %collective-permute-start.9 = (bf16[24,128,128]{2,1,0:T(8,128)(2,1)}, bf16[24,128,128]{2,1,0:T(8,128)(2,1)}, u32[]{:S(2)}, u32[]{:S(2)}) collective-permute-start(bf16[24,128,128]{2,1,0:T(8,128)(2,1)} %get-tuple-element.258), channel_id=1, source_target_pairs={{0,16},{4,20},{8,24},{12,28},{16,0},{20,4},{24,8},{28,12},{1,17},{... | collective-permute-start | bytes 2359304 | tf_op jit(solution)/shard_map/ppermute | solution.py:639
  346.9 60.2 %collective-permute-start.20 = (bf16[80,128,128]{2,1,0:T(8,128)(2,1)}, bf16[80,128,128]{2,1,0:T(8,128)(2,1)}, u32[]{:S(2)}, u32[]{:S(2)}) collective-permute-start(bf16[80,128,128]{2,1,0:T(8,128)(2,1)} %get-tuple-element.183), channel_id=1, source_target_pairs={{0,4},{4,0},{8,12},{12,8},{16,20},{20,16},{24,28},{28,24},{1,5},{5... | collective-permute-start | bytes 7864328 | tf_op jit(solution)/shard_map/ppermute | solution.py:632
  354.4 31.5 %collective-permute-start.12 = (bf16[37,128,128]{2,1,0:T(8,128)(2,1)S(1)}, bf16[37,128,128]{2,1,0:T(8,128)(2,1)S(1)}, u32[]{:S(2)}, u32[]{:S(2)}) collective-permute-start(bf16[37,128,128]{2,1,0:T(8,128)(2,1)S(1)} %pad_maximum_fusion.1), channel_id=1, source_target_pairs={{0,1},{4,5},{8,9},{12,13},{16,17},{20,21},{24,25},{28,29}} | collective-permute-start | bytes 3637256 | tf_op jit(solution)/shard_map/ppermute | solution.py:592
  366.6 29.3 %collective-permute-start.13 = (bf16[37,128,128]{2,1,0:T(8,128)(2,1)S(1)}, bf16[37,128,128]{2,1,0:T(8,128)(2,1)S(1)}, u32[]{:S(2)}, u32[]{:S(2)}) collective-permute-start(bf16[37,128,128]{2,1,0:T(8,128)(2,1)S(1)} %pad_maximum_fusion.1), channel_id=1, source_target_pairs={{2,1},{6,5},{10,9},{14,13},{18,17},{22,21},{26,25},{30,29}} | collective-permute-start | bytes 3637256 | tf_op jit(solution)/shard_map/ppermute | solution.py:592
  382.4 20.4 %collective-permute-start.10 = (bf16[28,128,128]{2,1,0:T(8,128)(2,1)S(1)}, bf16[28,128,128]{2,1,0:T(8,128)(2,1)S(1)}, u32[]{:S(2)}, u32[]{:S(2)}) collective-permute-start(bf16[28,128,128]{2,1,0:T(8,128)(2,1)S(1)} %get-tuple-element.253), channel_id=1, source_target_pairs={{0,8},{4,12},{8,0},{12,4},{16,24},{20,28},{24,16},{28,20},{1,9},{5... | collective-permute-start | bytes 2752520 | tf_op jit(solution)/shard_map/ppermute | solution.py:639
  383.9 20.1 %collective-permute-start.11 = (bf16[28,128,128]{2,1,0:T(8,128)(2,1)S(1)}, bf16[28,128,128]{2,1,0:T(8,128)(2,1)S(1)}, u32[]{:S(2)}, u32[]{:S(2)}) collective-permute-start(bf16[28,128,128]{2,1,0:T(8,128)(2,1)S(1)} %get-tuple-element.252), channel_id=1, source_target_pairs={{0,16},{4,20},{8,24},{12,28},{16,0},{20,4},{24,8},{28,12},{1,17},{... | collective-permute-start | bytes 2752520 | tf_op jit(solution)/shard_map/ppermute | solution.py:639
  385.9 22.3 %collective-permute-start.18 = (bf16[24,128,128]{2,1,0:T(8,128)(2,1)S(1)}, bf16[24,128,128]{2,1,0:T(8,128)(2,1)S(1)}, u32[]{:S(2)}, u32[]{:S(2)}) collective-permute-start(bf16[24,128,128]{2,1,0:T(8,128)(2,1)S(1)} %pad_maximum_fusion.3), channel_id=1, source_target_pairs={{0,1},{4,5},{8,9},{12,13},{16,17},{20,21},{24,25},{28,29}} | collective-permute-start | bytes 2359304 | tf_op jit(solution)/shard_map/ppermute | solution.py:592
  395.8 19.7 %collective-permute-start.19 = (bf16[24,128,128]{2,1,0:T(8,128)(2,1)S(1)}, bf16[24,128,128]{2,1,0:T(8,128)(2,1)S(1)}, u32[]{:S(2)}, u32[]{:S(2)}) collective-permute-start(bf16[24,128,128]{2,1,0:T(8,128)(2,1)S(1)} %pad_maximum_fusion.3), channel_id=1, source_target_pairs={{2,1},{6,5},{10,9},{14,13},{18,17},{22,21},{26,25},{30,29}} | collective-permute-start | bytes 2359304 | tf_op jit(solution)/shard_map/ppermute | solution.py:592
  402.7 18.2 %collective-permute-start.23 = (bf16[37,128,128]{2,1,0:T(8,128)(2,1)S(1)}, bf16[37,128,128]{2,1,0:T(8,128)(2,1)S(1)}, u32[]{:S(2)}, u32[]{:S(2)}) collective-permute-start(bf16[37,128,128]{2,1,0:T(8,128)(2,1)S(1)} %add_convert_fusion), channel_id=1, source_target_pairs={{1,0},{5,4},{9,8},{13,12},{17,16},{21,20},{25,24},{29,28}} | collective-permute-start | bytes 3637256 | tf_op jit(solution)/shard_map/ppermute | solution.py:599
  404.0 27.4 %collective-permute-start.24 = (bf16[37,128,128]{2,1,0:T(8,128)(2,1)S(1)}, bf16[37,128,128]{2,1,0:T(8,128)(2,1)S(1)}, u32[]{:S(2)}, u32[]{:S(2)}) collective-permute-start(bf16[37,128,128]{2,1,0:T(8,128)(2,1)S(1)} %add_convert_fusion), channel_id=1, source_target_pairs={{1,2},{5,6},{9,10},{13,14},{17,18},{21,22},{25,26},{29,30}} | collective-permute-start | bytes 3637256 | tf_op jit(solution)/shard_map/ppermute | solution.py:599
  415.5 19.3 %collective-permute-start.26 = (bf16[20,128,128]{2,1,0:T(8,128)(2,1)S(1)}, bf16[20,128,128]{2,1,0:T(8,128)(2,1)S(1)}, u32[]{:S(2)}, u32[]{:S(2)}) collective-permute-start(bf16[20,128,128]{2,1,0:T(8,128)(2,1)S(1)} %get-tuple-element.265), channel_id=1, source_target_pairs={{0,8},{4,12},{8,0},{12,4},{16,24},{20,28},{24,16},{28,20},{1,9},{5... | collective-permute-start | bytes 1966088 | tf_op jit(solution)/shard_map/ppermute | solution.py:639
  431.3 24.8 %collective-permute-start.25 = (bf16[37,128,128]{2,1,0:T(8,128)(2,1)S(1)}, bf16[37,128,128]{2,1,0:T(8,128)(2,1)S(1)}, u32[]{:S(2)}, u32[]{:S(2)}) collective-permute-start(bf16[37,128,128]{2,1,0:T(8,128)(2,1)S(1)} %collective-permute-done.24), channel_id=1, source_target_pairs={{2,3},{6,7},{10,11},{14,15},{18,19},{22,23},{26,27},{30,31}} | collective-permute-start | bytes 3637256 | tf_op jit(solution)/shard_map/ppermute | solution.py:606
  444.7 18.5 %collective-permute-start.31 = (bf16[24,128,128]{2,1,0:T(8,128)(2,1)}, bf16[24,128,128]{2,1,0:T(8,128)(2,1)}, u32[]{:S(2)}, u32[]{:S(2)}) collective-permute-start(bf16[24,128,128]{2,1,0:T(8,128)(2,1)} %add_convert_fusion.4), channel_id=1, source_target_pairs={{1,2},{5,6},{9,10},{13,14},{17,18},{21,22},{25,26},{29,30}} | collective-permute-start | bytes 2359304 | tf_op jit(solution)/shard_map/ppermute | solution.py:599
  448.5 18.0 %collective-permute-start.33 = (bf16[20,128,128]{2,1,0:T(8,128)(2,1)}, bf16[20,128,128]{2,1,0:T(8,128)(2,1)}, u32[]{:S(2)}, u32[]{:S(2)}) collective-permute-start(bf16[20,128,128]{2,1,0:T(8,128)(2,1)} %pad_maximum_fusion.4), channel_id=1, source_target_pairs={{0,1},{4,5},{8,9},{12,13},{16,17},{20,21},{24,25},{28,29}} | collective-permute-start | bytes 1966088 | tf_op jit(solution)/shard_map/ppermute | solution.py:592
  459.1 26.2 %collective-permute-start.38 = (bf16[28,128,128]{2,1,0:T(8,128)(2,1)S(1)}, bf16[28,128,128]{2,1,0:T(8,128)(2,1)}, u32[]{:S(2)}, u32[]{:S(2)}) collective-permute-start(bf16[28,128,128]{2,1,0:T(8,128)(2,1)S(1)} %add_convert_fusion.1), channel_id=1, source_target_pairs={{1,2},{5,6},{9,10},{13,14},{17,18},{21,22},{25,26},{29,30}} | collective-permute-start | bytes 2752520 | tf_op jit(solution)/shard_map/ppermute | solution.py:599
  463.2 33.0 %collective-permute-start.32 = (bf16[24,128,128]{2,1,0:T(8,128)(2,1)}, bf16[24,128,128]{2,1,0:T(8,128)(2,1)}, u32[]{:S(2)}, u32[]{:S(2)}) collective-permute-start(bf16[24,128,128]{2,1,0:T(8,128)(2,1)} %collective-permute-done.31), channel_id=1, source_target_pairs={{2,3},{6,7},{10,11},{14,15},{18,19},{22,23},{26,27},{30,31}} | collective-permute-start | bytes 2359304 | tf_op jit(solution)/shard_map/ppermute | solution.py:606
  469.0 21.7 %collective-permute-start.35 = (bf16[20,128,128]{2,1,0:T(8,128)(2,1)}, bf16[20,128,128]{2,1,0:T(8,128)(2,1)}, u32[]{:S(2)}, u32[]{:S(2)}) collective-permute-start(bf16[20,128,128]{2,1,0:T(8,128)(2,1)} %add_convert_fusion.7), channel_id=1, source_target_pairs={{1,0},{5,4},{9,8},{13,12},{17,16},{21,20},{25,24},{29,28}} | collective-permute-start | bytes 1966088 | tf_op jit(solution)/shard_map/ppermute | solution.py:599
  470.5 24.3 %collective-permute-start.36 = (bf16[20,128,128]{2,1,0:T(8,128)(2,1)}, bf16[20,128,128]{2,1,0:T(8,128)(2,1)}, u32[]{:S(2)}, u32[]{:S(2)}) collective-permute-start(bf16[20,128,128]{2,1,0:T(8,128)(2,1)} %add_convert_fusion.7), channel_id=1, source_target_pairs={{1,2},{5,6},{9,10},{13,14},{17,18},{21,22},{25,26},{29,30}} | collective-permute-start | bytes 1966088 | tf_op jit(solution)/shard_map/ppermute | solution.py:599
  485.3 18.3 %collective-permute-start.39 = (bf16[28,128,128]{2,1,0:T(8,128)(2,1)}, bf16[28,128,128]{2,1,0:T(8,128)(2,1)}, u32[]{:S(2)}, u32[]{:S(2)}) collective-permute-start(bf16[28,128,128]{2,1,0:T(8,128)(2,1)} %collective-permute-done.38), channel_id=1, source_target_pairs={{2,3},{6,7},{10,11},{14,15},{18,19},{22,23},{26,27},{30,31}} | collective-permute-start | bytes 2752520 | tf_op jit(solution)/shard_map/ppermute | solution.py:606
  536.0 39.3 %collective-permute-start.44 = (bf16[145,768]{1,0:T(8,128)(2,1)}, bf16[145,768]{1,0:T(8,128)(2,1)S(1)}, u32[]{:S(2)}, u32[]{:S(2)}) collective-permute-start(bf16[145,768]{1,0:T(8,128)(2,1)} %get-tuple-element.274), channel_id=1, source_target_pairs={{0,1},{1,2},{2,3},{4,5},{5,6},{6,7},{8,9},{9,10},{10,11},{12,13},{... | collective-permute-start | bytes 668168 | tf_op jit(solution)/shard_map/ppermute | solution.py:530
  540.1 35.3 %collective-permute-start.45 = (bf16[145,768]{1,0:T(8,128)(2,1)}, bf16[145,768]{1,0:T(8,128)(2,1)S(1)}, u32[]{:S(2)}, u32[]{:S(2)}) collective-permute-start(bf16[145,768]{1,0:T(8,128)(2,1)} %get-tuple-element.273), channel_id=1, source_target_pairs={{0,2},{1,3},{2,0},{4,6},{5,7},{6,4},{8,10},{9,11},{10,8},{12,14},{... | collective-permute-start | bytes 668168 | tf_op jit(solution)/shard_map/ppermute | solution.py:530
  542.0 33.4 %collective-permute-start.46 = (bf16[145,768]{1,0:T(8,128)(2,1)S(1)}, bf16[145,768]{1,0:T(8,128)(2,1)S(1)}, u32[]{:S(2)}, u32[]{:S(2)}) collective-permute-start(bf16[145,768]{1,0:T(8,128)(2,1)S(1)} %get-tuple-element.272), channel_id=1, source_target_pairs={{0,3},{1,0},{2,1},{4,7},{5,4},{6,5},{8,11},{9,8},{10,9},{12,15},{1... | collective-permute-start | bytes 668168 | tf_op jit(solution)/shard_map/ppermute | solution.py:530
  (49 other events, 523.7 us)
Sparse Core Ops, SparseCore 0:
  13.0 139.6 all-gather.1
  274.5 78.3 reduce-scatter.2

commit v10 on v9

--- a/solution.py
+++ b/solution.py
@@ -786,8 +786,8 @@
         sequence.round((two, "turn"))
         sequence.round((three, "plane"))
         sequence.round((one, "part"))
+        sequence.round((top, "last"))
         sequence.round((two, "meet"))
-        sequence.round((top, "last"))
         sequence.round((three, "turn"))
         sequence.round((three, "meet"))
         sequence.round((two, "part"), (top, "end"))

time: 594 us -> 605 us (1.019)
  starting transfers between devices: 74.6 us -> 80.7 us
    ppermute x4, starting transfers between devices: 15.2 us -> 23.1 us  [go_meet(): lax.ppermute(plane, 'band', [(2, 1)])]
  transfers between devices with their start and end apart: 49 -> 49, of which waited for: 24 -> 21; matrix products, arithmetic and copies ran while one was open for 10% -> 10% of each run, Pallas kernels for 25% -> 24%
where the time goes in v10:
time: 605 us; the launch traced here: 596 us
  waiting for transfers between devices  212 us (35%)
  Pallas kernels  198 us (33%)
  starting transfers between devices  80.7 us (13%)
  other arithmetic  52.2 us (9%)
  local copies, waits for them, and re-layouts  35.1 us (6%)
  between operations  18.8 us (3%)
    pallas_call x2, Pallas kernels, backward_layer(): pl.pallas_call(functools.partial(backward_kernel, len(begun), zones), out...  114 us
    all_gather x1, waiting for transfers between devices, shards(): gathered = lax.all_gather(master.astype(bf16), 'dp', axis=0, tiled=True)  87.7 us
    pallas_call x2, Pallas kernels, forward_layer(): pl.pallas_call(forward_kernel, out_shape=[S((rows, D), f32)] + saved, in_...  53.9 us
    pallas_call x1, Pallas kernels, optimizer(): pl.pallas_call(optimizer_kernel, grid=(count // per,), out_shape=[S(maste...  29.9 us
    ppermute x6, waiting for transfers between devices, go_plane(): lax.ppermute(send_x, 'dp', ALONG_X)  28 us
    ppermute x4, waiting for transfers between devices, go_part(): lax.ppermute(total, 'band', [(1, 2)])  27.9 us
    ppermute x4, starting transfers between devices, go_meet(): lax.ppermute(plane, 'band', [(2, 1)])  23.1 us
    ppermute x4, waiting for transfers between devices, go_meet(): lax.ppermute(plane, 'band', [(2, 1)])  18.5 us
  transfers between devices with their start and end apart: 49, of which 21 were waited for; matrix products, arithmetic and copies ran while one was open for 10% of the time, Pallas kernels for 24%

profile of v10, /device:TPU:16, one launch (start us, length us, event | category | flops | bytes accessed | tf_op | source)
XLA Modules:
  0.0 596.2 jit_solution(10414163547446559056)
XLA Ops:
  7.2 5.6 convert_element_type.307
  16.9 4.4 collective-permute-start.1
  25.5 5.3 scatter_custom_fusion
  34.6 3.9 gather_fusion
  42.1 6.3 %collective-permute-done.1 = bf16[2,145,768]{2,1,0:T(8,128)(2,1)} collective-permute-done((bf16[2,145,768]{2,1,0:T(8,128)(2,1)S(1)}, bf16[2,145,768]{2,1,0:T(8,128)(2,1)}, u32[]{:S(2)}, u32[]{:S(2)}) %collective-permute-start.1) | collective-permute-done | bytes 445472 | tf_op jit(solution)/shard_map/ppermute | solution.py:519
  49.5 8.9 %collective-permute-done.2 = bf16[2,145,768]{2,1,0:T(8,128)(2,1)} collective-permute-done((bf16[2,145,768]{2,1,0:T(8,128)(2,1)S(1)}, bf16[2,145,768]{2,1,0:T(8,128)(2,1)}, u32[]{:S(2)}, u32[]{:S(2)}) %collective-permute-start.2) | collective-permute-done | bytes 445472 | tf_op jit(solution)/shard_map/ppermute | solution.py:519
  65.0 87.7 %all-gather.2.cloned.1.call-done.w_hbm = bf16[864,128,128]{2,1,0:T(8,128)(2,1)} async-done(((bf16[108,128,128]{2,1,0:T(8,128)(2,1)}), bf16[864,128,128]{2,1,0:T(8,128)(2,1)}) %all-gather.2.cloned.1.call-update) | async-done | bytes 28311568 | tf_op jit(solution)/shard_map/all_gather | solution.py:704
  152.7 26.7 %forward_block.2 = (f32[592,768]{1,0:T(8,128)}, bf16[592,768]{1,0:T(8,128)(2,1)}, bf16[640,768]{1,0:T(8,128)(2,1)}, bf16[640,768]{1,0:T(8,128)(2,1)}, bf16[640,7...) custom-call(s32[432]{0:T(512)} %get-tuple-element.288.slots, ...), custom_call_target="tpu_custom_call" | custom-call | flops 8380219392 | bytes 41943040 | tf_op jit(solution)/shard_map/forward_block/pallas_call | solution.py:419
  179.4 27.2 %forward_block.3 = (f32[592,768]{1,0:T(8,128)}, bf16[592,768]{1,0:T(8,128)(2,1)}, bf16[640,768]{1,0:T(8,128)(2,1)}, bf16[640,768]{1,0:T(8,128)(2,1)}, bf16[640,7...) custom-call(s32[432]{0:T(512)} %get-tuple-element.287.slots, ...), custom_call_target="tpu_custom_call" | custom-call | flops 8380219392 | bytes 41943040 | tf_op jit(solution)/shard_map/forward_block/pallas_call | solution.py:419
  209.3 3.4 collective-permute-start.3
  217.4 56.9 %backward_block.2 = (f32[592,768]{1,0:T(8,128)}, f32[2,768]{1,0:T(2,128)}, bf16[288,128,128]{2,1,0:T(8,128)(2,1)}, bf16[96,128,128]{2,1,0:T(8,128)(2,1)}, bf16[9...) custom-call(s32[432]{0:T(512)} %get-tuple-element.286.places, ...), custom_call_target="tpu_custom_call" | custom-call | flops 22143565824 | bytes 62914560 | tf_op jit(solution)/shard_map/backward_block/pallas_call | solution.py:446
  275.1 57.0 %backward_block.3 = (f32[592,768]{1,0:T(8,128)}, f32[2,768]{1,0:T(2,128)}, bf16[288,128,128]{2,1,0:T(8,128)(2,1)}, bf16[96,128,128]{2,1,0:T(8,128)(2,1)}, bf16[9...) custom-call(s32[432]{0:T(512)} %get-tuple-element.285.places, ...), custom_call_target="tpu_custom_call", output_to_operand_aliasing={{3}: (21, {}), {4}: (22, {}), {5}: (23, {}), {6}: (24, {}),... | custom-call | flops 22143565824 | bytes 62914560 | tf_op jit(solution)/shard_map/backward_block/pallas_call | solution.py:446
  332.7 9.1 %collective-permute-done.7 = bf16[96,128,128]{2,1,0:T(8,128)(2,1)S(1)} collective-permute-done((bf16[96,128,128]{2,1,0:T(8,128)(2,1)}, bf16[96,128,128]{2,1,0:T(8,128)(2,1)S(1)}, u32[]{:S(2)}, u32[]{:S(2)}) %collective-permute-start.7) | collective-permute-done | bytes 3145760 | tf_op jit(solution)/shard_map/ppermute | solution.py:632
  347.0 5.8 reduce-scatter.3.cloned.1.call-done
  355.1 11.5 %collective-permute-done.8 = bf16[24,128,128]{2,1,0:T(8,128)(2,1)} collective-permute-done((bf16[24,128,128]{2,1,0:T(8,128)(2,1)}, bf16[24,128,128]{2,1,0:T(8,128)(2,1)}, u32[]{:S(2)}, u32[]{:S(2)}) %collective-permute-start.8) | collective-permute-done | bytes 786464 | tf_op jit(solution)/shard_map/ppermute | solution.py:639
  366.6 3.9 collective-permute-start.13
  376.1 6.3 %collective-permute-done.14 = bf16[12,128,128]{2,1,0:T(8,128)(2,1)S(1)} collective-permute-done((bf16[12,128,128]{2,1,0:T(8,128)(2,1)S(1)}, bf16[12,128,128]{2,1,0:T(8,128)(2,1)S(1)}, u32[]{:S(2)}, u32[]{:S(2)}) %collective-permute-start.14) | collective-permute-done | bytes 393248 | tf_op jit(solution)/shard_map/ppermute | solution.py:639
  385.9 9.9 %collective-permute-done.13 = bf16[37,128,128]{2,1,0:T(8,128)(2,1)S(1)} collective-permute-done((bf16[37,128,128]{2,1,0:T(8,128)(2,1)S(1)}, bf16[37,128,128]{2,1,0:T(8,128)(2,1)S(1)}, u32[]{:S(2)}, u32[]{:S(2)}) %collective-permute-start.13) | collective-permute-done | bytes 1212448 | tf_op jit(solution)/shard_map/ppermute | solution.py:592
  398.0 4.7 collective-permute-done.10
  404.0 4.9 collective-permute-start.21
  414.0 8.6 %collective-permute-done.21 = bf16[24,128,128]{2,1,0:T(8,128)(2,1)S(1)} collective-permute-done((bf16[24,128,128]{2,1,0:T(8,128)(2,1)S(1)}, bf16[24,128,128]{2,1,0:T(8,128)(2,1)S(1)}, u32[]{:S(2)}, u32[]{:S(2)}) %collective-permute-start.21) | collective-permute-done | bytes 786464 | tf_op jit(solution)/shard_map/ppermute | solution.py:592
  425.3 5.0 collective-permute-done.19
  434.3 4.4 collective-permute-start.24
  441.7 5.5 collective-permute-done.28
  454.0 9.9 %collective-permute-start.34 = (bf16[20,128,128]{2,1,0:T(8,128)(2,1)}, bf16[20,128,128]{2,1,0:T(8,128)(2,1)}, u32[]{:S(2)}, u32[]{:S(2)}) collective-permute-start(bf16[20,128,128]{2,1,0:T(8,128)(2,1)} %pad_maximum_fusion.4), channel_id=1, source_target_pairs={{2,1},{6,5},{10,9},{14,13},{18,17},{22,21},{26,25},{30,29}} | collective-permute-start | bytes 1966088 | tf_op jit(solution)/shard_map/ppermute | solution.py:592
  469.8 3.9 collective-permute-done.31
  481.1 15.8 %collective-permute-done.38 = bf16[28,128,128]{2,1,0:T(8,128)(2,1)} collective-permute-done((bf16[28,128,128]{2,1,0:T(8,128)(2,1)S(1)}, bf16[28,128,128]{2,1,0:T(8,128)(2,1)}, u32[]{:S(2)}, u32[]{:S(2)}) %collective-permute-start.38) | collective-permute-done | bytes 917536 | tf_op jit(solution)/shard_map/ppermute | solution.py:599
  509.3 7.1 %collective-permute-done.39 = bf16[28,128,128]{2,1,0:T(8,128)(2,1)} collective-permute-done((bf16[28,128,128]{2,1,0:T(8,128)(2,1)}, bf16[28,128,128]{2,1,0:T(8,128)(2,1)}, u32[]{:S(2)}, u32[]{:S(2)}) %collective-permute-start.39) | collective-permute-done | bytes 917536 | tf_op jit(solution)/shard_map/ppermute | solution.py:606
  517.8 5.7 collective-permute-done.40
  526.9 5.1 multiply_reduce_fusion
  547.4 4.1 collective-permute-start.44
  556.2 29.9 %optimizer.1 = (f32[108,128,128]{2,1,0:T(8,128)}, f32[108,2,128,128]{3,2,1,0:T(8,128)}, f32[108,128,128]{2,1,0:T(8,128)}, bf16[108,128,128]{2,1,0:T(8,128)(2,1)}) custom-call(f32[1]{0:T(128)} %bitcast.28.factor, s32[108]{0:T(128)} %dynamic-slice_reduce_fusion.rank, bf16[108,128,128]{2,1,0:T(8,128)(2,1)} %get-tuple-element.247.g_ref, f32[108,128,128]{2,1,0:T(8,128)} %m_ref.1, ...), custom_call_target="tpu_custom_call" | custom-call | tf_op jit(solution)/shard_map/optimizer/pallas_call | solution.py:495
  (244 shorter events, 123.0 us)
Async XLA Ops:
  7.2 145.5 %all-gather.2.cloned.1.call-start = ((), (), s32[]{:S(2)}) async-start(), calls=%async_computation.2 | async-start | bytes 31850496 | tf_op jit(solution)/shard_map/all_gather | solution.py:704
  12.9 340.0 %reduce-scatter.3.cloned.1.call-start = ((), (), s32[]{:S(2)}) async-start(), calls=%async_computation.3 | async-start | bytes 10616832 | tf_op jit(solution)/shard_map/reduce_scatter | solution.py:769
  15.4 25.6 %collective-permute-start = (bf16[2,145,768]{2,1,0:T(8,128)(2,1)}, bf16[2,145,768]{2,1,0:T(8,128)(2,1)}, u32[]{:S(2)}, u32[]{:S(2)}) collective-permute-start(bf16[2,145,768]{2,1,0:T(8,128)(2,1)} %get-tuple-element.270), channel_id=1, source_target_pairs={{0,1},{1,2},{3,0},{4,5},{5,6},{7,4},{8,9},{9,10},{11,8},{12,13},{1... | collective-permute-start | bytes 1336328 | tf_op jit(solution)/shard_map/ppermute | solution.py:519
  16.9 31.6 %collective-permute-start.1 = (bf16[2,145,768]{2,1,0:T(8,128)(2,1)S(1)}, bf16[2,145,768]{2,1,0:T(8,128)(2,1)}, u32[]{:S(2)}, u32[]{:S(2)}) collective-permute-start(bf16[2,145,768]{2,1,0:T(8,128)(2,1)S(1)} %get-tuple-element.269), channel_id=1, source_target_pairs={{0,2},{2,0},{3,1},{4,6},{6,4},{7,5},{8,10},{10,8},{11,9},{12,14},{... | collective-permute-start | bytes 1336328 | tf_op jit(solution)/shard_map/ppermute | solution.py:519
  21.3 37.1 %collective-permute-start.2 = (bf16[2,145,768]{2,1,0:T(8,128)(2,1)S(1)}, bf16[2,145,768]{2,1,0:T(8,128)(2,1)}, u32[]{:S(2)}, u32[]{:S(2)}) collective-permute-start(bf16[2,145,768]{2,1,0:T(8,128)(2,1)S(1)} %get-tuple-element.268), channel_id=1, source_target_pairs={{1,0},{2,1},{3,2},{5,4},{6,5},{7,6},{9,8},{10,9},{11,10},{13,12},{... | collective-permute-start | bytes 1336328 | tf_op jit(solution)/shard_map/ppermute | solution.py:519
  209.3 65.0 %collective-permute-start.3 = (bf16[145,768]{1,0:T(8,128)(2,1)S(1)}, bf16[145,768]{1,0:T(8,128)(2,1)S(1)}, u32[]{:S(2)}, u32[]{:S(2)}) collective-permute-start(bf16[145,768]{1,0:T(8,128)(2,1)S(1)} %get-tuple-element.278), channel_id=1, source_target_pairs={{0,1},{1,2},{2,3},{4,5},{5,6},{6,7},{8,9},{9,10},{10,11},{12,13},{... | collective-permute-start | bytes 668168 | tf_op jit(solution)/shard_map/ppermute | solution.py:530
  212.7 61.6 %collective-permute-start.4 = (bf16[145,768]{1,0:T(8,128)(2,1)S(1)}, bf16[145,768]{1,0:T(8,128)(2,1)S(1)}, u32[]{:S(2)}, u32[]{:S(2)}) collective-permute-start(bf16[145,768]{1,0:T(8,128)(2,1)S(1)} %get-tuple-element.277), channel_id=1, source_target_pairs={{0,2},{1,3},{2,0},{4,6},{5,7},{6,4},{8,10},{9,11},{10,8},{12,14},{... | collective-permute-start | bytes 668168 | tf_op jit(solution)/shard_map/ppermute | solution.py:530
  215.1 59.2 %collective-permute-start.5 = (bf16[145,768]{1,0:T(8,128)(2,1)S(1)}, bf16[145,768]{1,0:T(8,128)(2,1)S(1)}, u32[]{:S(2)}, u32[]{:S(2)}) collective-permute-start(bf16[145,768]{1,0:T(8,128)(2,1)S(1)} %get-tuple-element.276), channel_id=1, source_target_pairs={{0,3},{1,0},{2,1},{4,7},{5,4},{6,5},{8,11},{9,8},{10,9},{12,15},{1... | collective-permute-start | bytes 668168 | tf_op jit(solution)/shard_map/ppermute | solution.py:530
  332.2 41.6 %collective-permute-start.6 = (bf16[112,128,128]{2,1,0:T(8,128)(2,1)}, bf16[112,128,128]{2,1,0:T(8,128)(2,1)}, u32[]{:S(2)}, u32[]{:S(2)}) collective-permute-start(bf16[112,128,128]{2,1,0:T(8,128)(2,1)} %get-tuple-element.180), channel_id=1, source_target_pairs={{0,4},{4,0},{8,12},{12,8},{16,20},{20,16},{24,28},{28,24},{1,5},{5... | collective-permute-start | bytes 11010056 | tf_op jit(solution)/shard_map/ppermute | solution.py:632
  344.9 21.6 %collective-permute-start.8 = (bf16[24,128,128]{2,1,0:T(8,128)(2,1)}, bf16[24,128,128]{2,1,0:T(8,128)(2,1)}, u32[]{:S(2)}, u32[]{:S(2)}) collective-permute-start(bf16[24,128,128]{2,1,0:T(8,128)(2,1)} %get-tuple-element.259), channel_id=1, source_target_pairs={{0,8},{4,12},{8,0},{12,4},{16,24},{20,28},{24,16},{28,20},{1,9},{5... | collective-permute-start | bytes 2359304 | tf_op jit(solution)/shard_map/ppermute | solution.py:639
  346.4 24.1 %collective-permute-start.9 = (bf16[24,128,128]{2,1,0:T(8,128)(2,1)}, bf16[24,128,128]{2,1,0:T(8,128)(2,1)}, u32[]{:S(2)}, u32[]{:S(2)}) collective-permute-start(bf16[24,128,128]{2,1,0:T(8,128)(2,1)} %get-tuple-element.258), channel_id=1, source_target_pairs={{0,16},{4,20},{8,24},{12,28},{16,0},{20,4},{24,8},{28,12},{1,17},{... | collective-permute-start | bytes 2359304 | tf_op jit(solution)/shard_map/ppermute | solution.py:639
  346.9 63.7 %collective-permute-start.22 = (bf16[80,128,128]{2,1,0:T(8,128)(2,1)}, bf16[80,128,128]{2,1,0:T(8,128)(2,1)}, u32[]{:S(2)}, u32[]{:S(2)}) collective-permute-start(bf16[80,128,128]{2,1,0:T(8,128)(2,1)} %get-tuple-element.183), channel_id=1, source_target_pairs={{0,4},{4,0},{8,12},{12,8},{16,20},{20,16},{24,28},{28,24},{1,5},{5... | collective-permute-start | bytes 7864328 | tf_op jit(solution)/shard_map/ppermute | solution.py:632
  354.4 31.5 %collective-permute-start.12 = (bf16[37,128,128]{2,1,0:T(8,128)(2,1)S(1)}, bf16[37,128,128]{2,1,0:T(8,128)(2,1)S(1)}, u32[]{:S(2)}, u32[]{:S(2)}) collective-permute-start(bf16[37,128,128]{2,1,0:T(8,128)(2,1)S(1)} %pad_maximum_fusion.1), channel_id=1, source_target_pairs={{0,1},{4,5},{8,9},{12,13},{16,17},{20,21},{24,25},{28,29}} | collective-permute-start | bytes 3637256 | tf_op jit(solution)/shard_map/ppermute | solution.py:592
  366.6 29.3 %collective-permute-start.13 = (bf16[37,128,128]{2,1,0:T(8,128)(2,1)S(1)}, bf16[37,128,128]{2,1,0:T(8,128)(2,1)S(1)}, u32[]{:S(2)}, u32[]{:S(2)}) collective-permute-start(bf16[37,128,128]{2,1,0:T(8,128)(2,1)S(1)} %pad_maximum_fusion.1), channel_id=1, source_target_pairs={{2,1},{6,5},{10,9},{14,13},{18,17},{22,21},{26,25},{30,29}} | collective-permute-start | bytes 3637256 | tf_op jit(solution)/shard_map/ppermute | solution.py:592
  382.4 20.4 %collective-permute-start.10 = (bf16[28,128,128]{2,1,0:T(8,128)(2,1)S(1)}, bf16[28,128,128]{2,1,0:T(8,128)(2,1)S(1)}, u32[]{:S(2)}, u32[]{:S(2)}) collective-permute-start(bf16[28,128,128]{2,1,0:T(8,128)(2,1)S(1)} %get-tuple-element.253), channel_id=1, source_target_pairs={{0,8},{4,12},{8,0},{12,4},{16,24},{20,28},{24,16},{28,20},{1,9},{5... | collective-permute-start | bytes 2752520 | tf_op jit(solution)/shard_map/ppermute | solution.py:639
  383.9 20.2 %collective-permute-start.11 = (bf16[28,128,128]{2,1,0:T(8,128)(2,1)S(1)}, bf16[28,128,128]{2,1,0:T(8,128)(2,1)S(1)}, u32[]{:S(2)}, u32[]{:S(2)}) collective-permute-start(bf16[28,128,128]{2,1,0:T(8,128)(2,1)S(1)} %get-tuple-element.252), channel_id=1, source_target_pairs={{0,16},{4,20},{8,24},{12,28},{16,0},{20,4},{24,8},{28,12},{1,17},{... | collective-permute-start | bytes 2752520 | tf_op jit(solution)/shard_map/ppermute | solution.py:639
  396.4 27.6 %collective-permute-start.18 = (bf16[37,128,128]{2,1,0:T(8,128)(2,1)S(1)}, bf16[37,128,128]{2,1,0:T(8,128)(2,1)S(1)}, u32[]{:S(2)}, u32[]{:S(2)}) collective-permute-start(bf16[37,128,128]{2,1,0:T(8,128)(2,1)S(1)} %add_convert_fusion), channel_id=1, source_target_pairs={{1,0},{5,4},{9,8},{13,12},{17,16},{21,20},{25,24},{29,28}} | collective-permute-start | bytes 3637256 | tf_op jit(solution)/shard_map/ppermute | solution.py:599
  402.7 27.6 %collective-permute-start.19 = (bf16[37,128,128]{2,1,0:T(8,128)(2,1)S(1)}, bf16[37,128,128]{2,1,0:T(8,128)(2,1)S(1)}, u32[]{:S(2)}, u32[]{:S(2)}) collective-permute-start(bf16[37,128,128]{2,1,0:T(8,128)(2,1)S(1)} %add_convert_fusion), channel_id=1, source_target_pairs={{1,2},{5,6},{9,10},{13,14},{17,18},{21,22},{25,26},{29,30}} | collective-permute-start | bytes 3637256 | tf_op jit(solution)/shard_map/ppermute | solution.py:599
  410.6 21.2 %collective-permute-start.16 = (bf16[14,128,128]{2,1,0:T(8,128)(2,1)S(1)}, bf16[14,128,128]{2,1,0:T(8,128)(2,1)S(1)}, u32[]{:S(2)}, u32[]{:S(2)}) collective-permute-start(bf16[14,128,128]{2,1,0:T(8,128)(2,1)S(1)} %get-tuple-element.251), channel_id=1, source_target_pairs={{0,8},{4,12},{8,0},{12,4},{16,24},{20,28},{24,16},{28,20},{1,9},{5... | collective-permute-start | bytes 1376264 | tf_op jit(solution)/shard_map/ppermute | solution.py:639
  412.1 19.6 %collective-permute-start.17 = (bf16[14,128,128]{2,1,0:T(8,128)(2,1)S(1)}, bf16[14,128,128]{2,1,0:T(8,128)(2,1)S(1)}, u32[]{:S(2)}, u32[]{:S(2)}) collective-permute-start(bf16[14,128,128]{2,1,0:T(8,128)(2,1)S(1)} %get-tuple-element.250), channel_id=1, source_target_pairs={{0,16},{4,20},{8,24},{12,28},{16,0},{20,4},{24,8},{28,12},{1,17},{... | collective-permute-start | bytes 1376264 | tf_op jit(solution)/shard_map/ppermute | solution.py:639
  430.4 33.5 %collective-permute-start.25 = (bf16[37,128,128]{2,1,0:T(8,128)(2,1)S(1)}, bf16[37,128,128]{2,1,0:T(8,128)(2,1)S(1)}, u32[]{:S(2)}, u32[]{:S(2)}) collective-permute-start(bf16[37,128,128]{2,1,0:T(8,128)(2,1)S(1)} %collective-permute-done.19), channel_id=1, source_target_pairs={{2,3},{6,7},{10,11},{14,15},{18,19},{22,23},{26,27},{30,31}} | collective-permute-start | bytes 3637256 | tf_op jit(solution)/shard_map/ppermute | solution.py:606
  434.3 19.7 %collective-permute-start.24 = (bf16[28,128,128]{2,1,0:T(8,128)(2,1)S(1)}, bf16[28,128,128]{2,1,0:T(8,128)(2,1)S(1)}, u32[]{:S(2)}, u32[]{:S(2)}) collective-permute-start(bf16[28,128,128]{2,1,0:T(8,128)(2,1)S(1)} %pad_maximum_fusion.2), channel_id=1, source_target_pairs={{2,1},{6,5},{10,9},{14,13},{18,17},{22,21},{26,25},{30,29}} | collective-permute-start | bytes 2752520 | tf_op jit(solution)/shard_map/ppermute | solution.py:592
  448.7 25.0 %collective-permute-start.31 = (bf16[24,128,128]{2,1,0:T(8,128)(2,1)}, bf16[24,128,128]{2,1,0:T(8,128)(2,1)}, u32[]{:S(2)}, u32[]{:S(2)}) collective-permute-start(bf16[24,128,128]{2,1,0:T(8,128)(2,1)} %add_convert_fusion.4), channel_id=1, source_target_pairs={{1,2},{5,6},{9,10},{13,14},{17,18},{21,22},{25,26},{29,30}} | collective-permute-start | bytes 2359304 | tf_op jit(solution)/shard_map/ppermute | solution.py:599
  452.5 23.3 %collective-permute-start.33 = (bf16[20,128,128]{2,1,0:T(8,128)(2,1)}, bf16[20,128,128]{2,1,0:T(8,128)(2,1)}, u32[]{:S(2)}, u32[]{:S(2)}) collective-permute-start(bf16[20,128,128]{2,1,0:T(8,128)(2,1)} %pad_maximum_fusion.4), channel_id=1, source_target_pairs={{0,1},{4,5},{8,9},{12,13},{16,17},{20,21},{24,25},{28,29}} | collective-permute-start | bytes 1966088 | tf_op jit(solution)/shard_map/ppermute | solution.py:592
  454.0 21.8 %collective-permute-start.34 = (bf16[20,128,128]{2,1,0:T(8,128)(2,1)}, bf16[20,128,128]{2,1,0:T(8,128)(2,1)}, u32[]{:S(2)}, u32[]{:S(2)}) collective-permute-start(bf16[20,128,128]{2,1,0:T(8,128)(2,1)} %pad_maximum_fusion.4), channel_id=1, source_target_pairs={{2,1},{6,5},{10,9},{14,13},{18,17},{22,21},{26,25},{30,29}} | collective-permute-start | bytes 1966088 | tf_op jit(solution)/shard_map/ppermute | solution.py:592
  466.9 30.0 %collective-permute-start.38 = (bf16[28,128,128]{2,1,0:T(8,128)(2,1)S(1)}, bf16[28,128,128]{2,1,0:T(8,128)(2,1)}, u32[]{:S(2)}, u32[]{:S(2)}) collective-permute-start(bf16[28,128,128]{2,1,0:T(8,128)(2,1)S(1)} %add_convert_fusion.1), channel_id=1, source_target_pairs={{1,2},{5,6},{9,10},{13,14},{17,18},{21,22},{25,26},{29,30}} | collective-permute-start | bytes 2752520 | tf_op jit(solution)/shard_map/ppermute | solution.py:599
  473.7 33.1 %collective-permute-start.32 = (bf16[24,128,128]{2,1,0:T(8,128)(2,1)}, bf16[24,128,128]{2,1,0:T(8,128)(2,1)}, u32[]{:S(2)}, u32[]{:S(2)}) collective-permute-start(bf16[24,128,128]{2,1,0:T(8,128)(2,1)} %collective-permute-done.31), channel_id=1, source_target_pairs={{2,3},{6,7},{10,11},{14,15},{18,19},{22,23},{26,27},{30,31}} | collective-permute-start | bytes 2359304 | tf_op jit(solution)/shard_map/ppermute | solution.py:606
  478.3 24.0 %collective-permute-start.35 = (bf16[20,128,128]{2,1,0:T(8,128)(2,1)}, bf16[20,128,128]{2,1,0:T(8,128)(2,1)}, u32[]{:S(2)}, u32[]{:S(2)}) collective-permute-start(bf16[20,128,128]{2,1,0:T(8,128)(2,1)} %add_convert_fusion.7), channel_id=1, source_target_pairs={{1,0},{5,4},{9,8},{13,12},{17,16},{21,20},{25,24},{29,28}} | collective-permute-start | bytes 1966088 | tf_op jit(solution)/shard_map/ppermute | solution.py:599
  479.8 25.6 %collective-permute-start.36 = (bf16[20,128,128]{2,1,0:T(8,128)(2,1)}, bf16[20,128,128]{2,1,0:T(8,128)(2,1)}, u32[]{:S(2)}, u32[]{:S(2)}) collective-permute-start(bf16[20,128,128]{2,1,0:T(8,128)(2,1)} %add_convert_fusion.7), channel_id=1, source_target_pairs={{1,2},{5,6},{9,10},{13,14},{17,18},{21,22},{25,26},{29,30}} | collective-permute-start | bytes 1966088 | tf_op jit(solution)/shard_map/ppermute | solution.py:599
  547.4 39.3 %collective-permute-start.44 = (bf16[145,768]{1,0:T(8,128)(2,1)}, bf16[145,768]{1,0:T(8,128)(2,1)S(1)}, u32[]{:S(2)}, u32[]{:S(2)}) collective-permute-start(bf16[145,768]{1,0:T(8,128)(2,1)} %get-tuple-element.274), channel_id=1, source_target_pairs={{0,1},{1,2},{2,3},{4,5},{5,6},{6,7},{8,9},{9,10},{10,11},{12,13},{... | collective-permute-start | bytes 668168 | tf_op jit(solution)/shard_map/ppermute | solution.py:530
  551.5 35.3 %collective-permute-start.45 = (bf16[145,768]{1,0:T(8,128)(2,1)}, bf16[145,768]{1,0:T(8,128)(2,1)S(1)}, u32[]{:S(2)}, u32[]{:S(2)}) collective-permute-start(bf16[145,768]{1,0:T(8,128)(2,1)} %get-tuple-element.273), channel_id=1, source_target_pairs={{0,2},{1,3},{2,0},{4,6},{5,7},{6,4},{8,10},{9,11},{10,8},{12,14},{... | collective-permute-start | bytes 668168 | tf_op jit(solution)/shard_map/ppermute | solution.py:530
  553.4 33.4 %collective-permute-start.46 = (bf16[145,768]{1,0:T(8,128)(2,1)S(1)}, bf16[145,768]{1,0:T(8,128)(2,1)S(1)}, u32[]{:S(2)}, u32[]{:S(2)}) collective-permute-start(bf16[145,768]{1,0:T(8,128)(2,1)S(1)} %get-tuple-element.272), channel_id=1, source_target_pairs={{0,3},{1,0},{2,1},{4,7},{5,4},{6,5},{8,11},{9,8},{10,9},{12,15},{1... | collective-permute-start | bytes 668168 | tf_op jit(solution)/shard_map/ppermute | solution.py:530
  (49 other events, 535.1 us)
Sparse Core Ops, SparseCore 0:
  13.0 139.6 all-gather.1
  274.5 78.3 reduce-scatter.2
